TPU v7x, 32 devices: a whole 2x2x4 slice. The times are simulated.
32 devices in a mesh: grp: 4 (over z), rep: 8 (over y, x, core).
Axes of the slice: x: 2, y: 2, z: 4, core: 2. Of those that a mesh axis runs over, the one named last changes fastest.
Arguments:
- ids: int32 [32, 1024], P(('grp', 'rep')), may hold values from 0 to 30527
- lengths: int32 [32], P(('grp', 'rep')), may hold values from 256 to 1024, as said below
- picks: int32 [32, 128], P(('grp', 'rep')), may hold values from 0 to 1023, as said below
- labels: int32 [32, 128], P(('grp', 'rep')), may hold values from 0 to 30527
- loss_mask: int32 [32, 128], P(('grp', 'rep')), may hold values from 0 to 1, as said below
- table: float32 [30528, 768], P('grp')
- w_qkv: float32 [768, 2304], P('grp'), may hold values from -0.21875 to 0.21875
- w_out: float32 [768, 768], P('grp'), may hold values from -1.75 to 1.75
- w_gu: float32 [768, 6144], P('grp'), may hold values from -0.21875 to 0.21875
- w_down: float32 [3072, 768], P('grp'), may hold values from -0.109375 to 0.109375
- norms: float32 [6, 768], replicated
- table_rows: float32 [30528], P('grp')
- table_cols: float32 [768], replicated
- qkv_rows: float32 [768], P('grp')
- qkv_cols: float32 [2304], replicated
- out_rows: float32 [768], P('grp')
- out_cols: float32 [768], replicated
- gu_rows: float32 [768], P('grp')
- gu_cols: float32 [6144], replicated
- down_rows: float32 [3072], P('grp')
- down_cols: float32 [768], replicated
- norms_moment: float32 [6, 768], replicated
Outputs:
- loss_sum: float32 [], replicated
- loss_count: float32 [], replicated
- clip_norm: float32 [], replicated
- table_grad: float32 [30528, 768], P('grp')
- table_rows_new: float32 [30528], P('grp')
- table_cols_new: float32 [768], replicated
- table_new: float32 [30528, 768], P('grp')
- qkv_grad: float32 [768, 2304], P('grp')
- qkv_rows_new: float32 [768], P('grp')
- qkv_cols_new: float32 [2304], replicated
- qkv_new: float32 [768, 2304], P('grp')
- out_grad: float32 [768, 768], P('grp')
- out_rows_new: float32 [768], P('grp')
- out_cols_new: float32 [768], replicated
- out_new: float32 [768, 768], P('grp')
- gu_grad: float32 [768, 6144], P('grp')
- gu_rows_new: float32 [768], P('grp')
- gu_cols_new: float32 [6144], replicated
- gu_new: float32 [768, 6144], P('grp')
- down_grad: float32 [3072, 768], P('grp')
- down_rows_new: float32 [3072], P('grp')
- down_cols_new: float32 [768], replicated
- down_new: float32 [3072, 768], P('grp')
- norms_grad: float32 [6, 768], replicated
- norms_moment_new: float32 [6, 768], replicated
- norms_new: float32 [6, 768], replicated
Inputs may be any that keep to these rules, and one draw needn't show every extreme that they name: `lengths`: some sequence of every draw holds 1024 valid tokens and another 1024 // 4. `picks`: each pick lies below its sequence's length. `loss_mask`: the first pick of every sequence counts.
All inputs are finite; a program needn't handle non-finite values.
Results may differ from a plain program's by a relative error of at most 0.0035.
The roundings to bfloat16 on the way count: a program that leaves them out, or rounds other values in their place, can miss the bound.
Values may be sent and summed in bfloat16 or wider, within the bound.
No kernel may reach another device: no remote copies, remote signals or barrier semaphores. Data moves between devices by JAX's collectives and lax.ppermute only.
A program may use at most 384 MiB of HBM per device.

v0:
```python
import math

import jax
import jax.numpy as jnp
from jax import lax
from jax.sharding import PartitionSpec as P

HEADS = 12
HD = 64
STEP = 10


ln_eps = 1e-05
rope_base = 10000.0
clip_limit = 0.01
rate_matrix = 0.03
rate_norm = 0.3
neg_large = -1e30


def joined_2(value, axis, join):
    pieces = jax.tree.map(lambda part: lax.all_gather(part, axis), value)
    head = jax.tree.map(lambda part: part[0], pieces)
    tail = jax.tree.map(lambda part: part[1:], pieces)
    so_far, _ = lax.scan(lambda so_far, section: (join(so_far, section), None), head, tail)
    return so_far


def contract(left, right, left_dim, right_dim):
    return lax.dot_general(
        left, right, (((left_dim,), (right_dim,)), ((), ())), preferred_element_type=jnp.float32
    )


def layer_norm(values, gain, shift):
    center = values - jnp.mean(values, axis=-1, keepdims=True)
    spread = jnp.mean(center * center, axis=-1, keepdims=True)
    return center * lax.rsqrt(spread + ln_eps) * gain + shift


def rope_tables(length):
    freqs = rope_base ** (-jnp.arange(HD // 2, dtype=jnp.float32) * 2.0 / HD)
    angles = jnp.arange(length, dtype=jnp.float32)[:, None] * freqs[None, :]
    angles = jnp.concatenate([angles, angles], axis=-1)
    return (jnp.cos(angles)[:, None, :], jnp.sin(angles)[:, None, :])


def rotary(values, cosine, sine):
    half = values.shape[-1] // 2
    turned = jnp.concatenate([-values[..., half:], values[..., :half]], axis=-1)
    return values * cosine + turned * sine


def rotary_back(grads, cosine, sine):
    half = grads.shape[-1] // 2
    scaled = grads * sine
    turned = jnp.concatenate([scaled[..., half:], -scaled[..., :half]], axis=-1)
    return grads * cosine + turned


def swiglu(joined):
    middle = joined.shape[-1] // 2
    return jax.nn.silu(joined[:, :middle]) * joined[:, middle:]


def block_scores(query, keys, keep):
    scores = jnp.einsum(
        "qhd,khd->hqk", query, keys, preferred_element_type=jnp.float32
    ) / math.sqrt(HD)
    return jnp.where(keep[None, None, :], scores, neg_large)


def attention_forward(queries, keys, values, lengths, length):
    block_rows = min(512, length)

    def one_sequence(items):
        seq_q, seq_k, seq_v, size = items
        keep = jnp.arange(length) < size

        def one_block(query):
            scores = block_scores(query, seq_k, keep)
            peak = jnp.max(scores, axis=-1, keepdims=True)
            weights = jnp.exp(scores - peak)
            totals = jnp.sum(weights, axis=-1, keepdims=True)
            probs = (weights / totals).astype(jnp.bfloat16)
            result = jnp.einsum("hqk,khd->qhd", probs, seq_v, preferred_element_type=jnp.float32)
            return (result, (peak + jnp.log(totals))[..., 0])

        blocks = seq_q.reshape(-1, block_rows, HEADS, HD)
        result, log_sums = lax.map(one_block, blocks)
        return (result.reshape(length, HEADS, HD), log_sums)

    return lax.map(one_sequence, (queries, keys, values, lengths))


def attention_backward(queries, keys, values, mixed_grad, log_sums, lengths, length):
    block_rows = min(512, length)

    def one_sequence(items):
        seq_q, seq_k, seq_v, seq_d, seq_l, size = items
        keep = jnp.arange(length) < size

        def one_block(carry, block):
            query, dmixed, log_sum = block
            probs = jnp.exp(block_scores(query, seq_k, keep) - log_sum[..., None])
            dprobs = jnp.einsum("qhd,khd->hqk", dmixed, seq_v, preferred_element_type=jnp.float32)
            inner = jnp.sum(probs * dprobs, axis=-1, keepdims=True)
            dscore = (probs * (dprobs - inner)).astype(jnp.bfloat16)
            dquery = jnp.einsum(
                "hqk,khd->qhd", dscore, seq_k, preferred_element_type=jnp.float32
            ) / math.sqrt(HD)
            dkey = jnp.einsum(
                "hqk,qhd->khd", dscore, query, preferred_element_type=jnp.float32
            ) / math.sqrt(HD)
            dvalue = jnp.einsum(
                "hqk,qhd->khd",
                probs.astype(jnp.bfloat16),
                dmixed,
                preferred_element_type=jnp.float32,
            )
            return ((carry[0] + dkey, carry[1] + dvalue), dquery)

        zeros = jnp.zeros(seq_k.shape, jnp.float32)
        blocks = (
            seq_q.reshape(-1, block_rows, HEADS, HD),
            seq_d.reshape(-1, block_rows, HEADS, HD),
            seq_l,
        )
        (dkeys, dvalues), dqueries = lax.scan(one_block, (zeros, zeros), blocks)
        return (dqueries.reshape(length, HEADS, HD), dkeys, dvalues)

    return lax.map(one_sequence, (queries, keys, values, mixed_grad, log_sums, lengths))


def layer_forward(embed, weights, norms, lengths, seqs, length):
    w_qkv, w_out, w_gu, w_down = weights
    width = embed.shape[1]
    first = layer_norm(embed, norms[0], norms[1])
    first_low = first.astype(jnp.bfloat16)
    joined = jnp.dot(first_low, w_qkv, preferred_element_type=jnp.float32)
    cosine, sine = rope_tables(length)
    head_shape = (seqs, length, HEADS, HD)
    queries = rotary(joined[:, :width].reshape(head_shape), cosine, sine).astype(jnp.bfloat16)
    keys = rotary(joined[:, width : 2 * width].reshape(head_shape), cosine, sine).astype(
        jnp.bfloat16
    )
    values = joined[:, 2 * width :].reshape(head_shape).astype(jnp.bfloat16)
    mixed, log_sums = attention_forward(queries, keys, values, lengths, length)
    mixed_low = mixed.reshape(-1, width).astype(jnp.bfloat16)
    first_sum = first + jnp.dot(mixed_low, w_out, preferred_element_type=jnp.float32)
    second = layer_norm(first_sum, norms[2], norms[3])
    second_low = second.astype(jnp.bfloat16)
    gate_up = jnp.dot(second_low, w_gu, preferred_element_type=jnp.float32)
    hidden_low = swiglu(gate_up).astype(jnp.bfloat16)
    second_sum = second + jnp.dot(hidden_low, w_down, preferred_element_type=jnp.float32)
    final = layer_norm(second_sum, norms[4], norms[5])
    kept = (
        embed,
        first_low,
        queries,
        keys,
        values,
        log_sums,
        mixed_low,
        first_sum,
        second_low,
        gate_up,
        hidden_low,
        second_sum,
    )
    return (final, kept)


def layer_backward(final_grad, kept, weights, norms, lengths, seqs, length):
    (
        embed,
        first_low,
        queries,
        keys,
        values,
        log_sums,
        mixed_low,
        first_sum,
        second_low,
        gate_up,
        hidden_low,
        second_sum,
    ) = kept
    w_qkv, w_out, w_gu, w_down = weights
    width = embed.shape[1]
    _, pull = jax.vjp(layer_norm, second_sum, norms[4], norms[5])
    sum_grad, gain_three, shift_three = pull(final_grad)
    branch_low = sum_grad.astype(jnp.bfloat16)
    grad_down = contract(hidden_low, branch_low, 0, 0)
    hidden_grad = contract(branch_low, w_down, 1, 1)
    _, pull = jax.vjp(swiglu, gate_up)
    gate_low = pull(hidden_grad)[0].astype(jnp.bfloat16)
    grad_gu = contract(second_low, gate_low, 0, 0)
    second_grad = sum_grad + contract(gate_low, w_gu, 1, 1)
    _, pull = jax.vjp(layer_norm, first_sum, norms[2], norms[3])
    first_sum_grad, gain_two, shift_two = pull(second_grad)
    attn_low = first_sum_grad.astype(jnp.bfloat16)
    grad_out = contract(mixed_low, attn_low, 0, 0)
    mixed_grad = (
        contract(attn_low, w_out, 1, 1).astype(jnp.bfloat16).reshape(seqs, length, HEADS, HD)
    )
    query_grad, key_grad, value_grad = attention_backward(
        queries, keys, values, mixed_grad, log_sums, lengths, length
    )
    cosine, sine = rope_tables(length)
    joined_grad = jnp.concatenate(
        [
            rotary_back(query_grad, cosine, sine).reshape(-1, width),
            rotary_back(key_grad, cosine, sine).reshape(-1, width),
            value_grad.reshape(-1, width),
        ],
        axis=1,
    ).astype(jnp.bfloat16)
    grad_qkv = contract(first_low, joined_grad, 0, 0)
    first_grad = first_sum_grad + contract(joined_grad, w_qkv, 1, 1)
    _, pull = jax.vjp(layer_norm, embed, norms[0], norms[1])
    embed_grad, gain_one, shift_one = pull(first_grad)
    norm_grad = jnp.stack([gain_one, shift_one, gain_two, shift_two, gain_three, shift_three])
    return (embed_grad, (grad_qkv, grad_out, grad_gu, grad_down), norm_grad)


def merge_stats(first_part, second_part):
    peak = jnp.maximum(first_part[0], second_part[0])
    spread = first_part[1] * jnp.exp(first_part[0] - peak) + second_part[1] * jnp.exp(
        second_part[0] - peak
    )
    return (peak, spread, first_part[2] + second_part[2])


def body(
    ids,
    lengths,
    picks,
    labels,
    loss_mask,
    table,
    w_qkv,
    w_out,
    w_gu,
    w_down,
    norms,
    table_rows,
    table_cols,
    qkv_rows,
    qkv_cols,
    out_rows,
    out_cols,
    gu_rows,
    gu_cols,
    down_rows,
    down_cols,
    norms_moment,
):
    member = lax.axis_index("grp")
    groups = lax.axis_size("grp")
    seqs, length = ids.shape
    width = table.shape[1]
    vocab_rows = table.shape[0]
    pick_count = picks.shape[1]
    table_low = table.astype(jnp.bfloat16)
    group_ids, group_labels, group_mask = (
        lax.all_gather(ids, "grp", axis=0, tiled=True),
        lax.all_gather(labels, "grp", axis=0, tiled=True),
        lax.all_gather(loss_mask, "grp", axis=0, tiled=True),
    )
    local_ids = group_ids.reshape(-1) - member * vocab_rows
    owned = (local_ids >= 0) & (local_ids < vocab_rows)
    safe_ids = jnp.where(owned, local_ids, 0)
    found = jnp.where(owned[:, None], table_low[safe_ids].astype(jnp.float32), 0.0)
    embed = lax.psum_scatter(
        found.astype(jnp.bfloat16), "grp", scatter_dimension=0, tiled=True
    ).astype(jnp.float32)
    weights = (
        lax.all_gather(w_qkv.astype(jnp.bfloat16), "grp", axis=0, tiled=True),
        lax.all_gather(w_out.astype(jnp.bfloat16), "grp", axis=0, tiled=True),
        lax.all_gather(w_gu.astype(jnp.bfloat16), "grp", axis=0, tiled=True),
        lax.all_gather(w_down.astype(jnp.bfloat16), "grp", axis=0, tiled=True),
    )
    final, kept = layer_forward(embed, weights, norms, lengths, seqs, length)
    flat_picks = (jnp.arange(seqs, dtype=jnp.int32)[:, None] * length + picks).reshape(-1)
    chosen = final[flat_picks].astype(jnp.bfloat16)
    group_chosen = lax.all_gather(chosen, "grp", axis=0, tiled=True)
    logits = contract(group_chosen, table_low, 1, 1)
    peak = jnp.max(logits, axis=1)
    spread = jnp.sum(jnp.exp(logits - peak[:, None]), axis=1)
    local_labels = group_labels.reshape(-1) - member * vocab_rows
    hits = jnp.arange(vocab_rows, dtype=jnp.int32)[None, :] == local_labels[:, None]
    target = jnp.sum(jnp.where(hits, logits, 0.0), axis=1)
    peak_all, spread_all, target_all = joined_2((peak, spread, target), "grp", merge_stats)
    log_total = peak_all + jnp.log(spread_all)
    counted = group_mask.reshape(-1) > 0
    terms = jnp.where(counted, log_total - target_all, 0.0)
    own_rows = seqs * pick_count
    own_terms = lax.dynamic_slice_in_dim(terms, member * own_rows, own_rows)
    loss_sum, loss_count = lax.psum(
        (jnp.sum(own_terms), jnp.sum(loss_mask).astype(jnp.float32)), ("grp", "rep")
    )
    row_scale = jnp.where(counted, 1.0 / loss_count, 0.0)
    dlogits = (
        (jnp.exp(logits - log_total[:, None]) - hits.astype(jnp.float32)) * row_scale[:, None]
    ).astype(jnp.bfloat16)
    table_grad = contract(dlogits, group_chosen, 0, 0)
    chosen_part = jnp.dot(dlogits, table_low, preferred_element_type=jnp.float32)
    chosen_grad = lax.psum_scatter(chosen_part, "grp", scatter_dimension=0, tiled=True)
    final_grad = jnp.zeros((seqs * length, width), jnp.float32).at[flat_picks].add(chosen_grad)
    embed_grad, matrix_grads, norm_grad = layer_backward(
        final_grad, kept, weights, norms, lengths, seqs, length
    )
    group_embed = lax.all_gather(embed_grad.astype(jnp.bfloat16), "grp", axis=0, tiled=True)
    table_grad = table_grad + jnp.zeros_like(table_grad).at[safe_ids].add(
        jnp.where(owned[:, None], group_embed.astype(jnp.float32), 0.0)
    )
    qkv_part, out_part, gu_part, down_part = (
        lax.psum_scatter(matrix_grads[0], "grp", scatter_dimension=0, tiled=True),
        lax.psum_scatter(matrix_grads[1], "grp", scatter_dimension=0, tiled=True),
        lax.psum_scatter(matrix_grads[2], "grp", scatter_dimension=0, tiled=True),
        lax.psum_scatter(matrix_grads[3], "grp", scatter_dimension=0, tiled=True),
    )
    grads = lax.psum((table_grad, qkv_part, out_part, gu_part, down_part), "rep")
    norm_sum = lax.psum(norm_grad, ("grp", "rep"))
    masters = (table, w_qkv, w_out, w_gu, w_down)
    old_rows = (table_rows, qkv_rows, out_rows, gu_rows, down_rows)
    old_cols = (table_cols, qkv_cols, out_cols, gu_cols, down_cols)
    decay = 1.0 - float(STEP) ** (-0.8)
    norm_square = jnp.sum(norm_sum * norm_sum)
    local_square = sum((jnp.sum(gradient * gradient) for gradient in grads))
    clip_norm = jnp.sqrt(lax.psum(local_square, "grp") + norm_square)
    factor = clip_limit / jnp.maximum(clip_norm, clip_limit)
    clipped = [gradient * factor for gradient in grads]
    new_rows = [
        decay * rows + (1.0 - decay) * jnp.mean(gradient * gradient, axis=1)
        for rows, gradient in zip(old_rows, clipped)
    ]
    col_parts = [jnp.sum(gradient * gradient, axis=0) for gradient in clipped]
    row_parts = [jnp.sum(rows) for rows in new_rows]
    summed = lax.psum(
        (
            col_parts[0],
            col_parts[1],
            col_parts[2],
            col_parts[3],
            col_parts[4],
            row_parts[0],
            row_parts[1],
            row_parts[2],
            row_parts[3],
            row_parts[4],
        ),
        "grp",
    )
    col_totals = summed[:5]
    row_totals = summed[5:]
    outputs = []
    for place in range(5):
        full_rows = clipped[place].shape[0] * groups
        new_cols = decay * old_cols[place] + (1.0 - decay) * col_totals[place] / full_rows
        scale = new_rows[place][:, None] * new_cols[None, :] / (row_totals[place] / full_rows)
        new_master = masters[place] - rate_matrix * clipped[place] * lax.rsqrt(scale)
        outputs.extend([clipped[place], new_rows[place], new_cols, new_master])
    norm_clipped = norm_sum * factor
    moment_new = decay * norms_moment + (1.0 - decay) * norm_clipped * norm_clipped
    norms_new = norms - rate_norm * norm_clipped * lax.rsqrt(moment_new)
    return (
        (loss_sum, loss_count, clip_norm) + tuple(outputs) + (norm_clipped, moment_new, norms_new)
    )


def solution(mesh):
    in_specs = (
        P(("grp", "rep"), None),
        P(("grp", "rep")),
        P(("grp", "rep"), None),
        P(("grp", "rep"), None),
        P(("grp", "rep"), None),
        P("grp", None),
        P("grp", None),
        P("grp", None),
        P("grp", None),
        P("grp", None),
        P(),
        P("grp"),
        P(),
        P("grp"),
        P(),
        P("grp"),
        P(),
        P("grp"),
        P(),
        P("grp"),
        P(),
        P(),
    )
    out_specs = (
        P(),
        P(),
        P(),
        P("grp", None),
        P("grp"),
        P(),
        P("grp", None),
        P("grp", None),
        P("grp"),
        P(),
        P("grp", None),
        P("grp", None),
        P("grp"),
        P(),
        P("grp", None),
        P("grp", None),
        P("grp"),
        P(),
        P("grp", None),
        P("grp", None),
        P("grp"),
        P(),
        P("grp", None),
        P(),
        P(),
        P(),
    )
    return jax.shard_map(body, mesh=mesh, in_specs=in_specs, out_specs=out_specs, check_vma=False)
```

profile of v0, /device:TPU:1, one launch (start us, length us, event | category | flops | bytes accessed | tf_op | source)
XLA Modules:
  0.0 2311.9 jit_solution(5879023914083331855)
XLA Ops:
  31.8 24.9 %gather_fusion = bf16[4096,768]{1,0:T(8,128)(2,1)} fusion(bf16[7632,768]{1,0:T(8,128)(2,1)} %convert_element_type.98, s32[4096]{0:T(1024)S(1)} %broadcast_clamp_fusion), kind=kCustom, calls=%fused_computation | custom fusion | bytes 12599296 | tf_op jit(solution)/shard_map/gather | solution.py:274
  101.0 51.9 %psum.134 = f32[]{:T(128)} all-reduce(f32[]{:T(128)S(6)} %convert_element_type.115), channel_id=1, replica_groups=mesh['grp'=4,'rep'=8] {'grp','rep'}, use_global_device_ids=true, to_apply=%region_19.20 | all-reduce | flops 1 | bytes 8 | tf_op jit(solution)/shard_map/psum | solution.py:300
  160.8 28.6 %reduce-scatter.7.cloned.1.call-done = bf16[1024,768]{0,1:T(8,128)(2,1)} async-done(((bf16[4096,768]{0,1:T(8,128)(2,1)}), bf16[1024,768]{0,1:T(8,128)(2,1)}) %reduce-scatter.7.cloned.1.call-update) | async-done | bytes 1572880 | tf_op jit(solution)/shard_map/reduce_scatter | solution.py:275
  193.1 68.8 %all-gather.15.cloned.1.call-done = bf16[768,2304]{1,0:T(8,128)(2,1)} async-done(((bf16[192,2304]{1,0:T(8,128)(2,1)}), bf16[768,2304]{1,0:T(8,128)(2,1)}) %all-gather.15.cloned.1.call-update) | async-done | bytes 3538960 | tf_op jit(solution)/shard_map/all_gather | solution.py:279
  305.0 69.0 %while.63 = (s32[]{:T(128)}, bf16[2,512,12,64]{1,3,2,0:T(8,128)(2,1)}, f32[2,12,512]{2,1,0:T(8,128)S(1)}, bf16[2,512,12,64]{1,3,2,0:T(8,128)(2,1)S(1)}, bf16[102...) while((s32[]{:T(128)}, ...), condition=%wide.region_6.7_spmd.clone, body=%wide.region_3.6_spmd.clone.sunk | while | flops 1686105088 | bytes 87519864 | solution.py:90
  384.4 76.9 %all-gather.19.cloned.1.call-done = bf16[768,6144]{1,0:T(8,128)(2,1)} async-done(((bf16[192,6144]{1,0:T(8,128)(2,1)}), bf16[768,6144]{1,0:T(8,128)(2,1)}) %all-gather.19.cloned.1.call-update) | async-done | bytes 9437200 | tf_op jit(solution)/shard_map/all_gather | solution.py:281
  461.3 17.8 fusion.89
  492.1 58.1 %all-gather.21.cloned.1.call-done = bf16[3072,768]{1,0:T(8,128)(2,1)} async-done(((bf16[768,768]{1,0:T(8,128)(2,1)}), bf16[3072,768]{1,0:T(8,128)(2,1)}) %all-gather.21.cloned.1.call-update) | async-done | bytes 4718608 | tf_op jit(solution)/shard_map/all_gather | solution.py:282
  567.3 16.2 all_gather.51
  627.4 14.2 fusion.86
  641.7 43.0 %reduce-scatter.9.cloned.1.call-done = f32[128,768]{1,0:T(8,128)} async-done(((f32[512,768]{1,0:T(8,128)}), f32[128,768]{1,0:T(8,128)}) %reduce-scatter.9.cloned.1.call-update) | async-done | bytes 393232 | tf_op jit(solution)/shard_map/reduce_scatter | solution.py:309
  696.5 21.5 fusion.65
  718.0 19.5 multiply_reduce_fusion.8
  750.2 228.8 %while.64 = (s32[]{:T(128)}, f32[1024,12,64]{0,2,1:T(8,128)}, f32[1024,12,64]{0,2,1:T(8,128)}, f32[2,512,12,64]{1,0,3,2:T(2,128)}, bf16[2,512,12,64]{1,3,2,0:T(8...) while((s32[]{:T(128)}, f32[1024,12,64]{0,2,1:T(8,128)}, ...), condition=%wide.region_28.29_spmd.clone, body=%wide.region_26.28_spmd.clone.sunk | while | flops 4125223936 | bytes 229824208 | solution.py:129
  762.6 16.5 multiply_reduce_fusion.24
  779.1 21.4 multiply_convert_fusion.6
  813.2 28.7 %dynamic_update_slice.33 = f32[2,512,12,64]{1,0,3,2:T(2,128)} dynamic-update-slice(f32[2,512,12,64]{1,0,3,2:T(2,128)} %get-tuple-element.699, f32[1,512,12,64]{1,0,3,2:T(1,128)S(1)} %copy.161, s32[]{:T(128)} %get-tuple-element.696, s32[]{:T(128)} %constant.184.clone.1..sunk, s32[]{:T(128)} %constant.184.clone.1..sunk, s32[]{:T(128)} %constant.184.clone.1..sunk) | dynamic-update-slice | bytes 3145732 | tf_op jit(solution)/shard_map/while/body/eval_jaxpr/while/body/jit(dynamic_update_index_in_dim)/dynamic_update_slice | solution.py:90
  875.8 16.5 multiply_reduce_fusion.24
  892.3 21.4 multiply_convert_fusion.6
  926.4 28.7 %dynamic_update_slice.33 = f32[2,512,12,64]{1,0,3,2:T(2,128)} dynamic-update-slice(f32[2,512,12,64]{1,0,3,2:T(2,128)} %get-tuple-element.699, f32[1,512,12,64]{1,0,3,2:T(1,128)S(1)} %copy.161, s32[]{:T(128)} %get-tuple-element.696, s32[]{:T(128)} %constant.184.clone.1..sunk, s32[]{:T(128)} %constant.184.clone.1..sunk, s32[]{:T(128)} %constant.184.clone.1..sunk) | dynamic-update-slice | bytes 3145732 | tf_op jit(solution)/shard_map/while/body/eval_jaxpr/while/body/jit(dynamic_update_index_in_dim)/dynamic_update_slice | solution.py:90
  1034.0 23.6 %fusion.60 = f32[768,6144]{1,0:T(8,128)} fusion(f32[1024,3072]{1,0:T(8,128)} %get-tuple-element.447, f32[1024,3072]{1,0:T(8,128)} %get-tuple-element.446, f32[1024,768]{0,1:T(8,128)S(1)} %copy-done.10, f32[768]{0:T(1024)S(1)} %copy-done.54, f32[768]{0:T(1024)S(1)} %copy-done.50, f32[1024]{0:T(1024)S(1)} %copy-done.48, f32[1024]{0:T(1024)S(1)} %copy-done.46), kind=kOutput, calls=%fused_computation.128 | convolution fusion | flops 9680191488 | bytes 47200256 | tf_op jit(solution)/shard_map/dot_general | solution.py:30
  1058.8 19.6 fusion.87
  1078.4 41.5 %all-gather.23.cloned.1.call-done = bf16[4096,768]{0,1:T(8,128)(2,1)} async-done(((bf16[1024,768]{0,1:T(8,128)(2,1)}), bf16[4096,768]{0,1:T(8,128)(2,1)}) %all-gather.23.cloned.1.call-update) | async-done | bytes 6291472 | tf_op jit(solution)/shard_map/all_gather | solution.py:314
  1141.6 43.9 %scatter_fusion = f32[7632,768]{1,0:T(8,128)} fusion(f32[7632,768]{1,0:T(8,128)} %fusion.87, s32[4096]{0:T(1024)S(1)} %bitcast.201, f32[4096,768]{1,0:T(8,128)} %copy.96), kind=kCustom, calls=%fused_computation.3 | custom fusion | flops 3145728 | bytes 37765120 | tf_op jit(solution)/shard_map/scatter-add | solution.py:315
  1185.5 108.7 %reduce-scatter.11.cloned.1.call-done = f32[192,2304]{1,0:T(8,128)} async-done(((f32[768,2304]{1,0:T(8,128)}), f32[192,2304]{1,0:T(8,128)}) %reduce-scatter.11.cloned.1.call-update) | async-done | bytes 1769488 | tf_op jit(solution)/shard_map/reduce_scatter | solution.py:319
  1294.2 163.6 %reduce-scatter.17.cloned.1.call-done = f32[768,768]{1,0:T(8,128)} async-done(((f32[3072,768]{1,0:T(8,128)}), f32[768,768]{1,0:T(8,128)}) %reduce-scatter.17.cloned.1.call-update) | async-done | bytes 2359312 | tf_op jit(solution)/shard_map/reduce_scatter | solution.py:322
  1457.8 317.8 %reduce-scatter.15.cloned.1.call-done = f32[192,6144]{1,0:T(8,128)} async-done(((f32[768,6144]{1,0:T(8,128)}), f32[192,6144]{1,0:T(8,128)}) %reduce-scatter.15.cloned.1.call-update) | async-done | bytes 4718608 | tf_op jit(solution)/shard_map/reduce_scatter | solution.py:321
  1777.9 43.2 %all-reduce.2 = (f32[]{:T(128)}, f32[6,768]{1,0:T(8,128)S(1)}) all-reduce(f32[]{:T(128)} %dynamic-slice_reduce_fusion, f32[6,768]{1,0:T(8,128)S(1)} %stack.2), channel_id=1, replica_groups=mesh['grp'=4,'rep'=8] {'grp','rep'}, use_global_device_ids=true, to_apply=%region_17.18 | all-reduce | flops 4609 | bytes 36872 | tf_op jit(solution)/shard_map/psum | solution.py:300
  1821.1 358.3 %all-reduce.7.cloned.1.call-done = (f32[7632,768]{1,0:T(8,128)}, f32[192,2304]{1,0:T(8,128)}, f32[192,768]{1,0:T(8,128)}, f32[192,6144]{1,0:T(8,128)}, f32[768,768]{1,0:T(8,128)}) async-done(((f32[7632,768]{1,0:T(8,128)}, f32[192,2304]{1,0:T(8,128)}, f32[192,768]{1,0:T(8,128)}, f32[192,6144]{1,0:T(8,128)}, f32[768,768]{1,0:T(8,128)}), (f32[7632,768]{1,0:T(8,128)}, f32[192,2304]{1,0:T(8,128)}, ...) | async-done | bytes 32882704 | tf_op jit(solution)/shard_map/psum | solution.py:324
  2220.8 18.8 multiply_reduce_fusion.2
  2244.5 14.1 all-reduce.4
  2285.8 18.0 multiply_subtract_fusion
  (441 shorter events, 539.6 us)
Async XLA Ops:
  7.2 182.2 %reduce-scatter.7.cloned.1.call-start = ((), (), s32[]{:S(2)}) async-start(), calls=%async_computation.6 | async-start | bytes 7864320 | tf_op jit(solution)/shard_map/reduce_scatter | solution.py:275
  73.4 188.5 %all-gather.15.cloned.1.call-start = ((), (), s32[]{:S(2)}) async-start(), calls=%async_computation.7 | async-start | bytes 4423680 | tf_op jit(solution)/shard_map/all_gather | solution.py:279
  75.9 304.0 %all-gather.17.cloned.1.call-start = ((), (), s32[]{:S(2)}) async-start(), calls=%async_computation.8 | async-start | bytes 1474560 | tf_op jit(solution)/shard_map/all_gather | solution.py:280
  76.7 384.6 %all-gather.19.cloned.1.call-start = ((), (), s32[]{:S(2)}) async-start(), calls=%async_computation.9 | async-start | bytes 11796480 | tf_op jit(solution)/shard_map/all_gather | solution.py:281
  81.0 469.2 %all-gather.21.cloned.1.call-start = ((), (), s32[]{:S(2)}) async-start(), calls=%async_computation.10 | async-start | bytes 5898240 | tf_op jit(solution)/shard_map/all_gather | solution.py:282
  82.2 602.5 %reduce-scatter.9.cloned.1.call-start = ((), (), s32[]{:S(2)}) async-start(), calls=%async_computation.11 | async-start | bytes 1966080 | tf_op jit(solution)/shard_map/reduce_scatter | solution.py:309
  83.0 185.2 %copy-start.74 = (f32[768]{0:T(1024)}, f32[768]{0:T(1024)S(1)}, u32[]{:S(2)}) copy-start(f32[768]{0:T(1024)S(1)} %get-tuple-element.345) | copy-start | bytes 9220
  83.0 185.2 %copy-start.94 = (f32[768]{0:T(1024)}, f32[768]{0:T(1024)S(1)}, u32[]{:S(2)}) copy-start(f32[768]{0:T(1024)S(1)} %get-tuple-element.344) | copy-start | bytes 9220
  84.7 215.7 %copy-start.28 = (f32[1024,64]{0,1:T(8,128)}, f32[1024,64]{0,1:T(8,128)S(1)}, u32[]{:S(2)}) copy-start(f32[1024,64]{0,1:T(8,128)S(1)} %get-tuple-element.458) | copy-start | bytes 786436
  189.4 72.5 %copy-start.14 = (bf16[1024,768]{0,1:T(8,128)(2,1)S(1)}, bf16[1024,768]{0,1:T(8,128)(2,1)}, u32[]{:S(2)}) copy-start(bf16[1024,768]{0,1:T(8,128)(2,1)} %reduce-scatter.7.cloned.1.call-done) | copy-start | bytes 4718596
  191.2 77.0 %copy-start.62 = (f32[1024]{0:T(1024)}, f32[1024]{0:T(1024)S(1)}, u32[]{:S(2)}) copy-start(f32[1024]{0:T(1024)S(1)} %broadcast_multiply_fusion.10) | copy-start | bytes 12292
  193.1 75.2 %copy-start.69 = (f32[1024]{0:T(1024)}, f32[1024]{0:T(1024)S(1)}, u32[]{:S(2)}) copy-start(f32[1024]{0:T(1024)S(1)} %fusion.48) | copy-start | bytes 12292
  193.1 75.2 %copy-start.71 = (f32[1024]{0:T(1024)}, f32[1024]{0:T(1024)S(1)}, u32[]{:S(2)}) copy-start(f32[1024]{0:T(1024)S(1)} %fusion.75) | copy-start | bytes 12292
  384.0 95.2 %copy-start.8 = (f32[1024,768]{0,1:T(8,128)}, f32[1024,768]{0,1:T(8,128)S(1)}, u32[]{:S(2)}) copy-start(f32[1024,768]{0,1:T(8,128)S(1)} %get-tuple-element.464) | copy-start | bytes 9437188
  384.0 77.3 %copy-start.49 = (f32[768]{0:T(1024)S(1)}, f32[768]{0:T(1024)}, u32[]{:S(2)}) copy-start(f32[768]{0:T(1024)} %get-tuple-element.343) | copy-start | bytes 9220
  384.0 77.3 %copy-start.53 = (f32[768]{0:T(1024)S(1)}, f32[768]{0:T(1024)}, u32[]{:S(2)}) copy-start(f32[768]{0:T(1024)} %get-tuple-element.342) | copy-start | bytes 9220
  384.0 353.5 %copy-start.45 = (f32[1024]{0:T(1024)}, f32[1024]{0:T(1024)S(1)}, u32[]{:S(2)}) copy-start(f32[1024]{0:T(1024)S(1)} %broadcast_multiply_fusion.9) | copy-start | bytes 12292
  384.4 353.1 %copy-start.47 = (f32[1024]{0:T(1024)}, f32[1024]{0:T(1024)S(1)}, u32[]{:S(2)}) copy-start(f32[1024]{0:T(1024)S(1)} %fusion.76) | copy-start | bytes 12292
  593.2 33.6 %copy-start.101 = (pred[4,128]{1,0:T(4,128)(4,1)S(1)}, pred[4,128]{1,0:T(4,128)(4,1)}, u32[]{:S(2)}) copy-start(pred[4,128]{1,0:T(4,128)(4,1)} %compare_reduce_fusion) | copy-start | bytes 1540
  641.6 478.2 %all-gather.23.cloned.1.call-start = ((), (), s32[]{:S(2)}) async-start(), calls=%async_computation.12 | async-start | bytes 7864320 | tf_op jit(solution)/shard_map/all_gather | solution.py:314
  1005.0 180.5 %reduce-scatter.13.cloned.1.call-start = ((), (), s32[]{:S(2)}) async-start(), calls=%async_computation.14 | async-start | bytes 2949120 | tf_op jit(solution)/shard_map/reduce_scatter | solution.py:320
  1009.8 284.3 %reduce-scatter.11.cloned.1.call-start = ((), (), s32[]{:S(2)}) async-start(), calls=%async_computation.13 | async-start | bytes 8847360 | tf_op jit(solution)/shard_map/reduce_scatter | solution.py:319
  1019.9 437.8 %reduce-scatter.17.cloned.1.call-start = ((), (), s32[]{:S(2)}) async-start(), calls=%async_computation.16 | async-start | bytes 11796480 | tf_op jit(solution)/shard_map/reduce_scatter | solution.py:322
  1032.2 743.4 %reduce-scatter.15.cloned.1.call-start = ((), (), s32[]{:S(2)}) async-start(), calls=%async_computation.15 | async-start | bytes 23592960 | tf_op jit(solution)/shard_map/reduce_scatter | solution.py:321
  1057.7 62.2 %copy-start.68 = (pred[1,8,4,128]{3,1,2,0:T(8,128)(4,1)S(1)}, pred[1,8,4,128]{3,1,2,0:T(8,128)(4,1)}, u32[]{:S(2)}) copy-start(pred[1,8,4,128]{3,1,2,0:T(8,128)(4,1)} %copy-done.67) | copy-start | bytes 12292
  1057.7 1121.7 %all-reduce.7.cloned.1.call-start = ((), (), s32[]{:S(2)}) async-start(), calls=%async_computation.17 | async-start | bytes 65765376 | tf_op jit(solution)/shard_map/psum | solution.py:324
  1821.1 378.7 %copy-start.58 = (f32[6,768]{1,0:T(8,128)}, f32[6,768]{1,0:T(8,128)S(1)}, u32[]{:S(2)}) copy-start(f32[6,768]{1,0:T(8,128)S(1)} %get-tuple-element.396) | copy-start | bytes 55300
  2219.2 60.3 %copy-start.37 = (f32[192,768]{1,0:T(8,128)}, f32[192,768]{1,0:T(8,128)S(1)}, u32[]{:S(2)}) copy-start(f32[192,768]{1,0:T(8,128)S(1)} %get-tuple-element.425) | copy-start | bytes 1769476
  2220.7 22.6 copy-start.103
  2220.8 47.1 %copy-start.22 = (f32[768,768]{1,0:T(8,128)S(1)}, f32[768,768]{1,0:T(8,128)}, u32[]{:S(2)}) copy-start(f32[768,768]{1,0:T(8,128)} %get-tuple-element.419) | copy-start | bytes 7077892
  2220.8 58.8 %copy-start.36 = (f32[192,768]{1,0:T(8,128)S(1)}, f32[192,768]{1,0:T(8,128)}, u32[]{:S(2)}) copy-start(f32[192,768]{1,0:T(8,128)} %param.35) | copy-start | bytes 1769476
  2240.9 30.7 %copy-start.79 = (f32[768]{0:T(1024)}, f32[768]{0:T(1024)S(1)}, u32[]{:S(2)}) copy-start(f32[768]{0:T(1024)S(1)} %get-tuple-element.418) | copy-start | bytes 9220
  (96 other events, 672.0 us)
Sparse Core Ops, SparseCore 0:
  73.5 115.8 reduce-scatter.6
  191.5 70.3 all-gather.14
  264.1 28.4 all-gather.16
  294.6 166.6 all-gather.18
  462.7 87.4 all-gather.20
  641.8 42.9 reduce-scatter.8
  1005.1 114.6 all-gather.22
  1122.8 45.8 reduce-scatter.12
  1170.9 123.1 reduce-scatter.10
  1296.4 161.3 reduce-scatter.16
  1460.7 314.8 reduce-scatter.14
  1781.5 397.7 all-reduce.6
where the time goes:
time: 2330 us; the launch traced here: 2310 us
  waiting for transfers between devices  1270 us (55%)
  matrix products  342 us (15%)
  other arithmetic  305 us (13%)
  blocking collectives  191 us (8%)
  local copies, waits for them, and re-layouts  181 us (8%)
  between operations  25.9 us (1%)
    psum x1, waiting for transfers between devices, body(): lax.psum((table_grad, qkv_part, out_part, gu_part, down_part), 'rep')  358 us
    reduce_scatter x1, waiting for transfers between devices, body(): lax.psum_scatter(matrix_grads[2], 'grp', scatter_dimension=0, tiled=True)  318 us
    reduce_scatter x1, waiting for transfers between devices, body(): lax.psum_scatter(matrix_grads[3], 'grp', scatter_dimension=0, tiled=True)  164 us
    dot_general x10, matrix products, contract(): lax.dot_general(left, right, (((left_dim,), (right_dim,)), ((), ())), pre...  125 us
    reduce_scatter x1, waiting for transfers between devices, body(): lax.psum_scatter(matrix_grads[0], 'grp', scatter_dimension=0, tiled=True)  109 us
    psum x2, blocking collectives, body(): lax.psum((jnp.sum(own_terms), jnp.sum(loss_mask).astype(jnp.float32)), ('...  95.1 us
    all_gather x1, waiting for transfers between devices, body(): lax.all_gather(w_gu.astype(jnp.bfloat16), 'grp', axis=0, tiled=True)  76.9 us
    all_gather x1, waiting for transfers between devices, body(): lax.all_gather(w_qkv.astype(jnp.bfloat16), 'grp', axis=0, tiled=True)  68.8 us
  transfers between devices with their start and end apart: 12, of which 10 were waited for; matrix products, arithmetic and copies ran while one was open for 13% of the time, Pallas kernels for 0%

commit v1 on v0

--- a/solution.py
+++ b/solution.py
@@ -3,6 +3,8 @@
 import jax
 import jax.numpy as jnp
 from jax import lax
+from jax.experimental import pallas as pl
+from jax.experimental.pallas import tpu as pltpu
 from jax.sharding import PartitionSpec as P
 
 HEADS = 12
@@ -16,14 +18,145 @@
 rate_matrix = 0.03
 rate_norm = 0.3
 neg_large = -1e30
-
-
-def joined_2(value, axis, join):
-    pieces = jax.tree.map(lambda part: lax.all_gather(part, axis), value)
-    head = jax.tree.map(lambda part: part[0], pieces)
-    tail = jax.tree.map(lambda part: part[1:], pieces)
-    so_far, _ = lax.scan(lambda so_far, section: (join(so_far, section), None), head, tail)
-    return so_far
+low_type = jnp.bfloat16
+
+
+def flip(value, bit):
+    size = lax.axis_size("rep")
+    return lax.ppermute(value, "rep", [(i, i ^ bit) for i in range(size)])
+
+
+def turn(value, offset):
+    size = lax.axis_size("grp")
+    return lax.ppermute(value, "grp", [(i, (i + offset) % size) for i in range(size)])
+
+
+def blank(shape, dtype):
+    return pl.pallas_call(
+        lambda out_ref: None,
+        out_shape=jax.ShapeDtypeStruct(shape, dtype),
+        out_specs=pl.BlockSpec(memory_space=pl.ANY),
+    )()
+
+
+def replica_bits():
+    size = lax.axis_size("rep")
+    chip_bits = [1 << j for j in range(1, size.bit_length() - 1)]
+    middle = len(chip_bits) // 2
+    return chip_bits, chip_bits[middle:] + chip_bits[:middle]
+
+
+def spread(piece, order):
+    have = {0: piece}
+    for bit in order:
+        have.update({place ^ bit: flip(part, bit) for place, part in have.items()})
+    return have
+
+
+def plane_gather(piece):
+    replica = lax.axis_index("rep")
+    replicas = lax.axis_size("rep")
+    if replicas > 8:
+        return lax.all_gather(piece, "rep")
+    middle = piece.shape[-1] // 2
+    whole = blank((replicas,) + piece.shape, piece.dtype)
+    rest = (0,) * (piece.ndim - 1)
+    for column, part, order in zip(
+        (0, middle), (piece[..., :middle], piece[..., middle:]), reversed(replica_bits())
+    ):
+        for place, got in spread(part, order + [1]).items():
+            whole = lax.dynamic_update_slice(whole, got[None], (replica ^ place,) + rest + (column,))
+    return whole
+
+
+def fold(chunks, axis):
+    replica = lax.axis_index("rep")
+    size = lax.axis_size("rep")
+    if size > 8:
+        return lax.psum_scatter(chunks, "rep", scatter_dimension=axis)
+    left = [1 << j for j in reversed(range(size.bit_length() - 1))]
+    shape = chunks.shape
+    value = chunks.reshape(shape[:axis] + (2,) * len(left) + shape[axis + 1 :])
+
+    def run(value, left, bits):
+        left = list(left)
+        for bit in bits:
+            place = axis + left.index(bit)
+            mine = (replica // bit) % 2
+            sent = lax.dynamic_index_in_dim(value, 1 - mine, place, keepdims=False)
+            kept = lax.dynamic_index_in_dim(value, mine, place, keepdims=False)
+            value = kept + flip(sent.astype(low_type), bit).astype(jnp.float32)
+            left.remove(bit)
+        return value, left
+
+    value, left = run(value, left, [1])
+    first, second = replica_bits()
+    middle = shape[-1] // 2
+    one, _ = run(value[..., :middle], left, first)
+    two, _ = run(value[..., middle:], left, second)
+    return jnp.concatenate([one, two], axis=-1)
+
+
+def across(chunks):
+    member = lax.axis_index("grp")
+    size = lax.axis_size("grp")
+    total = lax.dynamic_index_in_dim(chunks, member, 0, keepdims=False)
+    for offset in range(1, size):
+        sent = lax.dynamic_index_in_dim(chunks, (member + offset) % size, 0, keepdims=False)
+        total = total + turn(sent.astype(low_type), offset).astype(jnp.float32)
+    return total
+
+
+def across_wide(chunks):
+    member = lax.axis_index("grp")
+    size = lax.axis_size("grp")
+    total = lax.dynamic_index_in_dim(chunks, member, 0, keepdims=False)
+    for offset in range(1, size):
+        sent = lax.dynamic_index_in_dim(chunks, (member + offset) % size, 0, keepdims=False)
+        total = total + turn(sent, offset)
+    return total
+
+
+def group_gather(value):
+    member = lax.axis_index("grp")
+    size = lax.axis_size("grp")
+    result = jnp.zeros((size,) + value.shape, value.dtype)
+    result = lax.dynamic_update_index_in_dim(result, value, member, 0)
+    for offset in range(1, size):
+        result = lax.dynamic_update_index_in_dim(
+            result, turn(value, offset), (member + size - offset) % size, 0
+        )
+    return result
+
+
+def weight_gather(shards):
+    member = lax.axis_index("grp")
+    groups = lax.axis_size("grp")
+    replica = lax.axis_index("rep")
+    replicas = lax.axis_size("rep")
+    if replicas > 8:
+        return [lax.all_gather(shard, "grp", tiled=True) for shard in shards]
+    results = []
+    first, _ = replica_bits()
+    for shard in shards:
+        rows, columns = shard.shape
+        part_rows = rows // replicas
+        parts = shard.reshape(replicas, part_rows, columns)
+        own = lax.dynamic_index_in_dim(parts, replica, 0, keepdims=False)
+        fetched = jnp.stack([turn(own, offset) for offset in range(1, groups)])
+        have = spread(fetched, first + [1])
+        whole = blank((groups, replicas, part_rows, columns), shard.dtype)
+        whole = lax.dynamic_update_index_in_dim(whole, parts, member, 0)
+        for place, piece in have.items():
+            slot = replica ^ place
+            for offset in range(1, groups):
+                whole = lax.dynamic_update_slice(
+                    whole,
+                    piece[offset - 1][None, None],
+                    ((member + groups - offset) % groups, slot, 0, 0),
+                )
+        results.append(whole.reshape(groups * rows, columns))
+    return results
 
 
 def contract(left, right, left_dim, right_dim):
@@ -171,6 +304,14 @@
     return (final, kept)
 
 
+def gradient_share(gradient):
+    groups = lax.axis_size("grp")
+    replicas = lax.axis_size("rep")
+    rows, columns = gradient.shape
+    chunks = gradient.reshape(groups, replicas, rows // (groups * replicas), columns)
+    return across(fold(chunks, 1))
+
+
 def layer_backward(final_grad, kept, weights, norms, lengths, seqs, length):
     (
         embed,
@@ -191,16 +332,16 @@
     _, pull = jax.vjp(layer_norm, second_sum, norms[4], norms[5])
     sum_grad, gain_three, shift_three = pull(final_grad)
     branch_low = sum_grad.astype(jnp.bfloat16)
-    grad_down = contract(hidden_low, branch_low, 0, 0)
+    grad_down = gradient_share(contract(hidden_low, branch_low, 0, 0))
     hidden_grad = contract(branch_low, w_down, 1, 1)
     _, pull = jax.vjp(swiglu, gate_up)
     gate_low = pull(hidden_grad)[0].astype(jnp.bfloat16)
-    grad_gu = contract(second_low, gate_low, 0, 0)
+    grad_gu = gradient_share(contract(second_low, gate_low, 0, 0))
     second_grad = sum_grad + contract(gate_low, w_gu, 1, 1)
     _, pull = jax.vjp(layer_norm, first_sum, norms[2], norms[3])
     first_sum_grad, gain_two, shift_two = pull(second_grad)
     attn_low = first_sum_grad.astype(jnp.bfloat16)
-    grad_out = contract(mixed_low, attn_low, 0, 0)
+    grad_out = gradient_share(contract(mixed_low, attn_low, 0, 0))
     mixed_grad = (
         contract(attn_low, w_out, 1, 1).astype(jnp.bfloat16).reshape(seqs, length, HEADS, HD)
     )
@@ -216,7 +357,7 @@
         ],
         axis=1,
     ).astype(jnp.bfloat16)
-    grad_qkv = contract(first_low, joined_grad, 0, 0)
+    grad_qkv = gradient_share(contract(first_low, joined_grad, 0, 0))
     first_grad = first_sum_grad + contract(joined_grad, w_qkv, 1, 1)
     _, pull = jax.vjp(layer_norm, embed, norms[0], norms[1])
     embed_grad, gain_one, shift_one = pull(first_grad)
@@ -258,110 +399,127 @@
 ):
     member = lax.axis_index("grp")
     groups = lax.axis_size("grp")
+    replica = lax.axis_index("rep")
+    replicas = lax.axis_size("rep")
     seqs, length = ids.shape
     width = table.shape[1]
     vocab_rows = table.shape[0]
     pick_count = picks.shape[1]
-    table_low = table.astype(jnp.bfloat16)
-    group_ids, group_labels, group_mask = (
-        lax.all_gather(ids, "grp", axis=0, tiled=True),
-        lax.all_gather(labels, "grp", axis=0, tiled=True),
-        lax.all_gather(loss_mask, "grp", axis=0, tiled=True),
-    )
-    local_ids = group_ids.reshape(-1) - member * vocab_rows
+    own_rows = seqs * pick_count
+    block = -(-vocab_rows // (16 * replicas)) * 16
+    padded = block * replicas
+
+    packed = jnp.concatenate([ids.reshape(-1), labels.reshape(-1), loss_mask.reshape(-1)])
+    group_packed = group_gather(packed)
+    tokens = seqs * length
+    group_ids = group_packed[:, :tokens].reshape(-1)
+    group_labels = group_packed[:, tokens : tokens + own_rows].reshape(-1)
+    group_mask = group_packed[:, tokens + own_rows :].reshape(-1)
+    loss_count = jnp.sum(group_mask).astype(jnp.float32)[None]
+    for j in range(replicas.bit_length() - 1):
+        loss_count = loss_count + flip(loss_count, 1 << j)
+    loss_count = loss_count[0]
+
+    table_low = jnp.pad(table.astype(jnp.bfloat16), ((0, padded - vocab_rows), (0, 0)))
+    local_ids = group_ids - member * vocab_rows
     owned = (local_ids >= 0) & (local_ids < vocab_rows)
     safe_ids = jnp.where(owned, local_ids, 0)
-    found = jnp.where(owned[:, None], table_low[safe_ids].astype(jnp.float32), 0.0)
+    found = jnp.where(owned[:, None], table[safe_ids], 0.0)
     embed = lax.psum_scatter(
         found.astype(jnp.bfloat16), "grp", scatter_dimension=0, tiled=True
     ).astype(jnp.float32)
-    weights = (
-        lax.all_gather(w_qkv.astype(jnp.bfloat16), "grp", axis=0, tiled=True),
-        lax.all_gather(w_out.astype(jnp.bfloat16), "grp", axis=0, tiled=True),
-        lax.all_gather(w_gu.astype(jnp.bfloat16), "grp", axis=0, tiled=True),
-        lax.all_gather(w_down.astype(jnp.bfloat16), "grp", axis=0, tiled=True),
+    weights = weight_gather(
+        [
+            w_qkv.astype(jnp.bfloat16),
+            w_out.astype(jnp.bfloat16),
+            w_gu.astype(jnp.bfloat16),
+            w_down.astype(jnp.bfloat16),
+        ]
     )
     final, kept = layer_forward(embed, weights, norms, lengths, seqs, length)
     flat_picks = (jnp.arange(seqs, dtype=jnp.int32)[:, None] * length + picks).reshape(-1)
     chosen = final[flat_picks].astype(jnp.bfloat16)
-    group_chosen = lax.all_gather(chosen, "grp", axis=0, tiled=True)
-    logits = contract(group_chosen, table_low, 1, 1)
+    group_chosen = group_gather(chosen).reshape(groups * own_rows, width)
+    places = jnp.arange(padded, dtype=jnp.int32)[None, :]
+    logits = jnp.where(places < vocab_rows, contract(group_chosen, table_low, 1, 1), neg_large)
     peak = jnp.max(logits, axis=1)
-    spread = jnp.sum(jnp.exp(logits - peak[:, None]), axis=1)
-    local_labels = group_labels.reshape(-1) - member * vocab_rows
-    hits = jnp.arange(vocab_rows, dtype=jnp.int32)[None, :] == local_labels[:, None]
+    spread_sum = jnp.sum(jnp.exp(logits - peak[:, None]), axis=1)
+    local_labels = group_labels - member * vocab_rows
+    inside = (local_labels >= 0) & (local_labels < vocab_rows)
+    hits = (places == local_labels[:, None]) & inside[:, None]
     target = jnp.sum(jnp.where(hits, logits, 0.0), axis=1)
-    peak_all, spread_all, target_all = joined_2((peak, spread, target), "grp", merge_stats)
+    stats = group_gather(jnp.stack([peak, spread_sum, target]))
+    so_far = (stats[0, 0], stats[0, 1], stats[0, 2])
+    for place in range(1, groups):
+        so_far = merge_stats(so_far, (stats[place, 0], stats[place, 1], stats[place, 2]))
+    peak_all, spread_all, target_all = so_far
     log_total = peak_all + jnp.log(spread_all)
-    counted = group_mask.reshape(-1) > 0
+    counted = group_mask > 0
     terms = jnp.where(counted, log_total - target_all, 0.0)
-    own_rows = seqs * pick_count
     own_terms = lax.dynamic_slice_in_dim(terms, member * own_rows, own_rows)
-    loss_sum, loss_count = lax.psum(
-        (jnp.sum(own_terms), jnp.sum(loss_mask).astype(jnp.float32)), ("grp", "rep")
-    )
     row_scale = jnp.where(counted, 1.0 / loss_count, 0.0)
     dlogits = (
         (jnp.exp(logits - log_total[:, None]) - hits.astype(jnp.float32)) * row_scale[:, None]
     ).astype(jnp.bfloat16)
+    chosen_part = jnp.dot(dlogits, table_low, preferred_element_type=jnp.float32)
+    chosen_grad = across_wide(chosen_part.reshape(groups, own_rows, width))
     table_grad = contract(dlogits, group_chosen, 0, 0)
-    chosen_part = jnp.dot(dlogits, table_low, preferred_element_type=jnp.float32)
-    chosen_grad = lax.psum_scatter(chosen_part, "grp", scatter_dimension=0, tiled=True)
     final_grad = jnp.zeros((seqs * length, width), jnp.float32).at[flat_picks].add(chosen_grad)
     embed_grad, matrix_grads, norm_grad = layer_backward(
         final_grad, kept, weights, norms, lengths, seqs, length
     )
     group_embed = lax.all_gather(embed_grad.astype(jnp.bfloat16), "grp", axis=0, tiled=True)
-    table_grad = table_grad + jnp.zeros_like(table_grad).at[safe_ids].add(
+    table_grad = table_grad.at[safe_ids].add(
         jnp.where(owned[:, None], group_embed.astype(jnp.float32), 0.0)
     )
-    qkv_part, out_part, gu_part, down_part = (
-        lax.psum_scatter(matrix_grads[0], "grp", scatter_dimension=0, tiled=True),
-        lax.psum_scatter(matrix_grads[1], "grp", scatter_dimension=0, tiled=True),
-        lax.psum_scatter(matrix_grads[2], "grp", scatter_dimension=0, tiled=True),
-        lax.psum_scatter(matrix_grads[3], "grp", scatter_dimension=0, tiled=True),
-    )
-    grads = lax.psum((table_grad, qkv_part, out_part, gu_part, down_part), "rep")
-    norm_sum = lax.psum(norm_grad, ("grp", "rep"))
-    masters = (table, w_qkv, w_out, w_gu, w_down)
+    shares = (fold(table_grad.reshape(replicas, block, width), 0),) + matrix_grads
+
     old_rows = (table_rows, qkv_rows, out_rows, gu_rows, down_rows)
     old_cols = (table_cols, qkv_cols, out_cols, gu_cols, down_cols)
+    masters = (table, w_qkv, w_out, w_gu, w_down)
+    col_parts = [jnp.sum(gradient * gradient, axis=0) for gradient in shares]
+    row_old = jnp.stack([jnp.sum(rows) for rows in old_rows]) / replicas
+    small = [norm_grad.reshape(-1)] + col_parts + [row_old, jnp.sum(own_terms)[None]]
+    totals = lax.psum(jnp.concatenate(small), ("grp", "rep"))
+    cuts = []
+    start = 0
+    for part in small:
+        cuts.append(totals[start : start + part.shape[0]])
+        start += part.shape[0]
+    norm_sum = cuts[0].reshape(norm_grad.shape)
+    col_totals = cuts[1:6]
+    old_totals = cuts[6]
+    loss_sum = cuts[7][0]
+    squares = [jnp.sum(part) for part in col_totals]
+    clip_norm = jnp.sqrt(sum(squares) + jnp.sum(norm_sum * norm_sum))
+    factor = clip_limit / jnp.maximum(clip_norm, clip_limit)
+    factor_square = factor * factor
     decay = 1.0 - float(STEP) ** (-0.8)
-    norm_square = jnp.sum(norm_sum * norm_sum)
-    local_square = sum((jnp.sum(gradient * gradient) for gradient in grads))
-    clip_norm = jnp.sqrt(lax.psum(local_square, "grp") + norm_square)
-    factor = clip_limit / jnp.maximum(clip_norm, clip_limit)
-    clipped = [gradient * factor for gradient in grads]
-    new_rows = [
-        decay * rows + (1.0 - decay) * jnp.mean(gradient * gradient, axis=1)
-        for rows, gradient in zip(old_rows, clipped)
-    ]
-    col_parts = [jnp.sum(gradient * gradient, axis=0) for gradient in clipped]
-    row_parts = [jnp.sum(rows) for rows in new_rows]
-    summed = lax.psum(
-        (
-            col_parts[0],
-            col_parts[1],
-            col_parts[2],
-            col_parts[3],
-            col_parts[4],
-            row_parts[0],
-            row_parts[1],
-            row_parts[2],
-            row_parts[3],
-            row_parts[4],
-        ),
-        "grp",
-    )
-    col_totals = summed[:5]
-    row_totals = summed[5:]
+
+    lows = [share.astype(low_type) for share in shares]
+    wholes = [plane_gather(low) for low in lows]
+    wholes = [whole.reshape(replicas * whole.shape[1], whole.shape[2]) for whole in wholes]
+    wholes[0] = wholes[0][:vocab_rows]
+
     outputs = []
     for place in range(5):
-        full_rows = clipped[place].shape[0] * groups
-        new_cols = decay * old_cols[place] + (1.0 - decay) * col_totals[place] / full_rows
-        scale = new_rows[place][:, None] * new_cols[None, :] / (row_totals[place] / full_rows)
-        new_master = masters[place] - rate_matrix * clipped[place] * lax.rsqrt(scale)
-        outputs.extend([clipped[place], new_rows[place], new_cols, new_master])
+        gradient = wholes[place].astype(jnp.float32)
+        rows, columns = gradient.shape
+        full_rows = rows * groups
+        new_cols = (
+            decay * old_cols[place]
+            + (1.0 - decay) * factor_square * col_totals[place] / full_rows
+        )
+        new_rows = decay * old_rows[place] + (1.0 - decay) * factor_square * jnp.mean(
+            gradient * gradient, axis=1
+        )
+        row_total = (
+            decay * old_totals[place] + (1.0 - decay) * factor_square * squares[place] / columns
+        )
+        clipped = gradient * factor
+        scale = new_rows[:, None] * new_cols[None, :] / (row_total / full_rows)
+        new_master = masters[place] - rate_matrix * clipped * lax.rsqrt(scale)
+        outputs.extend([clipped, new_rows, new_cols, new_master])
     norm_clipped = norm_sum * factor
     moment_new = decay * norms_moment + (1.0 - decay) * norm_clipped * norm_clipped
     norms_new = norms - rate_norm * norm_clipped * lax.rsqrt(moment_new)

time: 2330 us -> 1560 us (0.67)
  waiting for transfers between devices: 1270 us -> 318 us
  starting transfers between devices: 1.12 us -> 192 us
  blocking collectives: 191 us -> 45.4 us
  local copies, waits for them, and re-layouts: 181 us -> 323 us
  matrix products: 342 us -> 314 us
    reduce_scatter x5 -> x0, waiting for transfers between devices: 633 us -> none  [the longest x1 318 us: body(): lax.psum_scatter(matrix_grads[2], 'grp', scatter_dimension=0, tiled=True)]
    psum x1 -> x0, waiting for transfers between devices: 358 us -> none  [body(): lax.psum((table_grad, qkv_part, out_part, gu_part, down_part), 'rep')]
    ppermute x0 -> x162, waiting for transfers between devices: none -> 318 us  [the longest x126 229 us: flip(): return lax.ppermute(value, 'rep', [(i, i ^ bit) for i in range(size)])]
    all_gather x4 -> x0, waiting for transfers between devices: 204 us -> none  [the longest x1 76.9 us: body(): lax.all_gather(w_gu.astype(jnp.bfloat16), 'grp', axis=0, tiled=True)]
    ppermute x0 -> x162, starting transfers between devices: none -> 192 us  [the longest x126 110 us: flip(): return lax.ppermute(value, 'rep', [(i, i ^ bit) for i in range(size)])]
    dynamic_update_slice x0 -> x191, local copies, waits for them, and re-layouts: none -> 101 us  [the longest x96 53.3 us: weight_gather(): lax.dynamic_update_slice(whole, piece[offset - 1][None, None], ((member +...]
    psum x4 -> x1, blocking collectives: 119 us -> 45.4 us  [body(): totals = lax.psum(jnp.concatenate(small), ('grp', 'rep'))]
    all_gather x7 -> x0, blocking collectives: 71.3 us -> none  [the longest x3 27.8 us: joined_2(): pieces = jax.tree.map(lambda part: lax.all_gather(part, axis), value)]
  transfers between devices with their start and end apart: 12 -> 164, of which waited for: 10 -> 71; matrix products, arithmetic and copies ran while one was open for 13% -> 39% of each run, Pallas kernels for 0% -> 0%
where the time goes in v1:
time: 1560 us; the launch traced here: 1550 us
  local copies, waits for them, and re-layouts  323 us (21%)
  other arithmetic  322 us (21%)
  waiting for transfers between devices  318 us (20%)
  matrix products  314 us (20%)
  starting transfers between devices  192 us (12%)
  blocking collectives  45.4 us (3%)
  between operations  32.7 us (2%)
    ppermute x126, waiting for transfers between devices, flip(): return lax.ppermute(value, 'rep', [(i, i ^ bit) for i in range(size)])  229 us
    ppermute x126, starting transfers between devices, flip(): return lax.ppermute(value, 'rep', [(i, i ^ bit) for i in range(size)])  110 us
    dot_general x10, matrix products, contract(): lax.dot_general(left, right, (((left_dim,), (right_dim,)), ((), ())), pre...  103 us
    ppermute x36, waiting for transfers between devices, turn(): lax.ppermute(value, 'grp', [(i, (i + offset) % size) for i in range(size)])  89.6 us
    ppermute x36, starting transfers between devices, turn(): lax.ppermute(value, 'grp', [(i, (i + offset) % size) for i in range(size)])  82.5 us
    dynamic_update_slice x4, local copies, waits for them, and re-layouts, one_sequence(): result, log_sums = lax.map(one_block, blocks)  63.4 us
    dynamic_update_slice x96, local copies, waits for them, and re-layouts, weight_gather(): lax.dynamic_update_slice(whole, piece[offset - 1][None, None], ((member +...  53.3 us
    psum x1, blocking collectives, body(): totals = lax.psum(jnp.concatenate(small), ('grp', 'rep'))  45.4 us
  transfers between devices with their start and end apart: 164, of which 71 were waited for; matrix products, arithmetic and copies ran while one was open for 39% of the time, Pallas kernels for 0%

profile of v1, /device:TPU:1, one launch (start us, length us, event | category | flops | bytes accessed | tf_op | source)
XLA Modules:
  0.0 1549.4 jit_solution(4119750639889819121)
XLA Ops:
  46.8 12.4 convert_element_type.495
  64.4 26.7 %gather_fusion = bf16[4096,768]{1,0:T(8,128)(2,1)} fusion(f32[7632,768]{1,0:T(8,128)} %param.31, s32[4096]{0:T(1024)S(1)} %broadcast_clamp_fusion), kind=kCustom, calls=%fused_computation | custom fusion | bytes 12599296 | tf_op jit(solution)/shard_map/gather | solution.py:427
  219.8 22.6 %collective-permute-done.8 = bf16[3,24,2304]{2,1,0:T(8,128)(2,1)S(1)} collective-permute-done((bf16[3,24,2304]{2,1,0:T(8,128)(2,1)S(1)}, bf16[3,24,2304]{2,1,0:T(8,128)(2,1)S(1)}, u32[]{:S(2)}, u32[]{:S(2)}) %collective-permute-start.8) | collective-permute-done | bytes 331808 | tf_op jit(solution)/shard_map/ppermute | solution.py:26
  277.6 12.4 collective-permute-done.28
  346.5 70.1 %while.48 = (s32[]{:T(128)}, bf16[2,512,12,64]{1,3,2,0:T(8,128)(2,1)}, f32[2,12,512]{2,1,0:T(8,128)}, bf16[2,512,12,64]{1,3,2,0:T(8,128)(2,1)S(1)}, bf16[1024,12...) while((s32[]{:T(128)}, ...), condition=%wide.region_6.7_spmd.clone, body=%wide.region_3.6_spmd.clone.sunk | while | flops 1686105088 | bytes 87503992 | solution.py:223
  369.6 12.0 bitcast_dynamic-update-slice_fusion.65
  404.6 12.0 bitcast_dynamic-update-slice_fusion.65
  424.0 18.1 %fusion.258 = f32[1024,6144]{1,0:T(8,128)} fusion(bf16[768,6144]{1,0:T(8,128)(2,1)} %bitcast.105, f32[1024,768]{0,1:T(8,128)S(1)} %get-tuple-element.436, f32[768]{0:T(1024)S(1)} %copy-done.64, f32[768]{0:T(1024)S(1)} %copy-done.62, f32[1024]{0:T(1024)S(1)} %fusion.238, f32[1024]{0:T(1024)S(1)} %broadcast_multiply_fusion.7), kind=kOutput, calls=%fused_computation.719 | convolution fusion | flops 9667608576 | bytes 37763072 | tf_op jit(solution)/shard_map/dot_general | solution.py:286
  521.8 12.1 fusion.40
  550.0 12.1 collective-permute-done.53
  583.0 20.4 %fusion.83 = (f32[1024,3072]{1,0:T(8,128)}, f32[1024,3072]{1,0:T(8,128)}) fusion(f32[1024,6144]{1,0:T(8,128)} %fusion.258, bf16[3072,768]{1,0:T(8,128)(2,1)} %bitcast.136, f32[1024,768]{0,1:T(8,128)S(1)} %get-tuple-element.349, f32[1024]{0:T(1024)S(1)} %negate_multiply_fusion.2), kind=kOutput, calls=%fused_computation.192 | convolution fusion | flops 4871159808 | bytes 58200064 | tf_op jit(solution)/shard_map/dot_general | solution.py:163
  603.4 23.5 %fusion.72 = f32[768,6144]{1,0:T(8,128)} fusion(f32[1024,3072]{1,0:T(8,128)} %get-tuple-element.357, f32[1024,3072]{1,0:T(8,128)} %get-tuple-element.356, f32[1024,768]{0,1:T(8,128)S(1)} %copy-done.10, f32[768]{0:T(1024)S(1)} %copy-done.64, f32[768]{0:T(1024)S(1)} %copy-done.62, f32[1024]{0:T(1024)S(1)} %fusion.238, f32[1024]{0:T(1024)S(1)} %broadcast_multiply_fusion.7), kind=kOutput, calls=%fused_computation.168 | convolution fusion | flops 9680191488 | bytes 47200256 | tf_op jit(solution)/shard_map/dot_general | solution.py:163
  626.8 19.5 %multiply_reduce_fusion.2 = (f32[768]{0:T(1024)}, f32[1024]{0:T(1024)S(1)}, f32[768]{0:T(1024)}, f32[1024,768]{0,1:T(8,128)}) fusion(f32[1024,768]{0,1:T(8,128)S(1)} %copy-done.10, f32[1024]{0:T(1024)S(1)} %fusion.238, f32[1024]{0:T(1024)S(1)} %broadcast_multiply_fusion.7, f32[768]{0:T(1024)S(1)} %copy-done.62, bf16[768,6144]{1,0:T(8,128)(2,1)} %bitcast.105, ...), kind=kOutput, calls=%fused_computation.126 | convolution fusion | flops 9684120576 | bytes 44065792 | tf_op jit(solution)/shard_map/dot_general | solution.py:163
  678.3 229.3 %while.49 = (s32[]{:T(128)}, f32[1024,12,64]{0,2,1:T(8,128)}, f32[1024,12,64]{0,2,1:T(8,128)}, f32[2,512,12,64]{1,0,3,2:T(2,128)}, bf16[2,512,12,64]{1,3,2,0:T(8...) while((s32[]{:T(128)}, f32[1024,12,64]{0,2,1:T(8,128)}, ...), condition=%wide.region_22.23_spmd.clone, body=%wide.region_20.22_spmd.clone.sunk | while | flops 4125223936 | bytes 229824208 | solution.py:262
  690.5 16.6 %multiply_reduce_fusion.14 = (f32[12,512]{1,0:T(8,128)S(1)}, f32[12,512,1024]{2,1,0:T(8,128)}) fusion(f32[12,512,1024]{2,1,0:T(8,128)} %fusion.339, f32[12,512]{1,0:T(8,128)S(1)} %dynamic-slice_bitcast_fusion.8, pred[1024]{0:T(1024)(128)(4,1)S(1)} %iota_compare_fusion.7, bf16[1024,12,64]{0,2,1:T(8,128)(2,1)S(1)} %get-tuple-element.615, ...), kind=kOutput, calls=%fused_computation.22.clone.1 | convolution fusion | flops 836757504 | bytes 52741632 | tf_op jit(solution)/shard_map/while/body/eval_jaxpr/while/body/eval_jaxpr/qhd,khd->hqk/dot_general | solution.py:239
  707.1 21.4 %multiply_convert_fusion.4 = bf16[12,512,1024]{2,1,0:T(8,128)(2,1)} fusion(f32[12,512,1024]{2,1,0:T(8,128)} %get-tuple-element.557, f32[12,512,1024]{2,1,0:T(8,128)} %fusion.339, f32[12,512]{1,0:T(8,128)S(1)} %get-tuple-element.558, f32[12,512]{1,0:T(8,128)S(1)} %dynamic-slice_bitcast_fusion.8, pred[1024]{0:T(1024)(128)(4,1)S(1)} %iota_compare_fusion.7), kind=kLoop, calls=%fused_computation.21.clone.1 | loop fusion | flops 37748736 | bytes 62964736 | tf_op jit(solution)/shard_map/while/body/eval_jaxpr/while/body/eval_jaxpr/convert_element_type | solution.py:241
  741.3 28.7 %dynamic_update_slice.996 = f32[2,512,12,64]{1,0,3,2:T(2,128)} dynamic-update-slice(f32[2,512,12,64]{1,0,3,2:T(2,128)} %get-tuple-element.598, f32[1,512,12,64]{1,0,3,2:T(1,128)S(1)} %copy.202, s32[]{:T(128)} %get-tuple-element.595, s32[]{:T(128)} %constant.848.clone.1..sunk, s32[]{:T(128)} %constant.848.clone.1..sunk, s32[]{:T(128)} %constant.848.clone.1..sunk) | dynamic-update-slice | bytes 3145732 | tf_op jit(solution)/shard_map/while/body/eval_jaxpr/while/body/jit(dynamic_update_index_in_dim)/dynamic_update_slice | solution.py:223
  778.9 13.1 bitcast_add_fusion.32
  803.9 16.6 %multiply_reduce_fusion.14 = (f32[12,512]{1,0:T(8,128)S(1)}, f32[12,512,1024]{2,1,0:T(8,128)}) fusion(f32[12,512,1024]{2,1,0:T(8,128)} %fusion.339, f32[12,512]{1,0:T(8,128)S(1)} %dynamic-slice_bitcast_fusion.8, pred[1024]{0:T(1024)(128)(4,1)S(1)} %iota_compare_fusion.7, bf16[1024,12,64]{0,2,1:T(8,128)(2,1)S(1)} %get-tuple-element.615, ...), kind=kOutput, calls=%fused_computation.22.clone.1 | convolution fusion | flops 836757504 | bytes 52741632 | tf_op jit(solution)/shard_map/while/body/eval_jaxpr/while/body/eval_jaxpr/qhd,khd->hqk/dot_general | solution.py:239
  820.5 21.4 %multiply_convert_fusion.4 = bf16[12,512,1024]{2,1,0:T(8,128)(2,1)} fusion(f32[12,512,1024]{2,1,0:T(8,128)} %get-tuple-element.557, f32[12,512,1024]{2,1,0:T(8,128)} %fusion.339, f32[12,512]{1,0:T(8,128)S(1)} %get-tuple-element.558, f32[12,512]{1,0:T(8,128)S(1)} %dynamic-slice_bitcast_fusion.8, pred[1024]{0:T(1024)(128)(4,1)S(1)} %iota_compare_fusion.7), kind=kLoop, calls=%fused_computation.21.clone.1 | loop fusion | flops 37748736 | bytes 62964736 | tf_op jit(solution)/shard_map/while/body/eval_jaxpr/while/body/eval_jaxpr/convert_element_type | solution.py:241
  854.7 28.7 %dynamic_update_slice.996 = f32[2,512,12,64]{1,0,3,2:T(2,128)} dynamic-update-slice(f32[2,512,12,64]{1,0,3,2:T(2,128)} %get-tuple-element.598, f32[1,512,12,64]{1,0,3,2:T(1,128)S(1)} %copy.202, s32[]{:T(128)} %get-tuple-element.595, s32[]{:T(128)} %constant.848.clone.1..sunk, s32[]{:T(128)} %constant.848.clone.1..sunk, s32[]{:T(128)} %constant.848.clone.1..sunk) | dynamic-update-slice | bytes 3145732 | tf_op jit(solution)/shard_map/while/body/eval_jaxpr/while/body/jit(dynamic_update_index_in_dim)/dynamic_update_slice | solution.py:223
  893.2 14.0 bitcast_add_fusion.32
  1125.7 20.7 %collective-permute-done.77 = bf16[4,2,24,3072]{3,2,0,1:T(8,128)(2,1)S(1)} collective-permute-done((bf16[4,2,24,3072]{3,2,0,1:T(8,128)(2,1)S(1)}, bf16[4,2,24,3072]{3,2,0,1:T(8,128)(2,1)S(1)}, u32[]{:S(2)}, u32[]{:S(2)}) %collective-permute-start.77) | collective-permute-done | bytes 1179680 | tf_op jit(solution)/shard_map/ppermute | solution.py:26
  1151.1 11.8 collective-permute-done.78
  1174.8 14.0 collective-permute-done.82
  1213.0 12.6 copy.113
  1225.6 43.2 %scatter_fusion = f32[7680,768]{1,0:T(8,128)} fusion(f32[7680,768]{1,0:T(8,128)} %fusion.288, s32[4096]{0:T(1024)S(1)} %bitcast.1013, f32[4096,768]{1,0:T(8,128)} %copy.113), kind=kCustom, calls=%fused_computation.3 | custom fusion | flops 3145728 | bytes 37765120 | tf_op jit(solution)/shard_map/scatter-add | solution.py:472
  1286.9 11.8 bitcast_add_fusion.2
  1311.7 30.8 %collective-permute-done.56 = bf16[2,960,384]{2,1,0:T(8,128)(2,1)S(1)} collective-permute-done((bf16[2,960,384]{2,1,0:T(8,128)(2,1)S(1)}, bf16[2,960,384]{2,1,0:T(8,128)(2,1)S(1)}, u32[]{:S(2)}, u32[]{:S(2)}) %collective-permute-start.56) | collective-permute-done | bytes 1474592 | tf_op jit(solution)/shard_map/ppermute | solution.py:26
  1346.7 13.2 collective-permute-done.57
  1363.1 45.4 %psum.7 = f32[15366]{0:T(1024)S(1)} all-reduce(f32[15366]{0:T(1024)S(1)} %concatenate.96), channel_id=1, replica_groups=mesh['grp'=4,'rep'=8] {'grp','rep'}, use_global_device_ids=true, to_apply=%region_43.44 | all-reduce | flops 15366 | bytes 122928 | tf_op jit(solution)/shard_map/psum | solution.py:483
  1510.5 29.7 %multiply_subtract_fusion = (f32[7632,768]{1,0:T(8,128)}, f32[7632,768]{1,0:T(8,128)}) fusion(f32[7632,768]{1,0:T(8,128)} %param.31, f32[]{:T(128)S(6)} %div.275, f32[768]{0:T(1024)S(1)} %get-tuple-element.420, f32[7632]{0:T(1024)S(1)} %multiply_add_fusion.2, f32[]{:T(128)S(6)} %div.271, bf16[7680,768]{1,0:T(8,128)(2,1)} %bitcast.271), kind=kLoop, calls=%fused_computation.52 | loop fusion | flops 41029632 | bytes 82092872 | tf_op jit(solution)/shard_map/sub | solution.py:521
  (1081 shorter events, 918.2 us)
Async XLA Ops:
  7.2 295.2 %reduce-scatter.2.cloned.1.call-start = ((), (), s32[]{:S(2)}) async-start(), calls=%async_computation.1 | async-start | bytes 7864320 | tf_op jit(solution)/shard_map/reduce_scatter | solution.py:428
  10.7 187.3 %collective-permute-start.23 = (bf16[24,6144]{1,0:T(8,128)(2,1)}, bf16[24,6144]{1,0:T(8,128)(2,1)}, u32[]{:S(2)}, u32[]{:S(2)}) collective-permute-start(bf16[24,6144]{1,0:T(8,128)(2,1)} %dynamic-slice_bitcast_fusion.4), channel_id=1, source_target_pairs={{0,8},{8,16},{16,24},{24,0},{1,9},{9,17},{17,25},{25,1},{2,10},{10... | collective-permute-start | bytes 884744 | tf_op jit(solution)/shard_map/ppermute | solution.py:31
  12.8 187.6 %collective-permute-start.24 = (bf16[24,6144]{1,0:T(8,128)(2,1)}, bf16[24,6144]{1,0:T(8,128)(2,1)}, u32[]{:S(2)}, u32[]{:S(2)}) collective-permute-start(bf16[24,6144]{1,0:T(8,128)(2,1)} %dynamic-slice_bitcast_fusion.4), channel_id=1, source_target_pairs={{0,16},{8,24},{16,0},{24,8},{1,17},{9,25},{17,1},{25,9},{2,18},{10... | collective-permute-start | bytes 884744 | tf_op jit(solution)/shard_map/ppermute | solution.py:31
  15.1 44.1 %collective-permute-start = (s32[1280]{0:T(1024)S(1)}, s32[1280]{0:T(1024)}, u32[]{:S(2)}, u32[]{:S(2)}) collective-permute-start(s32[1280]{0:T(1024)S(1)} %pad_add_fusion), channel_id=1, source_target_pairs={{0,8},{8,16},{16,24},{24,0},{1,9},{9,17},{17,25},{25,1},{2,10},{10... | collective-permute-start | bytes 15368 | tf_op jit(solution)/shard_map/ppermute | solution.py:31
  15.2 45.2 %collective-permute-start.1 = (s32[1280]{0:T(1024)S(1)}, s32[1280]{0:T(1024)}, u32[]{:S(2)}, u32[]{:S(2)}) collective-permute-start(s32[1280]{0:T(1024)S(1)} %pad_add_fusion), channel_id=1, source_target_pairs={{0,16},{8,24},{16,0},{24,8},{1,17},{9,25},{17,1},{25,9},{2,18},{10... | collective-permute-start | bytes 15368 | tf_op jit(solution)/shard_map/ppermute | solution.py:31
  16.5 45.9 %collective-permute-start.2 = (s32[1280]{0:T(1024)S(1)}, s32[1280]{0:T(1024)}, u32[]{:S(2)}, u32[]{:S(2)}) collective-permute-start(s32[1280]{0:T(1024)S(1)} %pad_add_fusion), channel_id=1, source_target_pairs={{0,24},{8,0},{16,8},{24,16},{1,25},{9,1},{17,9},{25,17},{2,26},{10... | collective-permute-start | bytes 15368 | tf_op jit(solution)/shard_map/ppermute | solution.py:31
  59.3 142.8 %collective-permute-start.25 = (bf16[24,6144]{1,0:T(8,128)(2,1)}, bf16[24,6144]{1,0:T(8,128)(2,1)}, u32[]{:S(2)}, u32[]{:S(2)}) collective-permute-start(bf16[24,6144]{1,0:T(8,128)(2,1)} %dynamic-slice_bitcast_fusion.4), channel_id=1, source_target_pairs={{0,24},{8,0},{16,8},{24,16},{1,25},{9,1},{17,9},{25,17},{2,26},{10... | collective-permute-start | bytes 884744 | tf_op jit(solution)/shard_map/ppermute | solution.py:31
  60.4 61.0 %collective-permute-start.13 = (bf16[24,768]{1,0:T(8,128)(2,1)}, bf16[24,768]{1,0:T(8,128)(2,1)}, u32[]{:S(2)}, u32[]{:S(2)}) collective-permute-start(bf16[24,768]{1,0:T(8,128)(2,1)} %fusion.231), channel_id=1, source_target_pairs={{0,8},{8,16},{16,24},{24,0},{1,9},{9,17},{17,25},{25,1},{2,10},{10... | collective-permute-start | bytes 110600 | tf_op jit(solution)/shard_map/ppermute | solution.py:31
  108.4 1095.2 %all-gather.2.cloned.1.call-start = ((), (), s32[]{:S(2)}) async-start(), calls=%async_computation.2 | async-start | bytes 7864320 | tf_op jit(solution)/shard_map/all_gather | solution.py:471
  197.9 45.9 %collective-permute-start.9 = (bf16[3,24,2304]{2,1,0:T(8,128)(2,1)S(1)}, bf16[3,24,2304]{2,1,0:T(8,128)(2,1)S(1)}, u32[]{:S(2)}, u32[]{:S(2)}) collective-permute-start(bf16[3,24,2304]{2,1,0:T(8,128)(2,1)S(1)} %pad_maximum_fusion.9), channel_id=1, source_target_pairs={{0,1},{1,0},{2,3},{3,2},{4,5},{5,4},{6,7},{7,6},{8,9},{9,8},{10,11... | collective-permute-start | bytes 995336 | tf_op jit(solution)/shard_map/ppermute | solution.py:26
  208.0 54.5 %collective-permute-start.39 = (bf16[3,96,768]{2,1,0:T(8,128)(2,1)S(1)}, bf16[3,96,768]{2,1,0:T(8,128)(2,1)S(1)}, u32[]{:S(2)}, u32[]{:S(2)}) collective-permute-start(bf16[3,96,768]{2,1,0:T(8,128)(2,1)S(1)} %pad_maximum_fusion.8), channel_id=1, source_target_pairs={{0,1},{1,0},{2,3},{3,2},{4,5},{5,4},{6,7},{7,6},{8,9},{9,8},{10,11... | collective-permute-start | bytes 1327112 | tf_op jit(solution)/shard_map/ppermute | solution.py:26
  208.6 60.6 %collective-permute-start.26 = (bf16[3,24,6144]{2,1,0:T(8,128)(2,1)S(1)}, bf16[3,24,6144]{2,1,0:T(8,128)(2,1)S(1)}, u32[]{:S(2)}, u32[]{:S(2)}) collective-permute-start(bf16[3,24,6144]{2,1,0:T(8,128)(2,1)S(1)} %pad_maximum_fusion.7), channel_id=1, source_target_pairs={{0,2},{1,3},{2,0},{3,1},{4,6},{5,7},{6,4},{7,5},{8,10},{9,11},{10,... | collective-permute-start | bytes 2654216 | tf_op jit(solution)/shard_map/ppermute | solution.py:26
  212.3 61.0 %collective-permute-start.27 = (bf16[3,24,6144]{2,1,0:T(8,128)(2,1)S(1)}, bf16[3,24,6144]{2,1,0:T(8,128)(2,1)S(1)}, u32[]{:S(2)}, u32[]{:S(2)}) collective-permute-start(bf16[3,24,6144]{2,1,0:T(8,128)(2,1)S(1)} %pad_maximum_fusion.7), channel_id=1, source_target_pairs={{0,4},{1,5},{2,6},{3,7},{4,0},{5,1},{6,2},{7,3},{8,12},{9,13},{10,... | collective-permute-start | bytes 2654216 | tf_op jit(solution)/shard_map/ppermute | solution.py:26
  242.4 51.1 %collective-permute-start.29 = (bf16[3,24,6144]{2,1,0:T(8,128)(2,1)S(1)}, bf16[3,24,6144]{2,1,0:T(8,128)(2,1)S(1)}, u32[]{:S(2)}, u32[]{:S(2)}) collective-permute-start(bf16[3,24,6144]{2,1,0:T(8,128)(2,1)S(1)} %pad_maximum_fusion.7), channel_id=1, source_target_pairs={{0,1},{1,0},{2,3},{3,2},{4,5},{5,4},{6,7},{7,6},{8,9},{9,8},{10,11... | collective-permute-start | bytes 2654216 | tf_op jit(solution)/shard_map/ppermute | solution.py:26
  653.1 349.2 %collective-permute-start.84 = (bf16[4,2,2,96,768]{4,3,0,2,1:T(8,128)(2,1)}, bf16[4,2,2,96,768]{4,3,0,2,1:T(8,128)(2,1)}, u32[]{:S(2)}, u32[]{:S(2)}) collective-permute-start(bf16[4,2,2,96,768]{4,3,0,2,1:T(8,128)(2,1)} %fusion.69), channel_id=1, source_target_pairs={{0,1},{1,0},{2,3},{3,2},{4,5},{5,4},{6,7},{7,6},{8,9},{9,8},{10,11... | collective-permute-start | bytes 7077896 | tf_op jit(solution)/shard_map/ppermute | solution.py:26
  662.2 449.9 %collective-permute-start.76 = (bf16[4,2,2,24,6144]{4,3,0,2,1:T(8,128)(2,1)}, bf16[4,2,2,24,6144]{4,3,0,2,1:T(8,128)(2,1)}, u32[]{:S(2)}, u32[]{:S(2)}) collective-permute-start(bf16[4,2,2,24,6144]{4,3,0,2,1:T(8,128)(2,1)} %fusion.46), channel_id=1, source_target_pairs={{0,1},{1,0},{2,3},{3,2},{4,5},{5,4},{6,7},{7,6},{8,9},{9,8},{10,11... | collective-permute-start | bytes 14155784 | tf_op jit(solution)/shard_map/ppermute | solution.py:26
  669.3 267.0 %collective-permute-start.68 = (bf16[4,2,2,24,768]{4,3,0,2,1:T(8,128)(2,1)}, bf16[4,2,2,24,768]{4,3,0,2,1:T(8,128)(2,1)}, u32[]{:S(2)}, u32[]{:S(2)}) collective-permute-start(bf16[4,2,2,24,768]{4,3,0,2,1:T(8,128)(2,1)} %fusion.95), channel_id=1, source_target_pairs={{0,1},{1,0},{2,3},{3,2},{4,5},{5,4},{6,7},{7,6},{8,9},{9,8},{10,11... | collective-permute-start | bytes 1769480 | tf_op jit(solution)/shard_map/ppermute | solution.py:26
  1005.4 45.9 %collective-permute-start.85 = (bf16[4,2,96,384]{3,2,0,1:T(8,128)(2,1)S(1)}, bf16[4,2,96,384]{3,2,0,1:T(8,128)(2,1)S(1)}, u32[]{:S(2)}, u32[]{:S(2)}) collective-permute-start(bf16[4,2,96,384]{3,2,0,1:T(8,128)(2,1)S(1)} %fusion.93), channel_id=1, source_target_pairs={{0,2},{1,3},{2,0},{3,1},{4,6},{5,7},{6,4},{7,5},{8,10},{9,11},{10,... | collective-permute-start | bytes 1769480 | tf_op jit(solution)/shard_map/ppermute | solution.py:26
  1015.6 36.6 %collective-permute-start.87 = (bf16[4,2,96,384]{3,2,0,1:T(8,128)(2,1)S(1)}, bf16[4,2,96,384]{3,2,0,1:T(8,128)(2,1)S(1)}, u32[]{:S(2)}, u32[]{:S(2)}) collective-permute-start(bf16[4,2,96,384]{3,2,0,1:T(8,128)(2,1)S(1)} %fusion.94), channel_id=1, source_target_pairs={{0,4},{1,5},{2,6},{3,7},{4,0},{5,1},{6,2},{7,3},{8,12},{9,13},{10,... | collective-permute-start | bytes 1769480 | tf_op jit(solution)/shard_map/ppermute | solution.py:26
  1108.3 63.5 %collective-permute-start.160 = (bf16[96,384]{1,0:T(8,128)(2,1)S(1)}, bf16[96,384]{1,0:T(8,128)(2,1)}, u32[]{:S(2)}, u32[]{:S(2)}) collective-permute-start(bf16[96,384]{1,0:T(8,128)(2,1)S(1)} %collective-permute-done.156), channel_id=1, source_target_pairs={{0,1},{1,0},{2,3},{3,2},{4,5},{5,4},{6,7},{7,6},{8,9},{9,8},{10,11... | collective-permute-start | bytes 221192 | tf_op jit(solution)/shard_map/ppermute | solution.py:26
  1109.3 64.0 %collective-permute-start.161 = (bf16[96,384]{1,0:T(8,128)(2,1)S(1)}, bf16[96,384]{1,0:T(8,128)(2,1)}, u32[]{:S(2)}, u32[]{:S(2)}) collective-permute-start(bf16[96,384]{1,0:T(8,128)(2,1)S(1)} %collective-permute-done.157), channel_id=1, source_target_pairs={{0,1},{1,0},{2,3},{3,2},{4,5},{5,4},{6,7},{7,6},{8,9},{9,8},{10,11... | collective-permute-start | bytes 221192 | tf_op jit(solution)/shard_map/ppermute | solution.py:26
  1191.1 82.7 %collective-permute-start.137 = (bf16[24,3072]{1,0:T(8,128)(2,1)}, bf16[24,3072]{1,0:T(8,128)(2,1)}, u32[]{:S(2)}, u32[]{:S(2)}) collective-permute-start(bf16[24,3072]{1,0:T(8,128)(2,1)} %get-tuple-element.399), channel_id=1, source_target_pairs={{0,1},{1,0},{2,3},{3,2},{4,5},{5,4},{6,7},{7,6},{8,9},{9,8},{10,11... | collective-permute-start | bytes 442376 | tf_op jit(solution)/shard_map/ppermute | solution.py:26
  1192.2 83.2 %collective-permute-start.141 = (bf16[24,3072]{1,0:T(8,128)(2,1)}, bf16[24,3072]{1,0:T(8,128)(2,1)S(1)}, u32[]{:S(2)}, u32[]{:S(2)}) collective-permute-start(bf16[24,3072]{1,0:T(8,128)(2,1)} %get-tuple-element.398), channel_id=1, source_target_pairs={{0,2},{1,3},{2,0},{3,1},{4,6},{5,7},{6,4},{7,5},{8,10},{9,11},{10,... | collective-permute-start | bytes 442376 | tf_op jit(solution)/shard_map/ppermute | solution.py:26
  1193.1 91.4 %collective-permute-start.142 = (bf16[24,3072]{1,0:T(8,128)(2,1)}, bf16[24,3072]{1,0:T(8,128)(2,1)S(1)}, u32[]{:S(2)}, u32[]{:S(2)}) collective-permute-start(bf16[24,3072]{1,0:T(8,128)(2,1)} %get-tuple-element.398), channel_id=1, source_target_pairs={{0,4},{1,5},{2,6},{3,7},{4,0},{5,1},{6,2},{7,3},{8,12},{9,13},{10,... | collective-permute-start | bytes 442376 | tf_op jit(solution)/shard_map/ppermute | solution.py:26
  1194.6 91.4 %collective-permute-start.144 = (bf16[24,3072]{1,0:T(8,128)(2,1)}, bf16[24,3072]{1,0:T(8,128)(2,1)}, u32[]{:S(2)}, u32[]{:S(2)}) collective-permute-start(bf16[24,3072]{1,0:T(8,128)(2,1)} %get-tuple-element.398), channel_id=1, source_target_pairs={{0,1},{1,0},{2,3},{3,2},{4,5},{5,4},{6,7},{7,6},{8,9},{9,8},{10,11... | collective-permute-start | bytes 442376 | tf_op jit(solution)/shard_map/ppermute | solution.py:26
  1201.1 74.5 %collective-permute-start.138 = (bf16[24,3072]{1,0:T(8,128)(2,1)S(1)}, bf16[24,3072]{1,0:T(8,128)(2,1)}, u32[]{:S(2)}, u32[]{:S(2)}) collective-permute-start(bf16[24,3072]{1,0:T(8,128)(2,1)S(1)} %collective-permute-done.134), channel_id=1, source_target_pairs={{0,1},{1,0},{2,3},{3,2},{4,5},{5,4},{6,7},{7,6},{8,9},{9,8},{10,11... | collective-permute-start | bytes 442376 | tf_op jit(solution)/shard_map/ppermute | solution.py:26
  1285.5 58.9 %collective-permute-start.147 = (bf16[24,3072]{1,0:T(8,128)(2,1)S(1)}, bf16[24,3072]{1,0:T(8,128)(2,1)}, u32[]{:S(2)}, u32[]{:S(2)}) collective-permute-start(bf16[24,3072]{1,0:T(8,128)(2,1)S(1)} %collective-permute-done.143), channel_id=1, source_target_pairs={{0,1},{1,0},{2,3},{3,2},{4,5},{5,4},{6,7},{7,6},{8,9},{9,8},{10,11... | collective-permute-start | bytes 442376 | tf_op jit(solution)/shard_map/ppermute | solution.py:26
  1309.2 34.4 %collective-permute-start.58 = (bf16[2,960,384]{2,1,0:T(8,128)(2,1)S(1)}, bf16[2,960,384]{2,1,0:T(8,128)(2,1)S(1)}, u32[]{:S(2)}, u32[]{:S(2)}) collective-permute-start(bf16[2,960,384]{2,1,0:T(8,128)(2,1)S(1)} %fusion.82), channel_id=1, source_target_pairs={{0,4},{1,5},{2,6},{3,7},{4,0},{5,1},{6,2},{7,3},{8,12},{9,13},{10,... | collective-permute-start | bytes 4423688 | tf_op jit(solution)/shard_map/ppermute | solution.py:26
  1422.7 35.1 %collective-permute-start.93 = (bf16[960,384]{1,0:T(8,128)(2,1)}, bf16[960,384]{1,0:T(8,128)(2,1)}, u32[]{:S(2)}, u32[]{:S(2)}) collective-permute-start(bf16[960,384]{1,0:T(8,128)(2,1)} %get-tuple-element.385), channel_id=1, source_target_pairs={{0,2},{1,3},{2,0},{3,1},{4,6},{5,7},{6,4},{7,5},{8,10},{9,11},{10,... | collective-permute-start | bytes 2211848 | tf_op jit(solution)/shard_map/ppermute | solution.py:26
  1423.3 50.4 %collective-permute-start.95 = (bf16[960,384]{1,0:T(8,128)(2,1)}, bf16[960,384]{1,0:T(8,128)(2,1)}, u32[]{:S(2)}, u32[]{:S(2)}) collective-permute-start(bf16[960,384]{1,0:T(8,128)(2,1)} %get-tuple-element.385), channel_id=1, source_target_pairs={{0,1},{1,0},{2,3},{3,2},{4,5},{5,4},{6,7},{7,6},{8,9},{9,8},{10,11... | collective-permute-start | bytes 2211848 | tf_op jit(solution)/shard_map/ppermute | solution.py:26
  1425.9 34.8 %collective-permute-start.99 = (bf16[960,384]{1,0:T(8,128)(2,1)}, bf16[960,384]{1,0:T(8,128)(2,1)}, u32[]{:S(2)}, u32[]{:S(2)}) collective-permute-start(bf16[960,384]{1,0:T(8,128)(2,1)} %get-tuple-element.384), channel_id=1, source_target_pairs={{0,2},{1,3},{2,0},{3,1},{4,6},{5,7},{6,4},{7,5},{8,10},{9,11},{10,... | collective-permute-start | bytes 2211848 | tf_op jit(solution)/shard_map/ppermute | solution.py:26
  1426.5 52.1 %collective-permute-start.100 = (bf16[960,384]{1,0:T(8,128)(2,1)}, bf16[960,384]{1,0:T(8,128)(2,1)}, u32[]{:S(2)}, u32[]{:S(2)}) collective-permute-start(bf16[960,384]{1,0:T(8,128)(2,1)} %get-tuple-element.384), channel_id=1, source_target_pairs={{0,4},{1,5},{2,6},{3,7},{4,0},{5,1},{6,2},{7,3},{8,12},{9,13},{10,... | collective-permute-start | bytes 2211848 | tf_op jit(solution)/shard_map/ppermute | solution.py:26
  (280 other events, 2962.5 us)
Sparse Core Ops, SparseCore 0:
  108.5 130.8 reduce-scatter.1
  960.5 138.1 all-gather.1

commit v2 on v1

v2 whole, which is shorter than its diff:
```python
import functools
import math

import jax
import jax.numpy as jnp
from jax import lax
from jax.experimental import pallas as pl
from jax.experimental.pallas import tpu as pltpu
from jax.sharding import PartitionSpec as P

HEADS = 12
HD = 64
STEP = 10
LANES = 128
ROWS = 256
CHUNK = 256
TILE = 240


ln_eps = 1e-05
rope_base = 10000.0
clip_limit = 0.01
rate_matrix = 0.03
rate_norm = 0.3
neg_large = -1e30
low_type = jnp.bfloat16
vmem = 56 * 1024 * 1024


def pair_lanes(shape):
    return lax.broadcasted_iota(jnp.int32, shape, len(shape) - 1)


def swap_halves(value):
    upper = (pair_lanes(value.shape) % HD) >= HD // 2
    return jnp.where(
        upper,
        pltpu.roll(value, HD // 2, axis=1),
        pltpu.roll(value, LANES - HD // 2, axis=1),
    )


def normalize(values, gain, shift):
    center = values - jnp.mean(values, axis=-1, keepdims=True)
    spread = jnp.mean(center * center, axis=-1, keepdims=True)
    return center * lax.rsqrt(spread + ln_eps) * gain + shift


def project_kernel(embed_ref, norms_ref, cosine_ref, sine_ref, w_ref, first_ref, low_ref, q_ref, k_ref, v_ref):
    first = normalize(embed_ref[...].astype(jnp.float32), norms_ref[0:1, :], norms_ref[1:2, :])
    first_ref[...] = first
    low = first.astype(low_type)
    low_ref[...] = low
    width = first.shape[1]
    cosine, sine = cosine_ref[...], sine_ref[...]
    for part, out_ref in enumerate((q_ref, k_ref)):
        joined = jnp.dot(low, w_ref[:, part * width : (part + 1) * width], preferred_element_type=jnp.float32)
        for start in range(0, width, LANES):
            piece = joined[:, start : start + LANES]
            out_ref[:, start : start + LANES] = (piece * cosine + swap_halves(piece) * sine).astype(low_type)
    v_ref[...] = jnp.dot(low, w_ref[:, 2 * width :], preferred_element_type=jnp.float32).astype(low_type)


def project(embed, norms, cosine, sine, weights):
    tokens, width = embed.shape
    row = lambda i: (i, 0)
    fixed = lambda i: (0, 0)
    low = jax.ShapeDtypeStruct((tokens, width), low_type)
    return pl.pallas_call(
        project_kernel,
        grid=(tokens // ROWS,),
        in_specs=[
            pl.BlockSpec((ROWS, width), row),
            pl.BlockSpec(norms.shape, fixed),
            pl.BlockSpec((ROWS, LANES), row),
            pl.BlockSpec((ROWS, LANES), row),
            pl.BlockSpec((width, 3 * width), fixed),
        ],
        out_specs=[pl.BlockSpec((ROWS, width), row)] * 5,
        out_shape=[jax.ShapeDtypeStruct((tokens, width), jnp.float32), low, low, low, low],
        compiler_params=pltpu.CompilerParams(vmem_limit_bytes=vmem),
        cost_estimate=pl.CostEstimate(flops=6 * tokens * width * width, bytes_accessed=20 * tokens * width, transcendentals=0),
    )(embed, norms, cosine, sine, weights)


def head_keys(k, bias, half):
    lanes = pair_lanes(k.shape)
    spare = HD - half * HD
    return jnp.where(lanes // HD == half, k, jnp.where(lanes == spare, bias, jnp.zeros_like(k)))


def head_queries(q, half, spare_value):
    lanes = pair_lanes(q.shape)
    spare = HD - half * HD
    scaled = q * jnp.asarray(1.0 / math.sqrt(HD), q.dtype)
    other = jnp.where(lanes == spare, jnp.full_like(q, spare_value), jnp.zeros_like(q))
    return jnp.where(lanes // HD == half, scaled, other)


def transposed_dot(left, right):
    return lax.dot_general(left, right, (((1,), (1,)), ((), ())), preferred_element_type=jnp.float32)


def key_bias(length_ref, tokens):
    place = lax.broadcasted_iota(jnp.int32, (tokens, LANES), 0)
    return jnp.where(place < length_ref[0], 0.0, neg_large).astype(low_type)


def attend_kernel(length_ref, q_ref, k_ref, v_ref, out_ref, log_ref, keys, turned):
    tokens = k_ref.shape[0]

    @pl.when(pl.program_id(1) == 0)
    def _():
        bias = key_bias(length_ref, tokens)
        for half in range(2):
            keys[half] = head_keys(k_ref[...], bias, half)
        turned[...] = v_ref[...].T

    parts = []
    for half in range(2):
        scores = transposed_dot(keys[half], head_queries(q_ref[...], half, 1.0))
        peak = jnp.max(scores, axis=0, keepdims=True)
        weights = jnp.exp(scores - peak)
        totals = jnp.sum(weights, axis=0, keepdims=True)
        probs = (weights * (1.0 / totals)).astype(low_type)
        parts.append(
            jnp.dot(turned[half * HD : (half + 1) * HD, :], probs, preferred_element_type=jnp.float32)
        )
        log_ref[0, half : half + 1, :] = peak + jnp.log(totals)
    out_ref[...] = jnp.concatenate(parts, axis=0).T.astype(low_type)


def attend(length, q, k, v):
    tokens, width = q.shape
    pairs = width // LANES
    own = lambda p, i, *_: (i, p)
    whole = lambda p, i, *_: (0, p)
    return pl.pallas_call(
        attend_kernel,
        grid_spec=pltpu.PrefetchScalarGridSpec(
            num_scalar_prefetch=1,
            grid=(pairs, tokens // ROWS),
            in_specs=[
                pl.BlockSpec((ROWS, LANES), own),
                pl.BlockSpec((tokens, LANES), whole),
                pl.BlockSpec((tokens, LANES), whole),
            ],
            out_specs=[
                pl.BlockSpec((ROWS, LANES), own),
                pl.BlockSpec((1, 2, ROWS), lambda p, i, *_: (p, 0, i)),
            ],
            scratch_shapes=[
                pltpu.VMEM((2, tokens, LANES), low_type),
                pltpu.VMEM((LANES, tokens), low_type),
            ],
        ),
        out_shape=[
            jax.ShapeDtypeStruct((tokens, width), low_type),
            jax.ShapeDtypeStruct((pairs, 2, tokens), jnp.float32),
        ],
        compiler_params=pltpu.CompilerParams(vmem_limit_bytes=vmem),
        cost_estimate=pl.CostEstimate(
            flops=16 * tokens * tokens * width, bytes_accessed=8 * tokens * width, transcendentals=tokens * tokens * width // HD
        ),
    )(length, q, k, v)


def rotate_back(grads, cosine, sine):
    return grads * cosine + swap_halves(grads * sine)


def attend_back_kernel(first_pair, length_ref, q_ref, k_ref, v_ref, d_ref, log_ref, cosq_ref, sinq_ref, cos_ref, sin_ref, *rest):
    dq_ref, dk_ref, dv_ref, keys, values, turned, dk_total, dv_total = rest[-8:]
    tokens = k_ref.shape[0]
    step = pl.program_id(1)

    @pl.when(step == 0)
    def _():
        bias = key_bias(length_ref, tokens)
        lanes = pair_lanes((tokens, LANES))
        for half in range(2):
            keys[half] = head_keys(k_ref[...], bias, half)
            values[half] = jnp.where(lanes // HD == half, v_ref[...], jnp.zeros_like(v_ref[...]))
        turned[...] = k_ref[...].T
        dk_total[...] = jnp.zeros_like(dk_total)
        dv_total[...] = jnp.zeros_like(dv_total)

    d = d_ref[...]
    lanes = pair_lanes(d.shape)
    parts = []
    dk = dv = None
    for half in range(2):
        scores = transposed_dot(keys[half], head_queries(q_ref[...], half, 1.0))
        probs = jnp.exp(scores - log_ref[0, half : half + 1, :])
        dprobs = transposed_dot(values[half], d)
        inner = jnp.sum(probs * dprobs, axis=0, keepdims=True)
        dscore = (probs * (dprobs - inner)).astype(low_type)
        parts.append(jnp.dot(turned[half * HD : (half + 1) * HD, :], dscore, preferred_element_type=jnp.float32))
        one_k = jnp.dot(dscore, head_queries(q_ref[...], half, 0.0), preferred_element_type=jnp.float32)
        one_v = jnp.dot(
            probs.astype(low_type), jnp.where(lanes // HD == half, d, jnp.zeros_like(d)), preferred_element_type=jnp.float32
        )
        dk = one_k if dk is None else dk + one_k
        dv = one_v if dv is None else dv + one_v
    dk_total[...] += dk
    dv_total[...] += dv
    dq = jnp.concatenate(parts, axis=0).T * (1.0 / math.sqrt(HD))
    dq_ref[...] = rotate_back(dq, cosq_ref[...], sinq_ref[...]).astype(low_type)

    @pl.when(step == pl.num_programs(1) - 1)
    def _():
        dk_ref[...] = rotate_back(dk_total[...], cos_ref[...], sin_ref[...]).astype(low_type)
        dv_ref[...] = dv_total[...].astype(low_type)


def attend_back(length, q, k, v, d, logs, cosine, sine, first_pair, pairs, after=()):
    tokens, width = q.shape
    own = lambda p, i, *_: (i, first_pair + p)
    whole = lambda p, i, *_: (0, first_pair + p)
    low = jax.ShapeDtypeStruct((tokens, pairs * LANES), low_type)
    fixed = pl.BlockSpec((tokens, LANES), lambda p, i, *_: (0, 0))
    row = pl.BlockSpec((ROWS, LANES), lambda p, i, *_: (i, 0))
    return pl.pallas_call(
        functools.partial(attend_back_kernel, first_pair),
        grid_spec=pltpu.PrefetchScalarGridSpec(
            num_scalar_prefetch=1,
            grid=(pairs, tokens // ROWS),
            in_specs=[
                pl.BlockSpec((ROWS, LANES), own),
                pl.BlockSpec((tokens, LANES), whole),
                pl.BlockSpec((tokens, LANES), whole),
                pl.BlockSpec((ROWS, LANES), own),
                pl.BlockSpec((1, 2, ROWS), lambda p, i, *_: (first_pair + p, 0, i)),
                row,
                row,
                fixed,
                fixed,
            ]
            + [pl.BlockSpec(memory_space=pl.ANY)] * len(after),
            out_specs=[
                pl.BlockSpec((ROWS, LANES), lambda p, i, *_: (i, p)),
                pl.BlockSpec((tokens, LANES), lambda p, i, *_: (0, p)),
                pl.BlockSpec((tokens, LANES), lambda p, i, *_: (0, p)),
            ],
            scratch_shapes=[
                pltpu.VMEM((2, tokens, LANES), low_type),
                pltpu.VMEM((2, tokens, LANES), low_type),
                pltpu.VMEM((LANES, tokens), low_type),
                pltpu.VMEM((tokens, LANES), jnp.float32),
                pltpu.VMEM((tokens, LANES), jnp.float32),
            ],
        ),
        out_shape=[low, low, low],
        compiler_params=pltpu.CompilerParams(vmem_limit_bytes=vmem),
        cost_estimate=pl.CostEstimate(
            flops=40 * tokens * tokens * pairs * LANES,
            bytes_accessed=16 * tokens * pairs * LANES,
            transcendentals=tokens * tokens * pairs * 2,
        ),
    )(length, q, k, v, d, logs, cosine, sine, cosine, sine, *after)


def blank(shape, dtype):
    return pl.pallas_call(
        lambda out_ref: None,
        out_shape=jax.ShapeDtypeStruct(shape, dtype),
        out_specs=pl.BlockSpec(memory_space=pl.ANY),
    )()


def lookup_kernel(places_ref, table_ref, out_ref, rows):
    base = pl.program_id(0) * CHUNK
    rows[...] = jnp.zeros_like(rows)

    def one(i, carry):
        place = places_ref[base + i]

        @pl.when(place >= 0)
        def _():
            rows[pl.ds(i, 1), :] = table_ref[pl.ds(place, 1), :]

        return carry

    lax.fori_loop(0, CHUNK, one, 0, unroll=8)
    out_ref[...] = rows[...].astype(low_type)


def lookup(places, table):
    count = places.shape[0]
    width = table.shape[1]
    return pl.pallas_call(
        lookup_kernel,
        grid_spec=pltpu.PrefetchScalarGridSpec(
            num_scalar_prefetch=1,
            grid=(count // CHUNK,),
            in_specs=[pl.BlockSpec(table.shape, lambda i, *_: (0, 0), pipeline_mode=pl.Buffered(1))],
            out_specs=pl.BlockSpec((CHUNK, width), lambda i, *_: (i, 0)),
            scratch_shapes=[pltpu.VMEM((CHUNK, width), jnp.float32)],
        ),
        out_shape=jax.ShapeDtypeStruct((count, width), low_type),
        compiler_params=pltpu.CompilerParams(vmem_limit_bytes=vmem),
        cost_estimate=pl.CostEstimate(flops=0, bytes_accessed=table.size * 8, transcendentals=0),
    )(places, table)


def table_grad_kernel(core_ref, starts_ref, places_ref, order_ref, dlogits_ref, chosen_ref, embed_ref, out_ref, rows, total):
    step = pl.program_id(0)
    count = embed_ref.shape[0]
    block = total.shape[0]

    @pl.when(step == 0)
    def _():
        for start in range(0, count, CHUNK):
            rows[start : start + CHUNK, :] = embed_ref[start : start + CHUNK, :].astype(jnp.float32)

    total[...] = jnp.dot(dlogits_ref[...], chosen_ref[...], preferred_element_type=jnp.float32)
    chunk = 2 * step + core_ref[0]
    base = chunk * block

    def one(i, carry):
        place = places_ref[i] - base
        total[pl.ds(place, 1), :] += rows[pl.ds(order_ref[i], 1), :]
        return carry

    lax.fori_loop(starts_ref[chunk], starts_ref[chunk + 1], one, 0)
    out_ref[0] = total[...].astype(out_ref.dtype)


def table_grad_half(core, starts, places, order, dlogits, chosen, embed, block, dtype):
    count, width = embed.shape
    picked = chosen.shape[0]
    chunks = dlogits.shape[0] // block // 2
    fixed = lambda i, *_: (0, 0)
    return pl.pallas_call(
        table_grad_kernel,
        grid_spec=pltpu.PrefetchScalarGridSpec(
            num_scalar_prefetch=4,
            grid=(chunks,),
            in_specs=[
                pl.BlockSpec((block, picked), lambda i, core, *_: (2 * i + core[0], 0)),
                pl.BlockSpec((picked, width), fixed),
                pl.BlockSpec((count, width), fixed, pipeline_mode=pl.Buffered(1)),
            ],
            out_specs=pl.BlockSpec((1, block, width), lambda i, *_: (i, 0, 0)),
            scratch_shapes=[pltpu.VMEM((count, width), jnp.float32), pltpu.VMEM((block, width), jnp.float32)],
        ),
        out_shape=jax.ShapeDtypeStruct((chunks, block, width), dtype),
        compiler_params=pltpu.CompilerParams(vmem_limit_bytes=vmem),
        cost_estimate=pl.CostEstimate(
            flops=2 * chunks * block * picked * width, bytes_accessed=8 * chunks * block * width, transcendentals=0
        ),
    )(core, starts, places, order, dlogits, chosen, embed)


TILE = 240

def update_kernel(slot_ref, scalars_ref, one_ref, two_ref, table_ref, rows_ref, cols_ref, *rest):
    grad_ref, new_ref, rows_new_ref = rest[-3:]
    gradient = jnp.concatenate([one_ref[...], two_ref[...]], axis=1).astype(jnp.float32)
    factor, row_mean = scalars_ref[0], scalars_ref[1]
    decay = 1.0 - float(STEP) ** (-0.8)
    old = jnp.broadcast_to(rows_ref[0], (LANES, TILE)).T[:, 0:1]
    means = jnp.mean(gradient * gradient, axis=1, keepdims=True)
    rows_new = decay * old + (1.0 - decay) * (means * factor * factor)
    clipped = gradient * factor
    grad_ref[...] = clipped
    scale = rows_new * cols_ref[...] / row_mean
    new_ref[...] = table_ref[...] - rate_matrix * clipped * lax.rsqrt(scale)
    rows_new_ref[0] = jnp.broadcast_to(rows_new, (TILE, LANES)).T[0:1, :]


def update(slot, scalars, one, two, table, rows, cols, so_far):
    block, half = one.shape
    width = 2 * half
    steps = block // TILE
    place = lambda i, slot: (slot[0] * steps + i, 0)
    place3 = lambda i, slot: (slot[0] * steps + i, 0, 0)
    own = lambda i, slot: (i, 0)
    fixed = lambda i, slot: (0, 0)
    any_space = pl.BlockSpec(memory_space=pl.ANY)
    return pl.pallas_call(
        update_kernel,
        grid_spec=pltpu.PrefetchScalarGridSpec(
            num_scalar_prefetch=1,
            grid=(steps,),
            in_specs=[
                pl.BlockSpec(memory_space=pltpu.SMEM),
                pl.BlockSpec((TILE, half), own),
                pl.BlockSpec((TILE, half), own),
                pl.BlockSpec((TILE, width), place),
                pl.BlockSpec((1, 1, TILE), place3),
                pl.BlockSpec((1, width), fixed),
                any_space,
                any_space,
                any_space,
            ],
            out_specs=[
                pl.BlockSpec((TILE, width), place),
                pl.BlockSpec((TILE, width), place),
                pl.BlockSpec((1, 1, TILE), place3),
            ],
        ),
        out_shape=[jax.ShapeDtypeStruct(part.shape, part.dtype) for part in so_far],
        input_output_aliases={7: 0, 8: 1, 9: 2},
        compiler_params=pltpu.CompilerParams(vmem_limit_bytes=vmem),
        cost_estimate=pl.CostEstimate(flops=10 * block * width, bytes_accessed=14 * block * width, transcendentals=block * width),
    )(slot, scalars, one, two, table, rows, cols, *so_far)


def assemble_kernel(members_ref, slots_ref, own_ref, *rest):
    pieces, out_ref, marks = rest[:-2], rest[-2], rest[-1]
    copies = [pltpu.make_async_copy(own_ref, out_ref.at[members_ref[0]], marks.at[0])]
    for place, piece in enumerate(pieces):
        for offset in range(piece.shape[0]):
            copies.append(
                pltpu.make_async_copy(
                    piece.at[offset],
                    out_ref.at[members_ref[offset + 1], slots_ref[place]],
                    marks.at[len(copies)],
                )
            )
    for copy in copies:
        copy.start()
    for copy in copies:
        copy.wait()


def assemble(members, slots, own, pieces):
    groups, replicas = members.shape[0], slots.shape[0]
    any_space = pl.BlockSpec(memory_space=pl.ANY)
    return pl.pallas_call(
        assemble_kernel,
        grid_spec=pltpu.PrefetchScalarGridSpec(
            num_scalar_prefetch=2,
            grid=(1,),
            in_specs=[any_space] * (1 + len(pieces)),
            out_specs=any_space,
            scratch_shapes=[pltpu.SemaphoreType.DMA((1 + replicas * (groups - 1),))],
        ),
        out_shape=jax.ShapeDtypeStruct((groups,) + own.shape, own.dtype),
        cost_estimate=pl.CostEstimate(flops=0, bytes_accessed=4 * groups * own.size, transcendentals=0),
    )(members, slots, own, *pieces)


def place_kernel(slots_ref, *rest):
    pieces, out_ref, marks = rest[:-2], rest[-2], rest[-1]
    copies = [
        pltpu.make_async_copy(piece, out_ref.at[slots_ref[place]], marks.at[place])
        for place, piece in enumerate(pieces)
    ]
    for copy in copies:
        copy.start()
    for copy in copies:
        copy.wait()


def lay_out(slots, pieces):
    any_space = pl.BlockSpec(memory_space=pl.ANY)
    return pl.pallas_call(
        place_kernel,
        grid_spec=pltpu.PrefetchScalarGridSpec(
            num_scalar_prefetch=1,
            grid=(1,),
            in_specs=[any_space] * len(pieces),
            out_specs=any_space,
            scratch_shapes=[pltpu.SemaphoreType.DMA((len(pieces),))],
        ),
        out_shape=jax.ShapeDtypeStruct((len(pieces),) + pieces[0].shape, pieces[0].dtype),
        cost_estimate=pl.CostEstimate(flops=0, bytes_accessed=4 * len(pieces) * pieces[0].size, transcendentals=0),
    )(slots, *pieces)


def flip(value, bit):
    size = lax.axis_size("rep")
    return lax.ppermute(value, "rep", [(i, i ^ bit) for i in range(size)])


def turn(value, offset):
    size = lax.axis_size("grp")
    return lax.ppermute(value, "grp", [(i, (i + offset) % size) for i in range(size)])


def spread(piece, order):
    have = {0: piece}
    for bit in order:
        have.update({place ^ bit: flip(part, bit) for place, part in have.items()})
    return have


def slots_of():
    return lax.axis_index("rep") ^ jnp.arange(lax.axis_size("rep"), dtype=jnp.int32)


def plane_gather(piece):
    if lax.axis_size("rep") != 8:
        return lax.all_gather(piece, "rep")
    have = spread(piece, [2, 4, 1])
    return lay_out(slots_of(), [have[place] for place in range(8)])


def halve(value, axis, bit):
    mine = (lax.axis_index("rep") // bit) % 2
    kept = lax.dynamic_index_in_dim(value, mine, axis, keepdims=False)
    sent = lax.dynamic_index_in_dim(value, 1 - mine, axis, keepdims=False)
    return kept, sent.astype(low_type)


class Fold:
    def __init__(self, axis):
        self.axis = axis
        self.quick = lax.axis_size("rep") == 8

    def cores(self, chunks):
        axis = self.axis
        if not self.quick:
            self.value = lax.psum_scatter(chunks, "rep", scatter_dimension=axis)
            return []
        shape = chunks.shape
        kept, sent = halve(chunks.reshape(shape[:axis] + (4, 2) + shape[axis + 1 :]), axis + 1, 1)
        return self.from_cores(kept, sent)

    def from_cores(self, kept, sent):
        self.kept, self.got = [kept], [flip(sent, 1)]
        return [sent]

    def planes(self):
        if not self.quick:
            return []
        axis = self.axis
        value = self.kept[0] + self.got[0].astype(jnp.float32)
        shape = value.shape
        value = value.reshape(shape[:axis] + (2, 2) + shape[axis + 1 :])
        middle = shape[-1] // 2
        one = halve(value[..., :middle], axis + 1, 2)
        two = halve(value[..., middle:], axis, 4)
        self.kept = [one[0], two[0]]
        self.got = [flip(one[1], 2), flip(two[1], 4)]
        return [one[1], two[1]]

    def crossed(self):
        if not self.quick:
            return []
        one, two = (kept + got.astype(jnp.float32) for kept, got in zip(self.kept, self.got))
        one, two = halve(one, self.axis, 4), halve(two, self.axis, 2)
        self.kept = [one[0], two[0]]
        self.got = [flip(one[1], 4), flip(two[1], 2)]
        return [one[1], two[1]]

    def halves(self):
        if not self.quick:
            middle = self.value.shape[-1] // 2
            return self.value[..., :middle], self.value[..., middle:]
        return tuple(kept + got.astype(jnp.float32) for kept, got in zip(self.kept, self.got))

    def members(self):
        value = jnp.concatenate(self.halves(), axis=-1)
        member = lax.axis_index("grp")
        size = lax.axis_size("grp")
        self.own = lax.dynamic_index_in_dim(value, member, 0, keepdims=False)
        sent = [
            lax.dynamic_index_in_dim(value, (member + offset) % size, 0, keepdims=False).astype(low_type)
            for offset in range(1, size)
        ]
        self.got = [turn(part, offset + 1) for offset, part in enumerate(sent)]
        return sent

    def total(self):
        return sum((got.astype(jnp.float32) for got in self.got), self.own)


def gradient_chunks(gradient):
    groups = lax.axis_size("grp")
    replicas = lax.axis_size("rep")
    rows, columns = gradient.shape
    return gradient.reshape(groups, replicas, rows // (groups * replicas), columns)


def across_wide(chunks):
    member = lax.axis_index("grp")
    size = lax.axis_size("grp")
    total = lax.dynamic_index_in_dim(chunks, member, 0, keepdims=False)
    for offset in range(1, size):
        sent = lax.dynamic_index_in_dim(chunks, (member + offset) % size, 0, keepdims=False)
        total = total + turn(sent, offset)
    return total


def group_gather(value):
    member = lax.axis_index("grp")
    size = lax.axis_size("grp")
    result = jnp.zeros((size,) + value.shape, value.dtype)
    result = lax.dynamic_update_index_in_dim(result, value, member, 0)
    for offset in range(1, size):
        result = lax.dynamic_update_index_in_dim(
            result, turn(value, offset), (member + size - offset) % size, 0
        )
    return result


def total_sum(value):
    for j in range(lax.axis_size("rep").bit_length() - 1):
        value = value + flip(value, 1 << j)
    return jnp.sum(group_gather(value), axis=0)


def weight_gather(shard):
    member = lax.axis_index("grp")
    groups = lax.axis_size("grp")
    replicas = lax.axis_size("rep")
    rows, columns = shard.shape
    if replicas != 8:
        return lax.all_gather(shard, "grp", tiled=True)
    parts = shard.reshape(replicas, rows // replicas, columns)
    own = lax.dynamic_index_in_dim(parts, lax.axis_index("rep"), 0, keepdims=False)
    fetched = jnp.stack([turn(own, offset) for offset in range(1, groups)])
    have = spread(fetched, [2, 4, 1])
    members = (member + groups - jnp.arange(groups, dtype=jnp.int32)) % groups
    whole = assemble(members, slots_of(), parts, [have[place] for place in range(replicas)])
    return whole.reshape(groups * rows, columns)


def contract(left, right, left_dim, right_dim):
    return lax.dot_general(
        left, right, (((left_dim,), (right_dim,)), ((), ())), preferred_element_type=jnp.float32
    )


def layer_norm(values, gain, shift):
    center = values - jnp.mean(values, axis=-1, keepdims=True)
    spread = jnp.mean(center * center, axis=-1, keepdims=True)
    return center * lax.rsqrt(spread + ln_eps) * gain + shift


def rope_tables(length):
    freqs = rope_base ** (-jnp.arange(HD // 2, dtype=jnp.float32) * 2.0 / HD)
    angles = jnp.arange(length, dtype=jnp.float32)[:, None] * freqs[None, :]
    cosine, sine = jnp.cos(angles), jnp.sin(angles)
    return (
        jnp.concatenate([cosine] * 4, axis=-1),
        jnp.concatenate([-sine, sine, -sine, sine], axis=-1),
    )


def swiglu(joined):
    middle = joined.shape[-1] // 2
    return jax.nn.silu(joined[:, :middle]) * joined[:, middle:]


def merge_stats(first_part, second_part):
    peak = jnp.maximum(first_part[0], second_part[0])
    spread = first_part[1] * jnp.exp(first_part[0] - peak) + second_part[1] * jnp.exp(
        second_part[0] - peak
    )
    return (peak, spread, first_part[2] + second_part[2])


def body(
    ids,
    lengths,
    picks,
    labels,
    loss_mask,
    table,
    w_qkv,
    w_out,
    w_gu,
    w_down,
    norms,
    table_rows,
    table_cols,
    qkv_rows,
    qkv_cols,
    out_rows,
    out_cols,
    gu_rows,
    gu_cols,
    down_rows,
    down_cols,
    norms_moment,
):
    member = lax.axis_index("grp")
    groups = lax.axis_size("grp")
    replica = lax.axis_index("rep")
    replicas = lax.axis_size("rep")
    seqs, length = ids.shape
    width = table.shape[1]
    vocab_rows = table.shape[0]
    own_rows = seqs * picks.shape[1]
    tokens = seqs * length
    block = -(-vocab_rows // (16 * replicas)) * 16
    padded = block * replicas

    packed = jnp.concatenate([ids.reshape(-1), labels.reshape(-1), loss_mask.reshape(-1)])
    group_packed = group_gather(packed)
    group_ids = group_packed[:, :tokens].reshape(-1)
    group_labels = group_packed[:, tokens : tokens + own_rows].reshape(-1)
    group_mask = group_packed[:, tokens + own_rows :].reshape(-1)
    shard_rows = w_qkv.shape[0]
    near = weight_gather(jnp.concatenate([w_qkv, w_out], axis=1).astype(low_type))
    far = weight_gather(
        jnp.concatenate([w_gu.astype(low_type), w_down.astype(low_type).reshape(shard_rows, -1)], axis=1)
    )
    loss_count = jnp.sum(group_mask).astype(jnp.float32)[None]
    for j in range(replicas.bit_length() - 1):
        loss_count = loss_count + flip(loss_count, 1 << j)
    loss_count = loss_count[0]

    local_ids = group_ids - member * vocab_rows
    owned = (local_ids >= 0) & (local_ids < vocab_rows)
    found = lookup(jnp.where(owned, local_ids, -1), table)
    embed = lax.psum_scatter(found, "grp", scatter_dimension=0, tiled=True)
    late_table, _ = lax.optimization_barrier((table, found))
    table_low = jnp.pad(late_table.astype(low_type), ((0, padded - vocab_rows), (0, 0)))
    places, order = lax.sort(
        (jnp.where(owned, local_ids, padded), jnp.arange(local_ids.shape[0], dtype=jnp.int32)), num_keys=1
    )
    bounds = jnp.arange(replicas + 1, dtype=jnp.int32) * block
    starts = jnp.sum((places[None, :] < bounds[:, None]).astype(jnp.int32), axis=1)

    w_out_low = near[:, 3 * width :]
    w_gu_low = far[:, : w_gu.shape[1]]
    w_down_low = far[:, w_gu.shape[1] :].reshape(-1, width)
    cosine, sine = rope_tables(length)
    first, first_low, queries, keys, values = project(embed, norms, cosine, sine, near)
    mixed_low, log_sums = attend(lengths, queries, keys, values)
    first_sum = first + jnp.dot(mixed_low, w_out_low, preferred_element_type=jnp.float32)
    second = layer_norm(first_sum, norms[2], norms[3])
    second_low = second.astype(low_type)
    gate_up = jnp.dot(second_low, w_gu_low, preferred_element_type=jnp.float32)
    hidden_low = swiglu(gate_up).astype(low_type)
    second_sum = second + jnp.dot(hidden_low, w_down_low, preferred_element_type=jnp.float32)
    final = layer_norm(second_sum, norms[4], norms[5])

    flat_picks = (jnp.arange(seqs, dtype=jnp.int32)[:, None] * length + picks).reshape(-1)
    chosen = final[flat_picks].astype(low_type)
    group_chosen = group_gather(chosen).reshape(groups * own_rows, width)
    rows_at = jnp.arange(padded, dtype=jnp.int32)[:, None]
    logits = jnp.where(rows_at < vocab_rows, contract(table_low, group_chosen, 1, 1), neg_large)
    peak = jnp.max(logits, axis=0)
    spread_sum = jnp.sum(jnp.exp(logits - peak[None, :]), axis=0)
    local_labels = group_labels - member * vocab_rows
    inside = (local_labels >= 0) & (local_labels < vocab_rows)
    hits = (rows_at == local_labels[None, :]) & inside[None, :]
    target = jnp.sum(jnp.where(hits, logits, 0.0), axis=0)
    stats = group_gather(jnp.stack([peak, spread_sum, target]))
    so_far = (stats[0, 0], stats[0, 1], stats[0, 2])
    for place in range(1, groups):
        so_far = merge_stats(so_far, (stats[place, 0], stats[place, 1], stats[place, 2]))
    peak_all, spread_all, target_all = so_far
    log_total = peak_all + jnp.log(spread_all)
    counted = group_mask > 0
    terms = jnp.where(counted, log_total - target_all, 0.0)
    own_terms = lax.dynamic_slice_in_dim(terms, member * own_rows, own_rows)
    row_scale = jnp.where(counted, 1.0 / loss_count, 0.0)
    dlogits = (
        (jnp.exp(logits - log_total[None, :]) - hits.astype(jnp.float32)) * row_scale[None, :]
    ).astype(low_type)
    chosen_part = contract(dlogits, table_low, 0, 0)
    chosen_grad = across_wide(chosen_part.reshape(groups, own_rows, width))
    final_grad = jnp.zeros((tokens, width), jnp.float32).at[flat_picks].add(chosen_grad)

    _, pull = jax.vjp(layer_norm, second_sum, norms[4], norms[5])
    sum_grad, gain_three, shift_three = pull(final_grad)
    branch_low = sum_grad.astype(low_type)
    down = Fold(1)
    down.cores(gradient_chunks(contract(hidden_low, branch_low, 0, 0)))
    hidden_grad = contract(branch_low, w_down_low, 1, 1)
    _, pull = jax.vjp(swiglu, gate_up)
    gate_low = pull(hidden_grad)[0].astype(low_type)
    gate = Fold(1)
    gate.cores(gradient_chunks(contract(second_low, gate_low, 0, 0)))
    second_grad = sum_grad + contract(gate_low, w_gu_low, 1, 1)
    _, pull = jax.vjp(layer_norm, first_sum, norms[2], norms[3])
    first_sum_grad, gain_two, shift_two = pull(second_grad)
    attn_low = first_sum_grad.astype(low_type)
    mixed_grad = contract(attn_low, w_out_low, 1, 1).astype(low_type)
    after = down.planes() + gate.planes()
    pairs = width // LANES
    one_part = attend_back(
        lengths, queries, keys, values, mixed_grad, log_sums, cosine, sine, 0, pairs // 2, after
    )
    after = down.crossed() + gate.crossed()
    two_part = attend_back(
        lengths, queries, keys, values, mixed_grad, log_sums, cosine, sine, pairs // 2, pairs // 2, after + list(one_part[:1])
    )
    joined_grad = jnp.concatenate(
        [side for parts in zip(one_part, two_part) for side in parts], axis=1
    )
    after = down.members() + gate.members()
    joined_grad, after = lax.optimization_barrier((joined_grad, after))
    first_grad = first_sum_grad + contract(joined_grad, near[:, : 3 * width], 1, 1)
    _, pull = jax.vjp(layer_norm, embed.astype(jnp.float32), norms[0], norms[1])
    embed_grad, gain_one, shift_one = pull(first_grad)
    norm_grad = jnp.stack([gain_one, shift_one, gain_two, shift_two, gain_three, shift_three])
    group_embed = lax.all_gather(embed_grad.astype(low_type), "grp", axis=0, tiled=True)
    join = Fold(1)
    join.cores(
        gradient_chunks(
            jnp.concatenate(
                [contract(first_low, joined_grad, 0, 0), contract(mixed_low, attn_low, 0, 0)], axis=1
            )
        )
    )
    join.planes()
    join.crossed()
    join.members()
    gu_share, down_share, join_share = gate.total(), down.total(), join.total()
    part_rows = join_share.shape[0]

    core = replica % 2
    half_args = (starts, places, order, dlogits, group_chosen, group_embed, block)
    head = Fold(0)
    if head.quick:
        sent = table_grad_half((1 - core)[None], *half_args, low_type)
        kept = table_grad_half(core[None], *half_args, jnp.float32)
        head.from_cores(kept, sent)
    else:
        sides = [table_grad_half(jnp.full((1,), j, jnp.int32), *half_args, jnp.float32) for j in range(2)]
        head.cores(jnp.stack(sides, axis=1).reshape(replicas, block, width))
    head.planes()
    head.crossed()
    table_one, table_two = head.halves()
    table_share = jnp.concatenate([table_one, table_two], axis=1)

    shares = (
        table_share,
        join_share[:, : 3 * width],
        join_share[:, 3 * width :],
        gu_share,
        down_share,
    )
    old_rows = (table_rows, qkv_rows, out_rows, gu_rows, down_rows)
    old_cols = (table_cols, qkv_cols, out_cols, gu_cols, down_cols)
    masters = (table, w_qkv, w_out, w_gu, w_down)
    col_parts = [jnp.sum(gradient * gradient, axis=0) for gradient in shares]
    row_old = jnp.stack([jnp.sum(rows) for rows in old_rows]) / replicas
    small = [norm_grad.reshape(-1)] + col_parts + [row_old, jnp.sum(own_terms)[None]]
    totals = total_sum(jnp.concatenate(small))
    cuts = []
    start = 0
    for part in small:
        cuts.append(totals[start : start + part.shape[0]])
        start += part.shape[0]
    norm_sum = cuts[0].reshape(norm_grad.shape)
    col_totals = cuts[1:6]
    old_totals = cuts[6]
    loss_sum = cuts[7][0]
    squares = [jnp.sum(part) for part in col_totals]
    clip_norm = jnp.sqrt(sum(squares) + jnp.sum(norm_sum * norm_sum))
    factor = clip_limit / jnp.maximum(clip_norm, clip_limit)
    decay = 1.0 - float(STEP) ** (-0.8)

    far_whole = plane_gather(
        jnp.concatenate(
            [gu_share.astype(low_type), down_share.astype(low_type).reshape(part_rows, -1)], axis=1
        )
    ).reshape(shard_rows, -1)
    near_whole = plane_gather(join_share.astype(low_type)).reshape(shard_rows, -1)
    wholes = [
        None,
        near_whole[:, : 3 * width],
        near_whole[:, 3 * width :],
        far_whole[:, : w_gu.shape[1]],
        far_whole[:, w_gu.shape[1] :].reshape(w_down.shape),
    ]
    table_one, table_two = table_one.astype(low_type), table_two.astype(low_type)

    outputs = []
    for place in range(5):
        rows, columns = masters[place].shape
        full_rows = rows * groups
        new_cols = (
            decay * old_cols[place] + (1.0 - decay) * (col_totals[place] * factor * factor) / full_rows
        )
        row_total = decay * old_totals[place] + (1.0 - decay) * (squares[place] * factor * factor) / columns
        row_mean = row_total / full_rows
        if place == 0 and head.quick:
            ones = spread(table_one, [4, 2, 1])
            twos = spread(table_two, [2, 4, 1])
            tiles = padded // TILE
            row_tiles = jnp.pad(table_rows, (0, padded - vocab_rows), constant_values=1.0).reshape(tiles, 1, TILE)
            scalars = jnp.stack([factor, row_mean])
            so_far = (
                blank(table.shape, jnp.float32),
                blank(table.shape, jnp.float32),
                blank((tiles, 1, TILE), jnp.float32),
            )
            slots = slots_of()
            for part in (0, 4, 2, 6, 1, 5, 3, 7):
                so_far = update(
                    slots[part][None], scalars, ones[part], twos[part], table, row_tiles, new_cols[None, :], so_far
                )
            outputs.extend([so_far[0], so_far[2].reshape(-1)[:vocab_rows], new_cols, so_far[1]])
            continue
        if place == 0:
            whole = plane_gather(jnp.concatenate([table_one, table_two], axis=1))
            gradient = whole.reshape(padded, width)[:vocab_rows].astype(jnp.float32)
        else:
            gradient = wholes[place].astype(jnp.float32)
        row_means = jnp.mean(gradient * gradient, axis=1)
        new_rows = decay * old_rows[place] + (1.0 - decay) * (row_means * factor * factor)
        clipped = gradient * factor
        scale = new_rows[:, None] * new_cols[None, :] / row_mean
        new_master = masters[place] - rate_matrix * clipped * lax.rsqrt(scale)
        outputs.extend([clipped, new_rows, new_cols, new_master])
    norm_clipped = norm_sum * factor
    moment_new = decay * norms_moment + (1.0 - decay) * norm_clipped * norm_clipped
    norms_new = norms - rate_norm * norm_clipped * lax.rsqrt(moment_new)
    return (
        (loss_sum, loss_count, clip_norm) + tuple(outputs) + (norm_clipped, moment_new, norms_new)
    )


def solution(mesh):
    in_specs = (
        P(("grp", "rep"), None),
        P(("grp", "rep")),
        P(("grp", "rep"), None),
        P(("grp", "rep"), None),
        P(("grp", "rep"), None),
        P("grp", None),
        P("grp", None),
        P("grp", None),
        P("grp", None),
        P("grp", None),
        P(),
        P("grp"),
        P(),
        P("grp"),
        P(),
        P("grp"),
        P(),
        P("grp"),
        P(),
        P("grp"),
        P(),
        P(),
    )
    out_specs = (
        P(),
        P(),
        P(),
        P("grp", None),
        P("grp"),
        P(),
        P("grp", None),
        P("grp", None),
        P("grp"),
        P(),
        P("grp", None),
        P("grp", None),
        P("grp"),
        P(),
        P("grp", None),
        P("grp", None),
        P("grp"),
        P(),
        P("grp", None),
        P("grp", None),
        P("grp"),
        P(),
        P("grp", None),
        P(),
        P(),
        P(),
    )
    return jax.shard_map(body, mesh=mesh, in_specs=in_specs, out_specs=out_specs, check_vma=False)
```

time: 1560 us -> 1980 us (1.27)
  Pallas kernels: 0.01 us -> 981 us
  local copies, waits for them, and re-layouts: 323 us -> 114 us
  matrix products: 314 us -> 152 us
  other arithmetic: 322 us -> 184 us
  blocking collectives: 45.4 us -> 0 us
  starting transfers between devices: 192 us -> 167 us
  waiting for transfers between devices: 318 us -> 338 us
    pallas_call x0 -> x19, Pallas kernels: none -> 981 us  [the longest x2 576 us: assemble(): pl.pallas_call(assemble_kernel, grid_spec=pltpu.PrefetchScalarGridSpec(nu...]
    dot_general x19 -> x3, matrix products: 211 us -> 26.3 us  [the longest x1 17.6 us: body(): gate_up = jnp.dot(second_low, w_gu_low, preferred_element_type=jnp.float32)]
    dynamic_update_slice x184 -> x0, local copies, waits for them, and re-layouts: 164 us -> none  [the longest x4 63.4 us: one_sequence(): result, log_sums = lax.map(one_block, blocks)]
    ppermute x126 -> x68, waiting for transfers between devices: 229 us -> 91.7 us  [flip(): return lax.ppermute(value, 'rep', [(i, i ^ bit) for i in range(size)])]
    ppermute x36 -> x30, waiting for transfers between devices: 89.6 us -> 172 us  [turn(): lax.ppermute(value, 'grp', [(i, (i + offset) % size) for i in range(size)])]
    all_gather x1, waiting for transfers between devices: 0.02 us -> 75 us  [body(): lax.all_gather(embed_grad.astype(low_type), 'grp', axis=0, tiled=True)]
    convert_element_type x22 -> x14, other arithmetic: 97.7 us -> 44.2 us  [the longest x1 12.6 us: body(): late_table.astype(low_type)]
    psum x1 -> x0, blocking collectives: 45.4 us -> none  [body(): totals = lax.psum(jnp.concatenate(small), ('grp', 'rep'))]
  transfers between devices with their start and end apart: 164 -> 100, of which waited for: 71 -> 31; matrix products, arithmetic and copies ran while one was open for 39% -> 14% of each run, Pallas kernels for 0% -> 44%
where the time goes in v2:
time: 1980 us; the launch traced here: 1970 us
  Pallas kernels  981 us (50%)
  waiting for transfers between devices  338 us (17%)
  other arithmetic  184 us (9%)
  starting transfers between devices  167 us (8%)
  matrix products  152 us (8%)
  local copies, waits for them, and re-layouts  114 us (6%)
  between operations  32.5 us (2%)
    pallas_call x2, Pallas kernels, assemble(): pl.pallas_call(assemble_kernel, grid_spec=pltpu.PrefetchScalarGridSpec(nu...  576 us
    ppermute x30, waiting for transfers between devices, turn(): lax.ppermute(value, 'grp', [(i, (i + offset) % size) for i in range(size)])  172 us
    pallas_call x2, Pallas kernels, lay_out(): pl.pallas_call(place_kernel, grid_spec=pltpu.PrefetchScalarGridSpec(num_s...  147 us
    dot_general x10, matrix products, contract(): lax.dot_general(left, right, (((left_dim,), (right_dim,)), ((), ())), pre...  126 us
    ppermute x68, starting transfers between devices, flip(): return lax.ppermute(value, 'rep', [(i, i ^ bit) for i in range(size)])  121 us
    ppermute x68, waiting for transfers between devices, flip(): return lax.ppermute(value, 'rep', [(i, i ^ bit) for i in range(size)])  91.7 us
    all_gather x1, waiting for transfers between devices, body(): lax.all_gather(embed_grad.astype(low_type), 'grp', axis=0, tiled=True)  75 us
    pallas_call x2, Pallas kernels, attend_back(): pl.pallas_call(functools.partial(attend_back_kernel, first_pair), grid_sp...  62.7 us
  transfers between devices with their start and end apart: 100, of which 31 were waited for; matrix products, arithmetic and copies ran while one was open for 14% of the time, Pallas kernels for 44%

profile of v2, /device:TPU:1, one launch (start us, length us, event | category | flops | bytes accessed | tf_op | source)
XLA Modules:
  0.0 1969.5 jit_solution(9589791040706946089)
XLA Ops:
  15.9 53.4 %shard_map.413 = bf16[4096,768]{1,0:T(8,128)(2,1)} custom-call(s32[4096]{0:T(1024)} %get-tuple-element.201.places_ref, f32[7632,768]{1,0:T(8,128)} %table_ref.17), custom_call_target="tpu_custom_call" | custom-call | bytes 46891008 | tf_op jit(solution)/shard_map/pallas_call | solution.py:291
  80.5 24.6 %collective-permute-done.15 = bf16[24,9216]{1,0:T(8,128)(2,1)S(1)} collective-permute-done((bf16[24,9216]{1,0:T(8,128)(2,1)S(1)}, bf16[24,9216]{1,0:T(8,128)(2,1)S(1)}, u32[]{:S(2)}, u32[]{:S(2)}) %collective-permute-start.15) | collective-permute-done | bytes 442400 | tf_op jit(solution)/shard_map/ppermute | solution.py:480
  105.1 52.3 %collective-permute-done.14 = bf16[24,9216]{1,0:T(8,128)(2,1)S(1)} collective-permute-done((bf16[24,9216]{1,0:T(8,128)(2,1)S(1)}, bf16[24,9216]{1,0:T(8,128)(2,1)S(1)}, u32[]{:S(2)}, u32[]{:S(2)}) %collective-permute-start.14) | collective-permute-done | bytes 442400 | tf_op jit(solution)/shard_map/ppermute | solution.py:480
  176.1 18.0 collective-permute-done.4
  204.7 15.6 collective-permute-start.29
  224.8 25.0 %collective-permute-start.31 = (f32[1]{0:T(128)}, f32[1]{0:T(128)}, u32[]{:S(2)}, u32[]{:S(2)}) collective-permute-start(f32[1]{0:T(128)} %add.564), channel_id=1, source_target_pairs={{0,4},{1,5},{2,6},{3,7},{4,0},{5,1},{6,2},{7,3},{8,12},{9,13},{10,... | collective-permute-start | bytes 20 | tf_op jit(solution)/shard_map/ppermute | solution.py:475
  250.4 14.8 collective-permute-start.6
  286.6 12.6 convert_element_type.338
  301.2 144.9 %shard_map.414 = bf16[4,8,24,3072]{3,2,1,0:T(8,128)(2,1)} custom-call(s32[4]{0:T(128)} %and_select_fusion.members_ref, s32[8]{0:T(128)} %iota_xor_fusion.slots_ref, bf16[8,24,3072]{2,1,0:T(8,128)(2,1)} %pad_maximum_fusion.2.own_ref, bf16[3,24,3072]{2,1,0:T(8,128)(2,1)} %pad_maximum_fusion.6.rest_0_, bf16[3,24,3072]{2,1,0:T(8,128)(2,1)} %copy-done.58, ...), custom_call_target="tpu_custom_call" | custom-call | bytes 9437184 | tf_op jit(solution)/shard_map/pallas_call | solution.py:431
  447.7 430.8 %shard_map.417 = bf16[4,8,24,9216]{3,2,1,0:T(8,128)(2,1)} custom-call(s32[4]{0:T(128)} %and_select_fusion.members_ref, s32[8]{0:T(128)} %iota_xor_fusion.slots_ref, bf16[8,24,9216]{2,1,0:T(8,128)(2,1)} %pad_maximum_fusion.1.own_ref, bf16[3,24,9216]{2,1,0:T(8,128)(2,1)} %pad_maximum_fusion.3.rest_0_, bf16[3,24,9216]{2,1,0:T(8,128)(2,1)} %copy-done.37, ...), custom_call_target="tpu_custom_call" | custom-call | bytes 28311552 | tf_op jit(solution)/shard_map/pallas_call | solution.py:431
  901.0 47.5 %shard_map.416 = (bf16[1024,768]{1,0:T(8,128)(2,1)}, f32[6,2,1024]{2,1,0:T(2,128)}) custom-call(s32[1]{0:T(128)S(6)} %copy.196.length_ref, bf16[1024,768]{1,0:T(8,128)(2,1)} %get-tuple-element.69.q_ref, bf16[1024,768]{1,0:T(8,128)(2,1)} %get-tuple-element.70.k_ref, bf16[1024,768]{1,0:T(8,128)(2,1)} %get-tuple-element.71.v_ref), custom_call_target="tpu_custom_call" | custom-call | flops 12884901888 | bytes 6291456 | tf_op jit(solution)/shard_map/pallas_call | solution.py:138
  952.8 17.6 fusion.10
  970.4 10.3 multiply_convert_fusion.1
  1008.1 11.6 select_reduce_fusion.1
  1047.9 11.8 fusion.4
  1068.3 25.4 %collective-permute-done.33 = f32[128,768]{1,0:T(8,128)S(1)} collective-permute-done((f32[128,768]{1,0:T(8,128)S(1)}, f32[128,768]{1,0:T(8,128)S(1)}, u32[]{:S(2)}, u32[]{:S(2)}) %collective-permute-start.33) | collective-permute-done | bytes 393248 | tf_op jit(solution)/shard_map/ppermute | solution.py:480
  1105.7 23.5 %fusion.39 = (f32[1024,3072]{1,0:T(8,128)}, f32[1024,3072]{1,0:T(8,128)}) fusion(f32[1024,6144]{1,0:T(8,128)} %fusion.10, bf16[3072,768]{1,0:T(8,128)(2,1)} %reshape.433, f32[1024,768]{1,0:T(8,128)} %get-tuple-element.153, f32[1024]{0:T(1024)S(1)} %negate_multiply_fusion.2), kind=kOutput, calls=%fused_computation.124 | convolution fusion | flops 4871159808 | bytes 58200064 | tf_op jit(solution)/shard_map/dot_general | solution.py:623
  1146.1 24.2 %fusion.31 = f32[768,6144]{1,0:T(8,128)} fusion(f32[1024,3072]{1,0:T(8,128)} %get-tuple-element.159, f32[1024,3072]{1,0:T(8,128)} %get-tuple-element.158, f32[1024,768]{1,0:T(8,128)S(1)} %get-tuple-element.157, f32[768]{0:T(1024)S(1)} %copy-done.72, f32[768]{0:T(1024)S(1)} %get-tuple-element.126, f32[1024]{0:T(1024)S(1)} %fusion.119, ...), kind=kOutput, calls=%fused_computation.110 | convolution fusion | flops 9680191488 | bytes 47200256 | tf_op jit(solution)/shard_map/dot_general | solution.py:623
  1176.9 19.6 multiply_reduce_fusion.1
  1205.1 10.1 collective-permute-done.38
  1238.3 31.5 %shard_map.418 = (bf16[1024,384]{1,0:T(8,128)(2,1)}, bf16[1024,384]{1,0:T(8,128)(2,1)}, bf16[1024,384]{1,0:T(8,128)(2,1)}) custom-call(s32[1]{0:T(128)S(6)} %copy.196.length_ref, bf16[1024,768]{1,0:T(8,128)(2,1)} %get-tuple-element.69.q_ref, bf16[1024,768]{1,0:T(8,128)(2,1)} %get-tuple-element.70.k_ref, bf16[1024,768]{1,0:T(8,128)(2,1)} %get-tuple-element.71.v_ref, ...), custom_call_target="tpu_custom_call" | custom-call | flops 16106127360 | bytes 6291456 | tf_op jit(solution)/shard_map/pallas_call | solution.py:223
  1276.7 31.3 %shard_map.419 = (bf16[1024,384]{1,0:T(8,128)(2,1)}, bf16[1024,384]{1,0:T(8,128)(2,1)}, bf16[1024,384]{1,0:T(8,128)(2,1)}) custom-call(s32[1]{0:T(128)S(6)} %copy.196.length_ref, bf16[1024,768]{1,0:T(8,128)(2,1)} %get-tuple-element.69.q_ref, bf16[1024,768]{1,0:T(8,128)(2,1)} %get-tuple-element.70.k_ref, bf16[1024,768]{1,0:T(8,128)(2,1)} %get-tuple-element.71.v_ref, ...), custom_call_target="tpu_custom_call" | custom-call | flops 16106127360 | bytes 6291456 | tf_op jit(solution)/shard_map/pallas_call | solution.py:223
  1391.2 14.0 collective-permute-done.62
  1412.9 75.0 %all-gather.2.cloned.1.call-done.embed_ref = bf16[4096,768]{1,0:T(8,128)(2,1)} async-done(((bf16[1024,768]{1,0:T(8,128)(2,1)}), bf16[4096,768]{1,0:T(8,128)(2,1)}) %all-gather.2.cloned.1.call-update) | async-done | bytes 6291472 | tf_op jit(solution)/shard_map/all_gather | solution.py:795
  1487.9 16.6 shard_map.421
  1524.8 10.7 collective-permute-done.51
  1535.6 15.2 shard_map.420
  1550.8 11.5 convert_add_fusion
  1576.4 32.4 %collective-permute-done.52 = bf16[4,24,1536]{2,1,0:T(8,128)(2,1)S(1)} collective-permute-done((bf16[4,24,1536]{2,1,0:T(8,128)(2,1)S(1)}, bf16[4,24,1536]{2,1,0:T(8,128)(2,1)S(1)}, u32[]{:S(2)}, u32[]{:S(2)}) %collective-permute-start.52) | collective-permute-done | bytes 294944 | tf_op jit(solution)/shard_map/ppermute | solution.py:475
  1619.4 10.2 collective-permute-done.56
  1664.4 109.0 %shard_map.434 = bf16[8,24,9216]{2,1,0:T(8,128)(2,1)} custom-call(s32[8]{0:T(128)} %iota_xor_fusion.slots_ref, bf16[24,9216]{1,0:T(8,128)(2,1)} %copy-done.35, bf16[24,9216]{1,0:T(8,128)(2,1)} %copy-done.51, bf16[24,9216]{1,0:T(8,128)(2,1)} %collective-permute-done.92.rest_2_, bf16[24,9216]{1,0:T(8,128)(2,1)} %copy-done.54, bf16[24,9216]{1,0:T(8,128)(2,1)} %copy-done.52, ...), custom_call_target="tpu_custom_call" | custom-call | bytes 7077888 | tf_op jit(solution)/shard_map/pallas_call | solution.py:459
  1779.2 37.7 %shard_map.433 = bf16[8,24,3072]{2,1,0:T(8,128)(2,1)} custom-call(s32[8]{0:T(128)} %iota_xor_fusion.slots_ref, bf16[24,3072]{1,0:T(8,128)(2,1)} %get-tuple-element.139.rest_0_, bf16[24,3072]{1,0:T(8,128)(2,1)} %collective-permute-done.84.rest_1_, bf16[24,3072]{1,0:T(8,128)(2,1)} %collective-permute-done.85.rest_2_, ...), custom_call_target="tpu_custom_call" | custom-call | bytes 2359296 | tf_op jit(solution)/shard_map/pallas_call | solution.py:459
  (646 shorter events, 548.3 us)
Async XLA Ops:
  7.2 884.6 %reduce-scatter.2.cloned.1.call-start = ((), (), s32[]{:S(2)}) async-start(), calls=%async_computation.1 | async-start | bytes 7864320 | tf_op jit(solution)/shard_map/reduce_scatter | solution.py:711
  69.3 1418.6 %all-gather.2.cloned.1.call-start = ((), (), s32[]{:S(2)}) async-start(), calls=%async_computation.2 | async-start | bytes 7864320 | tf_op jit(solution)/shard_map/all_gather | solution.py:795
  80.2 77.2 %collective-permute-start.14 = (bf16[24,9216]{1,0:T(8,128)(2,1)S(1)}, bf16[24,9216]{1,0:T(8,128)(2,1)S(1)}, u32[]{:S(2)}, u32[]{:S(2)}) collective-permute-start(bf16[24,9216]{1,0:T(8,128)(2,1)S(1)} %fusion.70), channel_id=1, source_target_pairs={{0,16},{8,24},{16,0},{24,8},{1,17},{9,25},{17,1},{25,9},{2,18},{10... | collective-permute-start | bytes 1327112 | tf_op jit(solution)/shard_map/ppermute | solution.py:480
  80.2 77.2 %collective-permute-start.13 = (bf16[24,9216]{1,0:T(8,128)(2,1)S(1)}, bf16[24,9216]{1,0:T(8,128)(2,1)S(1)}, u32[]{:S(2)}, u32[]{:S(2)}) collective-permute-start(bf16[24,9216]{1,0:T(8,128)(2,1)S(1)} %fusion.70), channel_id=1, source_target_pairs={{0,8},{8,16},{16,24},{24,0},{1,9},{9,17},{17,25},{25,1},{2,10},{10... | collective-permute-start | bytes 1327112 | tf_op jit(solution)/shard_map/ppermute | solution.py:480
  194.9 70.3 %collective-permute-start.7 = (bf16[3,24,3072]{2,1,0:T(8,128)(2,1)}, bf16[3,24,3072]{2,1,0:T(8,128)(2,1)}, u32[]{:S(2)}, u32[]{:S(2)}) collective-permute-start(bf16[3,24,3072]{2,1,0:T(8,128)(2,1)} %pad_maximum_fusion.6.rest_0_), channel_id=1, source_target_pairs={{0,2},{1,3},{2,0},{3,1},{4,6},{5,7},{6,4},{7,5},{8,10},{9,11},{10,... | collective-permute-start | bytes 1327112 | tf_op jit(solution)/shard_map/ppermute | solution.py:475
  195.5 72.5 %collective-permute-start.19 = (bf16[3,24,9216]{2,1,0:T(8,128)(2,1)}, bf16[3,24,9216]{2,1,0:T(8,128)(2,1)}, u32[]{:S(2)}, u32[]{:S(2)}) collective-permute-start(bf16[3,24,9216]{2,1,0:T(8,128)(2,1)} %pad_maximum_fusion.3.rest_0_), channel_id=1, source_target_pairs={{0,4},{1,5},{2,6},{3,7},{4,0},{5,1},{6,2},{7,3},{8,12},{9,13},{10,... | collective-permute-start | bytes 3981320 | tf_op jit(solution)/shard_map/ppermute | solution.py:475
  196.9 71.4 %collective-permute-start.21 = (bf16[3,24,9216]{2,1,0:T(8,128)(2,1)}, bf16[3,24,9216]{2,1,0:T(8,128)(2,1)}, u32[]{:S(2)}, u32[]{:S(2)}) collective-permute-start(bf16[3,24,9216]{2,1,0:T(8,128)(2,1)} %collective-permute-done.17.rest_2_), channel_id=1, source_target_pairs={{0,4},{1,5},{2,6},{3,7},{4,0},{5,1},{6,2},{7,3},{8,12},{9,13},{10,... | collective-permute-start | bytes 3981320 | tf_op jit(solution)/shard_map/ppermute | solution.py:475
  201.3 64.5 %collective-permute-start.9 = (bf16[3,24,3072]{2,1,0:T(8,128)(2,1)}, bf16[3,24,3072]{2,1,0:T(8,128)(2,1)S(1)}, u32[]{:S(2)}, u32[]{:S(2)}) collective-permute-start(bf16[3,24,3072]{2,1,0:T(8,128)(2,1)} %pad_maximum_fusion.6.rest_0_), channel_id=1, source_target_pairs={{0,4},{1,5},{2,6},{3,7},{4,0},{5,1},{6,2},{7,3},{8,12},{9,13},{10,... | collective-permute-start | bytes 1327112 | tf_op jit(solution)/shard_map/ppermute | solution.py:475
  267.4 178.8 %collective-permute-start.16 = (bf16[3,24,9216]{2,1,0:T(8,128)(2,1)}, bf16[3,24,9216]{2,1,0:T(8,128)(2,1)S(1)}, u32[]{:S(2)}, u32[]{:S(2)}) collective-permute-start(bf16[3,24,9216]{2,1,0:T(8,128)(2,1)} %pad_maximum_fusion.3.rest_0_), channel_id=1, source_target_pairs={{0,1},{1,0},{2,3},{3,2},{4,5},{5,4},{6,7},{7,6},{8,9},{9,8},{10,11... | collective-permute-start | bytes 3981320 | tf_op jit(solution)/shard_map/ppermute | solution.py:475
  267.8 178.4 %collective-permute-start.18 = (bf16[3,24,9216]{2,1,0:T(8,128)(2,1)}, bf16[3,24,9216]{2,1,0:T(8,128)(2,1)S(1)}, u32[]{:S(2)}, u32[]{:S(2)}) collective-permute-start(bf16[3,24,9216]{2,1,0:T(8,128)(2,1)} %collective-permute-done.17.rest_2_), channel_id=1, source_target_pairs={{0,1},{1,0},{2,3},{3,2},{4,5},{5,4},{6,7},{7,6},{8,9},{9,8},{10,11... | collective-permute-start | bytes 3981320 | tf_op jit(solution)/shard_map/ppermute | solution.py:475
  268.0 178.2 %collective-permute-start.20 = (bf16[3,24,9216]{2,1,0:T(8,128)(2,1)}, bf16[3,24,9216]{2,1,0:T(8,128)(2,1)}, u32[]{:S(2)}, u32[]{:S(2)}) collective-permute-start(bf16[3,24,9216]{2,1,0:T(8,128)(2,1)} %collective-permute-done.19.rest_4_), channel_id=1, source_target_pairs={{0,1},{1,0},{2,3},{3,2},{4,5},{5,4},{6,7},{7,6},{8,9},{9,8},{10,11... | collective-permute-start | bytes 3981320 | tf_op jit(solution)/shard_map/ppermute | solution.py:475
  268.3 177.9 %collective-permute-start.22 = (bf16[3,24,9216]{2,1,0:T(8,128)(2,1)}, bf16[3,24,9216]{2,1,0:T(8,128)(2,1)}, u32[]{:S(2)}, u32[]{:S(2)}) collective-permute-start(bf16[3,24,9216]{2,1,0:T(8,128)(2,1)} %collective-permute-done.21.rest_6_), channel_id=1, source_target_pairs={{0,1},{1,0},{2,3},{3,2},{4,5},{5,4},{6,7},{7,6},{8,9},{9,8},{10,11... | collective-permute-start | bytes 3981320 | tf_op jit(solution)/shard_map/ppermute | solution.py:475
  1143.2 53.3 %collective-permute-start.35 = (bf16[4,4,96,768]{3,2,1,0:T(8,128)(2,1)}, bf16[4,4,96,768]{3,2,1,0:T(8,128)(2,1)}, u32[]{:S(2)}, u32[]{:S(2)}) collective-permute-start(bf16[4,4,96,768]{3,2,1,0:T(8,128)(2,1)} %fusion.28), channel_id=1, source_target_pairs={{0,1},{1,0},{2,3},{3,2},{4,5},{5,4},{6,7},{7,6},{8,9},{9,8},{10,11... | collective-permute-start | bytes 7077896 | tf_op jit(solution)/shard_map/ppermute | solution.py:475
  1176.9 49.5 %collective-permute-start.36 = (bf16[4,4,24,6144]{3,2,0,1:T(8,128)(2,1)}, bf16[4,4,24,6144]{3,2,0,1:T(8,128)(2,1)}, u32[]{:S(2)}, u32[]{:S(2)}) collective-permute-start(bf16[4,4,24,6144]{3,2,0,1:T(8,128)(2,1)} %fusion.13), channel_id=1, source_target_pairs={{0,1},{1,0},{2,3},{3,2},{4,5},{5,4},{6,7},{7,6},{8,9},{9,8},{10,11... | collective-permute-start | bytes 14155784 | tf_op jit(solution)/shard_map/ppermute | solution.py:475
  1365.4 139.3 %collective-permute-start.50 = (bf16[4,4,24,3072]{3,2,0,1:T(8,128)(2,1)}, bf16[4,4,24,3072]{3,2,0,1:T(8,128)(2,1)}, u32[]{:S(2)}, u32[]{:S(2)}) collective-permute-start(bf16[4,4,24,3072]{3,2,0,1:T(8,128)(2,1)} %fusion.27), channel_id=1, source_target_pairs={{0,1},{1,0},{2,3},{3,2},{4,5},{5,4},{6,7},{7,6},{8,9},{9,8},{10,11... | collective-permute-start | bytes 7077896 | tf_op jit(solution)/shard_map/ppermute | solution.py:475
  1407.0 97.5 %collective-permute-start.60 = (bf16[24,6144]{1,0:T(8,128)(2,1)}, bf16[24,6144]{1,0:T(8,128)(2,1)S(1)}, u32[]{:S(2)}, u32[]{:S(2)}) collective-permute-start(bf16[24,6144]{1,0:T(8,128)(2,1)} %get-tuple-element.170), channel_id=1, source_target_pairs={{0,24},{8,0},{16,8},{24,16},{1,25},{9,1},{17,9},{25,17},{2,26},{10... | collective-permute-start | bytes 884744 | tf_op jit(solution)/shard_map/ppermute | solution.py:480
  1407.0 97.5 %collective-permute-start.59 = (bf16[24,6144]{1,0:T(8,128)(2,1)}, bf16[24,6144]{1,0:T(8,128)(2,1)S(1)}, u32[]{:S(2)}, u32[]{:S(2)}) collective-permute-start(bf16[24,6144]{1,0:T(8,128)(2,1)} %get-tuple-element.172), channel_id=1, source_target_pairs={{0,16},{8,24},{16,0},{24,8},{1,17},{9,25},{17,1},{25,9},{2,18},{10... | collective-permute-start | bytes 884744 | tf_op jit(solution)/shard_map/ppermute | solution.py:480
  1407.0 97.5 %collective-permute-start.58 = (bf16[24,6144]{1,0:T(8,128)(2,1)}, bf16[24,6144]{1,0:T(8,128)(2,1)S(1)}, u32[]{:S(2)}, u32[]{:S(2)}) collective-permute-start(bf16[24,6144]{1,0:T(8,128)(2,1)} %get-tuple-element.171), channel_id=1, source_target_pairs={{0,8},{8,16},{16,24},{24,0},{1,9},{9,17},{17,25},{25,1},{2,10},{10... | collective-permute-start | bytes 884744 | tf_op jit(solution)/shard_map/ppermute | solution.py:480
  1504.5 46.3 %collective-permute-start.45 = (bf16[4,960,768]{2,1,0:T(8,128)(2,1)}, bf16[4,960,768]{2,1,0:T(8,128)(2,1)}, u32[]{:S(2)}, u32[]{:S(2)}) collective-permute-start(bf16[4,960,768]{2,1,0:T(8,128)(2,1)} %shard_map.421), channel_id=1, source_target_pairs={{0,1},{1,0},{2,3},{3,2},{4,5},{5,4},{6,7},{7,6},{8,9},{9,8},{10,11... | collective-permute-start | bytes 17694728 | tf_op jit(solution)/shard_map/ppermute | solution.py:475
  1510.3 145.1 %collective-permute-start.91 = (bf16[24,9216]{1,0:T(8,128)(2,1)S(1)}, bf16[24,9216]{1,0:T(8,128)(2,1)S(1)}, u32[]{:S(2)}, u32[]{:S(2)}) collective-permute-start(bf16[24,9216]{1,0:T(8,128)(2,1)S(1)} %pad_maximum_fusion.7.rest_0_), channel_id=1, source_target_pairs={{0,1},{1,0},{2,3},{3,2},{4,5},{5,4},{6,7},{7,6},{8,9},{9,8},{10,11... | collective-permute-start | bytes 1327112 | tf_op jit(solution)/shard_map/ppermute | solution.py:475
  1511.1 106.0 %collective-permute-start.92 = (bf16[24,9216]{1,0:T(8,128)(2,1)S(1)}, bf16[24,9216]{1,0:T(8,128)(2,1)}, u32[]{:S(2)}, u32[]{:S(2)}) collective-permute-start(bf16[24,9216]{1,0:T(8,128)(2,1)S(1)} %pad_maximum_fusion.7.rest_0_), channel_id=1, source_target_pairs={{0,2},{1,3},{2,0},{3,1},{4,6},{5,7},{6,4},{7,5},{8,10},{9,11},{10,... | collective-permute-start | bytes 1327112 | tf_op jit(solution)/shard_map/ppermute | solution.py:475
  1523.6 50.3 %collective-permute-start.54 = (bf16[4,24,1536]{2,1,0:T(8,128)(2,1)S(1)}, bf16[4,24,1536]{2,1,0:T(8,128)(2,1)}, u32[]{:S(2)}, u32[]{:S(2)}) collective-permute-start(bf16[4,24,1536]{2,1,0:T(8,128)(2,1)S(1)} %fusion.78), channel_id=1, source_target_pairs={{0,2},{1,3},{2,0},{3,1},{4,6},{5,7},{6,4},{7,5},{8,10},{9,11},{10,... | collective-permute-start | bytes 884744 | tf_op jit(solution)/shard_map/ppermute | solution.py:475
  1655.4 118.6 %collective-permute-start.87 = (bf16[24,3072]{1,0:T(8,128)(2,1)}, bf16[24,3072]{1,0:T(8,128)(2,1)}, u32[]{:S(2)}, u32[]{:S(2)}) collective-permute-start(bf16[24,3072]{1,0:T(8,128)(2,1)} %get-tuple-element.139.rest_0_), channel_id=1, source_target_pairs={{0,4},{1,5},{2,6},{3,7},{4,0},{5,1},{6,2},{7,3},{8,12},{9,13},{10,... | collective-permute-start | bytes 442376 | tf_op jit(solution)/shard_map/ppermute | solution.py:475
  1657.1 117.0 %collective-permute-start.89 = (bf16[24,3072]{1,0:T(8,128)(2,1)}, bf16[24,3072]{1,0:T(8,128)(2,1)}, u32[]{:S(2)}, u32[]{:S(2)}) collective-permute-start(bf16[24,3072]{1,0:T(8,128)(2,1)} %collective-permute-done.85.rest_2_), channel_id=1, source_target_pairs={{0,4},{1,5},{2,6},{3,7},{4,0},{5,1},{6,2},{7,3},{8,12},{9,13},{10,... | collective-permute-start | bytes 442376 | tf_op jit(solution)/shard_map/ppermute | solution.py:475
  1658.2 116.4 %collective-permute-start.64 = (f32[15366]{0:T(1024)S(1)}, f32[15366]{0:T(1024)S(1)}, u32[]{:S(2)}, u32[]{:S(2)}) collective-permute-start(f32[15366]{0:T(1024)S(1)} %concatenate.65), channel_id=1, source_target_pairs={{0,1},{1,0},{2,3},{3,2},{4,5},{5,4},{6,7},{7,6},{8,9},{9,8},{10,11... | collective-permute-start | bytes 184400 | tf_op jit(solution)/shard_map/ppermute | solution.py:475
  1826.5 59.7 %collective-permute-start.70 = (bf16[960,384]{1,0:T(8,128)(2,1)}, bf16[960,384]{1,0:T(8,128)(2,1)}, u32[]{:S(2)}, u32[]{:S(2)}) collective-permute-start(bf16[960,384]{1,0:T(8,128)(2,1)} %get-tuple-element.143.one_ref), channel_id=1, source_target_pairs={{0,4},{1,5},{2,6},{3,7},{4,0},{5,1},{6,2},{7,3},{8,12},{9,13},{10,... | collective-permute-start | bytes 2211848 | tf_op jit(solution)/shard_map/ppermute | solution.py:475
  1827.4 58.9 %collective-permute-start.76 = (bf16[960,384]{1,0:T(8,128)(2,1)}, bf16[960,384]{1,0:T(8,128)(2,1)}, u32[]{:S(2)}, u32[]{:S(2)}) collective-permute-start(bf16[960,384]{1,0:T(8,128)(2,1)} %get-tuple-element.143.one_ref), channel_id=1, source_target_pairs={{0,2},{1,3},{2,0},{3,1},{4,6},{5,7},{6,4},{7,5},{8,10},{9,11},{10,... | collective-permute-start | bytes 2211848 | tf_op jit(solution)/shard_map/ppermute | solution.py:475
  1831.8 54.4 %collective-permute-start.73 = (bf16[960,384]{1,0:T(8,128)(2,1)}, bf16[960,384]{1,0:T(8,128)(2,1)}, u32[]{:S(2)}, u32[]{:S(2)}) collective-permute-start(bf16[960,384]{1,0:T(8,128)(2,1)} %get-tuple-element.141.two_ref), channel_id=1, source_target_pairs={{0,2},{1,3},{2,0},{3,1},{4,6},{5,7},{6,4},{7,5},{8,10},{9,11},{10,... | collective-permute-start | bytes 2211848 | tf_op jit(solution)/shard_map/ppermute | solution.py:475
  1836.5 50.4 %collective-permute-start.80 = (bf16[960,384]{1,0:T(8,128)(2,1)}, bf16[960,384]{1,0:T(8,128)(2,1)}, u32[]{:S(2)}, u32[]{:S(2)}) collective-permute-start(bf16[960,384]{1,0:T(8,128)(2,1)} %get-tuple-element.141.two_ref), channel_id=1, source_target_pairs={{0,4},{1,5},{2,6},{3,7},{4,0},{5,1},{6,2},{7,3},{8,12},{9,13},{10,... | collective-permute-start | bytes 2211848 | tf_op jit(solution)/shard_map/ppermute | solution.py:475
  1840.5 63.5 %collective-permute-start.82 = (bf16[960,384]{1,0:T(8,128)(2,1)}, bf16[960,384]{1,0:T(8,128)(2,1)}, u32[]{:S(2)}, u32[]{:S(2)}) collective-permute-start(bf16[960,384]{1,0:T(8,128)(2,1)} %get-tuple-element.143.one_ref), channel_id=1, source_target_pairs={{0,1},{1,0},{2,3},{3,2},{4,5},{5,4},{6,7},{7,6},{8,9},{9,8},{10,11... | collective-permute-start | bytes 2211848 | tf_op jit(solution)/shard_map/ppermute | solution.py:475
  1905.4 45.5 %collective-permute-start.72 = (bf16[960,384]{1,0:T(8,128)(2,1)S(1)}, bf16[960,384]{1,0:T(8,128)(2,1)S(1)}, u32[]{:S(2)}, u32[]{:S(2)}) collective-permute-start(bf16[960,384]{1,0:T(8,128)(2,1)S(1)} %collective-permute-done.71.one_ref), channel_id=1, source_target_pairs={{0,1},{1,0},{2,3},{3,2},{4,5},{5,4},{6,7},{7,6},{8,9},{9,8},{10,11... | collective-permute-start | bytes 2211848 | tf_op jit(solution)/shard_map/ppermute | solution.py:475
  1906.1 44.8 %collective-permute-start.75 = (bf16[960,384]{1,0:T(8,128)(2,1)}, bf16[960,384]{1,0:T(8,128)(2,1)S(1)}, u32[]{:S(2)}, u32[]{:S(2)}) collective-permute-start(bf16[960,384]{1,0:T(8,128)(2,1)} %collective-permute-done.74.two_ref), channel_id=1, source_target_pairs={{0,1},{1,0},{2,3},{3,2},{4,5},{5,4},{6,7},{7,6},{8,9},{9,8},{10,11... | collective-permute-start | bytes 2211848 | tf_op jit(solution)/shard_map/ppermute | solution.py:475
  (181 other events, 3624.5 us)
Sparse Core Ops, SparseCore 0:
  69.5 152.9 reduce-scatter.1
  1332.2 155.6 all-gather.1

commit v3 on v2

--- a/solution.py
+++ b/solution.py
@@ -268,39 +268,42 @@
     )()
 
 
-def lookup_kernel(places_ref, table_ref, out_ref, rows):
-    base = pl.program_id(0) * CHUNK
-    rows[...] = jnp.zeros_like(rows)
-
-    def one(i, carry):
-        place = places_ref[base + i]
-
-        @pl.when(place >= 0)
-        def _():
-            rows[pl.ds(i, 1), :] = table_ref[pl.ds(place, 1), :]
-
+def lookup_kernel(starts_ref, places_ref, order_ref, table_ref, out_ref, rows):
+    count = out_ref.shape[0]
+    owned = starts_ref[starts_ref.shape[0] - 1]
+    for start in range(0, count, CHUNK):
+        rows[start : start + CHUNK, :] = jnp.zeros((CHUNK, rows.shape[1]), jnp.float32)
+
+    def eight(step, carry):
+        for j in range(8):
+            i = step * 8 + j
+            valid = i < owned
+            source = jnp.where(valid, places_ref[i], 0)
+            target = jnp.where(valid, order_ref[i], count)
+            rows[pl.ds(target, 1), :] = table_ref[pl.ds(source, 1), :]
         return carry
 
-    lax.fori_loop(0, CHUNK, one, 0, unroll=8)
-    out_ref[...] = rows[...].astype(low_type)
-
-
-def lookup(places, table):
+    lax.fori_loop(0, (owned + 7) // 8, eight, 0)
+    for start in range(0, count, CHUNK):
+        out_ref[start : start + CHUNK, :] = rows[start : start + CHUNK, :].astype(low_type)
+
+
+def lookup(starts, places, order, table):
     count = places.shape[0]
     width = table.shape[1]
     return pl.pallas_call(
         lookup_kernel,
         grid_spec=pltpu.PrefetchScalarGridSpec(
-            num_scalar_prefetch=1,
-            grid=(count // CHUNK,),
+            num_scalar_prefetch=3,
+            grid=(1,),
             in_specs=[pl.BlockSpec(table.shape, lambda i, *_: (0, 0), pipeline_mode=pl.Buffered(1))],
-            out_specs=pl.BlockSpec((CHUNK, width), lambda i, *_: (i, 0)),
-            scratch_shapes=[pltpu.VMEM((CHUNK, width), jnp.float32)],
+            out_specs=pl.BlockSpec((count, width), lambda i, *_: (0, 0), pipeline_mode=pl.Buffered(1)),
+            scratch_shapes=[pltpu.VMEM((count + 8, width), jnp.float32)],
         ),
         out_shape=jax.ShapeDtypeStruct((count, width), low_type),
         compiler_params=pltpu.CompilerParams(vmem_limit_bytes=vmem),
-        cost_estimate=pl.CostEstimate(flops=0, bytes_accessed=table.size * 8, transcendentals=0),
-    )(places, table)
+        cost_estimate=pl.CostEstimate(flops=0, bytes_accessed=table.size * 12, transcendentals=0),
+    )(starts, places, order, table)
 
 
 def table_grad_kernel(core_ref, starts_ref, places_ref, order_ref, dlogits_ref, chosen_ref, embed_ref, out_ref, rows, total):
@@ -354,39 +357,48 @@
 
 TILE = 240
 
-def update_kernel(slot_ref, scalars_ref, one_ref, two_ref, table_ref, rows_ref, cols_ref, *rest):
+def update_kernel(parts, slots_ref, scalars_ref, *rest):
+    pieces = rest[: 4 * parts]
+    table_ref, rows_ref, cols_ref = rest[4 * parts : 4 * parts + 3]
     grad_ref, new_ref, rows_new_ref = rest[-3:]
-    gradient = jnp.concatenate([one_ref[...], two_ref[...]], axis=1).astype(jnp.float32)
-    factor, row_mean = scalars_ref[0], scalars_ref[1]
+    factor, rate = scalars_ref[0], scalars_ref[1]
     decay = 1.0 - float(STEP) ** (-0.8)
     old = jnp.broadcast_to(rows_ref[0], (LANES, TILE)).T[:, 0:1]
-    means = jnp.mean(gradient * gradient, axis=1, keepdims=True)
-    rows_new = decay * old + (1.0 - decay) * (means * factor * factor)
-    clipped = gradient * factor
-    grad_ref[...] = clipped
-    scale = rows_new * cols_ref[...] / row_mean
-    new_ref[...] = table_ref[...] - rate_matrix * clipped * lax.rsqrt(scale)
-    rows_new_ref[0] = jnp.broadcast_to(rows_new, (TILE, LANES)).T[0:1, :]
-
-
-def update(slot, scalars, one, two, table, rows, cols, so_far):
-    block, half = one.shape
-    width = 2 * half
+    for part in range(4):
+
+        @pl.when(pl.program_id(0) == part)
+        def _(part=part):
+            own = pieces[part * parts : (part + 1) * parts]
+            gradient = jnp.concatenate([piece[...] for piece in own], axis=1).astype(jnp.float32)
+            means = jnp.mean(gradient * gradient, axis=1, keepdims=True)
+            rows_new = decay * old + (1.0 - decay) * (means * factor * factor)
+            grad_ref[...] = gradient * factor
+            new_ref[...] = table_ref[...] - rate * gradient * lax.rsqrt(rows_new * cols_ref[...])
+            rows_new_ref[0] = jnp.broadcast_to(rows_new, (TILE, LANES)).T[0:1, :]
+
+
+def update(slots, scalars, pieces, table, rows, cols, so_far):
+    parts = len(pieces[0])
+    block = pieces[0][0].shape[0]
+    width = table.shape[1]
     steps = block // TILE
-    place = lambda i, slot: (slot[0] * steps + i, 0)
-    place3 = lambda i, slot: (slot[0] * steps + i, 0, 0)
-    own = lambda i, slot: (i, 0)
-    fixed = lambda i, slot: (0, 0)
+    place = lambda p, i, slots: (slots[p] * steps + i, 0)
+    place3 = lambda p, i, slots: (slots[p] * steps + i, 0, 0)
+
+    def own(part):
+        return lambda p, i, slots: (jnp.where(p < part, 0, jnp.where(p > part, steps - 1, i)), 0)
+
+    fixed = lambda p, i, slots: (0, 0)
     any_space = pl.BlockSpec(memory_space=pl.ANY)
+    given = 5 + 4 * parts
     return pl.pallas_call(
-        update_kernel,
+        functools.partial(update_kernel, parts),
         grid_spec=pltpu.PrefetchScalarGridSpec(
             num_scalar_prefetch=1,
-            grid=(steps,),
-            in_specs=[
-                pl.BlockSpec(memory_space=pltpu.SMEM),
-                pl.BlockSpec((TILE, half), own),
-                pl.BlockSpec((TILE, half), own),
+            grid=(4, steps),
+            in_specs=[pl.BlockSpec(memory_space=pltpu.SMEM)]
+            + [pl.BlockSpec((TILE, piece.shape[1]), own(part)) for part in range(4) for piece in pieces[part]]
+            + [
                 pl.BlockSpec((TILE, width), place),
                 pl.BlockSpec((1, 1, TILE), place3),
                 pl.BlockSpec((1, width), fixed),
@@ -401,73 +413,83 @@
             ],
         ),
         out_shape=[jax.ShapeDtypeStruct(part.shape, part.dtype) for part in so_far],
-        input_output_aliases={7: 0, 8: 1, 9: 2},
+        input_output_aliases={given: 0, given + 1: 1, given + 2: 2},
         compiler_params=pltpu.CompilerParams(vmem_limit_bytes=vmem),
-        cost_estimate=pl.CostEstimate(flops=10 * block * width, bytes_accessed=14 * block * width, transcendentals=block * width),
-    )(slot, scalars, one, two, table, rows, cols, *so_far)
-
-
-def assemble_kernel(members_ref, slots_ref, own_ref, *rest):
-    pieces, out_ref, marks = rest[:-2], rest[-2], rest[-1]
-    copies = [pltpu.make_async_copy(own_ref, out_ref.at[members_ref[0]], marks.at[0])]
+        cost_estimate=pl.CostEstimate(
+            flops=40 * block * width, bytes_accessed=56 * block * width, transcendentals=4 * block * width
+        ),
+    )(slots, scalars, *[piece for four in pieces for piece in four], table, rows, cols, *so_far)
+
+
+def stack_kernel(slots_ref, *refs):
+    pieces, out_ref = refs[:-1], refs[-1]
     for place, piece in enumerate(pieces):
-        for offset in range(piece.shape[0]):
-            copies.append(
-                pltpu.make_async_copy(
-                    piece.at[offset],
-                    out_ref.at[members_ref[offset + 1], slots_ref[place]],
-                    marks.at[len(copies)],
-                )
-            )
-    for copy in copies:
-        copy.start()
-    for copy in copies:
-        copy.wait()
-
-
-def assemble(members, slots, own, pieces):
-    groups, replicas = members.shape[0], slots.shape[0]
-    any_space = pl.BlockSpec(memory_space=pl.ANY)
+
+        @pl.when(pl.program_id(0) == place)
+        def _(piece=piece):
+            out_ref[0] = piece[...]
+
+
+def lay_out(slots, pieces):
+    shape = pieces[0].shape
     return pl.pallas_call(
-        assemble_kernel,
+        stack_kernel,
+        grid_spec=pltpu.PrefetchScalarGridSpec(
+            num_scalar_prefetch=1,
+            grid=(len(pieces),),
+            in_specs=[pl.BlockSpec(shape, lambda i, slots: (0, 0), pipeline_mode=pl.Buffered(1))] * len(pieces),
+            out_specs=pl.BlockSpec((1,) + shape, lambda i, slots: (slots[i], 0, 0)),
+        ),
+        out_shape=jax.ShapeDtypeStruct((len(pieces),) + shape, pieces[0].dtype),
+        compiler_params=pltpu.CompilerParams(vmem_limit_bytes=vmem),
+        cost_estimate=pl.CostEstimate(flops=0, bytes_accessed=4 * len(pieces) * pieces[0].size, transcendentals=0),
+    )(slots, *pieces)
+
+
+def columns_kernel(main, members_ref, slots_ref, *refs):
+    replicas = slots_ref.shape[0]
+    pieces, outs = refs[:replicas], refs[replicas + (len(refs) - replicas - (1 if main is None else 2)) :]
+    groups, rows = pieces[0].shape[0], pieces[0].shape[1]
+    for place, piece in enumerate(pieces):
+
+        @pl.when(pl.program_id(0) == place)
+        def _(piece=piece):
+            for offset in range(groups):
+                member = members_ref[offset]
+                at = pl.ds(pl.multiple_of(member * rows, rows), rows)
+                if main is None:
+                    outs[0][at, :] = piece[offset]
+                else:
+                    outs[0][at, :] = piece[offset, :, :main]
+                    half = piece.shape[2] - main
+                    outs[1][member, 0, :, :half] = piece[offset, : rows // 2, main:]
+                    outs[1][member, 0, :, half:] = piece[offset, rows // 2 :, main:]
+
+
+def lay_columns(members, slots, pieces, main=None, after=()):
+    groups, rows, columns = pieces[0].shape
+    replicas = len(pieces)
+    wide = columns if main is None else main
+    out_shape = [jax.ShapeDtypeStruct((groups * rows, replicas * wide), low_type)]
+    out_specs = [pl.BlockSpec((groups * rows, wide), lambda i, members, slots: (0, slots[i]))]
+    if main is not None:
+        out_shape.append(jax.ShapeDtypeStruct((groups, replicas, rows // 2, 2 * (columns - main)), low_type))
+        out_specs.append(
+            pl.BlockSpec((groups, 1, rows // 2, 2 * (columns - main)), lambda i, members, slots: (0, slots[i], 0, 0))
+        )
+    return pl.pallas_call(
+        functools.partial(columns_kernel, main),
         grid_spec=pltpu.PrefetchScalarGridSpec(
             num_scalar_prefetch=2,
-            grid=(1,),
-            in_specs=[any_space] * (1 + len(pieces)),
-            out_specs=any_space,
-            scratch_shapes=[pltpu.SemaphoreType.DMA((1 + replicas * (groups - 1),))],
+            grid=(replicas,),
+            in_specs=[pl.BlockSpec(pieces[0].shape, lambda i, *_: (0, 0, 0), pipeline_mode=pl.Buffered(1))] * replicas
+            + [pl.BlockSpec(memory_space=pl.ANY)] * len(after),
+            out_specs=out_specs,
         ),
-        out_shape=jax.ShapeDtypeStruct((groups,) + own.shape, own.dtype),
-        cost_estimate=pl.CostEstimate(flops=0, bytes_accessed=4 * groups * own.size, transcendentals=0),
-    )(members, slots, own, *pieces)
-
-
-def place_kernel(slots_ref, *rest):
-    pieces, out_ref, marks = rest[:-2], rest[-2], rest[-1]
-    copies = [
-        pltpu.make_async_copy(piece, out_ref.at[slots_ref[place]], marks.at[place])
-        for place, piece in enumerate(pieces)
-    ]
-    for copy in copies:
-        copy.start()
-    for copy in copies:
-        copy.wait()
-
-
-def lay_out(slots, pieces):
-    any_space = pl.BlockSpec(memory_space=pl.ANY)
-    return pl.pallas_call(
-        place_kernel,
-        grid_spec=pltpu.PrefetchScalarGridSpec(
-            num_scalar_prefetch=1,
-            grid=(1,),
-            in_specs=[any_space] * len(pieces),
-            out_specs=any_space,
-            scratch_shapes=[pltpu.SemaphoreType.DMA((len(pieces),))],
-        ),
-        out_shape=jax.ShapeDtypeStruct((len(pieces),) + pieces[0].shape, pieces[0].dtype),
-        cost_estimate=pl.CostEstimate(flops=0, bytes_accessed=4 * len(pieces) * pieces[0].size, transcendentals=0),
-    )(slots, *pieces)
+        out_shape=out_shape,
+        compiler_params=pltpu.CompilerParams(vmem_limit_bytes=vmem),
+        cost_estimate=pl.CostEstimate(flops=0, bytes_accessed=4 * replicas * pieces[0].size, transcendentals=0),
+    )(members, slots, *pieces, *after)
 
 
 def flip(value, bit):
@@ -506,8 +528,9 @@
 
 
 class Fold:
-    def __init__(self, axis):
+    def __init__(self, axis, order):
         self.axis = axis
+        self.order = order
         self.quick = lax.axis_size("rep") == 8
 
     def cores(self, chunks):
@@ -520,40 +543,28 @@
         return self.from_cores(kept, sent)
 
     def from_cores(self, kept, sent):
-        self.kept, self.got = [kept], [flip(sent, 1)]
+        self.kept, self.got = kept, flip(sent, 1)
         return [sent]
 
-    def planes(self):
+    def sum(self):
+        return self.kept + self.got.astype(jnp.float32) if self.quick else self.value
+
+    def plane(self, first):
         if not self.quick:
             return []
+        value = self.sum()
         axis = self.axis
-        value = self.kept[0] + self.got[0].astype(jnp.float32)
-        shape = value.shape
-        value = value.reshape(shape[:axis] + (2, 2) + shape[axis + 1 :])
-        middle = shape[-1] // 2
-        one = halve(value[..., :middle], axis + 1, 2)
-        two = halve(value[..., middle:], axis, 4)
-        self.kept = [one[0], two[0]]
-        self.got = [flip(one[1], 2), flip(two[1], 4)]
-        return [one[1], two[1]]
-
-    def crossed(self):
-        if not self.quick:
-            return []
-        one, two = (kept + got.astype(jnp.float32) for kept, got in zip(self.kept, self.got))
-        one, two = halve(one, self.axis, 4), halve(two, self.axis, 2)
-        self.kept = [one[0], two[0]]
-        self.got = [flip(one[1], 4), flip(two[1], 2)]
-        return [one[1], two[1]]
-
-    def halves(self):
-        if not self.quick:
-            middle = self.value.shape[-1] // 2
-            return self.value[..., :middle], self.value[..., middle:]
-        return tuple(kept + got.astype(jnp.float32) for kept, got in zip(self.kept, self.got))
+        bit = self.order[0 if first else 1]
+        if first:
+            shape = value.shape
+            value = value.reshape(shape[:axis] + (2, 2) + shape[axis + 1 :])
+            axis = axis + (1 if bit == 2 else 0)
+        self.kept, sent = halve(value, axis, bit)
+        self.got = flip(sent, bit)
+        return [sent]
 
     def members(self):
-        value = jnp.concatenate(self.halves(), axis=-1)
+        value = self.sum()
         member = lax.axis_index("grp")
         size = lax.axis_size("grp")
         self.own = lax.dynamic_index_in_dim(value, member, 0, keepdims=False)
@@ -561,11 +572,11 @@
             lax.dynamic_index_in_dim(value, (member + offset) % size, 0, keepdims=False).astype(low_type)
             for offset in range(1, size)
         ]
-        self.got = [turn(part, offset + 1) for offset, part in enumerate(sent)]
+        self.came = [turn(part, offset + 1) for offset, part in enumerate(sent)]
         return sent
 
     def total(self):
-        return sum((got.astype(jnp.float32) for got in self.got), self.own)
+        return sum((came.astype(jnp.float32) for came in self.came), self.own)
 
 
 def gradient_chunks(gradient):
@@ -600,23 +611,26 @@
 def total_sum(value):
     for j in range(lax.axis_size("rep").bit_length() - 1):
         value = value + flip(value, 1 << j)
-    return jnp.sum(group_gather(value), axis=0)
-
-
-def weight_gather(shard):
-    member = lax.axis_index("grp")
+    size = lax.axis_size("grp")
+    for j in range(size.bit_length() - 1):
+        value = value + lax.ppermute(value, "grp", [(i, i ^ (1 << j)) for i in range(size)])
+    return value
+
+
+def fetch(own):
     groups = lax.axis_size("grp")
+    return jnp.stack([own] + [turn(own, offset) for offset in range(1, groups)])
+
+
+def cut(value, axis):
     replicas = lax.axis_size("rep")
-    rows, columns = shard.shape
-    if replicas != 8:
-        return lax.all_gather(shard, "grp", tiled=True)
-    parts = shard.reshape(replicas, rows // replicas, columns)
-    own = lax.dynamic_index_in_dim(parts, lax.axis_index("rep"), 0, keepdims=False)
-    fetched = jnp.stack([turn(own, offset) for offset in range(1, groups)])
-    have = spread(fetched, [2, 4, 1])
-    members = (member + groups - jnp.arange(groups, dtype=jnp.int32)) % groups
-    whole = assemble(members, slots_of(), parts, [have[place] for place in range(replicas)])
-    return whole.reshape(groups * rows, columns)
+    size = value.shape[axis] // replicas
+    return lax.dynamic_slice_in_dim(value, lax.axis_index("rep") * size, size, axis)
+
+
+def members_of():
+    groups = lax.axis_size("grp")
+    return (lax.axis_index("grp") + groups - jnp.arange(groups, dtype=jnp.int32)) % groups
 
 
 def contract(left, right, left_dim, right_dim):
@@ -696,10 +710,13 @@
     group_labels = group_packed[:, tokens : tokens + own_rows].reshape(-1)
     group_mask = group_packed[:, tokens + own_rows :].reshape(-1)
     shard_rows = w_qkv.shape[0]
-    near = weight_gather(jnp.concatenate([w_qkv, w_out], axis=1).astype(low_type))
-    far = weight_gather(
-        jnp.concatenate([w_gu.astype(low_type), w_down.astype(low_type).reshape(shard_rows, -1)], axis=1)
-    )
+    quick = replicas == 8
+    near_shard = jnp.concatenate([w_qkv, w_out], axis=1)
+    if quick:
+        near_part = fetch(cut(near_shard, 1).astype(low_type))
+        down_part = cut(w_down, 0)
+        down_part = jnp.concatenate([down_part[:, : width // 2], down_part[:, width // 2 :]], axis=0)
+        far_part = fetch(jnp.concatenate([cut(w_gu, 1), down_part], axis=1).astype(low_type))
     loss_count = jnp.sum(group_mask).astype(jnp.float32)[None]
     for j in range(replicas.bit_length() - 1):
         loss_count = loss_count + flip(loss_count, 1 << j)
@@ -707,22 +724,40 @@
 
     local_ids = group_ids - member * vocab_rows
     owned = (local_ids >= 0) & (local_ids < vocab_rows)
-    found = lookup(jnp.where(owned, local_ids, -1), table)
-    embed = lax.psum_scatter(found, "grp", scatter_dimension=0, tiled=True)
-    late_table, _ = lax.optimization_barrier((table, found))
-    table_low = jnp.pad(late_table.astype(low_type), ((0, padded - vocab_rows), (0, 0)))
     places, order = lax.sort(
         (jnp.where(owned, local_ids, padded), jnp.arange(local_ids.shape[0], dtype=jnp.int32)), num_keys=1
     )
     bounds = jnp.arange(replicas + 1, dtype=jnp.int32) * block
     starts = jnp.sum((places[None, :] < bounds[:, None]).astype(jnp.int32), axis=1)
-
-    w_out_low = near[:, 3 * width :]
-    w_gu_low = far[:, : w_gu.shape[1]]
-    w_down_low = far[:, w_gu.shape[1] :].reshape(-1, width)
+    found = lookup(starts, places, order, table)
+    if quick:
+        found, near_part, far_part = lax.optimization_barrier((found, near_part, far_part))
+    embed = lax.psum_scatter(found, "grp", scatter_dimension=0, tiled=True)
+    late_table, _ = lax.optimization_barrier((table, found))
+    table_low = jnp.pad(late_table.astype(low_type), ((0, padded - vocab_rows), (0, 0)))
+
+    if quick:
+        near_have = spread(near_part, [2, 4, 1])
+        far_have = spread(far_part, [4, 2, 1])
+        (near,) = lay_columns(members_of(), slots_of(), [near_have[place] for place in range(replicas)])
+    else:
+        near = lax.all_gather(near_shard.astype(low_type), "grp", tiled=True)
     cosine, sine = rope_tables(length)
     first, first_low, queries, keys, values = project(embed, norms, cosine, sine, near)
     mixed_low, log_sums = attend(lengths, queries, keys, values)
+    if quick:
+        w_gu_low, w_down_low = lay_columns(
+            members_of(),
+            slots_of(),
+            [far_have[place] for place in range(replicas)],
+            w_gu.shape[1] // replicas,
+            (mixed_low,),
+        )
+        w_down_low = w_down_low.reshape(-1, width)
+    else:
+        w_gu_low = lax.all_gather(w_gu.astype(low_type), "grp", tiled=True)
+        w_down_low = lax.all_gather(w_down.astype(low_type), "grp", tiled=True)
+    w_out_low = near[:, 3 * width :]
     first_sum = first + jnp.dot(mixed_low, w_out_low, preferred_element_type=jnp.float32)
     second = layer_norm(first_sum, norms[2], norms[3])
     second_low = second.astype(low_type)
@@ -762,38 +797,45 @@
     _, pull = jax.vjp(layer_norm, second_sum, norms[4], norms[5])
     sum_grad, gain_three, shift_three = pull(final_grad)
     branch_low = sum_grad.astype(low_type)
-    down = Fold(1)
+    down = Fold(1, (2, 4))
     down.cores(gradient_chunks(contract(hidden_low, branch_low, 0, 0)))
     hidden_grad = contract(branch_low, w_down_low, 1, 1)
     _, pull = jax.vjp(swiglu, gate_up)
     gate_low = pull(hidden_grad)[0].astype(low_type)
-    gate = Fold(1)
+    gate = Fold(1, (4, 2))
     gate.cores(gradient_chunks(contract(second_low, gate_low, 0, 0)))
     second_grad = sum_grad + contract(gate_low, w_gu_low, 1, 1)
     _, pull = jax.vjp(layer_norm, first_sum, norms[2], norms[3])
     first_sum_grad, gain_two, shift_two = pull(second_grad)
     attn_low = first_sum_grad.astype(low_type)
     mixed_grad = contract(attn_low, w_out_low, 1, 1).astype(low_type)
-    after = down.planes() + gate.planes()
     pairs = width // LANES
-    one_part = attend_back(
-        lengths, queries, keys, values, mixed_grad, log_sums, cosine, sine, 0, pairs // 2, after
-    )
-    after = down.crossed() + gate.crossed()
-    two_part = attend_back(
-        lengths, queries, keys, values, mixed_grad, log_sums, cosine, sine, pairs // 2, pairs // 2, after + list(one_part[:1])
-    )
-    joined_grad = jnp.concatenate(
-        [side for parts in zip(one_part, two_part) for side in parts], axis=1
-    )
-    after = down.members() + gate.members()
-    joined_grad, after = lax.optimization_barrier((joined_grad, after))
+    third = pairs // 3
+    sides = []
+    for stage in range(3):
+        if stage < 2:
+            after = down.plane(stage == 0) + gate.plane(stage == 0)
+        else:
+            after = down.members() + gate.members()
+        after = after + [side[0] for side in sides[-1:]]
+        sides.append(
+            attend_back(
+                lengths, queries, keys, values, mixed_grad, log_sums, cosine, sine, stage * third, third, after
+            )
+        )
+    joined_grad = jnp.concatenate([side for parts in zip(*sides) for side in parts], axis=1)
     first_grad = first_sum_grad + contract(joined_grad, near[:, : 3 * width], 1, 1)
     _, pull = jax.vjp(layer_norm, embed.astype(jnp.float32), norms[0], norms[1])
     embed_grad, gain_one, shift_one = pull(first_grad)
     norm_grad = jnp.stack([gain_one, shift_one, gain_two, shift_two, gain_three, shift_three])
-    group_embed = lax.all_gather(embed_grad.astype(low_type), "grp", axis=0, tiled=True)
-    join = Fold(1)
+    parts = 3
+    wide = width // parts
+    embed_low = embed_grad.astype(low_type)
+    group_embeds = [
+        lax.all_gather(embed_low[:, part * wide : (part + 1) * wide], "grp", axis=0, tiled=True)
+        for part in range(parts)
+    ]
+    join = Fold(1, (2, 4))
     join.cores(
         gradient_chunks(
             jnp.concatenate(
@@ -801,29 +843,36 @@
             )
         )
     )
-    join.planes()
-    join.crossed()
+    join.plane(True)
+    join.plane(False)
     join.members()
     gu_share, down_share, join_share = gate.total(), down.total(), join.total()
     part_rows = join_share.shape[0]
-
     core = replica % 2
-    half_args = (starts, places, order, dlogits, group_chosen, group_embed, block)
-    head = Fold(0)
-    if head.quick:
-        sent = table_grad_half((1 - core)[None], *half_args, low_type)
-        kept = table_grad_half(core[None], *half_args, jnp.float32)
-        head.from_cores(kept, sent)
-    else:
-        sides = [table_grad_half(jnp.full((1,), j, jnp.int32), *half_args, jnp.float32) for j in range(2)]
-        head.cores(jnp.stack(sides, axis=1).reshape(replicas, block, width))
-    head.planes()
-    head.crossed()
-    table_one, table_two = head.halves()
-    table_share = jnp.concatenate([table_one, table_two], axis=1)
+    table_parts = []
+    for part in range(parts):
+        half_args = (
+            starts,
+            places,
+            order,
+            dlogits,
+            group_chosen[:, part * wide : (part + 1) * wide],
+            group_embeds[part],
+            block,
+        )
+        head = Fold(0, (4, 2) if part % 2 else (2, 4))
+        if quick:
+            sent = table_grad_half((1 - core)[None], *half_args, low_type)
+            kept = table_grad_half(core[None], *half_args, jnp.float32)
+            head.from_cores(kept, sent)
+        else:
+            both = [table_grad_half(jnp.full((1,), j, jnp.int32), *half_args, jnp.float32) for j in range(2)]
+            head.cores(jnp.stack(both, axis=1).reshape(replicas, block, wide))
+        head.plane(True)
+        head.plane(False)
+        table_parts.append(head.sum())
 
     shares = (
-        table_share,
         join_share[:, : 3 * width],
         join_share[:, 3 * width :],
         gu_share,
@@ -832,7 +881,9 @@
     old_rows = (table_rows, qkv_rows, out_rows, gu_rows, down_rows)
     old_cols = (table_cols, qkv_cols, out_cols, gu_cols, down_cols)
     masters = (table, w_qkv, w_out, w_gu, w_down)
-    col_parts = [jnp.sum(gradient * gradient, axis=0) for gradient in shares]
+    col_parts = [
+        jnp.concatenate([jnp.sum(gradient * gradient, axis=0) for gradient in table_parts])
+    ] + [jnp.sum(gradient * gradient, axis=0) for gradient in shares]
     row_old = jnp.stack([jnp.sum(rows) for rows in old_rows]) / replicas
     small = [norm_grad.reshape(-1)] + col_parts + [row_old, jnp.sum(own_terms)[None]]
     totals = total_sum(jnp.concatenate(small))
@@ -863,7 +914,7 @@
         far_whole[:, : w_gu.shape[1]],
         far_whole[:, w_gu.shape[1] :].reshape(w_down.shape),
     ]
-    table_one, table_two = table_one.astype(low_type), table_two.astype(low_type)
+    table_lows = [part.astype(low_type) for part in table_parts]
 
     outputs = []
     for place in range(5):
@@ -874,26 +925,33 @@
         )
         row_total = decay * old_totals[place] + (1.0 - decay) * (squares[place] * factor * factor) / columns
         row_mean = row_total / full_rows
-        if place == 0 and head.quick:
-            ones = spread(table_one, [4, 2, 1])
-            twos = spread(table_two, [2, 4, 1])
+        if place == 0 and quick:
+            have = [
+                spread(low, [2, 4, 1] if part % 2 else [4, 2, 1]) for part, low in enumerate(table_lows)
+            ]
             tiles = padded // TILE
             row_tiles = jnp.pad(table_rows, (0, padded - vocab_rows), constant_values=1.0).reshape(tiles, 1, TILE)
-            scalars = jnp.stack([factor, row_mean])
+            scalars = jnp.stack([factor, rate_matrix * factor * jnp.sqrt(row_mean)])
             so_far = (
                 blank(table.shape, jnp.float32),
                 blank(table.shape, jnp.float32),
                 blank((tiles, 1, TILE), jnp.float32),
             )
             slots = slots_of()
-            for part in (0, 4, 2, 6, 1, 5, 3, 7):
+            for four in ((0, 2, 4, 6), (1, 3, 5, 7)):
                 so_far = update(
-                    slots[part][None], scalars, ones[part], twos[part], table, row_tiles, new_cols[None, :], so_far
+                    jnp.stack([slots[part] for part in four]),
+                    scalars,
+                    [[got[part] for got in have] for part in four],
+                    table,
+                    row_tiles,
+                    new_cols[None, :],
+                    so_far,
                 )
             outputs.extend([so_far[0], so_far[2].reshape(-1)[:vocab_rows], new_cols, so_far[1]])
             continue
         if place == 0:
-            whole = plane_gather(jnp.concatenate([table_one, table_two], axis=1))
+            whole = plane_gather(jnp.concatenate(table_lows, axis=1))
             gradient = whole.reshape(padded, width)[:vocab_rows].astype(jnp.float32)
         else:
             gradient = wholes[place].astype(jnp.float32)

time: 1980 us -> 1190 us (0.60)
  Pallas kernels: 981 us -> 286 us
  waiting for transfers between devices: 338 us -> 295 us
  local copies, waits for them, and re-layouts: 114 us -> 76.1 us
    pallas_call x12 -> x6, Pallas kernels: 776 us -> 72.3 us  [the longest x2 42.9 us: update(): pl.pallas_call(functools.partial(update_kernel, parts), grid_spec=pltpu.P...]
    ppermute x68 -> x73, waiting for transfers between devices: 91.7 us -> 181 us  [flip(): return lax.ppermute(value, 'rep', [(i, i ^ bit) for i in range(size)])]
    all_gather x1 -> x3, waiting for transfers between devices: 75 us -> 0.01 us  [body(): lax.all_gather(embed_low[:, part * wide:(part + 1) * wide], 'grp', axis=0...]
    ppermute x30 -> x27, waiting for transfers between devices: 172 us -> 113 us  [turn(): lax.ppermute(value, 'grp', [(i, (i + offset) % size) for i in range(size)])]
    pallas_call x2 -> x6, Pallas kernels: 31.8 us -> 72.5 us  [table_grad_half(): pl.pallas_call(table_grad_kernel, grid_spec=pltpu.PrefetchScalarGridSpec(...]
    pallas_call x1, Pallas kernels: 53.4 us -> 18.9 us  [lookup(): pl.pallas_call(lookup_kernel, grid_spec=pltpu.PrefetchScalarGridSpec(num_...]
    ppermute x30 -> x27, starting transfers between devices: 46.6 us -> 39.4 us  [turn(): lax.ppermute(value, 'grp', [(i, (i + offset) % size) for i in range(size)])]
    ppermute x68 -> x73, starting transfers between devices: 121 us -> 126 us  [flip(): return lax.ppermute(value, 'rep', [(i, i ^ bit) for i in range(size)])]
  transfers between devices with their start and end apart: 100 -> 106, of which waited for: 31 -> 29; matrix products, arithmetic and copies ran while one was open for 14% -> 19% of each run, Pallas kernels for 44% -> 20%
where the time goes in v3:
time: 1190 us; the launch traced here: 1180 us
  waiting for transfers between devices  295 us (25%)
  Pallas kernels  286 us (24%)
  other arithmetic  175 us (15%)
  starting transfers between devices  169 us (14%)
  matrix products  149 us (13%)
  local copies, waits for them, and re-layouts  76.1 us (6%)
  between operations  32.5 us (3%)
    ppermute x73, waiting for transfers between devices, flip(): return lax.ppermute(value, 'rep', [(i, i ^ bit) for i in range(size)])  181 us
    ppermute x73, starting transfers between devices, flip(): return lax.ppermute(value, 'rep', [(i, i ^ bit) for i in range(size)])  126 us
    dot_general x10, matrix products, contract(): lax.dot_general(left, right, (((left_dim,), (right_dim,)), ((), ())), pre...  123 us
    ppermute x27, waiting for transfers between devices, turn(): lax.ppermute(value, 'grp', [(i, (i + offset) % size) for i in range(size)])  113 us
    pallas_call x6, Pallas kernels, table_grad_half(): pl.pallas_call(table_grad_kernel, grid_spec=pltpu.PrefetchScalarGridSpec(...  72.5 us
    pallas_call x3, Pallas kernels, attend_back(): pl.pallas_call(functools.partial(attend_back_kernel, first_pair), grid_sp...  65.6 us
    pallas_call x1, Pallas kernels, attend(): pl.pallas_call(attend_kernel, grid_spec=pltpu.PrefetchScalarGridSpec(num_...  47.6 us
    pallas_call x2, Pallas kernels, update(): pl.pallas_call(functools.partial(update_kernel, parts), grid_spec=pltpu.P...  42.9 us
  transfers between devices with their start and end apart: 106, of which 29 were waited for; matrix products, arithmetic and copies ran while one was open for 19% of the time, Pallas kernels for 20%

profile of v3, /device:TPU:1, one launch (start us, length us, event | category | flops | bytes accessed | tf_op | source)
XLA Modules:
  0.0 1181.3 jit_solution(7798281355431604470)
XLA Ops:
  30.4 18.9 %shard_map.413 = bf16[4096,768]{1,0:T(8,128)(2,1)} custom-call(s32[9]{0:T(128)} %convert_reduce_fusion.1.starts_ref, s32[4096]{0:T(1024)} %copy-done.36, s32[4096]{0:T(1024)} %get-tuple-element.57.order_ref, f32[7632,768]{1,0:T(8,128)} %rest_12_.3), custom_call_target="tpu_custom_call" | custom-call | bytes 70336512 | tf_op jit(solution)/shard_map/pallas_call | solution.py:294
  49.4 16.5 %collective-permute-done.7 = bf16[192,1152]{1,0:T(8,128)(2,1)S(1)} collective-permute-done((bf16[192,1152]{1,0:T(8,128)(2,1)S(1)}, bf16[192,1152]{1,0:T(8,128)(2,1)S(1)}, u32[]{:S(2)}, u32[]{:S(2)}) %collective-permute-start.7) | collective-permute-done | bytes 442400 | tf_op jit(solution)/shard_map/ppermute | solution.py:502
  70.1 35.2 %collective-permute-done.19.refs_4_ = bf16[4,192,1152]{2,1,0:T(8,128)(2,1)} collective-permute-done((bf16[4,192,1152]{2,1,0:T(8,128)(2,1)}, bf16[4,192,1152]{2,1,0:T(8,128)(2,1)}, u32[]{:S(2)}, u32[]{:S(2)}) %collective-permute-start.19) | collective-permute-done | bytes 1769504 | tf_op jit(solution)/shard_map/ppermute | solution.py:497
  113.7 42.0 %collective-permute-start.30 = (f32[1]{0:T(128)}, f32[1]{0:T(128)}, u32[]{:S(2)}, u32[]{:S(2)}) collective-permute-start(f32[1]{0:T(128)} %add.542), channel_id=1, source_target_pairs={{0,2},{1,3},{2,0},{3,1},{4,6},{5,7},{6,4},{7,5},{8,10},{9,11},{10,... | collective-permute-start | bytes 20 | tf_op jit(solution)/shard_map/ppermute | solution.py:497
  197.0 12.6 %convert_element_type.314 = bf16[7632,768]{1,0:T(8,128)(2,1)} convert(f32[7632,768]{1,0:T(8,128)} %rest_12_.3) | non-fusion elementwise | flops 5861376 | bytes 35168256 | tf_op jit(solution)/shard_map/convert_element_type | solution.py:737
  227.0 47.6 %shard_map.416 = (bf16[1024,768]{1,0:T(8,128)(2,1)}, f32[6,2,1024]{2,1,0:T(2,128)}) custom-call(s32[1]{0:T(128)S(6)} %copy.141.length_ref, bf16[1024,768]{1,0:T(8,128)(2,1)} %get-tuple-element.62.q_ref, bf16[1024,768]{1,0:T(8,128)(2,1)} %get-tuple-element.63.k_ref, bf16[1024,768]{1,0:T(8,128)(2,1)} %get-tuple-element.64.v_ref), custom_call_target="tpu_custom_call" | custom-call | flops 12884901888 | bytes 6291456 | tf_op jit(solution)/shard_map/pallas_call | solution.py:138
  278.8 11.7 shard_map.417
  290.6 17.3 %fusion.101 = f32[1024,6144]{1,0:T(8,128)} fusion(bf16[768,6144]{1,0:T(8,128)(2,1)} %get-tuple-element.67, f32[1024,768]{1,0:T(8,128)S(1)} %get-tuple-element.127, f32[768]{0:T(1024)S(1)} %get-tuple-element.103, f32[768]{0:T(1024)S(1)} %get-tuple-element.104, f32[1024]{0:T(1024)S(1)} %fusion.82, f32[1024]{0:T(1024)S(1)} %broadcast_multiply_fusion.1), kind=kOutput, calls=%fused_computation.300 | convolution fusion | flops 9667608576 | bytes 37763072 | tf_op jit(solution)/shard_map/dot_general | solution.py:764
  307.9 10.5 multiply_convert_fusion.1
  347.2 11.3 select_reduce_fusion.1
  386.2 11.8 fusion.4
  406.7 25.3 %collective-permute-done.33 = f32[128,768]{1,0:T(8,128)S(1)} collective-permute-done((f32[128,768]{1,0:T(8,128)S(1)}, f32[128,768]{1,0:T(8,128)S(1)}, u32[]{:S(2)}, u32[]{:S(2)}) %collective-permute-start.33) | collective-permute-done | bytes 393248 | tf_op jit(solution)/shard_map/ppermute | solution.py:502
  444.0 23.7 %fusion.31 = (f32[1024,3072]{1,0:T(8,128)}, f32[1024,3072]{1,0:T(8,128)}) fusion(f32[1024,6144]{1,0:T(8,128)} %fusion.101, bf16[3072,768]{1,0:T(8,128)(2,1)} %bitcast.313, f32[1024,768]{1,0:T(8,128)} %get-tuple-element.123, f32[1024]{0:T(1024)S(1)} %negate_multiply_fusion.2), kind=kOutput, calls=%fused_computation.95 | convolution fusion | flops 4871159808 | bytes 58200064 | tf_op jit(solution)/shard_map/dot_general | solution.py:637
  484.6 24.4 %fusion.25 = f32[768,6144]{1,0:T(8,128)} fusion(f32[1024,3072]{1,0:T(8,128)} %get-tuple-element.129, f32[1024,3072]{1,0:T(8,128)} %get-tuple-element.128, f32[1024,768]{1,0:T(8,128)S(1)} %get-tuple-element.127, f32[768]{0:T(1024)S(1)} %copy-done.85, f32[768]{0:T(1024)S(1)} %get-tuple-element.104, f32[1024]{0:T(1024)S(1)} %fusion.82, ...), kind=kOutput, calls=%fused_computation.88 | convolution fusion | flops 9680191488 | bytes 47200256 | tf_op jit(solution)/shard_map/dot_general | solution.py:637
  524.5 19.2 %multiply_reduce_fusion.1 = (f32[768]{0:T(1024)}, f32[1024]{0:T(1024)S(1)}, f32[768]{0:T(1024)}, f32[1024,768]{1,0:T(8,128)}) fusion(f32[1024,768]{1,0:T(8,128)S(1)} %get-tuple-element.127, f32[1024]{0:T(1024)S(1)} %fusion.82, f32[1024]{0:T(1024)S(1)} %broadcast_multiply_fusion.1, f32[768]{0:T(1024)S(1)} %get-tuple-element.104, ...), kind=kOutput, calls=%fused_computation.53 | convolution fusion | flops 9684120576 | bytes 44065792 | tf_op jit(solution)/shard_map/dot_general | solution.py:637
  576.5 50.5 %collective-permute-done.39 = bf16[4,96,768]{2,1,0:T(8,128)(2,1)S(1)} collective-permute-done((bf16[4,96,768]{2,1,0:T(8,128)(2,1)S(1)}, bf16[4,96,768]{2,1,0:T(8,128)(2,1)S(1)}, u32[]{:S(2)}, u32[]{:S(2)}) %collective-permute-start.39) | collective-permute-done | bytes 589856 | tf_op jit(solution)/shard_map/ppermute | solution.py:497
  632.2 22.1 %shard_map.418 = (bf16[1024,256]{1,0:T(8,128)(2,1)}, bf16[1024,256]{1,0:T(8,128)(2,1)}, bf16[1024,256]{1,0:T(8,128)(2,1)}) custom-call(s32[1]{0:T(128)S(6)} %copy.141.length_ref, bf16[1024,768]{1,0:T(8,128)(2,1)} %get-tuple-element.62.q_ref, bf16[1024,768]{1,0:T(8,128)(2,1)} %get-tuple-element.63.k_ref, bf16[1024,768]{1,0:T(8,128)(2,1)} %get-tuple-element.64.v_ref, ...), custom_call_target="tpu_custom_call" | custom-call | flops 10737418240 | bytes 4194304 | tf_op jit(solution)/shard_map/pallas_call | solution.py:223
  660.2 21.6 %shard_map.419 = (bf16[1024,256]{1,0:T(8,128)(2,1)}, bf16[1024,256]{1,0:T(8,128)(2,1)}, bf16[1024,256]{1,0:T(8,128)(2,1)}) custom-call(s32[1]{0:T(128)S(6)} %copy.141.length_ref, bf16[1024,768]{1,0:T(8,128)(2,1)} %get-tuple-element.62.q_ref, bf16[1024,768]{1,0:T(8,128)(2,1)} %get-tuple-element.63.k_ref, bf16[1024,768]{1,0:T(8,128)(2,1)} %get-tuple-element.64.v_ref, ...), custom_call_target="tpu_custom_call" | custom-call | flops 10737418240 | bytes 4194304 | tf_op jit(solution)/shard_map/pallas_call | solution.py:223
  685.1 21.9 %shard_map.420 = (bf16[1024,256]{1,0:T(8,128)(2,1)}, bf16[1024,256]{1,0:T(8,128)(2,1)}, bf16[1024,256]{1,0:T(8,128)(2,1)}) custom-call(s32[1]{0:T(128)S(6)} %copy.141.length_ref, bf16[1024,768]{1,0:T(8,128)(2,1)} %get-tuple-element.62.q_ref, bf16[1024,768]{1,0:T(8,128)(2,1)} %get-tuple-element.63.k_ref, bf16[1024,768]{1,0:T(8,128)(2,1)} %get-tuple-element.64.v_ref, ...), custom_call_target="tpu_custom_call" | custom-call | flops 10737418240 | bytes 4194304 | tf_op jit(solution)/shard_map/pallas_call | solution.py:223
  724.2 9.7 fusion.118
  788.0 44.1 %collective-permute-done.57 = bf16[24,6144]{1,0:T(8,128)(2,1)} collective-permute-done((bf16[24,6144]{1,0:T(8,128)(2,1)}, bf16[24,6144]{1,0:T(8,128)(2,1)}, u32[]{:S(2)}, u32[]{:S(2)}) %collective-permute-start.57) | collective-permute-done | bytes 294944 | tf_op jit(solution)/shard_map/ppermute | solution.py:502
  838.4 13.2 %shard_map.422 = bf16[4,960,256]{2,1,0:T(8,128)(2,1)} custom-call(s32[1]{0:T(128)} %bitcast.67.core_ref, s32[9]{0:T(128)} %convert_reduce_fusion.1.starts_ref, s32[4096]{0:T(1024)} %copy-done.36, s32[4096]{0:T(1024)} %get-tuple-element.57.order_ref, bf16[7680,512]{1,0:T(8,128)(2,1)} %copy-done, bf16[512,256]{1,0:T(8,128)(2,1)} %get-tuple-element.161.chosen_ref, ...), custom_call_target="tpu_custom_call" | custom-call | flops 1006632960 | bytes 7864320 | tf_op jit(solution)/shard_map/pallas_call | solution.py:337
  853.2 13.2 %shard_map.424 = bf16[4,960,256]{2,1,0:T(8,128)(2,1)} custom-call(s32[1]{0:T(128)} %bitcast.67.core_ref, s32[9]{0:T(128)} %convert_reduce_fusion.1.starts_ref, s32[4096]{0:T(1024)} %copy-done.36, s32[4096]{0:T(1024)} %get-tuple-element.57.order_ref, bf16[7680,512]{1,0:T(8,128)(2,1)} %copy-done, bf16[512,256]{1,0:T(8,128)(2,1)} %get-tuple-element.160.chosen_ref, ...), custom_call_target="tpu_custom_call" | custom-call | flops 1006632960 | bytes 7864320 | tf_op jit(solution)/shard_map/pallas_call | solution.py:337
  866.4 10.9 shard_map.421
  879.3 10.9 shard_map.423
  897.8 13.2 %shard_map.426 = bf16[4,960,256]{2,1,0:T(8,128)(2,1)} custom-call(s32[1]{0:T(128)} %bitcast.67.core_ref, s32[9]{0:T(128)} %convert_reduce_fusion.1.starts_ref, s32[4096]{0:T(1024)} %copy-done.36, s32[4096]{0:T(1024)} %get-tuple-element.57.order_ref, bf16[7680,512]{1,0:T(8,128)(2,1)} %copy-done, bf16[512,256]{1,0:T(8,128)(2,1)} %get-tuple-element.159.chosen_ref, ...), custom_call_target="tpu_custom_call" | custom-call | flops 1006632960 | bytes 7864320 | tf_op jit(solution)/shard_map/pallas_call | solution.py:337
  911.1 11.0 shard_map.425
  937.3 20.4 %collective-permute-done.42 = bf16[2,960,256]{2,1,0:T(8,128)(2,1)S(1)} collective-permute-done((bf16[2,960,256]{2,1,0:T(8,128)(2,1)S(1)}, bf16[2,960,256]{2,1,0:T(8,128)(2,1)S(1)}, u32[]{:S(2)}, u32[]{:S(2)}) %collective-permute-start.42) | collective-permute-done | bytes 983072 | tf_op jit(solution)/shard_map/ppermute | solution.py:497
  959.8 19.0 %collective-permute-done.48 = bf16[2,960,256]{2,1,0:T(8,128)(2,1)S(1)} collective-permute-done((bf16[2,960,256]{2,1,0:T(8,128)(2,1)S(1)}, bf16[2,960,256]{2,1,0:T(8,128)(2,1)S(1)}, u32[]{:S(2)}, u32[]{:S(2)}) %collective-permute-start.48) | collective-permute-done | bytes 983072 | tf_op jit(solution)/shard_map/ppermute | solution.py:497
  1096.3 9.8 collective-permute-done.80.rest_8_
  1126.2 21.4 %shard_map.430 = (f32[7632,768]{1,0:T(8,128)}, f32[7632,768]{1,0:T(8,128)}, f32[32,1,240]{2,1,0:T(1,128)}) custom-call(s32[4]{0:T(128)} %pad_add_fusion.2.slots_ref, f32[2]{0:T(128)} %pad_maximum_fusion.8.scalars_ref, bf16[960,256]{1,0:T(8,128)(2,1)} %get-tuple-element.138.rest_0_, ...), custom_call_target="tpu_custom_call", output_to_operand_aliasing={{0}: (17, {}), {1}: (18, {}), {2}: (19, {})} | custom-call | flops 29491200 | bytes 41287680 | tf_op jit(solution)/shard_map/pallas_call | solution.py:394
  1149.0 21.5 %shard_map.431 = (f32[7632,768]{1,0:T(8,128)}, f32[7632,768]{1,0:T(8,128)}, f32[32,1,240]{2,1,0:T(1,128)}) custom-call(s32[4]{0:T(128)} %pad_add_fusion.1.slots_ref, f32[2]{0:T(128)} %pad_maximum_fusion.8.scalars_ref, bf16[960,256]{1,0:T(8,128)(2,1)} %collective-permute-done.67.rest_0_, ...), custom_call_target="tpu_custom_call", output_to_operand_aliasing={{0}: (17, {}), {1}: (18, {}), {2}: (19, {})} | custom-call | flops 29491200 | bytes 41287680 | tf_op jit(solution)/shard_map/pallas_call | solution.py:394
  (669 shorter events, 486.4 us)
Async XLA Ops:
  7.2 210.6 %reduce-scatter.2.cloned.1.call-start = ((), (), s32[]{:S(2)}) async-start(), calls=%async_computation.1 | async-start | bytes 7864320 | tf_op jit(solution)/shard_map/reduce_scatter | solution.py:735
  23.2 42.7 %collective-permute-start.7 = (bf16[192,1152]{1,0:T(8,128)(2,1)S(1)}, bf16[192,1152]{1,0:T(8,128)(2,1)S(1)}, u32[]{:S(2)}, u32[]{:S(2)}) collective-permute-start(bf16[192,1152]{1,0:T(8,128)(2,1)S(1)} %pad_maximum_fusion.5), channel_id=1, source_target_pairs={{0,16},{8,24},{16,0},{24,8},{1,17},{9,25},{17,1},{25,9},{2,18},{10... | collective-permute-start | bytes 1327112 | tf_op jit(solution)/shard_map/ppermute | solution.py:502
  23.4 42.5 %collective-permute-start.6 = (bf16[192,1152]{1,0:T(8,128)(2,1)S(1)}, bf16[192,1152]{1,0:T(8,128)(2,1)S(1)}, u32[]{:S(2)}, u32[]{:S(2)}) collective-permute-start(bf16[192,1152]{1,0:T(8,128)(2,1)S(1)} %pad_maximum_fusion.5), channel_id=1, source_target_pairs={{0,8},{8,16},{16,24},{24,0},{1,9},{9,17},{17,25},{25,1},{2,10},{10... | collective-permute-start | bytes 1327112 | tf_op jit(solution)/shard_map/ppermute | solution.py:502
  67.3 771.2 %all-gather.4.cloned.1.call-start = ((), (), s32[]{:S(2)}) async-start(), calls=%async_computation.2 | async-start | bytes 2621440 | tf_op jit(solution)/shard_map/all_gather | solution.py:835
  67.3 38.0 %collective-permute-start.19 = (bf16[4,192,1152]{2,1,0:T(8,128)(2,1)}, bf16[4,192,1152]{2,1,0:T(8,128)(2,1)}, u32[]{:S(2)}, u32[]{:S(2)}) collective-permute-start(bf16[4,192,1152]{2,1,0:T(8,128)(2,1)} %pad_maximum_fusion.1.refs_0_), channel_id=1, source_target_pairs={{0,4},{1,5},{2,6},{3,7},{4,0},{5,1},{6,2},{7,3},{8,12},{9,13},{10,... | collective-permute-start | bytes 5308424 | tf_op jit(solution)/shard_map/ppermute | solution.py:497
  68.7 95.5 %collective-permute-start.10 = (bf16[4,192,384]{2,1,0:T(8,128)(2,1)S(1)}, bf16[4,192,384]{2,1,0:T(8,128)(2,1)S(1)}, u32[]{:S(2)}, u32[]{:S(2)}) collective-permute-start(bf16[4,192,384]{2,1,0:T(8,128)(2,1)S(1)} %pad_maximum_fusion.2.refs_0_), channel_id=1, source_target_pairs={{0,2},{1,3},{2,0},{3,1},{4,6},{5,7},{6,4},{7,5},{8,10},{9,11},{10,... | collective-permute-start | bytes 1769480 | tf_op jit(solution)/shard_map/ppermute | solution.py:497
  69.9 140.4 %collective-permute-start.17 = (bf16[4,192,1152]{2,1,0:T(8,128)(2,1)}, bf16[4,192,1152]{2,1,0:T(8,128)(2,1)}, u32[]{:S(2)}, u32[]{:S(2)}) collective-permute-start(bf16[4,192,1152]{2,1,0:T(8,128)(2,1)} %pad_maximum_fusion.1.refs_0_), channel_id=1, source_target_pairs={{0,2},{1,3},{2,0},{3,1},{4,6},{5,7},{6,4},{7,5},{8,10},{9,11},{10,... | collective-permute-start | bytes 5308424 | tf_op jit(solution)/shard_map/ppermute | solution.py:497
  105.4 112.1 %collective-permute-start.21 = (bf16[4,192,1152]{2,1,0:T(8,128)(2,1)}, bf16[4,192,1152]{2,1,0:T(8,128)(2,1)}, u32[]{:S(2)}, u32[]{:S(2)}) collective-permute-start(bf16[4,192,1152]{2,1,0:T(8,128)(2,1)} %collective-permute-done.19.refs_4_), channel_id=1, source_target_pairs={{0,2},{1,3},{2,0},{3,1},{4,6},{5,7},{6,4},{7,5},{8,10},{9,11},{10,... | collective-permute-start | bytes 5308424 | tf_op jit(solution)/shard_map/ppermute | solution.py:497
  113.7 43.0 %collective-permute-start.30 = (f32[1]{0:T(128)}, f32[1]{0:T(128)}, u32[]{:S(2)}, u32[]{:S(2)}) collective-permute-start(f32[1]{0:T(128)} %add.542), channel_id=1, source_target_pairs={{0,2},{1,3},{2,0},{3,1},{4,6},{5,7},{6,4},{7,5},{8,10},{9,11},{10,... | collective-permute-start | bytes 20 | tf_op jit(solution)/shard_map/ppermute | solution.py:497
  167.4 42.2 %collective-permute-start.11 = (bf16[4,192,384]{2,1,0:T(8,128)(2,1)S(1)}, bf16[4,192,384]{2,1,0:T(8,128)(2,1)S(1)}, u32[]{:S(2)}, u32[]{:S(2)}) collective-permute-start(bf16[4,192,384]{2,1,0:T(8,128)(2,1)S(1)} %collective-permute-done.10.refs_2_), channel_id=1, source_target_pairs={{0,1},{1,0},{2,3},{3,2},{4,5},{5,4},{6,7},{7,6},{8,9},{9,8},{10,11... | collective-permute-start | bytes 1769480 | tf_op jit(solution)/shard_map/ppermute | solution.py:497
  209.6 69.2 %collective-permute-start.16 = (bf16[4,192,1152]{2,1,0:T(8,128)(2,1)}, bf16[4,192,1152]{2,1,0:T(8,128)(2,1)}, u32[]{:S(2)}, u32[]{:S(2)}) collective-permute-start(bf16[4,192,1152]{2,1,0:T(8,128)(2,1)} %pad_maximum_fusion.1.refs_0_), channel_id=1, source_target_pairs={{0,1},{1,0},{2,3},{3,2},{4,5},{5,4},{6,7},{7,6},{8,9},{9,8},{10,11... | collective-permute-start | bytes 5308424 | tf_op jit(solution)/shard_map/ppermute | solution.py:497
  209.7 69.1 %collective-permute-start.20 = (bf16[4,192,1152]{2,1,0:T(8,128)(2,1)}, bf16[4,192,1152]{2,1,0:T(8,128)(2,1)}, u32[]{:S(2)}, u32[]{:S(2)}) collective-permute-start(bf16[4,192,1152]{2,1,0:T(8,128)(2,1)} %collective-permute-done.19.refs_4_), channel_id=1, source_target_pairs={{0,1},{1,0},{2,3},{3,2},{4,5},{5,4},{6,7},{7,6},{8,9},{9,8},{10,11... | collective-permute-start | bytes 5308424 | tf_op jit(solution)/shard_map/ppermute | solution.py:497
  210.2 68.6 %collective-permute-start.18 = (bf16[4,192,1152]{2,1,0:T(8,128)(2,1)}, bf16[4,192,1152]{2,1,0:T(8,128)(2,1)}, u32[]{:S(2)}, u32[]{:S(2)}) collective-permute-start(bf16[4,192,1152]{2,1,0:T(8,128)(2,1)} %collective-permute-done.17.refs_2_), channel_id=1, source_target_pairs={{0,1},{1,0},{2,3},{3,2},{4,5},{5,4},{6,7},{7,6},{8,9},{9,8},{10,11... | collective-permute-start | bytes 5308424 | tf_op jit(solution)/shard_map/ppermute | solution.py:497
  217.4 61.4 %collective-permute-start.22 = (bf16[4,192,1152]{2,1,0:T(8,128)(2,1)}, bf16[4,192,1152]{2,1,0:T(8,128)(2,1)}, u32[]{:S(2)}, u32[]{:S(2)}) collective-permute-start(bf16[4,192,1152]{2,1,0:T(8,128)(2,1)} %collective-permute-done.21.refs_6_), channel_id=1, source_target_pairs={{0,1},{1,0},{2,3},{3,2},{4,5},{5,4},{6,7},{7,6},{8,9},{9,8},{10,11... | collective-permute-start | bytes 5308424 | tf_op jit(solution)/shard_map/ppermute | solution.py:497
  481.7 35.6 %collective-permute-start.35 = (bf16[4,4,96,768]{3,2,1,0:T(8,128)(2,1)}, bf16[4,4,96,768]{3,2,1,0:T(8,128)(2,1)}, u32[]{:S(2)}, u32[]{:S(2)}) collective-permute-start(bf16[4,4,96,768]{3,2,1,0:T(8,128)(2,1)} %fusion.23), channel_id=1, source_target_pairs={{0,1},{1,0},{2,3},{3,2},{4,5},{5,4},{6,7},{7,6},{8,9},{9,8},{10,11... | collective-permute-start | bytes 7077896 | tf_op jit(solution)/shard_map/ppermute | solution.py:497
  516.0 38.1 %collective-permute-start.36 = (bf16[4,4,24,6144]{3,2,0,1:T(8,128)(2,1)}, bf16[4,4,24,6144]{3,2,0,1:T(8,128)(2,1)}, u32[]{:S(2)}, u32[]{:S(2)}) collective-permute-start(bf16[4,4,24,6144]{3,2,0,1:T(8,128)(2,1)} %fusion.9), channel_id=1, source_target_pairs={{0,1},{1,0},{2,3},{3,2},{4,5},{5,4},{6,7},{7,6},{8,9},{9,8},{10,11... | collective-permute-start | bytes 14155784 | tf_op jit(solution)/shard_map/ppermute | solution.py:497
  562.3 91.9 %collective-permute-start.38 = (bf16[4,2,24,6144]{3,2,0,1:T(8,128)(2,1)}, bf16[4,2,24,6144]{3,2,0,1:T(8,128)(2,1)}, u32[]{:S(2)}, u32[]{:S(2)}) collective-permute-start(bf16[4,2,24,6144]{3,2,0,1:T(8,128)(2,1)} %fusion.22), channel_id=1, source_target_pairs={{0,4},{1,5},{2,6},{3,7},{4,0},{5,1},{6,2},{7,3},{8,12},{9,13},{10,... | collective-permute-start | bytes 7077896 | tf_op jit(solution)/shard_map/ppermute | solution.py:497
  564.0 62.9 %collective-permute-start.39 = (bf16[4,96,768]{2,1,0:T(8,128)(2,1)S(1)}, bf16[4,96,768]{2,1,0:T(8,128)(2,1)S(1)}, u32[]{:S(2)}, u32[]{:S(2)}) collective-permute-start(bf16[4,96,768]{2,1,0:T(8,128)(2,1)S(1)} %fusion.45.rest_0_), channel_id=1, source_target_pairs={{0,4},{1,5},{2,6},{3,7},{4,0},{5,1},{6,2},{7,3},{8,12},{9,13},{10,... | collective-permute-start | bytes 1769480 | tf_op jit(solution)/shard_map/ppermute | solution.py:497
  724.2 129.0 %all-gather.6.cloned.1.call-start = ((), (), s32[]{:S(2)}) async-start(), calls=%async_computation.3 | async-start | bytes 2621440 | tf_op jit(solution)/shard_map/all_gather | solution.py:835
  749.7 148.0 %all-gather.8.cloned.1.call-start = ((), (), s32[]{:S(2)}) async-start(), calls=%async_computation.4 | async-start | bytes 2621440 | tf_op jit(solution)/shard_map/all_gather | solution.py:835
  761.2 72.8 %collective-permute-start.51 = (bf16[4,2,24,3072]{3,2,0,1:T(8,128)(2,1)}, bf16[4,2,24,3072]{3,2,0,1:T(8,128)(2,1)}, u32[]{:S(2)}, u32[]{:S(2)}) collective-permute-start(bf16[4,2,24,3072]{3,2,0,1:T(8,128)(2,1)} %fusion.34), channel_id=1, source_target_pairs={{0,2},{1,3},{2,0},{3,1},{4,6},{5,7},{6,4},{7,5},{8,10},{9,11},{10,... | collective-permute-start | bytes 3538952 | tf_op jit(solution)/shard_map/ppermute | solution.py:497
  774.3 57.7 %collective-permute-start.57 = (bf16[24,6144]{1,0:T(8,128)(2,1)}, bf16[24,6144]{1,0:T(8,128)(2,1)}, u32[]{:S(2)}, u32[]{:S(2)}) collective-permute-start(bf16[24,6144]{1,0:T(8,128)(2,1)} %get-tuple-element.141.rest_4_), channel_id=1, source_target_pairs={{0,16},{8,24},{16,0},{24,8},{1,17},{9,25},{17,1},{25,9},{2,18},{10... | collective-permute-start | bytes 884744 | tf_op jit(solution)/shard_map/ppermute | solution.py:502
  783.8 48.3 %collective-permute-start.56 = (bf16[24,6144]{1,0:T(8,128)(2,1)S(1)}, bf16[24,6144]{1,0:T(8,128)(2,1)}, u32[]{:S(2)}, u32[]{:S(2)}) collective-permute-start(bf16[24,6144]{1,0:T(8,128)(2,1)S(1)} %copy-done.69), channel_id=1, source_target_pairs={{0,8},{8,16},{16,24},{24,0},{1,9},{9,17},{17,25},{25,1},{2,10},{10... | collective-permute-start | bytes 884744 | tf_op jit(solution)/shard_map/ppermute | solution.py:502
  836.4 41.0 %collective-permute-start.52 = (bf16[4,24,3072]{2,1,0:T(8,128)(2,1)S(1)}, bf16[4,24,3072]{2,1,0:T(8,128)(2,1)}, u32[]{:S(2)}, u32[]{:S(2)}) collective-permute-start(bf16[4,24,3072]{2,1,0:T(8,128)(2,1)S(1)} %fusion.46), channel_id=1, source_target_pairs={{0,4},{1,5},{2,6},{3,7},{4,0},{5,1},{6,2},{7,3},{8,12},{9,13},{10,... | collective-permute-start | bytes 1769480 | tf_op jit(solution)/shard_map/ppermute | solution.py:497
  851.7 76.4 %collective-permute-start.41 = (bf16[4,960,256]{2,1,0:T(8,128)(2,1)}, bf16[4,960,256]{2,1,0:T(8,128)(2,1)}, u32[]{:S(2)}, u32[]{:S(2)}) collective-permute-start(bf16[4,960,256]{2,1,0:T(8,128)(2,1)} %shard_map.422), channel_id=1, source_target_pairs={{0,1},{1,0},{2,3},{3,2},{4,5},{5,4},{6,7},{7,6},{8,9},{9,8},{10,11... | collective-permute-start | bytes 5898248 | tf_op jit(solution)/shard_map/ppermute | solution.py:497
  866.4 64.6 %collective-permute-start.44 = (bf16[4,960,256]{2,1,0:T(8,128)(2,1)}, bf16[4,960,256]{2,1,0:T(8,128)(2,1)}, u32[]{:S(2)}, u32[]{:S(2)}) collective-permute-start(bf16[4,960,256]{2,1,0:T(8,128)(2,1)} %shard_map.424), channel_id=1, source_target_pairs={{0,1},{1,0},{2,3},{3,2},{4,5},{5,4},{6,7},{7,6},{8,9},{9,8},{10,11... | collective-permute-start | bytes 5898248 | tf_op jit(solution)/shard_map/ppermute | solution.py:497
  922.2 76.0 %collective-permute-start.95 = (bf16[24,9216]{1,0:T(8,128)(2,1)S(1)}, bf16[24,9216]{1,0:T(8,128)(2,1)S(1)}, u32[]{:S(2)}, u32[]{:S(2)}) collective-permute-start(bf16[24,9216]{1,0:T(8,128)(2,1)S(1)} %copy-done.32), channel_id=1, source_target_pairs={{0,1},{1,0},{2,3},{3,2},{4,5},{5,4},{6,7},{7,6},{8,9},{9,8},{10,11... | collective-permute-start | bytes 1327112 | tf_op jit(solution)/shard_map/ppermute | solution.py:497
  934.7 44.1 %collective-permute-start.48 = (bf16[2,960,256]{2,1,0:T(8,128)(2,1)S(1)}, bf16[2,960,256]{2,1,0:T(8,128)(2,1)S(1)}, u32[]{:S(2)}, u32[]{:S(2)}) collective-permute-start(bf16[2,960,256]{2,1,0:T(8,128)(2,1)S(1)} %fusion.40), channel_id=1, source_target_pairs={{0,2},{1,3},{2,0},{3,1},{4,6},{5,7},{6,4},{7,5},{8,10},{9,11},{10,... | collective-permute-start | bytes 2949128 | tf_op jit(solution)/shard_map/ppermute | solution.py:497
  936.8 50.1 %collective-permute-start.98 = (bf16[24,9216]{1,0:T(8,128)(2,1)S(1)}, bf16[24,9216]{1,0:T(8,128)(2,1)S(1)}, u32[]{:S(2)}, u32[]{:S(2)}) collective-permute-start(bf16[24,9216]{1,0:T(8,128)(2,1)S(1)} %copy-done.32), channel_id=1, source_target_pairs={{0,4},{1,5},{2,6},{3,7},{4,0},{5,1},{6,2},{7,3},{8,12},{9,13},{10,... | collective-permute-start | bytes 1327112 | tf_op jit(solution)/shard_map/ppermute | solution.py:497
  1112.3 35.4 %collective-permute-start.81 = (bf16[960,256]{1,0:T(8,128)(2,1)}, bf16[960,256]{1,0:T(8,128)(2,1)S(1)}, u32[]{:S(2)}, u32[]{:S(2)}) collective-permute-start(bf16[960,256]{1,0:T(8,128)(2,1)} %collective-permute-done.80.rest_8_), channel_id=1, source_target_pairs={{0,1},{1,0},{2,3},{3,2},{4,5},{5,4},{6,7},{7,6},{8,9},{9,8},{10,11... | collective-permute-start | bytes 1474568 | tf_op jit(solution)/shard_map/ppermute | solution.py:497
  1112.6 35.0 %collective-permute-start.79 = (bf16[960,256]{1,0:T(8,128)(2,1)}, bf16[960,256]{1,0:T(8,128)(2,1)S(1)}, u32[]{:S(2)}, u32[]{:S(2)}) collective-permute-start(bf16[960,256]{1,0:T(8,128)(2,1)} %collective-permute-done.78.rest_7_), channel_id=1, source_target_pairs={{0,1},{1,0},{2,3},{3,2},{4,5},{5,4},{6,7},{7,6},{8,9},{9,8},{10,11... | collective-permute-start | bytes 1474568 | tf_op jit(solution)/shard_map/ppermute | solution.py:497
  1112.8 34.9 %collective-permute-start.83 = (bf16[960,256]{1,0:T(8,128)(2,1)S(1)}, bf16[960,256]{1,0:T(8,128)(2,1)S(1)}, u32[]{:S(2)}, u32[]{:S(2)}) collective-permute-start(bf16[960,256]{1,0:T(8,128)(2,1)S(1)} %collective-permute-done.82.rest_9_), channel_id=1, source_target_pairs={{0,1},{1,0},{2,3},{3,2},{4,5},{5,4},{6,7},{7,6},{8,9},{9,8},{10,11... | collective-permute-start | bytes 1474568 | tf_op jit(solution)/shard_map/ppermute | solution.py:497
  (202 other events, 3342.2 us)
Sparse Core Ops, SparseCore 0:
  67.4 111.5 reduce-scatter.1
  724.3 47.6 all-gather.3
  774.1 69.9 all-gather.5
  846.1 44.9 all-gather.7

commit v4 on v3

--- a/solution.py
+++ b/solution.py
@@ -309,24 +309,28 @@
 def table_grad_kernel(core_ref, starts_ref, places_ref, order_ref, dlogits_ref, chosen_ref, embed_ref, out_ref, rows, total):
     step = pl.program_id(0)
     count = embed_ref.shape[0]
-    block = total.shape[0]
+    block = total.shape[0] - 8
 
     @pl.when(step == 0)
     def _():
         for start in range(0, count, CHUNK):
             rows[start : start + CHUNK, :] = embed_ref[start : start + CHUNK, :].astype(jnp.float32)
 
-    total[...] = jnp.dot(dlogits_ref[...], chosen_ref[...], preferred_element_type=jnp.float32)
+    total[:block, :] = jnp.dot(dlogits_ref[...], chosen_ref[...], preferred_element_type=jnp.float32)
     chunk = 2 * step + core_ref[0]
     base = chunk * block
-
-    def one(i, carry):
-        place = places_ref[i] - base
-        total[pl.ds(place, 1), :] += rows[pl.ds(order_ref[i], 1), :]
+    first, last = starts_ref[chunk], starts_ref[chunk + 1]
+
+    def eight(turn, carry):
+        for j in range(8):
+            i = first + turn * 8 + j
+            at = jnp.minimum(i, count - 1)
+            place = jnp.where(i < last, places_ref[at] - base, block)
+            total[pl.ds(place, 1), :] += rows[pl.ds(order_ref[at], 1), :]
         return carry
 
-    lax.fori_loop(starts_ref[chunk], starts_ref[chunk + 1], one, 0)
-    out_ref[0] = total[...].astype(out_ref.dtype)
+    lax.fori_loop(0, (last - first + 7) // 8, eight, 0)
+    out_ref[0] = total[:block, :].astype(out_ref.dtype)
 
 
 def table_grad_half(core, starts, places, order, dlogits, chosen, embed, block, dtype):
@@ -345,7 +349,7 @@
                 pl.BlockSpec((count, width), fixed, pipeline_mode=pl.Buffered(1)),
             ],
             out_specs=pl.BlockSpec((1, block, width), lambda i, *_: (i, 0, 0)),
-            scratch_shapes=[pltpu.VMEM((count, width), jnp.float32), pltpu.VMEM((block, width), jnp.float32)],
+            scratch_shapes=[pltpu.VMEM((count, width), jnp.float32), pltpu.VMEM((block + 8, width), jnp.float32)],
         ),
         out_shape=jax.ShapeDtypeStruct((chunks, block, width), dtype),
         compiler_params=pltpu.CompilerParams(vmem_limit_bytes=vmem),
@@ -373,7 +377,7 @@
             means = jnp.mean(gradient * gradient, axis=1, keepdims=True)
             rows_new = decay * old + (1.0 - decay) * (means * factor * factor)
             grad_ref[...] = gradient * factor
-            new_ref[...] = table_ref[...] - rate * gradient * lax.rsqrt(rows_new * cols_ref[...])
+            new_ref[...] = table_ref[...] - gradient * (rate * lax.rsqrt(rows_new)) * cols_ref[...]
             rows_new_ref[0] = jnp.broadcast_to(rows_new, (TILE, LANES)).T[0:1, :]
 
 
@@ -492,6 +496,9 @@
     )(members, slots, *pieces, *after)
 
 
+tie = lax.optimization_barrier
+
+
 def flip(value, bit):
     size = lax.axis_size("rep")
     return lax.ppermute(value, "rep", [(i, i ^ bit) for i in range(size)])
@@ -608,9 +615,14 @@
     return result
 
 
-def total_sum(value):
-    for j in range(lax.axis_size("rep").bit_length() - 1):
+def plane_sum(value):
+    for j in range(1, lax.axis_size("rep").bit_length() - 1):
         value = value + flip(value, 1 << j)
+    return value
+
+
+def rest_sum(value):
+    value = value + flip(value, 1)
     size = lax.axis_size("grp")
     for j in range(size.bit_length() - 1):
         value = value + lax.ppermute(value, "grp", [(i, i ^ (1 << j)) for i in range(size)])
@@ -717,10 +729,6 @@
         down_part = cut(w_down, 0)
         down_part = jnp.concatenate([down_part[:, : width // 2], down_part[:, width // 2 :]], axis=0)
         far_part = fetch(jnp.concatenate([cut(w_gu, 1), down_part], axis=1).astype(low_type))
-    loss_count = jnp.sum(group_mask).astype(jnp.float32)[None]
-    for j in range(replicas.bit_length() - 1):
-        loss_count = loss_count + flip(loss_count, 1 << j)
-    loss_count = loss_count[0]
 
     local_ids = group_ids - member * vocab_rows
     owned = (local_ids >= 0) & (local_ids < vocab_rows)
@@ -740,24 +748,27 @@
         near_have = spread(near_part, [2, 4, 1])
         far_have = spread(far_part, [4, 2, 1])
         (near,) = lay_columns(members_of(), slots_of(), [near_have[place] for place in range(replicas)])
-    else:
-        near = lax.all_gather(near_shard.astype(low_type), "grp", tiled=True)
-    cosine, sine = rope_tables(length)
-    first, first_low, queries, keys, values = project(embed, norms, cosine, sine, near)
-    mixed_low, log_sums = attend(lengths, queries, keys, values)
-    if quick:
         w_gu_low, w_down_low = lay_columns(
             members_of(),
             slots_of(),
             [far_have[place] for place in range(replicas)],
             w_gu.shape[1] // replicas,
-            (mixed_low,),
         )
         w_down_low = w_down_low.reshape(-1, width)
+        embed, near, w_gu_low, w_down_low, table_low = tie((embed, near, w_gu_low, w_down_low, table_low))
     else:
+        near = lax.all_gather(near_shard.astype(low_type), "grp", tiled=True)
         w_gu_low = lax.all_gather(w_gu.astype(low_type), "grp", tiled=True)
         w_down_low = lax.all_gather(w_down.astype(low_type), "grp", tiled=True)
     w_out_low = near[:, 3 * width :]
+    cosine, sine = rope_tables(length)
+    first, first_low, queries, keys, values = project(embed, norms, cosine, sine, near)
+    queries, group_mask = tie((queries, group_mask))
+    loss_count = jnp.sum(group_mask).astype(jnp.float32)[None]
+    for j in range(replicas.bit_length() - 1):
+        loss_count = loss_count + flip(loss_count, 1 << j)
+    loss_count = loss_count[0]
+    mixed_low, log_sums = attend(lengths, queries, keys, values)
     first_sum = first + jnp.dot(mixed_low, w_out_low, preferred_element_type=jnp.float32)
     second = layer_norm(first_sum, norms[2], norms[3])
     second_low = second.astype(low_type)
@@ -802,9 +813,14 @@
     hidden_grad = contract(branch_low, w_down_low, 1, 1)
     _, pull = jax.vjp(swiglu, gate_up)
     gate_low = pull(hidden_grad)[0].astype(low_type)
-    gate = Fold(1, (4, 2))
-    gate.cores(gradient_chunks(contract(second_low, gate_low, 0, 0)))
+    gate_low, _ = tie((gate_low, down.plane(True)))
+    gate, up = Fold(1, (4, 2)), Fold(1, (2, 4))
+    middle = gate_up.shape[1] // 2
+    sent = gate.cores(gradient_chunks(contract(second_low, gate_low[:, :middle], 0, 0)))
+    sent += up.cores(gradient_chunks(contract(second_low, gate_low[:, middle:], 0, 0)))
+    gate_low, _ = tie((gate_low, sent))
     second_grad = sum_grad + contract(gate_low, w_gu_low, 1, 1)
+    second_grad, _ = tie((second_grad, gate.plane(True) + up.plane(True) + down.plane(False)))
     _, pull = jax.vjp(layer_norm, first_sum, norms[2], norms[3])
     first_sum_grad, gain_two, shift_two = pull(second_grad)
     attn_low = first_sum_grad.astype(low_type)
@@ -813,28 +829,24 @@
     third = pairs // 3
     sides = []
     for stage in range(3):
-        if stage < 2:
-            after = down.plane(stage == 0) + gate.plane(stage == 0)
-        else:
-            after = down.members() + gate.members()
-        after = after + [side[0] for side in sides[-1:]]
+        if stage:
+            sent = gate.plane(False) + up.plane(False) + down.members() if stage == 1 else gate.members() + up.members()
+            mixed_grad, sides[-1], _ = tie((mixed_grad, sides[-1], sent))
         sides.append(
-            attend_back(
-                lengths, queries, keys, values, mixed_grad, log_sums, cosine, sine, stage * third, third, after
-            )
+            attend_back(lengths, queries, keys, values, mixed_grad, log_sums, cosine, sine, stage * third, third)
         )
     joined_grad = jnp.concatenate([side for parts in zip(*sides) for side in parts], axis=1)
     first_grad = first_sum_grad + contract(joined_grad, near[:, : 3 * width], 1, 1)
     _, pull = jax.vjp(layer_norm, embed.astype(jnp.float32), norms[0], norms[1])
     embed_grad, gain_one, shift_one = pull(first_grad)
     norm_grad = jnp.stack([gain_one, shift_one, gain_two, shift_two, gain_three, shift_three])
-    parts = 3
-    wide = width // parts
+    cuts_at = (0, width // 2, width // 6 * 5, width)
+    spans = list(zip(cuts_at[:-1], cuts_at[1:]))
     embed_low = embed_grad.astype(low_type)
-    group_embeds = [
-        lax.all_gather(embed_low[:, part * wide : (part + 1) * wide], "grp", axis=0, tiled=True)
-        for part in range(parts)
-    ]
+    group_embeds = []
+    for begin, end in spans:
+        piece, _ = tie((embed_low[:, begin:end], group_embeds[-1:]))
+        group_embeds.append(lax.all_gather(piece, "grp", axis=0, tiled=True))
     join = Fold(1, (2, 4))
     join.cores(
         gradient_chunks(
@@ -843,34 +855,46 @@
             )
         )
     )
-    join.plane(True)
-    join.plane(False)
-    join.members()
-    gu_share, down_share, join_share = gate.total(), down.total(), join.total()
-    part_rows = join_share.shape[0]
+    sent = join.plane(True)
+    gu_share = jnp.concatenate([gate.total(), up.total()], axis=1)
+    down_share = down.total()
+    part_rows = gu_share.shape[0]
+    far_low = jnp.concatenate(
+        [gu_share.astype(low_type), down_share.astype(low_type).reshape(part_rows, -1)], axis=1
+    )
+    if quick:
+        far_got = spread(far_low, [2, 4, 1])
+        group_embeds[0], _, _ = tie((group_embeds[0], sent, list(far_got.values())))
     core = replica % 2
-    table_parts = []
-    for part in range(parts):
+    heads = [Fold(0, (4, 2) if part % 2 else (2, 4)) for part in range(3)]
+    for part, (begin, end) in enumerate(spans):
+        head = heads[part]
+        if part == 1:
+            group_embeds[1], _ = tie((group_embeds[1], heads[0].plane(True) + join.plane(False)))
+        if part == 2:
+            sent = heads[1].plane(True) + heads[0].plane(False) + join.members()
+            group_embeds[2], _ = tie((group_embeds[2], sent))
         half_args = (
             starts,
             places,
             order,
             dlogits,
-            group_chosen[:, part * wide : (part + 1) * wide],
+            group_chosen[:, begin:end],
             group_embeds[part],
             block,
         )
-        head = Fold(0, (4, 2) if part % 2 else (2, 4))
         if quick:
             sent = table_grad_half((1 - core)[None], *half_args, low_type)
             kept = table_grad_half(core[None], *half_args, jnp.float32)
             head.from_cores(kept, sent)
         else:
             both = [table_grad_half(jnp.full((1,), j, jnp.int32), *half_args, jnp.float32) for j in range(2)]
-            head.cores(jnp.stack(both, axis=1).reshape(replicas, block, wide))
-        head.plane(True)
-        head.plane(False)
-        table_parts.append(head.sum())
+            head.cores(jnp.stack(both, axis=1).reshape(replicas, block, end - begin))
+    heads[2].plane(True)
+    heads[1].plane(False)
+    heads[2].plane(False)
+    table_parts = [head.sum() for head in heads]
+    join_share = join.total()
 
     shares = (
         join_share[:, : 3 * width],
@@ -886,7 +910,10 @@
     ] + [jnp.sum(gradient * gradient, axis=0) for gradient in shares]
     row_old = jnp.stack([jnp.sum(rows) for rows in old_rows]) / replicas
     small = [norm_grad.reshape(-1)] + col_parts + [row_old, jnp.sum(own_terms)[None]]
-    totals = total_sum(jnp.concatenate(small))
+    plane_totals = plane_sum(jnp.concatenate(small))
+    table_lows = [table_parts[0].astype(low_type), jnp.concatenate(table_parts[1:], axis=1).astype(low_type)]
+    plane_totals, table_lows = tie((plane_totals, table_lows))
+    totals = rest_sum(plane_totals)
     cuts = []
     start = 0
     for part in small:
@@ -901,11 +928,11 @@
     factor = clip_limit / jnp.maximum(clip_norm, clip_limit)
     decay = 1.0 - float(STEP) ** (-0.8)
 
-    far_whole = plane_gather(
-        jnp.concatenate(
-            [gu_share.astype(low_type), down_share.astype(low_type).reshape(part_rows, -1)], axis=1
-        )
-    ).reshape(shard_rows, -1)
+    if quick:
+        far_whole = lay_out(slots_of(), [far_got[place] for place in range(replicas)])
+    else:
+        far_whole = plane_gather(far_low)
+    far_whole = far_whole.reshape(shard_rows, -1)
     near_whole = plane_gather(join_share.astype(low_type)).reshape(shard_rows, -1)
     wholes = [
         None,
@@ -914,7 +941,6 @@
         far_whole[:, : w_gu.shape[1]],
         far_whole[:, w_gu.shape[1] :].reshape(w_down.shape),
     ]
-    table_lows = [part.astype(low_type) for part in table_parts]
 
     outputs = []
     for place in range(5):
@@ -945,7 +971,7 @@
                     [[got[part] for got in have] for part in four],
                     table,
                     row_tiles,
-                    new_cols[None, :],
+                    lax.rsqrt(new_cols)[None, :],
                     so_far,
                 )
             outputs.extend([so_far[0], so_far[2].reshape(-1)[:vocab_rows], new_cols, so_far[1]])

time: 1190 us -> 1120 us (0.941)
  starting transfers between devices: 169 us -> 124 us
  waiting for transfers between devices: 295 us -> 266 us
  local copies, waits for them, and re-layouts: 76.1 us -> 99.3 us
  Pallas kernels: 286 us -> 272 us
    ppermute x27 -> x30, waiting for transfers between devices: 113 us -> 54.4 us  [turn(): lax.ppermute(value, 'grp', [(i, (i + offset) % size) for i in range(size)])]
    ppermute x73 -> x69, starting transfers between devices: 126 us -> 80.9 us  [flip(): return lax.ppermute(value, 'rep', [(i, i ^ bit) for i in range(size)])]
    ppermute x73 -> x69, waiting for transfers between devices: 181 us -> 198 us  [flip(): return lax.ppermute(value, 'rep', [(i, i ^ bit) for i in range(size)])]
    pallas_call x6, Pallas kernels: 72.5 us -> 59.6 us  [table_grad_half(): pl.pallas_call(table_grad_kernel, grid_spec=pltpu.PrefetchScalarGridSpec(...]
    all_gather x3, waiting for transfers between devices: 0.01 us -> 11.9 us  [body(): group_embeds.append(lax.all_gather(piece, 'grp', axis=0, tiled=True))]
    dot_general x10 -> x11, matrix products: 123 us -> 112 us  [contract(): lax.dot_general(left, right, (((left_dim,), (right_dim,)), ((), ())), pre...]
    unnamed x264 -> x242, local copies, waits for them, and re-layouts: 26.8 us -> 35.7 us
    add x15 -> x18, other arithmetic: 28.4 us -> 35.7 us  [sum(): self.kept + self.got.astype(jnp.float32)]
  transfers between devices with their start and end apart: 106 -> 105, of which waited for: 29 -> 30; matrix products, arithmetic and copies ran while one was open for 19% -> 24% of each run, Pallas kernels for 20% -> 16%
where the time goes in v4:
time: 1120 us; the launch traced here: 1110 us
  Pallas kernels  272 us (24%)
  waiting for transfers between devices  266 us (24%)
  other arithmetic  178 us (16%)
  matrix products  138 us (12%)
  starting transfers between devices  124 us (11%)
  local copies, waits for them, and re-layouts  99.3 us (9%)
  between operations  31.7 us (3%)
    ppermute x69, waiting for transfers between devices, flip(): return lax.ppermute(value, 'rep', [(i, i ^ bit) for i in range(size)])  198 us
    dot_general x11, matrix products, contract(): lax.dot_general(left, right, (((left_dim,), (right_dim,)), ((), ())), pre...  112 us
    ppermute x69, starting transfers between devices, flip(): return lax.ppermute(value, 'rep', [(i, i ^ bit) for i in range(size)])  80.9 us
    pallas_call x3, Pallas kernels, attend_back(): pl.pallas_call(functools.partial(attend_back_kernel, first_pair), grid_sp...  65.4 us
    pallas_call x6, Pallas kernels, table_grad_half(): pl.pallas_call(table_grad_kernel, grid_spec=pltpu.PrefetchScalarGridSpec(...  59.6 us
    ppermute x30, waiting for transfers between devices, turn(): lax.ppermute(value, 'grp', [(i, (i + offset) % size) for i in range(size)])  54.4 us
    pallas_call x1, Pallas kernels, attend(): pl.pallas_call(attend_kernel, grid_spec=pltpu.PrefetchScalarGridSpec(num_...  47.7 us
    pallas_call x2, Pallas kernels, update(): pl.pallas_call(functools.partial(update_kernel, parts), grid_spec=pltpu.P...  43.1 us
  transfers between devices with their start and end apart: 105, of which 30 were waited for; matrix products, arithmetic and copies ran while one was open for 24% of the time, Pallas kernels for 16%

profile of v4, /device:TPU:1, one launch (start us, length us, event | category | flops | bytes accessed | tf_op | source)
XLA Modules:
  0.0 1110.0 jit_solution(6675780420344583204)
XLA Ops:
  30.5 17.1 %shard_map.413 = bf16[4096,768]{1,0:T(8,128)(2,1)} custom-call(s32[9]{0:T(128)} %convert_reduce_fusion.1.starts_ref, s32[4096]{0:T(1024)} %copy-done.43, s32[4096]{0:T(1024)} %get-tuple-element.83.order_ref, f32[7632,768]{1,0:T(8,128)} %rest_8_.3), custom_call_target="tpu_custom_call" | custom-call | bytes 70336512 | tf_op jit(solution)/shard_map/pallas_call | solution.py:294
  47.7 18.1 %collective-permute-done.7 = bf16[192,1152]{1,0:T(8,128)(2,1)S(1)} collective-permute-done((bf16[192,1152]{1,0:T(8,128)(2,1)S(1)}, bf16[192,1152]{1,0:T(8,128)(2,1)S(1)}, u32[]{:S(2)}, u32[]{:S(2)}) %collective-permute-start.7) | collective-permute-done | bytes 442400 | tf_op jit(solution)/shard_map/ppermute | solution.py:509
  70.7 35.3 %collective-permute-done.19.refs_4_ = bf16[4,192,1152]{2,1,0:T(8,128)(2,1)} collective-permute-done((bf16[4,192,1152]{2,1,0:T(8,128)(2,1)S(1)}, bf16[4,192,1152]{2,1,0:T(8,128)(2,1)}, u32[]{:S(2)}, u32[]{:S(2)}) %collective-permute-start.19) | collective-permute-done | bytes 1769504 | tf_op jit(solution)/shard_map/ppermute | solution.py:504
  113.0 45.2 %collective-permute-done.10.refs_2_ = bf16[4,192,384]{2,1,0:T(8,128)(2,1)} collective-permute-done((bf16[4,192,384]{2,1,0:T(8,128)(2,1)S(1)}, bf16[4,192,384]{2,1,0:T(8,128)(2,1)}, u32[]{:S(2)}, u32[]{:S(2)}) %collective-permute-start.10) | collective-permute-done | bytes 589856 | tf_op jit(solution)/shard_map/ppermute | solution.py:504
  170.3 10.8 collective-permute-done.14.refs_6_
  206.4 11.7 %shard_map.415 = (bf16[768,6144]{1,0:T(8,128)(2,1)}, bf16[4,8,96,768]{3,2,1,0:T(8,128)(2,1)}) custom-call(s32[4]{0:T(128)} %and_select_fusion.members_ref, s32[8]{0:T(128)} %iota_xor_fusion.slots_ref, bf16[4,192,1152]{2,1,0:T(8,128)(2,1)} %copy-done.23, bf16[4,192,1152]{2,1,0:T(8,128)(2,1)} %collective-permute-done.16.refs_1_, ...), custom_call_target="tpu_custom_call" | custom-call | bytes 28311552 | tf_op jit(solution)/shard_map/pallas_call | solution.py:484
  219.8 9.2 shard_map.416
  229.0 47.7 %shard_map.417 = (bf16[1024,768]{1,0:T(8,128)(2,1)}, f32[6,2,1024]{2,1,0:T(2,128)}) custom-call(s32[1]{0:T(128)S(6)} %copy.138.length_ref, bf16[1024,768]{1,0:T(8,128)(2,1)} %get-tuple-element.95.q_ref, bf16[1024,768]{1,0:T(8,128)(2,1)} %get-tuple-element.96.k_ref, bf16[1024,768]{1,0:T(8,128)(2,1)} %get-tuple-element.97.v_ref), custom_call_target="tpu_custom_call" | custom-call | flops 12884901888 | bytes 6291456 | tf_op jit(solution)/shard_map/pallas_call | solution.py:138
  280.5 17.6 %fusion.118 = f32[1024,6144]{1,0:T(8,128)} fusion(bf16[768,6144]{1,0:T(8,128)(2,1)} %get-tuple-element.99, f32[1024,768]{1,0:T(8,128)S(1)} %get-tuple-element.238, f32[768]{0:T(1024)S(1)} %get-tuple-element.155, f32[768]{0:T(1024)S(1)} %get-tuple-element.156, f32[1024]{0:T(1024)S(1)} %fusion.88, f32[1024]{0:T(1024)S(1)} %broadcast_multiply_fusion.1), kind=kOutput, calls=%fused_computation.326 | convolution fusion | flops 9667608576 | bytes 37763072 | tf_op jit(solution)/shard_map/dot_general | solution.py:775
  298.1 10.4 multiply_convert_fusion.1
  342.8 10.7 select_reduce_fusion.1
  376.9 11.8 %fusion.120 = f32[512,768]{1,0:T(8,128)S(1)} fusion(bf16[7680,512]{1,0:T(8,128)(2,1)S(1)} %multiply_convert_fusion.dlogits_ref, bf16[7680,768]{1,0:T(8,128)(2,1)} %pad.14), kind=kOutput, calls=%fused_computation.327 | convolution fusion | flops 6039797760 | bytes 21233664 | tf_op jit(solution)/shard_map/dot_general | solution.py:649
  397.8 24.2 %collective-permute-done.33 = f32[128,768]{1,0:T(8,128)S(1)} collective-permute-done((f32[128,768]{1,0:T(8,128)S(1)}, f32[128,768]{1,0:T(8,128)S(1)}, u32[]{:S(2)}, u32[]{:S(2)}) %collective-permute-start.33) | collective-permute-done | bytes 393248 | tf_op jit(solution)/shard_map/ppermute | solution.py:509
  433.1 8.9 fusion.99
  450.8 23.8 %fusion.31 = (f32[1024,3072]{1,0:T(8,128)}, f32[1024,3072]{1,0:T(8,128)}) fusion(f32[1024,6144]{1,0:T(8,128)} %fusion.118, bf16[3072,768]{1,0:T(8,128)(2,1)} %bitcast.345, f32[1024,768]{1,0:T(8,128)} %copy-done.32, f32[1024]{0:T(1024)S(1)} %negate_multiply_fusion.2), kind=kOutput, calls=%fused_computation.99 | convolution fusion | flops 4871159808 | bytes 58200064 | tf_op jit(solution)/shard_map/dot_general | solution.py:649
  474.6 9.4 add_convert_fusion
  506.8 12.2 %collective-permute-done.38 = bf16[4,2,96,768]{3,2,1,0:T(8,128)(2,1)} collective-permute-done((bf16[4,2,96,768]{3,2,1,0:T(8,128)(2,1)S(1)}, bf16[4,2,96,768]{3,2,1,0:T(8,128)(2,1)}, u32[]{:S(2)}, u32[]{:S(2)}) %collective-permute-start.38) | collective-permute-done | bytes 1179680 | tf_op jit(solution)/shard_map/ppermute | solution.py:504
  538.6 16.9 %add_add_fusion.4 = f32[1024,768]{1,0:T(8,128)} fusion(f32[1024,768]{1,0:T(8,128)S(1)} %copy-done.33, bf16[1024,6144]{1,0:T(8,128)(2,1)} %copy-done.3, bf16[768,6144]{1,0:T(8,128)(2,1)} %get-tuple-element.99, f32[1024]{0:T(1024)S(1)} %negate_multiply_fusion.2), kind=kOutput, calls=%fused_computation.60 | convolution fusion | flops 9665249280 | bytes 28315648 | tf_op jit(solution)/shard_map/dot_general | solution.py:649
  576.4 21.8 %shard_map.418 = (bf16[1024,256]{1,0:T(8,128)(2,1)}, bf16[1024,256]{1,0:T(8,128)(2,1)}, bf16[1024,256]{1,0:T(8,128)(2,1)}) custom-call(s32[1]{0:T(128)S(6)} %copy.138.length_ref, bf16[1024,768]{1,0:T(8,128)(2,1)} %get-tuple-element.95.q_ref, bf16[1024,768]{1,0:T(8,128)(2,1)} %get-tuple-element.96.k_ref, bf16[1024,768]{1,0:T(8,128)(2,1)} %get-tuple-element.97.v_ref, ...), custom_call_target="tpu_custom_call" | custom-call | flops 10737418240 | bytes 4194304 | tf_op jit(solution)/shard_map/pallas_call | solution.py:223
  609.6 21.8 %shard_map.419 = (bf16[1024,256]{1,0:T(8,128)(2,1)}, bf16[1024,256]{1,0:T(8,128)(2,1)}, bf16[1024,256]{1,0:T(8,128)(2,1)}) custom-call(s32[1]{0:T(128)S(6)} %copy.138.length_ref, bf16[1024,768]{1,0:T(8,128)(2,1)} %get-tuple-element.95.q_ref, bf16[1024,768]{1,0:T(8,128)(2,1)} %get-tuple-element.96.k_ref, bf16[1024,768]{1,0:T(8,128)(2,1)} %get-tuple-element.97.v_ref, ...), custom_call_target="tpu_custom_call" | custom-call | flops 10737418240 | bytes 4194304 | tf_op jit(solution)/shard_map/pallas_call | solution.py:223
  641.5 21.7 %shard_map.420 = (bf16[1024,256]{1,0:T(8,128)(2,1)}, bf16[1024,256]{1,0:T(8,128)(2,1)}, bf16[1024,256]{1,0:T(8,128)(2,1)}) custom-call(s32[1]{0:T(128)S(6)} %copy.138.length_ref, bf16[1024,768]{1,0:T(8,128)(2,1)} %get-tuple-element.95.q_ref, bf16[1024,768]{1,0:T(8,128)(2,1)} %get-tuple-element.96.k_ref, bf16[1024,768]{1,0:T(8,128)(2,1)} %get-tuple-element.97.v_ref, ...), custom_call_target="tpu_custom_call" | custom-call | flops 10737418240 | bytes 4194304 | tf_op jit(solution)/shard_map/pallas_call | solution.py:223
  682.7 9.7 fusion.121
  692.3 9.5 pad_maximum_fusion
  752.5 10.7 shard_map.422
  768.2 24.2 %collective-permute-done.64 = bf16[4,2,24,3072]{3,2,0,1:T(8,128)(2,1)} collective-permute-done((bf16[4,2,24,3072]{3,2,0,1:T(8,128)(2,1)S(1)}, bf16[4,2,24,3072]{3,2,0,1:T(8,128)(2,1)}, u32[]{:S(2)}, u32[]{:S(2)}) %collective-permute-start.64) | collective-permute-done | bytes 1179680 | tf_op jit(solution)/shard_map/ppermute | solution.py:504
  796.0 11.9 %shard_map.421 = f32[4,960,384]{2,1,0:T(8,128)} custom-call(s32[1]{0:T(128)} %bitcast.77.core_ref, s32[9]{0:T(128)} %convert_reduce_fusion.1.starts_ref, s32[4096]{0:T(1024)} %copy-done.43, s32[4096]{0:T(1024)} %get-tuple-element.83.order_ref, bf16[7680,512]{1,0:T(8,128)(2,1)} %copy-done, bf16[512,384]{1,0:T(8,128)(2,1)} %slice.269.chosen_ref, ...), custom_call_target="tpu_custom_call" | custom-call | flops 1509949440 | bytes 11796480 | tf_op jit(solution)/shard_map/pallas_call | solution.py:341
  815.7 9.3 shard_map.424
  852.9 10.5 shard_map.423
  916.3 21.7 %collective-permute-done.63 = bf16[960,384]{1,0:T(8,128)(2,1)S(1)} collective-permute-done((bf16[960,384]{1,0:T(8,128)(2,1)S(1)}, bf16[960,384]{1,0:T(8,128)(2,1)S(1)}, u32[]{:S(2)}, u32[]{:S(2)}) %collective-permute-start.63) | collective-permute-done | bytes 737312 | tf_op jit(solution)/shard_map/ppermute | solution.py:504
  1038.8 11.4 %collective-permute-done.92.rest_7_ = bf16[960,384]{1,0:T(8,128)(2,1)} collective-permute-done((bf16[960,384]{1,0:T(8,128)(2,1)}, bf16[960,384]{1,0:T(8,128)(2,1)}, u32[]{:S(2)}, u32[]{:S(2)}) %collective-permute-start.92) | collective-permute-done | bytes 737312 | tf_op jit(solution)/shard_map/ppermute | solution.py:504
  1054.4 21.5 %shard_map.430 = (f32[7632,768]{1,0:T(8,128)}, f32[7632,768]{1,0:T(8,128)}, f32[32,1,240]{2,1,0:T(1,128)}) custom-call(s32[4]{0:T(128)} %pad_add_fusion.2.slots_ref, f32[2]{0:T(128)} %pad_maximum_fusion.10.scalars_ref, bf16[960,384]{1,0:T(8,128)(2,1)} %get-tuple-element.130.rest_0_, ...), custom_call_target="tpu_custom_call", output_to_operand_aliasing={{0}: (13, {}), {1}: (14, {}), {2}: (15, {})} | custom-call | flops 29491200 | bytes 41287680 | tf_op jit(solution)/shard_map/pallas_call | solution.py:398
  1077.8 21.6 %shard_map.431 = (f32[7632,768]{1,0:T(8,128)}, f32[7632,768]{1,0:T(8,128)}, f32[32,1,240]{2,1,0:T(1,128)}) custom-call(s32[4]{0:T(128)} %pad_add_fusion.1.slots_ref, f32[2]{0:T(128)} %pad_maximum_fusion.10.scalars_ref, bf16[960,384]{1,0:T(8,128)(2,1)} %collective-permute-done.80.rest_0_, ...), custom_call_target="tpu_custom_call", output_to_operand_aliasing={{0}: (13, {}), {1}: (14, {}), {2}: (15, {})} | custom-call | flops 29491200 | bytes 41287680 | tf_op jit(solution)/shard_map/pallas_call | solution.py:398
  (664 shorter events, 509.8 us)
Async XLA Ops:
  7.2 210.9 %reduce-scatter.2.cloned.1.call-start = ((), (), s32[]{:S(2)}) async-start(), calls=%async_computation.1 | async-start | bytes 7864320 | tf_op jit(solution)/shard_map/reduce_scatter | solution.py:743
  23.2 42.7 %collective-permute-start.7 = (bf16[192,1152]{1,0:T(8,128)(2,1)S(1)}, bf16[192,1152]{1,0:T(8,128)(2,1)S(1)}, u32[]{:S(2)}, u32[]{:S(2)}) collective-permute-start(bf16[192,1152]{1,0:T(8,128)(2,1)S(1)} %pad_maximum_fusion.7), channel_id=1, source_target_pairs={{0,16},{8,24},{16,0},{24,8},{1,17},{9,25},{17,1},{25,9},{2,18},{10... | collective-permute-start | bytes 1327112 | tf_op jit(solution)/shard_map/ppermute | solution.py:509
  23.4 42.5 %collective-permute-start.6 = (bf16[192,1152]{1,0:T(8,128)(2,1)S(1)}, bf16[192,1152]{1,0:T(8,128)(2,1)S(1)}, u32[]{:S(2)}, u32[]{:S(2)}) collective-permute-start(bf16[192,1152]{1,0:T(8,128)(2,1)S(1)} %pad_maximum_fusion.7), channel_id=1, source_target_pairs={{0,8},{8,16},{16,24},{24,0},{1,9},{9,17},{17,25},{25,1},{2,10},{10... | collective-permute-start | bytes 1327112 | tf_op jit(solution)/shard_map/ppermute | solution.py:509
  68.1 684.3 %all-gather.4.cloned.1.call-start = ((), (), s32[]{:S(2)}) async-start(), calls=%async_computation.2 | async-start | bytes 3932160 | tf_op jit(solution)/shard_map/all_gather | solution.py:849
  69.5 94.0 %collective-permute-start.17 = (bf16[4,192,1152]{2,1,0:T(8,128)(2,1)S(1)}, bf16[4,192,1152]{2,1,0:T(8,128)(2,1)}, u32[]{:S(2)}, u32[]{:S(2)}) collective-permute-start(bf16[4,192,1152]{2,1,0:T(8,128)(2,1)S(1)} %pad_maximum_fusion.1.refs_0_), channel_id=1, source_target_pairs={{0,2},{1,3},{2,0},{3,1},{4,6},{5,7},{6,4},{7,5},{8,10},{9,11},{10,... | collective-permute-start | bytes 5308424 | tf_op jit(solution)/shard_map/ppermute | solution.py:504
  106.0 57.9 %collective-permute-start.21 = (bf16[4,192,1152]{2,1,0:T(8,128)(2,1)}, bf16[4,192,1152]{2,1,0:T(8,128)(2,1)}, u32[]{:S(2)}, u32[]{:S(2)}) collective-permute-start(bf16[4,192,1152]{2,1,0:T(8,128)(2,1)} %collective-permute-done.19.refs_4_), channel_id=1, source_target_pairs={{0,2},{1,3},{2,0},{3,1},{4,6},{5,7},{6,4},{7,5},{8,10},{9,11},{10,... | collective-permute-start | bytes 5308424 | tf_op jit(solution)/shard_map/ppermute | solution.py:504
  107.3 50.9 %collective-permute-start.10 = (bf16[4,192,384]{2,1,0:T(8,128)(2,1)S(1)}, bf16[4,192,384]{2,1,0:T(8,128)(2,1)}, u32[]{:S(2)}, u32[]{:S(2)}) collective-permute-start(bf16[4,192,384]{2,1,0:T(8,128)(2,1)S(1)} %pad_maximum_fusion.3.refs_0_), channel_id=1, source_target_pairs={{0,2},{1,3},{2,0},{3,1},{4,6},{5,7},{6,4},{7,5},{8,10},{9,11},{10,... | collective-permute-start | bytes 1769480 | tf_op jit(solution)/shard_map/ppermute | solution.py:504
  107.5 53.7 %collective-permute-start.12 = (bf16[4,192,384]{2,1,0:T(8,128)(2,1)S(1)}, bf16[4,192,384]{2,1,0:T(8,128)(2,1)S(1)}, u32[]{:S(2)}, u32[]{:S(2)}) collective-permute-start(bf16[4,192,384]{2,1,0:T(8,128)(2,1)S(1)} %pad_maximum_fusion.3.refs_0_), channel_id=1, source_target_pairs={{0,4},{1,5},{2,6},{3,7},{4,0},{5,1},{6,2},{7,3},{8,12},{9,13},{10,... | collective-permute-start | bytes 1769480 | tf_op jit(solution)/shard_map/ppermute | solution.py:504
  108.8 52.5 %collective-permute-start.9 = (bf16[4,192,384]{2,1,0:T(8,128)(2,1)S(1)}, bf16[4,192,384]{2,1,0:T(8,128)(2,1)S(1)}, u32[]{:S(2)}, u32[]{:S(2)}) collective-permute-start(bf16[4,192,384]{2,1,0:T(8,128)(2,1)S(1)} %pad_maximum_fusion.3.refs_0_), channel_id=1, source_target_pairs={{0,1},{1,0},{2,3},{3,2},{4,5},{5,4},{6,7},{7,6},{8,9},{9,8},{10,11... | collective-permute-start | bytes 1769480 | tf_op jit(solution)/shard_map/ppermute | solution.py:504
  161.3 45.1 %collective-permute-start.16 = (bf16[4,192,1152]{2,1,0:T(8,128)(2,1)S(1)}, bf16[4,192,1152]{2,1,0:T(8,128)(2,1)}, u32[]{:S(2)}, u32[]{:S(2)}) collective-permute-start(bf16[4,192,1152]{2,1,0:T(8,128)(2,1)S(1)} %pad_maximum_fusion.1.refs_0_), channel_id=1, source_target_pairs={{0,1},{1,0},{2,3},{3,2},{4,5},{5,4},{6,7},{7,6},{8,9},{9,8},{10,11... | collective-permute-start | bytes 5308424 | tf_op jit(solution)/shard_map/ppermute | solution.py:504
  163.1 43.3 %collective-permute-start.20 = (bf16[4,192,1152]{2,1,0:T(8,128)(2,1)}, bf16[4,192,1152]{2,1,0:T(8,128)(2,1)}, u32[]{:S(2)}, u32[]{:S(2)}) collective-permute-start(bf16[4,192,1152]{2,1,0:T(8,128)(2,1)} %collective-permute-done.19.refs_4_), channel_id=1, source_target_pairs={{0,1},{1,0},{2,3},{3,2},{4,5},{5,4},{6,7},{7,6},{8,9},{9,8},{10,11... | collective-permute-start | bytes 5308424 | tf_op jit(solution)/shard_map/ppermute | solution.py:504
  163.5 42.9 %collective-permute-start.18 = (bf16[4,192,1152]{2,1,0:T(8,128)(2,1)}, bf16[4,192,1152]{2,1,0:T(8,128)(2,1)}, u32[]{:S(2)}, u32[]{:S(2)}) collective-permute-start(bf16[4,192,1152]{2,1,0:T(8,128)(2,1)} %collective-permute-done.17.refs_2_), channel_id=1, source_target_pairs={{0,1},{1,0},{2,3},{3,2},{4,5},{5,4},{6,7},{7,6},{8,9},{9,8},{10,11... | collective-permute-start | bytes 5308424 | tf_op jit(solution)/shard_map/ppermute | solution.py:504
  164.0 42.5 %collective-permute-start.22 = (bf16[4,192,1152]{2,1,0:T(8,128)(2,1)}, bf16[4,192,1152]{2,1,0:T(8,128)(2,1)}, u32[]{:S(2)}, u32[]{:S(2)}) collective-permute-start(bf16[4,192,1152]{2,1,0:T(8,128)(2,1)} %collective-permute-done.21.refs_6_), channel_id=1, source_target_pairs={{0,1},{1,0},{2,3},{3,2},{4,5},{5,4},{6,7},{7,6},{8,9},{9,8},{10,11... | collective-permute-start | bytes 5308424 | tf_op jit(solution)/shard_map/ppermute | solution.py:504
  635.9 68.8 %collective-permute-start.50 = (bf16[24,3072]{1,0:T(8,128)(2,1)}, bf16[24,3072]{1,0:T(8,128)(2,1)S(1)}, u32[]{:S(2)}, u32[]{:S(2)}) collective-permute-start(bf16[24,3072]{1,0:T(8,128)(2,1)} %get-tuple-element.200), channel_id=1, source_target_pairs={{0,24},{8,0},{16,8},{24,16},{1,25},{9,1},{17,9},{25,17},{2,26},{10... | collective-permute-start | bytes 442376 | tf_op jit(solution)/shard_map/ppermute | solution.py:509
  637.7 67.0 %collective-permute-start.49 = (bf16[24,3072]{1,0:T(8,128)(2,1)}, bf16[24,3072]{1,0:T(8,128)(2,1)}, u32[]{:S(2)}, u32[]{:S(2)}) collective-permute-start(bf16[24,3072]{1,0:T(8,128)(2,1)} %get-tuple-element.201), channel_id=1, source_target_pairs={{0,16},{8,24},{16,0},{24,8},{1,17},{9,25},{17,1},{25,9},{2,18},{10... | collective-permute-start | bytes 442376 | tf_op jit(solution)/shard_map/ppermute | solution.py:509
  637.7 71.5 %collective-permute-start.48 = (bf16[24,3072]{1,0:T(8,128)(2,1)}, bf16[24,3072]{1,0:T(8,128)(2,1)}, u32[]{:S(2)}, u32[]{:S(2)}) collective-permute-start(bf16[24,3072]{1,0:T(8,128)(2,1)} %get-tuple-element.202), channel_id=1, source_target_pairs={{0,8},{8,16},{16,24},{24,0},{1,9},{9,17},{17,25},{25,1},{2,10},{10... | collective-permute-start | bytes 442376 | tf_op jit(solution)/shard_map/ppermute | solution.py:509
  638.3 72.0 %collective-permute-start.47 = (bf16[24,3072]{1,0:T(8,128)(2,1)}, bf16[24,3072]{1,0:T(8,128)(2,1)S(1)}, u32[]{:S(2)}, u32[]{:S(2)}) collective-permute-start(bf16[24,3072]{1,0:T(8,128)(2,1)} %get-tuple-element.203), channel_id=1, source_target_pairs={{0,24},{8,0},{16,8},{24,16},{1,25},{9,1},{17,9},{25,17},{2,26},{10... | collective-permute-start | bytes 442376 | tf_op jit(solution)/shard_map/ppermute | solution.py:509
  640.9 69.4 %collective-permute-start.46 = (bf16[24,3072]{1,0:T(8,128)(2,1)}, bf16[24,3072]{1,0:T(8,128)(2,1)S(1)}, u32[]{:S(2)}, u32[]{:S(2)}) collective-permute-start(bf16[24,3072]{1,0:T(8,128)(2,1)} %get-tuple-element.204), channel_id=1, source_target_pairs={{0,16},{8,24},{16,0},{24,8},{1,17},{9,25},{17,1},{25,9},{2,18},{10... | collective-permute-start | bytes 442376 | tf_op jit(solution)/shard_map/ppermute | solution.py:509
  682.2 133.4 %all-gather.6.cloned.1.call-start = ((), (), s32[]{:S(2)}) async-start(), calls=%async_computation.3 | async-start | bytes 2621440 | tf_op jit(solution)/shard_map/all_gather | solution.py:849
  763.2 44.7 %collective-permute-start.61 = (bf16[4,960,384]{2,1,0:T(8,128)(2,1)}, bf16[4,960,384]{2,1,0:T(8,128)(2,1)}, u32[]{:S(2)}, u32[]{:S(2)}) collective-permute-start(bf16[4,960,384]{2,1,0:T(8,128)(2,1)} %shard_map.422), channel_id=1, source_target_pairs={{0,1},{1,0},{2,3},{3,2},{4,5},{5,4},{6,7},{7,6},{8,9},{9,8},{10,11... | collective-permute-start | bytes 8847368 | tf_op jit(solution)/shard_map/ppermute | solution.py:504
  766.5 116.5 %all-gather.8.cloned.1.call-start = ((), (), s32[]{:S(2)}) async-start(), calls=%async_computation.4 | async-start | bytes 1310720 | tf_op jit(solution)/shard_map/all_gather | solution.py:849
  794.8 49.2 %collective-permute-start.68 = (bf16[4,24,3072]{2,1,0:T(8,128)(2,1)S(1)}, bf16[4,24,3072]{2,1,0:T(8,128)(2,1)}, u32[]{:S(2)}, u32[]{:S(2)}) collective-permute-start(bf16[4,24,3072]{2,1,0:T(8,128)(2,1)S(1)} %fusion.46), channel_id=1, source_target_pairs={{0,4},{1,5},{2,6},{3,7},{4,0},{5,1},{6,2},{7,3},{8,12},{9,13},{10,... | collective-permute-start | bytes 1769480 | tf_op jit(solution)/shard_map/ppermute | solution.py:504
  825.0 47.2 %collective-permute-start.65 = (bf16[4,960,256]{2,1,0:T(8,128)(2,1)}, bf16[4,960,256]{2,1,0:T(8,128)(2,1)}, u32[]{:S(2)}, u32[]{:S(2)}) collective-permute-start(bf16[4,960,256]{2,1,0:T(8,128)(2,1)} %shard_map.424), channel_id=1, source_target_pairs={{0,1},{1,0},{2,3},{3,2},{4,5},{5,4},{6,7},{7,6},{8,9},{9,8},{10,11... | collective-permute-start | bytes 5898248 | tf_op jit(solution)/shard_map/ppermute | solution.py:504
  846.0 46.7 %collective-permute-start.74 = (bf16[24,3072]{1,0:T(8,128)(2,1)}, bf16[24,3072]{1,0:T(8,128)(2,1)}, u32[]{:S(2)}, u32[]{:S(2)}) collective-permute-start(bf16[24,3072]{1,0:T(8,128)(2,1)} %get-tuple-element.197), channel_id=1, source_target_pairs={{0,24},{8,0},{16,8},{24,16},{1,25},{9,1},{17,9},{25,17},{2,26},{10... | collective-permute-start | bytes 442376 | tf_op jit(solution)/shard_map/ppermute | solution.py:509
  852.5 40.2 %collective-permute-start.73 = (bf16[24,3072]{1,0:T(8,128)(2,1)}, bf16[24,3072]{1,0:T(8,128)(2,1)}, u32[]{:S(2)}, u32[]{:S(2)}) collective-permute-start(bf16[24,3072]{1,0:T(8,128)(2,1)} %get-tuple-element.198), channel_id=1, source_target_pairs={{0,16},{8,24},{16,0},{24,8},{1,17},{9,25},{17,1},{25,9},{2,18},{10... | collective-permute-start | bytes 442376 | tf_op jit(solution)/shard_map/ppermute | solution.py:509
  852.5 40.2 %collective-permute-start.72 = (bf16[24,3072]{1,0:T(8,128)(2,1)}, bf16[24,3072]{1,0:T(8,128)(2,1)}, u32[]{:S(2)}, u32[]{:S(2)}) collective-permute-start(bf16[24,3072]{1,0:T(8,128)(2,1)} %get-tuple-element.199), channel_id=1, source_target_pairs={{0,8},{8,16},{16,24},{24,0},{1,9},{9,17},{17,25},{25,1},{2,10},{10... | collective-permute-start | bytes 442376 | tf_op jit(solution)/shard_map/ppermute | solution.py:509
  894.5 63.5 %collective-permute-start.97 = (bf16[24,3072]{1,0:T(8,128)(2,1)}, bf16[24,3072]{1,0:T(8,128)(2,1)}, u32[]{:S(2)}, u32[]{:S(2)}) collective-permute-start(bf16[24,3072]{1,0:T(8,128)(2,1)} %get-tuple-element.165.refs_0_), channel_id=1, source_target_pairs={{0,4},{1,5},{2,6},{3,7},{4,0},{5,1},{6,2},{7,3},{8,12},{9,13},{10,... | collective-permute-start | bytes 442376 | tf_op jit(solution)/shard_map/ppermute | solution.py:504
  900.0 58.6 %collective-permute-start.99 = (bf16[24,3072]{1,0:T(8,128)(2,1)}, bf16[24,3072]{1,0:T(8,128)(2,1)}, u32[]{:S(2)}, u32[]{:S(2)}) collective-permute-start(bf16[24,3072]{1,0:T(8,128)(2,1)} %collective-permute-done.95.refs_2_), channel_id=1, source_target_pairs={{0,4},{1,5},{2,6},{3,7},{4,0},{5,1},{6,2},{7,3},{8,12},{9,13},{10,... | collective-permute-start | bytes 442376 | tf_op jit(solution)/shard_map/ppermute | solution.py:504
  982.9 49.4 %collective-permute-start.81 = (bf16[960,384]{1,0:T(8,128)(2,1)}, bf16[960,384]{1,0:T(8,128)(2,1)}, u32[]{:S(2)}, u32[]{:S(2)}) collective-permute-start(bf16[960,384]{1,0:T(8,128)(2,1)} %pad_maximum_fusion.2.rest_1_), channel_id=1, source_target_pairs={{0,1},{1,0},{2,3},{3,2},{4,5},{5,4},{6,7},{7,6},{8,9},{9,8},{10,11... | collective-permute-start | bytes 2211848 | tf_op jit(solution)/shard_map/ppermute | solution.py:504
  1032.3 43.6 %collective-permute-start.85 = (bf16[960,384]{1,0:T(8,128)(2,1)}, bf16[960,384]{1,0:T(8,128)(2,1)S(1)}, u32[]{:S(2)}, u32[]{:S(2)}) collective-permute-start(bf16[960,384]{1,0:T(8,128)(2,1)} %collective-permute-done.84.rest_3_), channel_id=1, source_target_pairs={{0,1},{1,0},{2,3},{3,2},{4,5},{5,4},{6,7},{7,6},{8,9},{9,8},{10,11... | collective-permute-start | bytes 2211848 | tf_op jit(solution)/shard_map/ppermute | solution.py:504
  1034.5 41.5 %collective-permute-start.87 = (bf16[960,384]{1,0:T(8,128)(2,1)}, bf16[960,384]{1,0:T(8,128)(2,1)S(1)}, u32[]{:S(2)}, u32[]{:S(2)}) collective-permute-start(bf16[960,384]{1,0:T(8,128)(2,1)} %collective-permute-done.86.rest_4_), channel_id=1, source_target_pairs={{0,1},{1,0},{2,3},{3,2},{4,5},{5,4},{6,7},{7,6},{8,9},{9,8},{10,11... | collective-permute-start | bytes 2211848 | tf_op jit(solution)/shard_map/ppermute | solution.py:504
  1037.8 38.2 %collective-permute-start.89 = (bf16[960,384]{1,0:T(8,128)(2,1)}, bf16[960,384]{1,0:T(8,128)(2,1)S(1)}, u32[]{:S(2)}, u32[]{:S(2)}) collective-permute-start(bf16[960,384]{1,0:T(8,128)(2,1)} %collective-permute-done.88.rest_5_), channel_id=1, source_target_pairs={{0,1},{1,0},{2,3},{3,2},{4,5},{5,4},{6,7},{7,6},{8,9},{9,8},{10,11... | collective-permute-start | bytes 2211848 | tf_op jit(solution)/shard_map/ppermute | solution.py:504
  (190 other events, 2907.0 us)
Sparse Core Ops, SparseCore 0:
  68.2 111.4 reduce-scatter.1
  682.4 70.0 all-gather.3
  766.6 45.8 all-gather.5
  844.1 38.7 all-gather.7

commit v5 on v4

--- a/solution.py
+++ b/solution.py
@@ -14,7 +14,7 @@
 LANES = 128
 ROWS = 256
 CHUNK = 256
-TILE = 240
+TILE = 480
 
 
 ln_eps = 1e-05
@@ -306,18 +306,25 @@
     )(starts, places, order, table)
 
 
-def table_grad_kernel(core_ref, starts_ref, places_ref, order_ref, dlogits_ref, chosen_ref, embed_ref, out_ref, rows, total):
+def table_grad_kernel(core_ref, starts_ref, places_ref, order_ref, dlogits_ref, chosen_ref, embed_ref, sent_ref, kept_ref, rows, total):
     step = pl.program_id(0)
-    count = embed_ref.shape[0]
-    block = total.shape[0] - 8
+    half = pl.num_programs(0) // 2
+    count, width = embed_ref.shape
+    block = kept_ref.shape[1]
+    tiles = width // LANES
 
     @pl.when(step == 0)
     def _():
         for start in range(0, count, CHUNK):
-            rows[start : start + CHUNK, :] = embed_ref[start : start + CHUNK, :].astype(jnp.float32)
-
-    total[:block, :] = jnp.dot(dlogits_ref[...], chosen_ref[...], preferred_element_type=jnp.float32)
-    chunk = 2 * step + core_ref[0]
+            some = embed_ref[start : start + CHUNK, :].astype(jnp.float32)
+            for j in range(tiles):
+                rows[pl.ds(start * 8 + j, CHUNK, stride=8), :] = some[:, j * LANES : (j + 1) * LANES]
+
+    product = jnp.dot(dlogits_ref[...], chosen_ref[...], preferred_element_type=jnp.float32)
+    for j in range(tiles):
+        total[pl.ds(j, block, stride=8), :] = product[:, j * LANES : (j + 1) * LANES]
+    side = jnp.where(step < half, 1 - core_ref[0], core_ref[0])
+    chunk = 2 * (step % half) + side
     base = chunk * block
     first, last = starts_ref[chunk], starts_ref[chunk + 1]
 
@@ -326,40 +333,62 @@
             i = first + turn * 8 + j
             at = jnp.minimum(i, count - 1)
             place = jnp.where(i < last, places_ref[at] - base, block)
-            total[pl.ds(place, 1), :] += rows[pl.ds(order_ref[at], 1), :]
+            to = pl.ds(pl.multiple_of(place * 8, 8), 8)
+            total[to, :] += rows[pl.ds(pl.multiple_of(order_ref[at] * 8, 8), 8), :]
         return carry
 
     lax.fori_loop(0, (last - first + 7) // 8, eight, 0)
-    out_ref[0] = total[:block, :].astype(out_ref.dtype)
-
-
-def table_grad_half(core, starts, places, order, dlogits, chosen, embed, block, dtype):
+    result = [total[pl.ds(j, block, stride=8), :] for j in range(tiles)]
+
+    @pl.when(step < half)
+    def _():
+        for j in range(tiles):
+            sent_ref[0, :, j * LANES : (j + 1) * LANES] = result[j].astype(sent_ref.dtype)
+
+    @pl.when(step >= half)
+    def _():
+        for j in range(tiles):
+            kept_ref[0, :, j * LANES : (j + 1) * LANES] = result[j]
+
+
+def table_grad_halves(core, starts, places, order, dlogits, chosen, embed, block, dtype):
     count, width = embed.shape
     picked = chosen.shape[0]
-    chunks = dlogits.shape[0] // block // 2
+    half = dlogits.shape[0] // block // 2
     fixed = lambda i, *_: (0, 0)
+
+    def chunk_at(i, core, *_):
+        return (2 * (i % half) + jnp.where(i < half, 1 - core[0], core[0]), 0)
+
     return pl.pallas_call(
         table_grad_kernel,
         grid_spec=pltpu.PrefetchScalarGridSpec(
             num_scalar_prefetch=4,
-            grid=(chunks,),
+            grid=(2 * half,),
             in_specs=[
-                pl.BlockSpec((block, picked), lambda i, core, *_: (2 * i + core[0], 0)),
+                pl.BlockSpec((block, picked), chunk_at),
                 pl.BlockSpec((picked, width), fixed),
                 pl.BlockSpec((count, width), fixed, pipeline_mode=pl.Buffered(1)),
             ],
-            out_specs=pl.BlockSpec((1, block, width), lambda i, *_: (i, 0, 0)),
-            scratch_shapes=[pltpu.VMEM((count, width), jnp.float32), pltpu.VMEM((block + 8, width), jnp.float32)],
-        ),
-        out_shape=jax.ShapeDtypeStruct((chunks, block, width), dtype),
+            out_specs=[
+                pl.BlockSpec((1, block, width), lambda i, *_: (jnp.minimum(i, half - 1), 0, 0)),
+                pl.BlockSpec((1, block, width), lambda i, *_: (jnp.maximum(i - half, 0), 0, 0)),
+            ],
+            scratch_shapes=[
+                pltpu.VMEM((count * 8, LANES), jnp.float32),
+                pltpu.VMEM((block * 8 + 8, LANES), jnp.float32),
+            ],
+        ),
+        out_shape=[
+            jax.ShapeDtypeStruct((half, block, width), dtype),
+            jax.ShapeDtypeStruct((half, block, width), jnp.float32),
+        ],
         compiler_params=pltpu.CompilerParams(vmem_limit_bytes=vmem),
         cost_estimate=pl.CostEstimate(
-            flops=2 * chunks * block * picked * width, bytes_accessed=8 * chunks * block * width, transcendentals=0
+            flops=4 * half * block * picked * width, bytes_accessed=16 * half * block * width, transcendentals=0
         ),
     )(core, starts, places, order, dlogits, chosen, embed)
 
-
-TILE = 240
 
 def update_kernel(parts, slots_ref, scalars_ref, *rest):
     pieces = rest[: 4 * parts]
@@ -450,50 +479,69 @@
     )(slots, *pieces)
 
 
-def columns_kernel(main, members_ref, slots_ref, *refs):
-    replicas = slots_ref.shape[0]
-    pieces, outs = refs[:replicas], refs[replicas + (len(refs) - replicas - (1 if main is None else 2)) :]
-    groups, rows = pieces[0].shape[0], pieces[0].shape[1]
+def columns_kernel(members_ref, slots_ref, own_ref, *refs):
+    pieces, out_ref = refs[:-1], refs[-1]
+    rows = own_ref.shape[0]
+
+    def at(offset):
+        return pl.ds(pl.multiple_of(members_ref[offset] * rows, rows), rows)
+
+    out_ref[at(0), :] = own_ref[...].astype(low_type)
     for place, piece in enumerate(pieces):
 
         @pl.when(pl.program_id(0) == place)
         def _(piece=piece):
-            for offset in range(groups):
-                member = members_ref[offset]
-                at = pl.ds(pl.multiple_of(member * rows, rows), rows)
-                if main is None:
-                    outs[0][at, :] = piece[offset]
-                else:
-                    outs[0][at, :] = piece[offset, :, :main]
-                    half = piece.shape[2] - main
-                    outs[1][member, 0, :, :half] = piece[offset, : rows // 2, main:]
-                    outs[1][member, 0, :, half:] = piece[offset, rows // 2 :, main:]
-
-
-def lay_columns(members, slots, pieces, main=None, after=()):
-    groups, rows, columns = pieces[0].shape
+            for offset in range(piece.shape[0]):
+                out_ref[at(offset + 1), :] = piece[offset]
+
+
+def lay_columns(members, slots, own, pieces):
+    others, rows, columns = pieces[0].shape
     replicas = len(pieces)
-    wide = columns if main is None else main
-    out_shape = [jax.ShapeDtypeStruct((groups * rows, replicas * wide), low_type)]
-    out_specs = [pl.BlockSpec((groups * rows, wide), lambda i, members, slots: (0, slots[i]))]
-    if main is not None:
-        out_shape.append(jax.ShapeDtypeStruct((groups, replicas, rows // 2, 2 * (columns - main)), low_type))
-        out_specs.append(
-            pl.BlockSpec((groups, 1, rows // 2, 2 * (columns - main)), lambda i, members, slots: (0, slots[i], 0, 0))
-        )
+    whole = jax.ShapeDtypeStruct(((others + 1) * rows, replicas * columns), low_type)
     return pl.pallas_call(
-        functools.partial(columns_kernel, main),
+        columns_kernel,
         grid_spec=pltpu.PrefetchScalarGridSpec(
             num_scalar_prefetch=2,
             grid=(replicas,),
-            in_specs=[pl.BlockSpec(pieces[0].shape, lambda i, *_: (0, 0, 0), pipeline_mode=pl.Buffered(1))] * replicas
-            + [pl.BlockSpec(memory_space=pl.ANY)] * len(after),
-            out_specs=out_specs,
-        ),
-        out_shape=out_shape,
+            in_specs=[pl.BlockSpec((rows, columns), lambda i, members, slots: (0, slots[i]))]
+            + [pl.BlockSpec(pieces[0].shape, lambda i, *_: (0, 0, 0), pipeline_mode=pl.Buffered(1))] * replicas,
+            out_specs=pl.BlockSpec(((others + 1) * rows, columns), lambda i, members, slots: (0, slots[i])),
+        ),
+        out_shape=whole,
         compiler_params=pltpu.CompilerParams(vmem_limit_bytes=vmem),
-        cost_estimate=pl.CostEstimate(flops=0, bytes_accessed=4 * replicas * pieces[0].size, transcendentals=0),
-    )(members, slots, *pieces, *after)
+        cost_estimate=pl.CostEstimate(flops=0, bytes_accessed=4 * whole.size, transcendentals=0),
+    )(members, slots, own, *pieces)
+
+
+def rows_kernel(members_ref, slots_ref, own_ref, *refs):
+    pieces, out_ref = refs[:-1], refs[-1]
+    out_ref[members_ref[0], 0] = own_ref[0].astype(low_type)
+    for place, piece in enumerate(pieces):
+
+        @pl.when(pl.program_id(0) == place)
+        def _(piece=piece):
+            for offset in range(piece.shape[0]):
+                out_ref[members_ref[offset + 1], 0] = piece[offset]
+
+
+def lay_rows(members, slots, own, pieces):
+    others, rows, columns = pieces[0].shape
+    replicas = len(pieces)
+    whole = jax.ShapeDtypeStruct((others + 1, replicas, rows, columns), low_type)
+    return pl.pallas_call(
+        rows_kernel,
+        grid_spec=pltpu.PrefetchScalarGridSpec(
+            num_scalar_prefetch=2,
+            grid=(replicas,),
+            in_specs=[pl.BlockSpec((1, rows, columns), lambda i, members, slots: (slots[i], 0, 0))]
+            + [pl.BlockSpec(pieces[0].shape, lambda i, *_: (0, 0, 0), pipeline_mode=pl.Buffered(1))] * replicas,
+            out_specs=pl.BlockSpec((others + 1, 1, rows, columns), lambda i, members, slots: (0, slots[i], 0, 0)),
+        ),
+        out_shape=whole,
+        compiler_params=pltpu.CompilerParams(vmem_limit_bytes=vmem),
+        cost_estimate=pl.CostEstimate(flops=0, bytes_accessed=4 * whole.size, transcendentals=0),
+    )(members, slots, own.reshape(replicas, rows, columns), *pieces).reshape(-1, columns)
 
 
 tie = lax.optimization_barrier
@@ -630,8 +678,7 @@
 
 
 def fetch(own):
-    groups = lax.axis_size("grp")
-    return jnp.stack([own] + [turn(own, offset) for offset in range(1, groups)])
+    return jnp.stack([turn(own, offset) for offset in range(1, lax.axis_size("grp"))])
 
 
 def cut(value, axis):
@@ -726,9 +773,8 @@
     near_shard = jnp.concatenate([w_qkv, w_out], axis=1)
     if quick:
         near_part = fetch(cut(near_shard, 1).astype(low_type))
-        down_part = cut(w_down, 0)
-        down_part = jnp.concatenate([down_part[:, : width // 2], down_part[:, width // 2 :]], axis=0)
-        far_part = fetch(jnp.concatenate([cut(w_gu, 1), down_part], axis=1).astype(low_type))
+        gu_part = fetch(cut(w_gu, 1).astype(low_type))
+        down_part = fetch(cut(w_down, 0).astype(low_type))
 
     local_ids = group_ids - member * vocab_rows
     owned = (local_ids >= 0) & (local_ids < vocab_rows)
@@ -737,24 +783,25 @@
     )
     bounds = jnp.arange(replicas + 1, dtype=jnp.int32) * block
     starts = jnp.sum((places[None, :] < bounds[:, None]).astype(jnp.int32), axis=1)
+    if quick:
+        places, near_part = tie((places, near_part))
     found = lookup(starts, places, order, table)
     if quick:
-        found, near_part, far_part = lax.optimization_barrier((found, near_part, far_part))
+        found, gu_part, down_part = tie((found, gu_part, down_part))
     embed = lax.psum_scatter(found, "grp", scatter_dimension=0, tiled=True)
     late_table, _ = lax.optimization_barrier((table, found))
     table_low = jnp.pad(late_table.astype(low_type), ((0, padded - vocab_rows), (0, 0)))
 
     if quick:
-        near_have = spread(near_part, [2, 4, 1])
-        far_have = spread(far_part, [4, 2, 1])
-        (near,) = lay_columns(members_of(), slots_of(), [near_have[place] for place in range(replicas)])
-        w_gu_low, w_down_low = lay_columns(
-            members_of(),
-            slots_of(),
-            [far_have[place] for place in range(replicas)],
-            w_gu.shape[1] // replicas,
-        )
-        w_down_low = w_down_low.reshape(-1, width)
+        members, slots = members_of(), slots_of()
+
+        def shared(part, order):
+            have = spread(part, order)
+            return [have[place] for place in range(replicas)]
+
+        near = lay_columns(members, slots, near_shard, shared(near_part, [4, 2, 1]))
+        w_gu_low = lay_columns(members, slots, w_gu, shared(gu_part, [2, 4, 1]))
+        w_down_low = lay_rows(members, slots, w_down, shared(down_part, [4, 2, 1]))
         embed, near, w_gu_low, w_down_low, table_low = tie((embed, near, w_gu_low, w_down_low, table_low))
     else:
         near = lax.all_gather(near_shard.astype(low_type), "grp", tiled=True)
@@ -840,21 +887,19 @@
     _, pull = jax.vjp(layer_norm, embed.astype(jnp.float32), norms[0], norms[1])
     embed_grad, gain_one, shift_one = pull(first_grad)
     norm_grad = jnp.stack([gain_one, shift_one, gain_two, shift_two, gain_three, shift_three])
-    cuts_at = (0, width // 2, width // 6 * 5, width)
-    spans = list(zip(cuts_at[:-1], cuts_at[1:]))
+    wide = width // 3
+    spans = [(part * wide, (part + 1) * wide) for part in range(3)]
     embed_low = embed_grad.astype(low_type)
-    group_embeds = []
-    for begin, end in spans:
-        piece, _ = tie((embed_low[:, begin:end], group_embeds[-1:]))
-        group_embeds.append(lax.all_gather(piece, "grp", axis=0, tiled=True))
+    join_grad = contract(first_low, joined_grad, 0, 0)
+    late_embed, join_grad = tie((embed_low, join_grad))
+    join_grad = jnp.concatenate([join_grad, contract(mixed_low, attn_low, 0, 0)], axis=1)
+    last_embed, join_grad = tie((late_embed, join_grad))
+    group_embeds = [
+        lax.all_gather(piece[:, begin:end], "grp", axis=0, tiled=True)
+        for piece, (begin, end) in zip((embed_low, late_embed, last_embed), spans)
+    ]
     join = Fold(1, (2, 4))
-    join.cores(
-        gradient_chunks(
-            jnp.concatenate(
-                [contract(first_low, joined_grad, 0, 0), contract(mixed_low, attn_low, 0, 0)], axis=1
-            )
-        )
-    )
+    join.cores(gradient_chunks(join_grad))
     sent = join.plane(True)
     gu_share = jnp.concatenate([gate.total(), up.total()], axis=1)
     down_share = down.total()
@@ -870,9 +915,9 @@
     for part, (begin, end) in enumerate(spans):
         head = heads[part]
         if part == 1:
-            group_embeds[1], _ = tie((group_embeds[1], heads[0].plane(True) + join.plane(False)))
+            group_embeds[1], _ = tie((group_embeds[1], heads[0].plane(True)))
         if part == 2:
-            sent = heads[1].plane(True) + heads[0].plane(False) + join.members()
+            sent = heads[1].plane(True) + heads[0].plane(False) + join.plane(False)
             group_embeds[2], _ = tie((group_embeds[2], sent))
         half_args = (
             starts,
@@ -883,16 +928,16 @@
             group_embeds[part],
             block,
         )
+        sent, kept = table_grad_halves(core[None], *half_args, low_type if quick else jnp.float32)
         if quick:
-            sent = table_grad_half((1 - core)[None], *half_args, low_type)
-            kept = table_grad_half(core[None], *half_args, jnp.float32)
             head.from_cores(kept, sent)
         else:
-            both = [table_grad_half(jnp.full((1,), j, jnp.int32), *half_args, jnp.float32) for j in range(2)]
+            both = [jnp.where(core == j, kept, sent) for j in range(2)]
             head.cores(jnp.stack(both, axis=1).reshape(replicas, block, end - begin))
     heads[2].plane(True)
     heads[1].plane(False)
     heads[2].plane(False)
+    join.members()
     table_parts = [head.sum() for head in heads]
     join_share = join.total()
 

time: 1120 us -> 1090 us (0.973)
  waiting for transfers between devices: 266 us -> 205 us
  starting transfers between devices: 124 us -> 158 us
    ppermute x69 -> x76, waiting for transfers between devices: 198 us -> 156 us  [flip(): return lax.ppermute(value, 'rep', [(i, i ^ bit) for i in range(size)])]
    ppermute x69 -> x76, starting transfers between devices: 80.9 us -> 100 us  [flip(): return lax.ppermute(value, 'rep', [(i, i ^ bit) for i in range(size)])]
    ppermute x30 -> x33, starting transfers between devices: 39.3 us -> 55.2 us  [turn(): lax.ppermute(value, 'grp', [(i, (i + offset) % size) for i in range(size)])]
    ppermute x30 -> x33, waiting for transfers between devices: 54.4 us -> 41.7 us  [turn(): lax.ppermute(value, 'grp', [(i, (i + offset) % size) for i in range(size)])]
    unnamed x242 -> x303, local copies, waits for them, and re-layouts: 35.7 us -> 33.8 us
    pallas_call x8 -> x6, Pallas kernels: 78.1 us -> 76.5 us  [the longest x3 49.4 us: table_grad_halves(): pl.pallas_call(table_grad_kernel, grid_spec=pltpu.PrefetchScalarGridSpec(...]
  transfers between devices with their start and end apart: 105 -> 115, of which waited for: 30 -> 31; matrix products, arithmetic and copies ran while one was open for 24% -> 25% of each run, Pallas kernels for 16% -> 16%
where the time goes in v5:
time: 1090 us; the launch traced here: 1070 us
  Pallas kernels  263 us (24%)
  waiting for transfers between devices  205 us (19%)
  other arithmetic  181 us (17%)
  starting transfers between devices  158 us (14%)
  matrix products  139 us (13%)
  local copies, waits for them, and re-layouts  95.4 us (9%)
  between operations  32.2 us (3%)
    ppermute x76, waiting for transfers between devices, flip(): return lax.ppermute(value, 'rep', [(i, i ^ bit) for i in range(size)])  156 us
    dot_general x11, matrix products, contract(): lax.dot_general(left, right, (((left_dim,), (right_dim,)), ((), ())), pre...  113 us
    ppermute x76, starting transfers between devices, flip(): return lax.ppermute(value, 'rep', [(i, i ^ bit) for i in range(size)])  100 us
    pallas_call x3, Pallas kernels, attend_back(): pl.pallas_call(functools.partial(attend_back_kernel, first_pair), grid_sp...  65.7 us
    ppermute x33, starting transfers between devices, turn(): lax.ppermute(value, 'grp', [(i, (i + offset) % size) for i in range(size)])  55.2 us
    pallas_call x3, Pallas kernels, table_grad_halves(): pl.pallas_call(table_grad_kernel, grid_spec=pltpu.PrefetchScalarGridSpec(...  49.4 us
    pallas_call x1, Pallas kernels, attend(): pl.pallas_call(attend_kernel, grid_spec=pltpu.PrefetchScalarGridSpec(num_...  47.7 us
    ppermute x33, waiting for transfers between devices, turn(): lax.ppermute(value, 'grp', [(i, (i + offset) % size) for i in range(size)])  41.7 us
  transfers between devices with their start and end apart: 115, of which 31 were waited for; matrix products, arithmetic and copies ran while one was open for 25% of the time, Pallas kernels for 16%

profile of v5, /device:TPU:1, one launch (start us, length us, event | category | flops | bytes accessed | tf_op | source)
XLA Modules:
  0.0 1073.5 jit_solution(13770136455691096304)
XLA Ops:
  32.9 15.6 %collective-permute-start.10 = (bf16[96,768]{1,0:T(8,128)(2,1)}, bf16[96,768]{1,0:T(8,128)(2,1)}, u32[]{:S(2)}, u32[]{:S(2)}) collective-permute-start(bf16[96,768]{1,0:T(8,128)(2,1)} %dynamic-slice_convert_fusion.23), channel_id=1, source_target_pairs={{0,16},{8,24},{16,0},{24,8},{1,17},{9,25},{17,1},{25,9},{2,18},{10... | collective-permute-start | bytes 442376 | tf_op jit(solution)/shard_map/ppermute | solution.py:557
  51.0 16.6 %shard_map.413 = bf16[4096,768]{1,0:T(8,128)(2,1)} custom-call(s32[9]{0:T(128)} %convert_reduce_fusion.1.starts_ref, s32[4096]{0:T(1024)} %copy-done.83, s32[4096]{0:T(1024)} %get-tuple-element.92.order_ref, f32[7632,768]{1,0:T(8,128)} %rest_8_.3), custom_call_target="tpu_custom_call" | custom-call | bytes 70336512 | tf_op jit(solution)/shard_map/pallas_call | solution.py:294
  70.0 14.6 %collective-permute-start.12 = (bf16[3,192,384]{2,1,0:T(8,128)(2,1)S(1)}, bf16[3,192,384]{2,1,0:T(8,128)(2,1)S(1)}, u32[]{:S(2)}, u32[]{:S(2)}) collective-permute-start(bf16[3,192,384]{2,1,0:T(8,128)(2,1)S(1)} %pad_maximum_fusion.6.refs_0_), channel_id=1, source_target_pairs={{0,1},{1,0},{2,3},{3,2},{4,5},{5,4},{6,7},{7,6},{8,9},{9,8},{10,11... | collective-permute-start | bytes 1327112 | tf_op jit(solution)/shard_map/ppermute | solution.py:552
  99.2 25.7 %collective-permute-done.27.refs_2_ = bf16[3,96,768]{2,1,0:T(8,128)(2,1)S(1)} collective-permute-done((bf16[3,96,768]{2,1,0:T(8,128)(2,1)S(1)}, bf16[3,96,768]{2,1,0:T(8,128)(2,1)S(1)}, u32[]{:S(2)}, u32[]{:S(2)}) %collective-permute-start.27) | collective-permute-done | bytes 442400 | tf_op jit(solution)/shard_map/ppermute | solution.py:552
  150.3 15.0 %collective-permute-done.24.refs_6_ = bf16[3,192,768]{2,1,0:T(8,128)(2,1)} collective-permute-done((bf16[3,192,768]{2,1,0:T(8,128)(2,1)S(1)}, bf16[3,192,768]{2,1,0:T(8,128)(2,1)}, u32[]{:S(2)}, u32[]{:S(2)}) %collective-permute-start.24) | collective-permute-done | bytes 884768 | tf_op jit(solution)/shard_map/ppermute | solution.py:552
  175.6 9.2 convert_element_type.372
  206.8 10.8 %shard_map.415 = bf16[768,6144]{1,0:T(8,128)(2,1)} custom-call(s32[4]{0:T(128)} %and_select_fusion.members_ref, s32[8]{0:T(128)} %iota_xor_fusion.slots_ref, f32[192,6144]{1,0:T(8,128)} %own_ref.1, bf16[3,192,768]{2,1,0:T(8,128)(2,1)} %copy-done.31, bf16[3,192,768]{2,1,0:T(8,128)(2,1)} %collective-permute-done.19.refs_1_, bf16[3,192,768]{2,1,0:T(8,128)(2,1)} %copy-done.50, ...), custom_call_target="tpu_custom_call" | custom-call | bytes 18874368 | tf_op jit(solution)/shard_map/pallas_call | solution.py:502
  219.3 9.2 shard_map.417
  228.5 47.7 %shard_map.418 = (bf16[1024,768]{1,0:T(8,128)(2,1)}, f32[6,2,1024]{2,1,0:T(2,128)}) custom-call(s32[1]{0:T(128)S(6)} %copy.139.length_ref, bf16[1024,768]{1,0:T(8,128)(2,1)} %get-tuple-element.103.q_ref, bf16[1024,768]{1,0:T(8,128)(2,1)} %get-tuple-element.104.k_ref, bf16[1024,768]{1,0:T(8,128)(2,1)} %get-tuple-element.105.v_ref), custom_call_target="tpu_custom_call" | custom-call | flops 12884901888 | bytes 6291456 | tf_op jit(solution)/shard_map/pallas_call | solution.py:138
  280.0 17.6 %fusion.116 = f32[1024,6144]{1,0:T(8,128)} fusion(bf16[768,6144]{1,0:T(8,128)(2,1)} %shard_map.415, f32[1024,768]{1,0:T(8,128)S(1)} %get-tuple-element.255, f32[768]{0:T(1024)S(1)} %get-tuple-element.171, f32[768]{0:T(1024)S(1)} %get-tuple-element.172, f32[1024]{0:T(1024)S(1)} %fusion.86, f32[1024]{0:T(1024)S(1)} %broadcast_multiply_fusion.1), kind=kOutput, calls=%fused_computation.324 | convolution fusion | flops 9667608576 | bytes 37763072 | tf_op jit(solution)/shard_map/dot_general | solution.py:822
  297.6 10.1 multiply_convert_fusion.1
  340.9 10.8 %select_reduce_fusion.1 = (f32[512]{0:T(512)S(1)}, f32[7680,512]{1,0:T(8,128)S(1)}) fusion(pred[7680]{0:T(1024)(128)(4,1)S(1)} %iota_compare_fusion.1, bf16[7680,768]{1,0:T(8,128)(2,1)} %pad.14, bf16[512,768]{1,0:T(8,128)(2,1)} %bitcast.21), kind=kOutput, calls=%fused_computation.9 | convolution fusion | flops 6047661568 | bytes 28321280 | tf_op jit(solution)/shard_map/dot_general | solution.py:696
  374.2 11.8 %fusion.118 = f32[512,768]{1,0:T(8,128)S(1)} fusion(bf16[7680,512]{1,0:T(8,128)(2,1)S(1)} %multiply_convert_fusion.dlogits_ref, bf16[7680,768]{1,0:T(8,128)(2,1)} %pad.14), kind=kOutput, calls=%fused_computation.325 | convolution fusion | flops 6039797760 | bytes 21233664 | tf_op jit(solution)/shard_map/dot_general | solution.py:696
  395.6 22.5 %collective-permute-done.43 = f32[128,768]{1,0:T(8,128)S(1)} collective-permute-done((f32[128,768]{1,0:T(8,128)S(1)}, f32[128,768]{1,0:T(8,128)S(1)}, u32[]{:S(2)}, u32[]{:S(2)}) %collective-permute-start.43) | collective-permute-done | bytes 393248 | tf_op jit(solution)/shard_map/ppermute | solution.py:557
  447.7 23.8 %fusion.30 = (f32[1024,3072]{1,0:T(8,128)}, f32[1024,3072]{1,0:T(8,128)}) fusion(f32[1024,6144]{1,0:T(8,128)} %fusion.116, bf16[3072,768]{1,0:T(8,128)(2,1)} %bitcast.316, f32[1024,768]{1,0:T(8,128)} %copy-done.35, f32[1024]{0:T(1024)S(1)} %negate_multiply_fusion.2), kind=kOutput, calls=%fused_computation.94 | convolution fusion | flops 4871159808 | bytes 58200064 | tf_op jit(solution)/shard_map/dot_general | solution.py:696
  471.5 9.4 add_convert_fusion
  502.9 13.0 %collective-permute-done.48 = bf16[4,2,96,768]{3,2,1,0:T(8,128)(2,1)} collective-permute-done((bf16[4,2,96,768]{3,2,1,0:T(8,128)(2,1)S(1)}, bf16[4,2,96,768]{3,2,1,0:T(8,128)(2,1)}, u32[]{:S(2)}, u32[]{:S(2)}) %collective-permute-start.48) | collective-permute-done | bytes 1179680 | tf_op jit(solution)/shard_map/ppermute | solution.py:552
  535.8 16.6 %add_add_fusion.4 = f32[1024,768]{1,0:T(8,128)} fusion(f32[1024,768]{1,0:T(8,128)S(1)} %copy-done.36, bf16[1024,6144]{1,0:T(8,128)(2,1)} %copy-done.3, bf16[768,6144]{1,0:T(8,128)(2,1)} %shard_map.415, f32[1024]{0:T(1024)S(1)} %negate_multiply_fusion.2), kind=kOutput, calls=%fused_computation.61 | convolution fusion | flops 9665249280 | bytes 28315648 | tf_op jit(solution)/shard_map/dot_general | solution.py:696
  574.5 21.9 %shard_map.419 = (bf16[1024,256]{1,0:T(8,128)(2,1)}, bf16[1024,256]{1,0:T(8,128)(2,1)}, bf16[1024,256]{1,0:T(8,128)(2,1)}) custom-call(s32[1]{0:T(128)S(6)} %copy.139.length_ref, bf16[1024,768]{1,0:T(8,128)(2,1)} %get-tuple-element.103.q_ref, bf16[1024,768]{1,0:T(8,128)(2,1)} %get-tuple-element.104.k_ref, bf16[1024,768]{1,0:T(8,128)(2,1)} %get-tuple-element.105.v_ref, ...), custom_call_target="tpu_custom_call" | custom-call | flops 10737418240 | bytes 4194304 | tf_op jit(solution)/shard_map/pallas_call | solution.py:223
  607.6 21.8 %shard_map.420 = (bf16[1024,256]{1,0:T(8,128)(2,1)}, bf16[1024,256]{1,0:T(8,128)(2,1)}, bf16[1024,256]{1,0:T(8,128)(2,1)}) custom-call(s32[1]{0:T(128)S(6)} %copy.139.length_ref, bf16[1024,768]{1,0:T(8,128)(2,1)} %get-tuple-element.103.q_ref, bf16[1024,768]{1,0:T(8,128)(2,1)} %get-tuple-element.104.k_ref, bf16[1024,768]{1,0:T(8,128)(2,1)} %get-tuple-element.105.v_ref, ...), custom_call_target="tpu_custom_call" | custom-call | flops 10737418240 | bytes 4194304 | tf_op jit(solution)/shard_map/pallas_call | solution.py:223
  639.6 22.0 %shard_map.421 = (bf16[1024,256]{1,0:T(8,128)(2,1)}, bf16[1024,256]{1,0:T(8,128)(2,1)}, bf16[1024,256]{1,0:T(8,128)(2,1)}) custom-call(s32[1]{0:T(128)S(6)} %copy.139.length_ref, bf16[1024,768]{1,0:T(8,128)(2,1)} %get-tuple-element.103.q_ref, bf16[1024,768]{1,0:T(8,128)(2,1)} %get-tuple-element.104.k_ref, bf16[1024,768]{1,0:T(8,128)(2,1)} %get-tuple-element.105.v_ref, ...), custom_call_target="tpu_custom_call" | custom-call | flops 10737418240 | bytes 4194304 | tf_op jit(solution)/shard_map/pallas_call | solution.py:223
  680.3 9.7 fusion.119
  690.0 9.2 pad_maximum_fusion
  746.5 16.5 %shard_map.422 = (bf16[4,960,256]{2,1,0:T(8,128)(2,1)}, f32[4,960,256]{2,1,0:T(8,128)}) custom-call(s32[1]{0:T(128)} %bitcast.78.core_ref, s32[9]{0:T(128)} %convert_reduce_fusion.1.starts_ref, s32[4096]{0:T(1024)} %copy-done.83, s32[4096]{0:T(1024)} %get-tuple-element.92.order_ref, bf16[7680,512]{1,0:T(8,128)(2,1)} %copy-done, ...), custom_call_target="tpu_custom_call" | custom-call | flops 2013265920 | bytes 15728640 | tf_op jit(solution)/shard_map/pallas_call | solution.py:363
  778.8 16.5 %shard_map.423 = (bf16[4,960,256]{2,1,0:T(8,128)(2,1)}, f32[4,960,256]{2,1,0:T(8,128)}) custom-call(s32[1]{0:T(128)} %bitcast.78.core_ref, s32[9]{0:T(128)} %convert_reduce_fusion.1.starts_ref, s32[4096]{0:T(1024)} %copy-done.83, s32[4096]{0:T(1024)} %get-tuple-element.92.order_ref, bf16[7680,512]{1,0:T(8,128)(2,1)} %copy-done, ...), custom_call_target="tpu_custom_call" | custom-call | flops 2013265920 | bytes 15728640 | tf_op jit(solution)/shard_map/pallas_call | solution.py:363
  799.3 20.1 %collective-permute-done.72 = bf16[2,960,256]{2,1,0:T(8,128)(2,1)S(1)} collective-permute-done((bf16[2,960,256]{2,1,0:T(8,128)(2,1)}, bf16[2,960,256]{2,1,0:T(8,128)(2,1)S(1)}, u32[]{:S(2)}, u32[]{:S(2)}) %collective-permute-start.72) | collective-permute-done | bytes 983072 | tf_op jit(solution)/shard_map/ppermute | solution.py:552
  825.5 16.4 %shard_map.424 = (bf16[4,960,256]{2,1,0:T(8,128)(2,1)}, f32[4,960,256]{2,1,0:T(8,128)}) custom-call(s32[1]{0:T(128)} %bitcast.78.core_ref, s32[9]{0:T(128)} %convert_reduce_fusion.1.starts_ref, s32[4096]{0:T(1024)} %copy-done.83, s32[4096]{0:T(1024)} %get-tuple-element.92.order_ref, bf16[7680,512]{1,0:T(8,128)(2,1)} %copy-done, ...), custom_call_target="tpu_custom_call" | custom-call | flops 2013265920 | bytes 15728640 | tf_op jit(solution)/shard_map/pallas_call | solution.py:363
  881.2 13.8 %collective-permute-done.105.refs_2_ = bf16[24,3072]{1,0:T(8,128)(2,1)} collective-permute-done((bf16[24,3072]{1,0:T(8,128)(2,1)}, bf16[24,3072]{1,0:T(8,128)(2,1)}, u32[]{:S(2)}, u32[]{:S(2)}) %collective-permute-start.105) | collective-permute-done | bytes 147488 | tf_op jit(solution)/shard_map/ppermute | solution.py:552
  899.1 9.0 collective-permute-done.73
  909.2 9.4 collective-permute-done.80
  1024.6 17.9 %shard_map.428 = (f32[7632,768]{1,0:T(8,128)}, f32[7632,768]{1,0:T(8,128)}, f32[16,1,480]{2,1,0:T(1,128)}) custom-call(s32[4]{0:T(128)} %pad_add_fusion.2.slots_ref, f32[2]{0:T(128)} %pad_maximum_fusion.10.scalars_ref, bf16[960,256]{1,0:T(8,128)(2,1)} %get-tuple-element.146.rest_0_, ...), custom_call_target="tpu_custom_call", output_to_operand_aliasing={{0}: (13, {}), {1}: (14, {}), {2}: (15, {})} | custom-call | flops 29491200 | bytes 41287680 | tf_op jit(solution)/shard_map/pallas_call | solution.py:427
  1044.8 18.2 %shard_map.429 = (f32[7632,768]{1,0:T(8,128)}, f32[7632,768]{1,0:T(8,128)}, f32[16,1,480]{2,1,0:T(1,128)}) custom-call(s32[4]{0:T(128)} %pad_add_fusion.1.slots_ref, f32[2]{0:T(128)} %pad_maximum_fusion.10.scalars_ref, bf16[960,256]{1,0:T(8,128)(2,1)} %collective-permute-done.90.rest_0_, ...), custom_call_target="tpu_custom_call", output_to_operand_aliasing={{0}: (13, {}), {1}: (14, {}), {2}: (15, {})} | custom-call | flops 29491200 | bytes 41287680 | tf_op jit(solution)/shard_map/pallas_call | solution.py:427
  (739 shorter events, 519.1 us)
Async XLA Ops:
  7.2 210.4 %reduce-scatter.2.cloned.1.call-start = ((), (), s32[]{:S(2)}) async-start(), calls=%async_computation.1 | async-start | bytes 7864320 | tf_op jit(solution)/shard_map/reduce_scatter | solution.py:791
  21.9 46.7 %collective-permute-start.8 = (bf16[192,768]{1,0:T(8,128)(2,1)}, bf16[192,768]{1,0:T(8,128)(2,1)S(1)}, u32[]{:S(2)}, u32[]{:S(2)}) collective-permute-start(bf16[192,768]{1,0:T(8,128)(2,1)} %dynamic-slice_convert_fusion.10), channel_id=1, source_target_pairs={{0,24},{8,0},{16,8},{24,16},{1,25},{9,1},{17,9},{25,17},{2,26},{10... | collective-permute-start | bytes 884744 | tf_op jit(solution)/shard_map/ppermute | solution.py:557
  31.4 37.3 %collective-permute-start.7 = (bf16[192,768]{1,0:T(8,128)(2,1)}, bf16[192,768]{1,0:T(8,128)(2,1)S(1)}, u32[]{:S(2)}, u32[]{:S(2)}) collective-permute-start(bf16[192,768]{1,0:T(8,128)(2,1)} %dynamic-slice_convert_fusion.10), channel_id=1, source_target_pairs={{0,16},{8,24},{16,0},{24,8},{1,17},{9,25},{17,1},{25,9},{2,18},{10... | collective-permute-start | bytes 884744 | tf_op jit(solution)/shard_map/ppermute | solution.py:557
  31.5 37.2 %collective-permute-start.6 = (bf16[192,768]{1,0:T(8,128)(2,1)}, bf16[192,768]{1,0:T(8,128)(2,1)}, u32[]{:S(2)}, u32[]{:S(2)}) collective-permute-start(bf16[192,768]{1,0:T(8,128)(2,1)} %dynamic-slice_convert_fusion.10), channel_id=1, source_target_pairs={{0,8},{8,16},{16,24},{24,0},{1,9},{9,17},{17,25},{25,1},{2,10},{10... | collective-permute-start | bytes 884744 | tf_op jit(solution)/shard_map/ppermute | solution.py:557
  32.9 34.8 %collective-permute-start.10 = (bf16[96,768]{1,0:T(8,128)(2,1)}, bf16[96,768]{1,0:T(8,128)(2,1)}, u32[]{:S(2)}, u32[]{:S(2)}) collective-permute-start(bf16[96,768]{1,0:T(8,128)(2,1)} %dynamic-slice_convert_fusion.23), channel_id=1, source_target_pairs={{0,16},{8,24},{16,0},{24,8},{1,17},{9,25},{17,1},{25,9},{2,18},{10... | collective-permute-start | bytes 442376 | tf_op jit(solution)/shard_map/ppermute | solution.py:557
  70.0 676.5 %all-gather.4.cloned.1.call-start = ((), (), s32[]{:S(2)}) async-start(), calls=%async_computation.2 | async-start | bytes 2621440 | tf_op jit(solution)/shard_map/all_gather | solution.py:898
  85.8 41.7 %collective-permute-start.20 = (bf16[3,192,768]{2,1,0:T(8,128)(2,1)S(1)}, bf16[3,192,768]{2,1,0:T(8,128)(2,1)S(1)}, u32[]{:S(2)}, u32[]{:S(2)}) collective-permute-start(bf16[3,192,768]{2,1,0:T(8,128)(2,1)S(1)} %pad_maximum_fusion.2.refs_0_), channel_id=1, source_target_pairs={{0,2},{1,3},{2,0},{3,1},{4,6},{5,7},{6,4},{7,5},{8,10},{9,11},{10,... | collective-permute-start | bytes 2654216 | tf_op jit(solution)/shard_map/ppermute | solution.py:552
  88.2 36.7 %collective-permute-start.27 = (bf16[3,96,768]{2,1,0:T(8,128)(2,1)S(1)}, bf16[3,96,768]{2,1,0:T(8,128)(2,1)S(1)}, u32[]{:S(2)}, u32[]{:S(2)}) collective-permute-start(bf16[3,96,768]{2,1,0:T(8,128)(2,1)S(1)} %pad_maximum_fusion.7.refs_0_), channel_id=1, source_target_pairs={{0,2},{1,3},{2,0},{3,1},{4,6},{5,7},{6,4},{7,5},{8,10},{9,11},{10,... | collective-permute-start | bytes 1327112 | tf_op jit(solution)/shard_map/ppermute | solution.py:552
  127.5 37.8 %collective-permute-start.24 = (bf16[3,192,768]{2,1,0:T(8,128)(2,1)S(1)}, bf16[3,192,768]{2,1,0:T(8,128)(2,1)}, u32[]{:S(2)}, u32[]{:S(2)}) collective-permute-start(bf16[3,192,768]{2,1,0:T(8,128)(2,1)S(1)} %collective-permute-done.20.refs_2_), channel_id=1, source_target_pairs={{0,4},{1,5},{2,6},{3,7},{4,0},{5,1},{6,2},{7,3},{8,12},{9,13},{10,... | collective-permute-start | bytes 2654216 | tf_op jit(solution)/shard_map/ppermute | solution.py:552
  146.3 60.4 %collective-permute-start.19 = (bf16[3,192,768]{2,1,0:T(8,128)(2,1)S(1)}, bf16[3,192,768]{2,1,0:T(8,128)(2,1)}, u32[]{:S(2)}, u32[]{:S(2)}) collective-permute-start(bf16[3,192,768]{2,1,0:T(8,128)(2,1)S(1)} %pad_maximum_fusion.2.refs_0_), channel_id=1, source_target_pairs={{0,1},{1,0},{2,3},{3,2},{4,5},{5,4},{6,7},{7,6},{8,9},{9,8},{10,11... | collective-permute-start | bytes 2654216 | tf_op jit(solution)/shard_map/ppermute | solution.py:552
  149.8 57.0 %collective-permute-start.21 = (bf16[3,192,768]{2,1,0:T(8,128)(2,1)S(1)}, bf16[3,192,768]{2,1,0:T(8,128)(2,1)}, u32[]{:S(2)}, u32[]{:S(2)}) collective-permute-start(bf16[3,192,768]{2,1,0:T(8,128)(2,1)S(1)} %collective-permute-done.20.refs_2_), channel_id=1, source_target_pairs={{0,1},{1,0},{2,3},{3,2},{4,5},{5,4},{6,7},{7,6},{8,9},{9,8},{10,11... | collective-permute-start | bytes 2654216 | tf_op jit(solution)/shard_map/ppermute | solution.py:552
  150.3 56.5 %collective-permute-start.23 = (bf16[3,192,768]{2,1,0:T(8,128)(2,1)S(1)}, bf16[3,192,768]{2,1,0:T(8,128)(2,1)}, u32[]{:S(2)}, u32[]{:S(2)}) collective-permute-start(bf16[3,192,768]{2,1,0:T(8,128)(2,1)S(1)} %collective-permute-done.22.refs_4_), channel_id=1, source_target_pairs={{0,1},{1,0},{2,3},{3,2},{4,5},{5,4},{6,7},{7,6},{8,9},{9,8},{10,11... | collective-permute-start | bytes 2654216 | tf_op jit(solution)/shard_map/ppermute | solution.py:552
  165.3 41.5 %collective-permute-start.25 = (bf16[3,192,768]{2,1,0:T(8,128)(2,1)}, bf16[3,192,768]{2,1,0:T(8,128)(2,1)}, u32[]{:S(2)}, u32[]{:S(2)}) collective-permute-start(bf16[3,192,768]{2,1,0:T(8,128)(2,1)} %collective-permute-done.24.refs_6_), channel_id=1, source_target_pairs={{0,1},{1,0},{2,3},{3,2},{4,5},{5,4},{6,7},{7,6},{8,9},{9,8},{10,11... | collective-permute-start | bytes 2654216 | tf_op jit(solution)/shard_map/ppermute | solution.py:552
  443.3 37.6 %collective-permute-start.45 = (bf16[4,4,96,768]{3,2,1,0:T(8,128)(2,1)}, bf16[4,4,96,768]{3,2,1,0:T(8,128)(2,1)}, u32[]{:S(2)}, u32[]{:S(2)}) collective-permute-start(bf16[4,4,96,768]{3,2,1,0:T(8,128)(2,1)} %fusion.22), channel_id=1, source_target_pairs={{0,1},{1,0},{2,3},{3,2},{4,5},{5,4},{6,7},{7,6},{8,9},{9,8},{10,11... | collective-permute-start | bytes 7077896 | tf_op jit(solution)/shard_map/ppermute | solution.py:552
  564.1 36.6 %collective-permute-start.49 = (bf16[4,2,24,3072]{3,2,0,1:T(8,128)(2,1)}, bf16[4,2,24,3072]{3,2,0,1:T(8,128)(2,1)}, u32[]{:S(2)}, u32[]{:S(2)}) collective-permute-start(bf16[4,2,24,3072]{3,2,0,1:T(8,128)(2,1)} %fusion.32), channel_id=1, source_target_pairs={{0,4},{1,5},{2,6},{3,7},{4,0},{5,1},{6,2},{7,3},{8,12},{9,13},{10,... | collective-permute-start | bytes 3538952 | tf_op jit(solution)/shard_map/ppermute | solution.py:552
  565.4 36.9 %collective-permute-start.50 = (bf16[4,2,24,3072]{3,2,0,1:T(8,128)(2,1)}, bf16[4,2,24,3072]{3,2,0,1:T(8,128)(2,1)}, u32[]{:S(2)}, u32[]{:S(2)}) collective-permute-start(bf16[4,2,24,3072]{3,2,0,1:T(8,128)(2,1)} %fusion.33), channel_id=1, source_target_pairs={{0,2},{1,3},{2,0},{3,1},{4,6},{5,7},{6,4},{7,5},{8,10},{9,11},{10,... | collective-permute-start | bytes 3538952 | tf_op jit(solution)/shard_map/ppermute | solution.py:552
  633.9 69.3 %collective-permute-start.60 = (bf16[24,3072]{1,0:T(8,128)(2,1)}, bf16[24,3072]{1,0:T(8,128)(2,1)}, u32[]{:S(2)}, u32[]{:S(2)}) collective-permute-start(bf16[24,3072]{1,0:T(8,128)(2,1)} %get-tuple-element.214), channel_id=1, source_target_pairs={{0,24},{8,0},{16,8},{24,16},{1,25},{9,1},{17,9},{25,17},{2,26},{10... | collective-permute-start | bytes 442376 | tf_op jit(solution)/shard_map/ppermute | solution.py:557
  635.7 67.7 %collective-permute-start.59 = (bf16[24,3072]{1,0:T(8,128)(2,1)}, bf16[24,3072]{1,0:T(8,128)(2,1)}, u32[]{:S(2)}, u32[]{:S(2)}) collective-permute-start(bf16[24,3072]{1,0:T(8,128)(2,1)} %get-tuple-element.215), channel_id=1, source_target_pairs={{0,16},{8,24},{16,0},{24,8},{1,17},{9,25},{17,1},{25,9},{2,18},{10... | collective-permute-start | bytes 442376 | tf_op jit(solution)/shard_map/ppermute | solution.py:557
  635.7 72.2 %collective-permute-start.58 = (bf16[24,3072]{1,0:T(8,128)(2,1)}, bf16[24,3072]{1,0:T(8,128)(2,1)}, u32[]{:S(2)}, u32[]{:S(2)}) collective-permute-start(bf16[24,3072]{1,0:T(8,128)(2,1)} %get-tuple-element.216), channel_id=1, source_target_pairs={{0,8},{8,16},{16,24},{24,0},{1,9},{9,17},{17,25},{25,1},{2,10},{10... | collective-permute-start | bytes 442376 | tf_op jit(solution)/shard_map/ppermute | solution.py:557
  636.1 73.1 %collective-permute-start.57 = (bf16[24,3072]{1,0:T(8,128)(2,1)}, bf16[24,3072]{1,0:T(8,128)(2,1)S(1)}, u32[]{:S(2)}, u32[]{:S(2)}) collective-permute-start(bf16[24,3072]{1,0:T(8,128)(2,1)} %get-tuple-element.217), channel_id=1, source_target_pairs={{0,24},{8,0},{16,8},{24,16},{1,25},{9,1},{17,9},{25,17},{2,26},{10... | collective-permute-start | bytes 442376 | tf_op jit(solution)/shard_map/ppermute | solution.py:557
  639.0 70.2 %collective-permute-start.56 = (bf16[24,3072]{1,0:T(8,128)(2,1)}, bf16[24,3072]{1,0:T(8,128)(2,1)}, u32[]{:S(2)}, u32[]{:S(2)}) collective-permute-start(bf16[24,3072]{1,0:T(8,128)(2,1)} %get-tuple-element.218), channel_id=1, source_target_pairs={{0,16},{8,24},{16,0},{24,8},{1,17},{9,25},{17,1},{25,9},{2,18},{10... | collective-permute-start | bytes 442376 | tf_op jit(solution)/shard_map/ppermute | solution.py:557
  679.8 99.0 %all-gather.6.cloned.1.call-start = ((), (), s32[]{:S(2)}) async-start(), calls=%async_computation.3 | async-start | bytes 2621440 | tf_op jit(solution)/shard_map/all_gather | solution.py:898
  725.1 100.3 %all-gather.8.cloned.1.call-start = ((), (), s32[]{:S(2)}) async-start(), calls=%async_computation.4 | async-start | bytes 2621440 | tf_op jit(solution)/shard_map/all_gather | solution.py:898
  880.7 53.4 %collective-permute-start.107 = (bf16[24,3072]{1,0:T(8,128)(2,1)}, bf16[24,3072]{1,0:T(8,128)(2,1)}, u32[]{:S(2)}, u32[]{:S(2)}) collective-permute-start(bf16[24,3072]{1,0:T(8,128)(2,1)} %get-tuple-element.181.refs_0_), channel_id=1, source_target_pairs={{0,4},{1,5},{2,6},{3,7},{4,0},{5,1},{6,2},{7,3},{8,12},{9,13},{10,... | collective-permute-start | bytes 442376 | tf_op jit(solution)/shard_map/ppermute | solution.py:552
  894.9 39.7 %collective-permute-start.109 = (bf16[24,3072]{1,0:T(8,128)(2,1)}, bf16[24,3072]{1,0:T(8,128)(2,1)}, u32[]{:S(2)}, u32[]{:S(2)}) collective-permute-start(bf16[24,3072]{1,0:T(8,128)(2,1)} %collective-permute-done.105.refs_2_), channel_id=1, source_target_pairs={{0,4},{1,5},{2,6},{3,7},{4,0},{5,1},{6,2},{7,3},{8,12},{9,13},{10,... | collective-permute-start | bytes 442376 | tf_op jit(solution)/shard_map/ppermute | solution.py:552
  955.4 51.3 %collective-permute-start.90 = (bf16[960,256]{1,0:T(8,128)(2,1)}, bf16[960,256]{1,0:T(8,128)(2,1)}, u32[]{:S(2)}, u32[]{:S(2)}) collective-permute-start(bf16[960,256]{1,0:T(8,128)(2,1)} %get-tuple-element.146.rest_0_), channel_id=1, source_target_pairs={{0,1},{1,0},{2,3},{3,2},{4,5},{5,4},{6,7},{7,6},{8,9},{9,8},{10,11... | collective-permute-start | bytes 1474568 | tf_op jit(solution)/shard_map/ppermute | solution.py:552
  956.2 37.5 %collective-permute-start.92 = (bf16[960,256]{1,0:T(8,128)(2,1)}, bf16[960,256]{1,0:T(8,128)(2,1)}, u32[]{:S(2)}, u32[]{:S(2)}) collective-permute-start(bf16[960,256]{1,0:T(8,128)(2,1)} %get-tuple-element.146.rest_0_), channel_id=1, source_target_pairs={{0,2},{1,3},{2,0},{3,1},{4,6},{5,7},{6,4},{7,5},{8,10},{9,11},{10,... | collective-permute-start | bytes 1474568 | tf_op jit(solution)/shard_map/ppermute | solution.py:552
  957.0 37.8 %collective-permute-start.96 = (bf16[960,256]{1,0:T(8,128)(2,1)}, bf16[960,256]{1,0:T(8,128)(2,1)}, u32[]{:S(2)}, u32[]{:S(2)}) collective-permute-start(bf16[960,256]{1,0:T(8,128)(2,1)} %get-tuple-element.146.rest_0_), channel_id=1, source_target_pairs={{0,4},{1,5},{2,6},{3,7},{4,0},{5,1},{6,2},{7,3},{8,12},{9,13},{10,... | collective-permute-start | bytes 1474568 | tf_op jit(solution)/shard_map/ppermute | solution.py:552
  958.9 48.8 %collective-permute-start.98 = (bf16[960,512]{1,0:T(8,128)(2,1)}, bf16[960,512]{1,0:T(8,128)(2,1)}, u32[]{:S(2)}, u32[]{:S(2)}) collective-permute-start(bf16[960,512]{1,0:T(8,128)(2,1)} %pad_maximum_fusion.1.rest_1_), channel_id=1, source_target_pairs={{0,4},{1,5},{2,6},{3,7},{4,0},{5,1},{6,2},{7,3},{8,12},{9,13},{10,... | collective-permute-start | bytes 2949128 | tf_op jit(solution)/shard_map/ppermute | solution.py:552
  1006.7 35.9 %collective-permute-start.91 = (bf16[960,512]{1,0:T(8,128)(2,1)}, bf16[960,512]{1,0:T(8,128)(2,1)S(1)}, u32[]{:S(2)}, u32[]{:S(2)}) collective-permute-start(bf16[960,512]{1,0:T(8,128)(2,1)} %pad_maximum_fusion.1.rest_1_), channel_id=1, source_target_pairs={{0,1},{1,0},{2,3},{3,2},{4,5},{5,4},{6,7},{7,6},{8,9},{9,8},{10,11... | collective-permute-start | bytes 2949128 | tf_op jit(solution)/shard_map/ppermute | solution.py:552
  1007.3 35.3 %collective-permute-start.95 = (bf16[960,512]{1,0:T(8,128)(2,1)}, bf16[960,512]{1,0:T(8,128)(2,1)S(1)}, u32[]{:S(2)}, u32[]{:S(2)}) collective-permute-start(bf16[960,512]{1,0:T(8,128)(2,1)} %collective-permute-done.94.rest_3_), channel_id=1, source_target_pairs={{0,1},{1,0},{2,3},{3,2},{4,5},{5,4},{6,7},{7,6},{8,9},{9,8},{10,11... | collective-permute-start | bytes 2949128 | tf_op jit(solution)/shard_map/ppermute | solution.py:552
  1007.6 35.0 %collective-permute-start.99 = (bf16[960,512]{1,0:T(8,128)(2,1)}, bf16[960,512]{1,0:T(8,128)(2,1)S(1)}, u32[]{:S(2)}, u32[]{:S(2)}) collective-permute-start(bf16[960,512]{1,0:T(8,128)(2,1)} %collective-permute-done.98.rest_5_), channel_id=1, source_target_pairs={{0,1},{1,0},{2,3},{3,2},{4,5},{5,4},{6,7},{7,6},{8,9},{9,8},{10,11... | collective-permute-start | bytes 2949128 | tf_op jit(solution)/shard_map/ppermute | solution.py:552
  (230 other events, 3717.4 us)
Sparse Core Ops, SparseCore 0:
  70.1 124.7 reduce-scatter.1
  679.9 51.9 all-gather.3
  734.1 44.6 all-gather.5
  780.8 44.6 all-gather.7

commit v6 on v5

--- a/solution.py
+++ b/solution.py
@@ -306,88 +306,61 @@
     )(starts, places, order, table)
 
 
-def table_grad_kernel(core_ref, starts_ref, places_ref, order_ref, dlogits_ref, chosen_ref, embed_ref, sent_ref, kept_ref, rows, total):
+def table_grad_kernel(core_ref, starts_ref, codes_ref, order_ref, dlogits_ref, chosen_ref, embed_ref, out_ref, rows, sums):
     step = pl.program_id(0)
-    half = pl.num_programs(0) // 2
     count, width = embed_ref.shape
-    block = kept_ref.shape[1]
-    tiles = width // LANES
+    block = out_ref.shape[1]
 
     @pl.when(step == 0)
     def _():
         for start in range(0, count, CHUNK):
-            some = embed_ref[start : start + CHUNK, :].astype(jnp.float32)
-            for j in range(tiles):
-                rows[pl.ds(start * 8 + j, CHUNK, stride=8), :] = some[:, j * LANES : (j + 1) * LANES]
-
-    product = jnp.dot(dlogits_ref[...], chosen_ref[...], preferred_element_type=jnp.float32)
-    for j in range(tiles):
-        total[pl.ds(j, block, stride=8), :] = product[:, j * LANES : (j + 1) * LANES]
-    side = jnp.where(step < half, 1 - core_ref[0], core_ref[0])
-    chunk = 2 * (step % half) + side
-    base = chunk * block
+            rows[start : start + CHUNK, :] = embed_ref[start : start + CHUNK, :].astype(jnp.float32)
+
+    sums[...] = jnp.zeros_like(sums)
+    chunk = 2 * step + core_ref[0]
     first, last = starts_ref[chunk], starts_ref[chunk + 1]
 
-    def eight(turn, carry):
+    def eight(turn, running):
         for j in range(8):
             i = first + turn * 8 + j
-            at = jnp.minimum(i, count - 1)
-            place = jnp.where(i < last, places_ref[at] - base, block)
-            to = pl.ds(pl.multiple_of(place * 8, 8), 8)
-            total[to, :] += rows[pl.ds(pl.multiple_of(order_ref[at] * 8, 8), 8), :]
-        return carry
-
-    lax.fori_loop(0, (last - first + 7) // 8, eight, 0)
-    result = [total[pl.ds(j, block, stride=8), :] for j in range(tiles)]
-
-    @pl.when(step < half)
-    def _():
-        for j in range(tiles):
-            sent_ref[0, :, j * LANES : (j + 1) * LANES] = result[j].astype(sent_ref.dtype)
-
-    @pl.when(step >= half)
-    def _():
-        for j in range(tiles):
-            kept_ref[0, :, j * LANES : (j + 1) * LANES] = result[j]
-
-
-def table_grad_halves(core, starts, places, order, dlogits, chosen, embed, block, dtype):
+            code = codes_ref[i]
+            place = jnp.where(i < last, code >> 1, block)
+            running = jnp.where(code & 1, running, 0.0) + rows[pl.ds(order_ref[i], 1), :]
+            sums[pl.ds(place, 1), :] = running
+        return running
+
+    lax.fori_loop(0, (last - first + 7) // 8, eight, jnp.zeros((1, width), jnp.float32))
+    product = jnp.dot(dlogits_ref[...], chosen_ref[...], preferred_element_type=jnp.float32)
+    out_ref[0] = (product + sums[:block, :]).astype(out_ref.dtype)
+
+
+def table_grad_half(core, starts, codes, order, dlogits, chosen, embed, block, dtype):
     count, width = embed.shape
     picked = chosen.shape[0]
-    half = dlogits.shape[0] // block // 2
+    chunks = dlogits.shape[0] // block // 2
     fixed = lambda i, *_: (0, 0)
-
-    def chunk_at(i, core, *_):
-        return (2 * (i % half) + jnp.where(i < half, 1 - core[0], core[0]), 0)
-
     return pl.pallas_call(
         table_grad_kernel,
         grid_spec=pltpu.PrefetchScalarGridSpec(
             num_scalar_prefetch=4,
-            grid=(2 * half,),
+            grid=(chunks,),
             in_specs=[
-                pl.BlockSpec((block, picked), chunk_at),
+                pl.BlockSpec((block, picked), lambda i, core, *_: (2 * i + core[0], 0)),
                 pl.BlockSpec((picked, width), fixed),
                 pl.BlockSpec((count, width), fixed, pipeline_mode=pl.Buffered(1)),
             ],
-            out_specs=[
-                pl.BlockSpec((1, block, width), lambda i, *_: (jnp.minimum(i, half - 1), 0, 0)),
-                pl.BlockSpec((1, block, width), lambda i, *_: (jnp.maximum(i - half, 0), 0, 0)),
+            out_specs=pl.BlockSpec((1, block, width), lambda i, *_: (i, 0, 0)),
+            scratch_shapes=[
+                pltpu.VMEM((count, width), jnp.float32),
+                pltpu.VMEM((block + 8, width), jnp.float32),
             ],
-            scratch_shapes=[
-                pltpu.VMEM((count * 8, LANES), jnp.float32),
-                pltpu.VMEM((block * 8 + 8, LANES), jnp.float32),
-            ],
-        ),
-        out_shape=[
-            jax.ShapeDtypeStruct((half, block, width), dtype),
-            jax.ShapeDtypeStruct((half, block, width), jnp.float32),
-        ],
+        ),
+        out_shape=jax.ShapeDtypeStruct((chunks, block, width), dtype),
         compiler_params=pltpu.CompilerParams(vmem_limit_bytes=vmem),
         cost_estimate=pl.CostEstimate(
-            flops=4 * half * block * picked * width, bytes_accessed=16 * half * block * width, transcendentals=0
-        ),
-    )(core, starts, places, order, dlogits, chosen, embed)
+            flops=2 * chunks * block * picked * width, bytes_accessed=8 * chunks * block * width, transcendentals=0
+        ),
+    )(core, starts, codes, order, dlogits, chosen, embed)
 
 
 def update_kernel(parts, slots_ref, scalars_ref, *rest):
@@ -587,6 +560,7 @@
         self.axis = axis
         self.order = order
         self.quick = lax.axis_size("rep") == 8
+        self.value = None
 
     def cores(self, chunks):
         axis = self.axis
@@ -602,7 +576,9 @@
         return [sent]
 
     def sum(self):
-        return self.kept + self.got.astype(jnp.float32) if self.quick else self.value
+        if self.value is None:
+            return self.kept + self.got.astype(jnp.float32)
+        return self.value
 
     def plane(self, first):
         if not self.quick:
@@ -615,7 +591,7 @@
             value = value.reshape(shape[:axis] + (2, 2) + shape[axis + 1 :])
             axis = axis + (1 if bit == 2 else 0)
         self.kept, sent = halve(value, axis, bit)
-        self.got = flip(sent, bit)
+        self.value, self.got = None, flip(sent, bit)
         return [sent]
 
     def members(self):
@@ -774,7 +750,6 @@
     if quick:
         near_part = fetch(cut(near_shard, 1).astype(low_type))
         gu_part = fetch(cut(w_gu, 1).astype(low_type))
-        down_part = fetch(cut(w_down, 0).astype(low_type))
 
     local_ids = group_ids - member * vocab_rows
     owned = (local_ids >= 0) & (local_ids < vocab_rows)
@@ -785,9 +760,12 @@
     starts = jnp.sum((places[None, :] < bounds[:, None]).astype(jnp.int32), axis=1)
     if quick:
         places, near_part = tie((places, near_part))
+    again = jnp.concatenate([jnp.zeros((1,), jnp.int32), (places[1:] == places[:-1]).astype(jnp.int32)])
+    codes = jnp.pad(places % block * 2 + again, (0, 8))
+    padded_order = jnp.pad(order, (0, 8))
     found = lookup(starts, places, order, table)
     if quick:
-        found, gu_part, down_part = tie((found, gu_part, down_part))
+        found, gu_part = tie((found, gu_part))
     embed = lax.psum_scatter(found, "grp", scatter_dimension=0, tiled=True)
     late_table, _ = lax.optimization_barrier((table, found))
     table_low = jnp.pad(late_table.astype(low_type), ((0, padded - vocab_rows), (0, 0)))
@@ -795,13 +773,18 @@
     if quick:
         members, slots = members_of(), slots_of()
 
-        def shared(part, order):
-            have = spread(part, order)
+        down_own, _ = tie((cut(w_down, 0), found))
+        down_part = fetch(down_own.astype(low_type))
+
+        def listed(have):
             return [have[place] for place in range(replicas)]
 
-        near = lay_columns(members, slots, near_shard, shared(near_part, [4, 2, 1]))
-        w_gu_low = lay_columns(members, slots, w_gu, shared(gu_part, [2, 4, 1]))
-        w_down_low = lay_rows(members, slots, w_down, shared(down_part, [4, 2, 1]))
+        near = lay_columns(members, slots, near_shard, listed(spread(near_part, [4, 2, 1])))
+        w_down_low = lay_rows(members, slots, w_down, listed(spread(down_part, [4, 2, 1])))
+        gu_have = spread(gu_part, [2, 4])
+        gu_have, near, w_down_low, table_low = tie((gu_have, near, w_down_low, table_low))
+        gu_have.update({place ^ 1: flip(part, 1) for place, part in gu_have.items()})
+        w_gu_low = lay_columns(members, slots, w_gu, listed(gu_have))
         embed, near, w_gu_low, w_down_low, table_low = tie((embed, near, w_gu_low, w_down_low, table_low))
     else:
         near = lax.all_gather(near_shard.astype(low_type), "grp", tiled=True)
@@ -887,76 +870,62 @@
     _, pull = jax.vjp(layer_norm, embed.astype(jnp.float32), norms[0], norms[1])
     embed_grad, gain_one, shift_one = pull(first_grad)
     norm_grad = jnp.stack([gain_one, shift_one, gain_two, shift_two, gain_three, shift_three])
-    wide = width // 3
-    spans = [(part * wide, (part + 1) * wide) for part in range(3)]
-    embed_low = embed_grad.astype(low_type)
-    join_grad = contract(first_low, joined_grad, 0, 0)
-    late_embed, join_grad = tie((embed_low, join_grad))
-    join_grad = jnp.concatenate([join_grad, contract(mixed_low, attn_low, 0, 0)], axis=1)
-    last_embed, join_grad = tie((late_embed, join_grad))
-    group_embeds = [
-        lax.all_gather(piece[:, begin:end], "grp", axis=0, tiled=True)
-        for piece, (begin, end) in zip((embed_low, late_embed, last_embed), spans)
-    ]
+    embed_low, joined_grad = tie((embed_grad.astype(low_type), joined_grad))
+    group_embed = lax.all_gather(embed_low, "grp", axis=0, tiled=True)
+
     join = Fold(1, (2, 4))
-    join.cores(gradient_chunks(join_grad))
-    sent = join.plane(True)
+    join.cores(
+        gradient_chunks(
+            jnp.concatenate(
+                [contract(first_low, joined_grad, 0, 0), contract(mixed_low, attn_low, 0, 0)], axis=1
+            )
+        )
+    )
+    join.plane(True)
+    join.plane(False)
+    join.members()
     gu_share = jnp.concatenate([gate.total(), up.total()], axis=1)
-    down_share = down.total()
+    down_share, join_share = down.total(), join.total()
     part_rows = gu_share.shape[0]
-    far_low = jnp.concatenate(
-        [gu_share.astype(low_type), down_share.astype(low_type).reshape(part_rows, -1)], axis=1
-    )
+    far_whole = plane_gather(
+        jnp.concatenate(
+            [gu_share.astype(low_type), down_share.astype(low_type).reshape(part_rows, -1)], axis=1
+        )
+    ).reshape(shard_rows, -1)
+    near_whole = plane_gather(join_share.astype(low_type)).reshape(shard_rows, -1)
+    shares = (join_share[:, : 3 * width], join_share[:, 3 * width :], gu_share, down_share)
+    share_cols = [jnp.sum(gradient * gradient, axis=0) for gradient in shares]
+    group_embed, near_whole, far_whole, share_cols = tie((group_embed, near_whole, far_whole, share_cols))
+
+    core = replica % 2
+    half_args = (starts, codes, padded_order, dlogits, group_chosen, group_embed, block)
+    heads = [Fold(0, (2, 4)), Fold(0, (4, 2))]
+    middle = width // 2
     if quick:
-        far_got = spread(far_low, [2, 4, 1])
-        group_embeds[0], _, _ = tie((group_embeds[0], sent, list(far_got.values())))
-    core = replica % 2
-    heads = [Fold(0, (4, 2) if part % 2 else (2, 4)) for part in range(3)]
-    for part, (begin, end) in enumerate(spans):
-        head = heads[part]
-        if part == 1:
-            group_embeds[1], _ = tie((group_embeds[1], heads[0].plane(True)))
-        if part == 2:
-            sent = heads[1].plane(True) + heads[0].plane(False) + join.plane(False)
-            group_embeds[2], _ = tie((group_embeds[2], sent))
-        half_args = (
-            starts,
-            places,
-            order,
-            dlogits,
-            group_chosen[:, begin:end],
-            group_embeds[part],
-            block,
-        )
-        sent, kept = table_grad_halves(core[None], *half_args, low_type if quick else jnp.float32)
-        if quick:
-            head.from_cores(kept, sent)
-        else:
-            both = [jnp.where(core == j, kept, sent) for j in range(2)]
-            head.cores(jnp.stack(both, axis=1).reshape(replicas, block, end - begin))
-    heads[2].plane(True)
-    heads[1].plane(False)
-    heads[2].plane(False)
-    join.members()
+        sent = table_grad_half((1 - core)[None], *half_args, low_type)
+        got = flip(sent, 1)
+        value = table_grad_half(core[None], *half_args, jnp.float32) + got.astype(jnp.float32)
+    else:
+        both = [table_grad_half(jnp.full((1,), j, jnp.int32), *half_args, jnp.float32) for j in range(2)]
+        value = jnp.stack(both, axis=1).reshape(replicas, block, width)
+        value = lax.psum_scatter(value, "rep", scatter_dimension=0)
+    for head, part in zip(heads, (value[..., :middle], value[..., middle:])):
+        head.value = part
+        head.plane(True)
+    for head in heads:
+        head.plane(False)
     table_parts = [head.sum() for head in heads]
-    join_share = join.total()
-
-    shares = (
-        join_share[:, : 3 * width],
-        join_share[:, 3 * width :],
-        gu_share,
-        down_share,
-    )
+
     old_rows = (table_rows, qkv_rows, out_rows, gu_rows, down_rows)
     old_cols = (table_cols, qkv_cols, out_cols, gu_cols, down_cols)
     masters = (table, w_qkv, w_out, w_gu, w_down)
     col_parts = [
         jnp.concatenate([jnp.sum(gradient * gradient, axis=0) for gradient in table_parts])
-    ] + [jnp.sum(gradient * gradient, axis=0) for gradient in shares]
+    ] + share_cols
     row_old = jnp.stack([jnp.sum(rows) for rows in old_rows]) / replicas
     small = [norm_grad.reshape(-1)] + col_parts + [row_old, jnp.sum(own_terms)[None]]
     plane_totals = plane_sum(jnp.concatenate(small))
-    table_lows = [table_parts[0].astype(low_type), jnp.concatenate(table_parts[1:], axis=1).astype(low_type)]
+    table_lows = [part.astype(low_type) for part in table_parts]
     plane_totals, table_lows = tie((plane_totals, table_lows))
     totals = rest_sum(plane_totals)
     cuts = []
@@ -973,12 +942,6 @@
     factor = clip_limit / jnp.maximum(clip_norm, clip_limit)
     decay = 1.0 - float(STEP) ** (-0.8)
 
-    if quick:
-        far_whole = lay_out(slots_of(), [far_got[place] for place in range(replicas)])
-    else:
-        far_whole = plane_gather(far_low)
-    far_whole = far_whole.reshape(shard_rows, -1)
-    near_whole = plane_gather(join_share.astype(low_type)).reshape(shard_rows, -1)
     wholes = [
         None,
         near_whole[:, : 3 * width],

time: 1090 us -> 1090 us (level)
  Pallas kernels: 263 us -> 244 us
  waiting for transfers between devices: 205 us -> 224 us
    ppermute x33, waiting for transfers between devices: 41.7 us -> 116 us  [turn(): lax.ppermute(value, 'grp', [(i, (i + offset) % size) for i in range(size)])]
    ppermute x76 -> x72, waiting for transfers between devices: 156 us -> 106 us  [flip(): return lax.ppermute(value, 'rep', [(i, i ^ bit) for i in range(size)])]
    pallas_call x3 -> x2, Pallas kernels: 49.4 us -> 29 us  [table_grad_half(): pl.pallas_call(table_grad_kernel, grid_spec=pltpu.PrefetchScalarGridSpec(...]
    ppermute x76 -> x72, starting transfers between devices: 100 us -> 82.1 us  [flip(): return lax.ppermute(value, 'rep', [(i, i ^ bit) for i in range(size)])]
    ppermute x33, starting transfers between devices: 55.2 us -> 69.1 us  [turn(): lax.ppermute(value, 'grp', [(i, (i + offset) % size) for i in range(size)])]
    unnamed x303 -> x287, local copies, waits for them, and re-layouts: 33.8 us -> 28 us
    add x18 -> x16, other arithmetic: 32.3 us -> 36.9 us  [the longest x14 25.1 us: sum(): return self.kept + self.got.astype(jnp.float32)]
    convert_element_type x18 -> x16, local copies, waits for them, and re-layouts: 18.9 us -> 22.7 us  [halve(): return (kept, sent.astype(low_type))]
  transfers between devices with their start and end apart: 115 -> 109, of which waited for: 31 -> 30; matrix products, arithmetic and copies ran while one was open for 25% -> 20% of each run, Pallas kernels for 16% -> 12%
where the time goes in v6:
time: 1090 us; the launch traced here: 1080 us
  Pallas kernels  244 us (22%)
  waiting for transfers between devices  224 us (21%)
  other arithmetic  185 us (17%)
  starting transfers between devices  154 us (14%)
  matrix products  139 us (13%)
  local copies, waits for them, and re-layouts  102 us (9%)
  between operations  32.3 us (3%)
    ppermute x33, waiting for transfers between devices, turn(): lax.ppermute(value, 'grp', [(i, (i + offset) % size) for i in range(size)])  116 us
    dot_general x11, matrix products, contract(): lax.dot_general(left, right, (((left_dim,), (right_dim,)), ((), ())), pre...  113 us
    ppermute x72, waiting for transfers between devices, flip(): return lax.ppermute(value, 'rep', [(i, i ^ bit) for i in range(size)])  106 us
    ppermute x72, starting transfers between devices, flip(): return lax.ppermute(value, 'rep', [(i, i ^ bit) for i in range(size)])  82.1 us
    ppermute x33, starting transfers between devices, turn(): lax.ppermute(value, 'grp', [(i, (i + offset) % size) for i in range(size)])  69.1 us
    pallas_call x3, Pallas kernels, attend_back(): pl.pallas_call(functools.partial(attend_back_kernel, first_pair), grid_sp...  65.8 us
    pallas_call x1, Pallas kernels, attend(): pl.pallas_call(attend_kernel, grid_spec=pltpu.PrefetchScalarGridSpec(num_...  47.7 us
    pallas_call x2, Pallas kernels, update(): pl.pallas_call(functools.partial(update_kernel, parts), grid_spec=pltpu.P...  36.1 us
  transfers between devices with their start and end apart: 109, of which 30 were waited for; matrix products, arithmetic and copies ran while one was open for 20% of the time, Pallas kernels for 12%

profile of v6, /device:TPU:1, one launch (start us, length us, event | category | flops | bytes accessed | tf_op | source)
XLA Modules:
  0.0 1081.1 jit_solution(3117319527687189875)
XLA Ops:
  37.7 17.4 %shard_map.413 = bf16[4096,768]{1,0:T(8,128)(2,1)} custom-call(s32[9]{0:T(128)} %convert_reduce_fusion.1.starts_ref, s32[4096]{0:T(1024)} %copy-done.76, s32[4096]{0:T(1024)} %get-tuple-element.95.order_ref, f32[7632,768]{1,0:T(8,128)} %rest_8_.3), custom_call_target="tpu_custom_call" | custom-call | bytes 70336512 | tf_op jit(solution)/shard_map/pallas_call | solution.py:294
  72.1 12.0 %collective-permute-done.20 = bf16[96,768]{1,0:T(8,128)(2,1)S(1)} collective-permute-done((bf16[96,768]{1,0:T(8,128)(2,1)S(1)}, bf16[96,768]{1,0:T(8,128)(2,1)S(1)}, u32[]{:S(2)}, u32[]{:S(2)}) %collective-permute-start.20) | collective-permute-done | bytes 147488 | tf_op jit(solution)/shard_map/ppermute | solution.py:530
  84.1 9.2 collective-permute-start.22
  97.8 26.3 %collective-permute-done.23.refs_2_ = bf16[3,96,768]{2,1,0:T(8,128)(2,1)S(1)} collective-permute-done((bf16[3,96,768]{2,1,0:T(8,128)(2,1)S(1)}, bf16[3,96,768]{2,1,0:T(8,128)(2,1)S(1)}, u32[]{:S(2)}, u32[]{:S(2)}) %collective-permute-start.23) | collective-permute-done | bytes 442400 | tf_op jit(solution)/shard_map/ppermute | solution.py:525
  184.0 10.8 %shard_map.416 = bf16[768,6144]{1,0:T(8,128)(2,1)} custom-call(s32[4]{0:T(128)} %and_select_fusion.members_ref, s32[8]{0:T(128)} %iota_xor_fusion.slots_ref, f32[192,6144]{1,0:T(8,128)} %own_ref.1, bf16[3,192,768]{2,1,0:T(8,128)(2,1)} %copy-done.26, bf16[3,192,768]{2,1,0:T(8,128)(2,1)} %collective-permute-done.29.refs_1_, bf16[3,192,768]{2,1,0:T(8,128)(2,1)} %copy-done.40, ...), custom_call_target="tpu_custom_call" | custom-call | bytes 18874368 | tf_op jit(solution)/shard_map/pallas_call | solution.py:475
  196.5 9.2 shard_map.417
  205.7 47.7 %shard_map.418 = (bf16[1024,768]{1,0:T(8,128)(2,1)}, f32[6,2,1024]{2,1,0:T(2,128)}) custom-call(s32[1]{0:T(128)S(6)} %copy.136.length_ref, bf16[1024,768]{1,0:T(8,128)(2,1)} %get-tuple-element.113.q_ref, bf16[1024,768]{1,0:T(8,128)(2,1)} %get-tuple-element.114.k_ref, bf16[1024,768]{1,0:T(8,128)(2,1)} %get-tuple-element.115.v_ref), custom_call_target="tpu_custom_call" | custom-call | flops 12884901888 | bytes 6291456 | tf_op jit(solution)/shard_map/pallas_call | solution.py:138
  257.2 17.8 %fusion.115 = f32[1024,6144]{1,0:T(8,128)} fusion(bf16[768,6144]{1,0:T(8,128)(2,1)} %shard_map.416, f32[1024,768]{1,0:T(8,128)S(1)} %get-tuple-element.258, f32[768]{0:T(1024)S(1)} %get-tuple-element.177, f32[768]{0:T(1024)S(1)} %get-tuple-element.178, f32[1024]{0:T(1024)S(1)} %fusion.85, f32[1024]{0:T(1024)S(1)} %broadcast_multiply_fusion.1), kind=kOutput, calls=%fused_computation.317 | convolution fusion | flops 9667608576 | bytes 37763072 | tf_op jit(solution)/shard_map/dot_general | solution.py:805
  275.0 9.9 multiply_convert_fusion.1
  317.7 10.9 %select_reduce_fusion.1 = (f32[512]{0:T(512)S(1)}, f32[7680,512]{1,0:T(8,128)S(1)}) fusion(pred[7680]{0:T(1024)(128)(4,1)S(1)} %iota_compare_fusion.1, bf16[7680,768]{1,0:T(8,128)(2,1)} %pad.21, bf16[512,768]{1,0:T(8,128)(2,1)} %bitcast.21.chosen_ref), kind=kOutput, calls=%fused_computation.9 | convolution fusion | flops 6047661568 | bytes 28321280 | tf_op jit(solution)/shard_map/dot_general | solution.py:672
  350.9 11.8 %fusion.117 = f32[512,768]{1,0:T(8,128)S(1)} fusion(bf16[7680,512]{1,0:T(8,128)(2,1)S(1)} %multiply_convert_fusion.dlogits_ref, bf16[7680,768]{1,0:T(8,128)(2,1)} %pad.21), kind=kOutput, calls=%fused_computation.318 | convolution fusion | flops 6039797760 | bytes 21233664 | tf_op jit(solution)/shard_map/dot_general | solution.py:672
  372.0 22.7 %collective-permute-done.43 = f32[128,768]{1,0:T(8,128)S(1)} collective-permute-done((f32[128,768]{1,0:T(8,128)S(1)}, f32[128,768]{1,0:T(8,128)S(1)}, u32[]{:S(2)}, u32[]{:S(2)}) %collective-permute-start.43) | collective-permute-done | bytes 393248 | tf_op jit(solution)/shard_map/ppermute | solution.py:530
  424.6 23.7 %fusion.32 = (f32[1024,3072]{1,0:T(8,128)}, f32[1024,3072]{1,0:T(8,128)}) fusion(f32[1024,6144]{1,0:T(8,128)} %fusion.115, bf16[3072,768]{1,0:T(8,128)(2,1)} %bitcast.296, f32[1024,768]{1,0:T(8,128)} %copy-done.30, f32[1024]{0:T(1024)S(1)} %negate_multiply_fusion.2), kind=kOutput, calls=%fused_computation.98 | convolution fusion | flops 4871159808 | bytes 58200064 | tf_op jit(solution)/shard_map/dot_general | solution.py:672
  448.3 9.4 add_convert_fusion
  497.3 17.4 %add_add_fusion.4 = f32[1024,768]{1,0:T(8,128)} fusion(f32[1024,768]{1,0:T(8,128)} %copy-done.30, bf16[1024,6144]{1,0:T(8,128)(2,1)} %copy-done.3, bf16[768,6144]{1,0:T(8,128)(2,1)} %shard_map.416, f32[1024]{0:T(1024)S(1)} %negate_multiply_fusion.2), kind=kOutput, calls=%fused_computation.59 | convolution fusion | flops 9665249280 | bytes 28315648 | tf_op jit(solution)/shard_map/dot_general | solution.py:672
  536.2 21.7 %shard_map.419 = (bf16[1024,256]{1,0:T(8,128)(2,1)}, bf16[1024,256]{1,0:T(8,128)(2,1)}, bf16[1024,256]{1,0:T(8,128)(2,1)}) custom-call(s32[1]{0:T(128)S(6)} %copy.136.length_ref, bf16[1024,768]{1,0:T(8,128)(2,1)} %get-tuple-element.113.q_ref, bf16[1024,768]{1,0:T(8,128)(2,1)} %get-tuple-element.114.k_ref, bf16[1024,768]{1,0:T(8,128)(2,1)} %get-tuple-element.115.v_ref, ...), custom_call_target="tpu_custom_call" | custom-call | flops 10737418240 | bytes 4194304 | tf_op jit(solution)/shard_map/pallas_call | solution.py:223
  569.8 22.3 %shard_map.420 = (bf16[1024,256]{1,0:T(8,128)(2,1)}, bf16[1024,256]{1,0:T(8,128)(2,1)}, bf16[1024,256]{1,0:T(8,128)(2,1)}) custom-call(s32[1]{0:T(128)S(6)} %copy.136.length_ref, bf16[1024,768]{1,0:T(8,128)(2,1)} %get-tuple-element.113.q_ref, bf16[1024,768]{1,0:T(8,128)(2,1)} %get-tuple-element.114.k_ref, bf16[1024,768]{1,0:T(8,128)(2,1)} %get-tuple-element.115.v_ref, ...), custom_call_target="tpu_custom_call" | custom-call | flops 10737418240 | bytes 4194304 | tf_op jit(solution)/shard_map/pallas_call | solution.py:223
  596.5 21.8 %shard_map.421 = (bf16[1024,256]{1,0:T(8,128)(2,1)}, bf16[1024,256]{1,0:T(8,128)(2,1)}, bf16[1024,256]{1,0:T(8,128)(2,1)}) custom-call(s32[1]{0:T(128)S(6)} %copy.136.length_ref, bf16[1024,768]{1,0:T(8,128)(2,1)} %get-tuple-element.113.q_ref, bf16[1024,768]{1,0:T(8,128)(2,1)} %get-tuple-element.114.k_ref, bf16[1024,768]{1,0:T(8,128)(2,1)} %get-tuple-element.115.v_ref, ...), custom_call_target="tpu_custom_call" | custom-call | flops 10737418240 | bytes 4194304 | tf_op jit(solution)/shard_map/pallas_call | solution.py:223
  636.4 9.8 fusion.118
  667.9 14.2 %collective-permute-done.74 = bf16[96,768]{1,0:T(8,128)(2,1)S(1)} collective-permute-done((bf16[96,768]{1,0:T(8,128)(2,1)S(1)}, bf16[96,768]{1,0:T(8,128)(2,1)S(1)}, u32[]{:S(2)}, u32[]{:S(2)}) %collective-permute-start.74) | collective-permute-done | bytes 147488 | tf_op jit(solution)/shard_map/ppermute | solution.py:530
  686.6 12.4 %collective-permute-start.68 = (bf16[24,3072]{1,0:T(8,128)(2,1)S(1)}, bf16[24,3072]{1,0:T(8,128)(2,1)S(1)}, u32[]{:S(2)}, u32[]{:S(2)}) collective-permute-start(bf16[24,3072]{1,0:T(8,128)(2,1)S(1)} %copy-done.93), channel_id=1, source_target_pairs={{0,16},{8,24},{16,0},{24,8},{1,17},{9,25},{17,1},{25,9},{2,18},{10... | collective-permute-start | bytes 442376 | tf_op jit(solution)/shard_map/ppermute | solution.py:530
  699.0 11.7 %collective-permute-done.71 = bf16[24,3072]{1,0:T(8,128)(2,1)S(1)} collective-permute-done((bf16[24,3072]{1,0:T(8,128)(2,1)S(1)}, bf16[24,3072]{1,0:T(8,128)(2,1)S(1)}, u32[]{:S(2)}, u32[]{:S(2)}) %collective-permute-start.71) | collective-permute-done | bytes 147488 | tf_op jit(solution)/shard_map/ppermute | solution.py:530
  717.2 24.0 %collective-permute-done.68 = bf16[24,3072]{1,0:T(8,128)(2,1)S(1)} collective-permute-done((bf16[24,3072]{1,0:T(8,128)(2,1)S(1)}, bf16[24,3072]{1,0:T(8,128)(2,1)S(1)}, u32[]{:S(2)}, u32[]{:S(2)}) %collective-permute-start.68) | collective-permute-done | bytes 147488 | tf_op jit(solution)/shard_map/ppermute | solution.py:530
  759.6 10.7 collective-permute-start.58
  778.3 22.3 %collective-permute-done.58 = bf16[24,3072]{1,0:T(8,128)(2,1)S(1)} collective-permute-done((bf16[24,3072]{1,0:T(8,128)(2,1)S(1)}, bf16[24,3072]{1,0:T(8,128)(2,1)S(1)}, u32[]{:S(2)}, u32[]{:S(2)}) %collective-permute-start.58) | collective-permute-done | bytes 147488 | tf_op jit(solution)/shard_map/ppermute | solution.py:530
  826.5 14.5 %shard_map.425 = bf16[4,960,768]{2,1,0:T(8,128)(2,1)} custom-call(s32[1]{0:T(128)} %bitcast.96.core_ref, s32[9]{0:T(128)} %convert_reduce_fusion.1.starts_ref, s32[4104]{0:T(1024)} %pad.24.codes_ref, s32[4104]{0:T(1024)} %pad.25.order_ref, bf16[7680,512]{1,0:T(8,128)(2,1)} %copy-done, bf16[512,768]{1,0:T(8,128)(2,1)} %bitcast.21.chosen_ref, ...), custom_call_target="tpu_custom_call" | custom-call | flops 3019898880 | bytes 23592960 | tf_op jit(solution)/shard_map/pallas_call | solution.py:342
  841.0 14.5 %shard_map.424 = f32[4,960,768]{2,1,0:T(8,128)} custom-call(s32[1]{0:T(128)} %bitcast.78.core_ref, s32[9]{0:T(128)} %convert_reduce_fusion.1.starts_ref, s32[4104]{0:T(1024)} %pad.24.codes_ref, s32[4104]{0:T(1024)} %pad.25.order_ref, bf16[7680,512]{1,0:T(8,128)(2,1)} %copy-done, bf16[512,768]{1,0:T(8,128)(2,1)} %bitcast.21.chosen_ref, ...), custom_call_target="tpu_custom_call" | custom-call | flops 3019898880 | bytes 23592960 | tf_op jit(solution)/shard_map/pallas_call | solution.py:342
  855.5 11.7 %convert_add_fusion = f32[4,960,768]{2,1,0:T(8,128)} fusion(f32[4,960,768]{2,1,0:T(8,128)} %shard_map.424, bf16[4,960,768]{2,1,0:T(8,128)(2,1)} %collective-permute-done.83), kind=kLoop, calls=%fused_computation.15 | loop fusion | flops 5898240 | bytes 29491200 | tf_op jit(solution)/shard_map/add | solution.py:907
  879.7 30.2 %collective-permute-done.84 = bf16[2,960,384]{2,1,0:T(8,128)(2,1)S(1)} collective-permute-done((bf16[2,960,384]{2,1,0:T(8,128)(2,1)S(1)}, bf16[2,960,384]{2,1,0:T(8,128)(2,1)S(1)}, u32[]{:S(2)}, u32[]{:S(2)}) %collective-permute-start.84) | collective-permute-done | bytes 1474592 | tf_op jit(solution)/shard_map/ppermute | solution.py:525
  1016.0 12.0 %collective-permute-done.105.rest_7_ = bf16[960,384]{1,0:T(8,128)(2,1)} collective-permute-done((bf16[960,384]{1,0:T(8,128)(2,1)}, bf16[960,384]{1,0:T(8,128)(2,1)}, u32[]{:S(2)}, u32[]{:S(2)}) %collective-permute-start.105) | collective-permute-done | bytes 737312 | tf_op jit(solution)/shard_map/ppermute | solution.py:525
  1032.2 17.9 %shard_map.429 = (f32[7632,768]{1,0:T(8,128)}, f32[7632,768]{1,0:T(8,128)}, f32[16,1,480]{2,1,0:T(1,128)}) custom-call(s32[4]{0:T(128)} %pad_add_fusion.2.slots_ref, f32[2]{0:T(128)} %pad_maximum_fusion.9.scalars_ref, bf16[960,384]{1,0:T(8,128)(2,1)} %get-tuple-element.150.rest_0_, ...), custom_call_target="tpu_custom_call", output_to_operand_aliasing={{0}: (13, {}), {1}: (14, {}), {2}: (15, {})} | custom-call | flops 29491200 | bytes 41287680 | tf_op jit(solution)/shard_map/pallas_call | solution.py:400
  1052.0 18.2 %shard_map.430 = (f32[7632,768]{1,0:T(8,128)}, f32[7632,768]{1,0:T(8,128)}, f32[16,1,480]{2,1,0:T(1,128)}) custom-call(s32[4]{0:T(128)} %pad_add_fusion.1.slots_ref, f32[2]{0:T(128)} %pad_maximum_fusion.9.scalars_ref, bf16[960,384]{1,0:T(8,128)(2,1)} %collective-permute-done.93.rest_0_, ...), custom_call_target="tpu_custom_call", output_to_operand_aliasing={{0}: (13, {}), {1}: (14, {}), {2}: (15, {})} | custom-call | flops 29491200 | bytes 41287680 | tf_op jit(solution)/shard_map/pallas_call | solution.py:400
  (701 shorter events, 502.5 us)
Async XLA Ops:
  7.2 187.6 %reduce-scatter.2.cloned.1.call-start = ((), (), s32[]{:S(2)}) async-start(), calls=%async_computation.1 | async-start | bytes 7864320 | tf_op jit(solution)/shard_map/reduce_scatter | solution.py:769
  19.6 35.5 %collective-permute-start.8 = (bf16[192,768]{1,0:T(8,128)(2,1)}, bf16[192,768]{1,0:T(8,128)(2,1)S(1)}, u32[]{:S(2)}, u32[]{:S(2)}) collective-permute-start(bf16[192,768]{1,0:T(8,128)(2,1)} %dynamic-slice_convert_fusion.9), channel_id=1, source_target_pairs={{0,24},{8,0},{16,8},{24,16},{1,25},{9,1},{17,9},{25,17},{2,26},{10... | collective-permute-start | bytes 884744 | tf_op jit(solution)/shard_map/ppermute | solution.py:530
  23.6 31.6 %collective-permute-start.7 = (bf16[192,768]{1,0:T(8,128)(2,1)}, bf16[192,768]{1,0:T(8,128)(2,1)S(1)}, u32[]{:S(2)}, u32[]{:S(2)}) collective-permute-start(bf16[192,768]{1,0:T(8,128)(2,1)} %dynamic-slice_convert_fusion.9), channel_id=1, source_target_pairs={{0,16},{8,24},{16,0},{24,8},{1,17},{9,25},{17,1},{25,9},{2,18},{10... | collective-permute-start | bytes 884744 | tf_op jit(solution)/shard_map/ppermute | solution.py:530
  56.3 770.2 %all-gather.2.cloned.1.call-start = ((), (), s32[]{:S(2)}) async-start(), calls=%async_computation.2 | async-start | bytes 7864320 | tf_op jit(solution)/shard_map/all_gather | solution.py:874
  93.3 42.3 %collective-permute-start.9 = (bf16[3,192,768]{2,1,0:T(8,128)(2,1)S(1)}, bf16[3,192,768]{2,1,0:T(8,128)(2,1)S(1)}, u32[]{:S(2)}, u32[]{:S(2)}) collective-permute-start(bf16[3,192,768]{2,1,0:T(8,128)(2,1)S(1)} %pad_maximum_fusion.1.refs_0_), channel_id=1, source_target_pairs={{0,2},{1,3},{2,0},{3,1},{4,6},{5,7},{6,4},{7,5},{8,10},{9,11},{10,... | collective-permute-start | bytes 2654216 | tf_op jit(solution)/shard_map/ppermute | solution.py:525
  95.6 38.0 %collective-permute-start.17 = (bf16[3,192,384]{2,1,0:T(8,128)(2,1)S(1)}, bf16[3,192,384]{2,1,0:T(8,128)(2,1)S(1)}, u32[]{:S(2)}, u32[]{:S(2)}) collective-permute-start(bf16[3,192,384]{2,1,0:T(8,128)(2,1)S(1)} %collective-permute-done.15.refs_4_), channel_id=1, source_target_pairs={{0,2},{1,3},{2,0},{3,1},{4,6},{5,7},{6,4},{7,5},{8,10},{9,11},{10,... | collective-permute-start | bytes 1327112 | tf_op jit(solution)/shard_map/ppermute | solution.py:525
  96.6 38.2 %collective-permute-start.14 = (bf16[3,192,384]{2,1,0:T(8,128)(2,1)S(1)}, bf16[3,192,384]{2,1,0:T(8,128)(2,1)S(1)}, u32[]{:S(2)}, u32[]{:S(2)}) collective-permute-start(bf16[3,192,384]{2,1,0:T(8,128)(2,1)S(1)} %collective-permute-done.13.refs_2_), channel_id=1, source_target_pairs={{0,1},{1,0},{2,3},{3,2},{4,5},{5,4},{6,7},{7,6},{8,9},{9,8},{10,11... | collective-permute-start | bytes 1327112 | tf_op jit(solution)/shard_map/ppermute | solution.py:525
  134.8 42.2 %collective-permute-start.10 = (bf16[3,192,768]{2,1,0:T(8,128)(2,1)S(1)}, bf16[3,192,768]{2,1,0:T(8,128)(2,1)S(1)}, u32[]{:S(2)}, u32[]{:S(2)}) collective-permute-start(bf16[3,192,768]{2,1,0:T(8,128)(2,1)S(1)} %pad_maximum_fusion.1.refs_0_), channel_id=1, source_target_pairs={{0,4},{1,5},{2,6},{3,7},{4,0},{5,1},{6,2},{7,3},{8,12},{9,13},{10,... | collective-permute-start | bytes 2654216 | tf_op jit(solution)/shard_map/ppermute | solution.py:525
  135.6 41.4 %collective-permute-start.11 = (bf16[3,192,768]{2,1,0:T(8,128)(2,1)S(1)}, bf16[3,192,768]{2,1,0:T(8,128)(2,1)}, u32[]{:S(2)}, u32[]{:S(2)}) collective-permute-start(bf16[3,192,768]{2,1,0:T(8,128)(2,1)S(1)} %collective-permute-done.9.refs_2_), channel_id=1, source_target_pairs={{0,4},{1,5},{2,6},{3,7},{4,0},{5,1},{6,2},{7,3},{8,12},{9,13},{10,... | collective-permute-start | bytes 2654216 | tf_op jit(solution)/shard_map/ppermute | solution.py:525
  136.8 31.9 %collective-permute-start.26 = (bf16[3,96,768]{2,1,0:T(8,128)(2,1)S(1)}, bf16[3,96,768]{2,1,0:T(8,128)(2,1)}, u32[]{:S(2)}, u32[]{:S(2)}) collective-permute-start(bf16[3,96,768]{2,1,0:T(8,128)(2,1)S(1)} %collective-permute-done.25.refs_4_), channel_id=1, source_target_pairs={{0,1},{1,0},{2,3},{3,2},{4,5},{5,4},{6,7},{7,6},{8,9},{9,8},{10,11... | collective-permute-start | bytes 1327112 | tf_op jit(solution)/shard_map/ppermute | solution.py:525
  420.0 37.7 %collective-permute-start.45 = (bf16[4,4,96,768]{3,2,1,0:T(8,128)(2,1)}, bf16[4,4,96,768]{3,2,1,0:T(8,128)(2,1)}, u32[]{:S(2)}, u32[]{:S(2)}) collective-permute-start(bf16[4,4,96,768]{3,2,1,0:T(8,128)(2,1)} %fusion.22), channel_id=1, source_target_pairs={{0,1},{1,0},{2,3},{3,2},{4,5},{5,4},{6,7},{7,6},{8,9},{9,8},{10,11... | collective-permute-start | bytes 7077896 | tf_op jit(solution)/shard_map/ppermute | solution.py:525
  526.5 35.8 %collective-permute-start.49 = (bf16[4,2,24,3072]{3,2,0,1:T(8,128)(2,1)}, bf16[4,2,24,3072]{3,2,0,1:T(8,128)(2,1)}, u32[]{:S(2)}, u32[]{:S(2)}) collective-permute-start(bf16[4,2,24,3072]{3,2,0,1:T(8,128)(2,1)} %fusion.34), channel_id=1, source_target_pairs={{0,4},{1,5},{2,6},{3,7},{4,0},{5,1},{6,2},{7,3},{8,12},{9,13},{10,... | collective-permute-start | bytes 3538952 | tf_op jit(solution)/shard_map/ppermute | solution.py:525
  526.7 37.3 %collective-permute-start.50 = (bf16[4,2,24,3072]{3,2,0,1:T(8,128)(2,1)}, bf16[4,2,24,3072]{3,2,0,1:T(8,128)(2,1)}, u32[]{:S(2)}, u32[]{:S(2)}) collective-permute-start(bf16[4,2,24,3072]{3,2,0,1:T(8,128)(2,1)} %fusion.35), channel_id=1, source_target_pairs={{0,2},{1,3},{2,0},{3,1},{4,6},{5,7},{6,4},{7,5},{8,10},{9,11},{10,... | collective-permute-start | bytes 3538952 | tf_op jit(solution)/shard_map/ppermute | solution.py:525
  658.5 53.9 %collective-permute-start.54 = (bf16[4,4,24,3072]{3,2,1,0:T(8,128)(2,1)}, bf16[4,4,24,3072]{3,2,1,0:T(8,128)(2,1)}, u32[]{:S(2)}, u32[]{:S(2)}) collective-permute-start(bf16[4,4,24,3072]{3,2,1,0:T(8,128)(2,1)} %fusion.24), channel_id=1, source_target_pairs={{0,1},{1,0},{2,3},{3,2},{4,5},{5,4},{6,7},{7,6},{8,9},{9,8},{10,11... | collective-permute-start | bytes 7077896 | tf_op jit(solution)/shard_map/ppermute | solution.py:525
  666.3 44.5 %collective-permute-start.71 = (bf16[24,3072]{1,0:T(8,128)(2,1)S(1)}, bf16[24,3072]{1,0:T(8,128)(2,1)S(1)}, u32[]{:S(2)}, u32[]{:S(2)}) collective-permute-start(bf16[24,3072]{1,0:T(8,128)(2,1)S(1)} %copy-done.95), channel_id=1, source_target_pairs={{0,16},{8,24},{16,0},{24,8},{1,17},{9,25},{17,1},{25,9},{2,18},{10... | collective-permute-start | bytes 442376 | tf_op jit(solution)/shard_map/ppermute | solution.py:530
  683.3 33.9 %collective-permute-start.69 = (bf16[24,3072]{1,0:T(8,128)(2,1)S(1)}, bf16[24,3072]{1,0:T(8,128)(2,1)S(1)}, u32[]{:S(2)}, u32[]{:S(2)}) collective-permute-start(bf16[24,3072]{1,0:T(8,128)(2,1)S(1)} %copy-done.94), channel_id=1, source_target_pairs={{0,24},{8,0},{16,8},{24,16},{1,25},{9,1},{17,9},{25,17},{2,26},{10... | collective-permute-start | bytes 442376 | tf_op jit(solution)/shard_map/ppermute | solution.py:530
  686.6 54.5 %collective-permute-start.68 = (bf16[24,3072]{1,0:T(8,128)(2,1)S(1)}, bf16[24,3072]{1,0:T(8,128)(2,1)S(1)}, u32[]{:S(2)}, u32[]{:S(2)}) collective-permute-start(bf16[24,3072]{1,0:T(8,128)(2,1)S(1)} %copy-done.93), channel_id=1, source_target_pairs={{0,16},{8,24},{16,0},{24,8},{1,17},{9,25},{17,1},{25,9},{2,18},{10... | collective-permute-start | bytes 442376 | tf_op jit(solution)/shard_map/ppermute | solution.py:530
  759.6 41.1 %collective-permute-start.58 = (bf16[24,3072]{1,0:T(8,128)(2,1)S(1)}, bf16[24,3072]{1,0:T(8,128)(2,1)S(1)}, u32[]{:S(2)}, u32[]{:S(2)}) collective-permute-start(bf16[24,3072]{1,0:T(8,128)(2,1)S(1)} %get-tuple-element.219), channel_id=1, source_target_pairs={{0,16},{8,24},{16,0},{24,8},{1,17},{9,25},{17,1},{25,9},{2,18},{10... | collective-permute-start | bytes 442376 | tf_op jit(solution)/shard_map/ppermute | solution.py:530
  770.3 32.5 %collective-permute-start.57 = (bf16[24,3072]{1,0:T(8,128)(2,1)S(1)}, bf16[24,3072]{1,0:T(8,128)(2,1)S(1)}, u32[]{:S(2)}, u32[]{:S(2)}) collective-permute-start(bf16[24,3072]{1,0:T(8,128)(2,1)S(1)} %get-tuple-element.217), channel_id=1, source_target_pairs={{0,8},{8,16},{16,24},{24,0},{1,9},{9,17},{17,25},{25,1},{2,10},{10... | collective-permute-start | bytes 442376 | tf_op jit(solution)/shard_map/ppermute | solution.py:530
  777.2 32.7 %collective-permute-start.78 = (bf16[24,9216]{1,0:T(8,128)(2,1)S(1)}, bf16[24,9216]{1,0:T(8,128)(2,1)S(1)}, u32[]{:S(2)}, u32[]{:S(2)}) collective-permute-start(bf16[24,9216]{1,0:T(8,128)(2,1)S(1)} %collective-permute-done.77.refs_2_), channel_id=1, source_target_pairs={{0,1},{1,0},{2,3},{3,2},{4,5},{5,4},{6,7},{7,6},{8,9},{9,8},{10,11... | collective-permute-start | bytes 1327112 | tf_op jit(solution)/shard_map/ppermute | solution.py:525
  778.2 31.7 %collective-permute-start.80 = (bf16[24,9216]{1,0:T(8,128)(2,1)S(1)}, bf16[24,9216]{1,0:T(8,128)(2,1)S(1)}, u32[]{:S(2)}, u32[]{:S(2)}) collective-permute-start(bf16[24,9216]{1,0:T(8,128)(2,1)S(1)} %collective-permute-done.79.refs_4_), channel_id=1, source_target_pairs={{0,1},{1,0},{2,3},{3,2},{4,5},{5,4},{6,7},{7,6},{8,9},{9,8},{10,11... | collective-permute-start | bytes 1327112 | tf_op jit(solution)/shard_map/ppermute | solution.py:525
  877.1 32.8 %collective-permute-start.84 = (bf16[2,960,384]{2,1,0:T(8,128)(2,1)S(1)}, bf16[2,960,384]{2,1,0:T(8,128)(2,1)S(1)}, u32[]{:S(2)}, u32[]{:S(2)}) collective-permute-start(bf16[2,960,384]{2,1,0:T(8,128)(2,1)S(1)} %fusion.31), channel_id=1, source_target_pairs={{0,2},{1,3},{2,0},{3,1},{4,6},{5,7},{6,4},{7,5},{8,10},{9,11},{10,... | collective-permute-start | bytes 4423688 | tf_op jit(solution)/shard_map/ppermute | solution.py:525
  878.1 34.1 %collective-permute-start.86 = (bf16[2,960,384]{2,1,0:T(8,128)(2,1)S(1)}, bf16[2,960,384]{2,1,0:T(8,128)(2,1)S(1)}, u32[]{:S(2)}, u32[]{:S(2)}) collective-permute-start(bf16[2,960,384]{2,1,0:T(8,128)(2,1)S(1)} %fusion.30), channel_id=1, source_target_pairs={{0,4},{1,5},{2,6},{3,7},{4,0},{5,1},{6,2},{7,3},{8,12},{9,13},{10,... | collective-permute-start | bytes 4423688 | tf_op jit(solution)/shard_map/ppermute | solution.py:525
  956.1 38.7 %collective-permute-start.93 = (bf16[960,384]{1,0:T(8,128)(2,1)}, bf16[960,384]{1,0:T(8,128)(2,1)}, u32[]{:S(2)}, u32[]{:S(2)}) collective-permute-start(bf16[960,384]{1,0:T(8,128)(2,1)} %get-tuple-element.150.rest_0_), channel_id=1, source_target_pairs={{0,1},{1,0},{2,3},{3,2},{4,5},{5,4},{6,7},{7,6},{8,9},{9,8},{10,11... | collective-permute-start | bytes 2211848 | tf_op jit(solution)/shard_map/ppermute | solution.py:525
  957.9 37.5 %collective-permute-start.95 = (bf16[960,384]{1,0:T(8,128)(2,1)}, bf16[960,384]{1,0:T(8,128)(2,1)}, u32[]{:S(2)}, u32[]{:S(2)}) collective-permute-start(bf16[960,384]{1,0:T(8,128)(2,1)} %get-tuple-element.150.rest_0_), channel_id=1, source_target_pairs={{0,2},{1,3},{2,0},{3,1},{4,6},{5,7},{6,4},{7,5},{8,10},{9,11},{10,... | collective-permute-start | bytes 2211848 | tf_op jit(solution)/shard_map/ppermute | solution.py:525
  958.4 51.5 %collective-permute-start.94 = (bf16[960,384]{1,0:T(8,128)(2,1)}, bf16[960,384]{1,0:T(8,128)(2,1)}, u32[]{:S(2)}, u32[]{:S(2)}) collective-permute-start(bf16[960,384]{1,0:T(8,128)(2,1)} %get-tuple-element.151.rest_1_), channel_id=1, source_target_pairs={{0,1},{1,0},{2,3},{3,2},{4,5},{5,4},{6,7},{7,6},{8,9},{9,8},{10,11... | collective-permute-start | bytes 2211848 | tf_op jit(solution)/shard_map/ppermute | solution.py:525
  958.8 38.5 %collective-permute-start.97 = (bf16[960,384]{1,0:T(8,128)(2,1)}, bf16[960,384]{1,0:T(8,128)(2,1)}, u32[]{:S(2)}, u32[]{:S(2)}) collective-permute-start(bf16[960,384]{1,0:T(8,128)(2,1)} %get-tuple-element.151.rest_1_), channel_id=1, source_target_pairs={{0,2},{1,3},{2,0},{3,1},{4,6},{5,7},{6,4},{7,5},{8,10},{9,11},{10,... | collective-permute-start | bytes 2211848 | tf_op jit(solution)/shard_map/ppermute | solution.py:525
  959.8 36.9 %collective-permute-start.99 = (bf16[960,384]{1,0:T(8,128)(2,1)}, bf16[960,384]{1,0:T(8,128)(2,1)}, u32[]{:S(2)}, u32[]{:S(2)}) collective-permute-start(bf16[960,384]{1,0:T(8,128)(2,1)} %get-tuple-element.150.rest_0_), channel_id=1, source_target_pairs={{0,4},{1,5},{2,6},{3,7},{4,0},{5,1},{6,2},{7,3},{8,12},{9,13},{10,... | collective-permute-start | bytes 2211848 | tf_op jit(solution)/shard_map/ppermute | solution.py:525
  1009.9 40.2 %collective-permute-start.98 = (bf16[960,384]{1,0:T(8,128)(2,1)}, bf16[960,384]{1,0:T(8,128)(2,1)S(1)}, u32[]{:S(2)}, u32[]{:S(2)}) collective-permute-start(bf16[960,384]{1,0:T(8,128)(2,1)} %collective-permute-done.97.rest_3_), channel_id=1, source_target_pairs={{0,1},{1,0},{2,3},{3,2},{4,5},{5,4},{6,7},{7,6},{8,9},{9,8},{10,11... | collective-permute-start | bytes 2211848 | tf_op jit(solution)/shard_map/ppermute | solution.py:525
  1012.2 37.9 %collective-permute-start.100 = (bf16[960,384]{1,0:T(8,128)(2,1)}, bf16[960,384]{1,0:T(8,128)(2,1)S(1)}, u32[]{:S(2)}, u32[]{:S(2)}) collective-permute-start(bf16[960,384]{1,0:T(8,128)(2,1)} %collective-permute-done.99.rest_4_), channel_id=1, source_target_pairs={{0,1},{1,0},{2,3},{3,2},{4,5},{5,4},{6,7},{7,6},{8,9},{9,8},{10,11... | collective-permute-start | bytes 2211848 | tf_op jit(solution)/shard_map/ppermute | solution.py:525
  1015.5 34.7 %collective-permute-start.102 = (bf16[960,384]{1,0:T(8,128)(2,1)}, bf16[960,384]{1,0:T(8,128)(2,1)S(1)}, u32[]{:S(2)}, u32[]{:S(2)}) collective-permute-start(bf16[960,384]{1,0:T(8,128)(2,1)} %collective-permute-done.101.rest_5_), channel_id=1, source_target_pairs={{0,1},{1,0},{2,3},{3,2},{4,5},{5,4},{6,7},{7,6},{8,9},{9,8},{10,11... | collective-permute-start | bytes 2211848 | tf_op jit(solution)/shard_map/ppermute | solution.py:525
  1015.6 34.6 %collective-permute-start.104 = (bf16[960,384]{1,0:T(8,128)(2,1)}, bf16[960,384]{1,0:T(8,128)(2,1)S(1)}, u32[]{:S(2)}, u32[]{:S(2)}) collective-permute-start(bf16[960,384]{1,0:T(8,128)(2,1)} %collective-permute-done.103.rest_6_), channel_id=1, source_target_pairs={{0,1},{1,0},{2,3},{3,2},{4,5},{5,4},{6,7},{7,6},{8,9},{9,8},{10,11... | collective-permute-start | bytes 2211848 | tf_op jit(solution)/shard_map/ppermute | solution.py:525
  (216 other events, 3596.8 us)
Sparse Core Ops, SparseCore 0:
  56.4 122.9 reduce-scatter.1
  660.9 155.0 all-gather.1

commit v7 on v6

--- a/solution.py
+++ b/solution.py
@@ -306,10 +306,11 @@
     )(starts, places, order, table)
 
 
-def table_grad_kernel(core_ref, starts_ref, codes_ref, order_ref, dlogits_ref, chosen_ref, embed_ref, out_ref, rows, sums):
+def table_grad_kernel(chunks_ref, starts_ref, codes_ref, order_ref, dlogits_ref, chosen_ref, embed_ref, *refs):
+    rows, sums = refs[-2:]
     step = pl.program_id(0)
     count, width = embed_ref.shape
-    block = out_ref.shape[1]
+    block = dlogits_ref.shape[0]
 
     @pl.when(step == 0)
     def _():
@@ -317,7 +318,7 @@
             rows[start : start + CHUNK, :] = embed_ref[start : start + CHUNK, :].astype(jnp.float32)
 
     sums[...] = jnp.zeros_like(sums)
-    chunk = 2 * step + core_ref[0]
+    chunk = chunks_ref[step]
     first, last = starts_ref[chunk], starts_ref[chunk + 1]
 
     def eight(turn, running):
@@ -331,46 +332,87 @@
 
     lax.fori_loop(0, (last - first + 7) // 8, eight, jnp.zeros((1, width), jnp.float32))
     product = jnp.dot(dlogits_ref[...], chosen_ref[...], preferred_element_type=jnp.float32)
-    out_ref[0] = (product + sums[:block, :]).astype(out_ref.dtype)
-
-
-def table_grad_half(core, starts, codes, order, dlogits, chosen, embed, block, dtype):
+    result = product + sums[:block, :]
+    if len(refs) == 3:
+        refs[0][0] = result.astype(refs[0].dtype)
+        return
+    got_ref, sent_x, kept_x, sent_y, kept_y = refs[:-2]
+    result = result + got_ref[0].astype(jnp.float32)
+    left, right = result[:, : width // 2], result[:, width // 2 :]
+
+    @pl.when(step % 2 == 0)
+    def _():
+        sent_x[0] = left.astype(sent_x.dtype)
+
+    @pl.when(step % 2 == 1)
+    def _():
+        kept_x[0] = left
+
+    @pl.when(step < 2)
+    def _():
+        sent_y[0] = right.astype(sent_y.dtype)
+
+    @pl.when(step >= 2)
+    def _():
+        kept_y[0] = right
+
+
+def table_grad_chunks(chunks, starts, codes, order, dlogits, chosen, embed, block, dtype, got=None):
     count, width = embed.shape
     picked = chosen.shape[0]
-    chunks = dlogits.shape[0] // block // 2
+    steps = chunks.shape[0]
     fixed = lambda i, *_: (0, 0)
+    in_specs = [
+        pl.BlockSpec((block, picked), lambda i, chunks, *_: (chunks[i], 0)),
+        pl.BlockSpec((picked, width), fixed),
+        pl.BlockSpec((count, width), fixed, pipeline_mode=pl.Buffered(1)),
+    ]
+    whole = pl.BlockSpec((1, block, width), lambda i, *_: (i, 0, 0))
+    if got is None:
+        out_shape = jax.ShapeDtypeStruct((steps, block, width), dtype)
+        out_specs = whole
+    else:
+        in_specs.append(whole)
+        half = (1, block, width // 2)
+        by_y = lambda i, *_: (i // 2, 0, 0)
+        low = jax.ShapeDtypeStruct((2, block, width // 2), low_type)
+        high = jax.ShapeDtypeStruct((2, block, width // 2), jnp.float32)
+        out_shape = [low, high, low, high]
+        out_specs = [
+            pl.BlockSpec(half, by_y),
+            pl.BlockSpec(half, by_y),
+            pl.BlockSpec(half, lambda i, *_: (jnp.minimum(i, 1), 0, 0)),
+            pl.BlockSpec(half, lambda i, *_: (jnp.maximum(i - 2, 0), 0, 0)),
+        ]
     return pl.pallas_call(
         table_grad_kernel,
         grid_spec=pltpu.PrefetchScalarGridSpec(
             num_scalar_prefetch=4,
-            grid=(chunks,),
-            in_specs=[
-                pl.BlockSpec((block, picked), lambda i, core, *_: (2 * i + core[0], 0)),
-                pl.BlockSpec((picked, width), fixed),
-                pl.BlockSpec((count, width), fixed, pipeline_mode=pl.Buffered(1)),
-            ],
-            out_specs=pl.BlockSpec((1, block, width), lambda i, *_: (i, 0, 0)),
+            grid=(steps,),
+            in_specs=in_specs,
+            out_specs=out_specs,
             scratch_shapes=[
                 pltpu.VMEM((count, width), jnp.float32),
                 pltpu.VMEM((block + 8, width), jnp.float32),
             ],
         ),
-        out_shape=jax.ShapeDtypeStruct((chunks, block, width), dtype),
+        out_shape=out_shape,
         compiler_params=pltpu.CompilerParams(vmem_limit_bytes=vmem),
         cost_estimate=pl.CostEstimate(
-            flops=2 * chunks * block * picked * width, bytes_accessed=8 * chunks * block * width, transcendentals=0
+            flops=2 * steps * block * picked * width, bytes_accessed=8 * steps * block * width, transcendentals=0
         ),
-    )(core, starts, codes, order, dlogits, chosen, embed)
-
-
-def update_kernel(parts, slots_ref, scalars_ref, *rest):
-    pieces = rest[: 4 * parts]
-    table_ref, rows_ref, cols_ref = rest[4 * parts : 4 * parts + 3]
+    )(chunks, starts, codes, order, dlogits, chosen, embed, *(() if got is None else (got,)))
+
+
+def update_kernel(places, parts, slots_ref, scalars_ref, *rest):
+    given = len(places) * parts
+    pieces = rest[:given]
+    table_ref, rows_ref, cols_ref = rest[given : given + 3]
     grad_ref, new_ref, rows_new_ref = rest[-3:]
     factor, rate = scalars_ref[0], scalars_ref[1]
     decay = 1.0 - float(STEP) ** (-0.8)
     old = jnp.broadcast_to(rows_ref[0], (LANES, TILE)).T[:, 0:1]
-    for part in range(4):
+    for part in range(len(places)):
 
         @pl.when(pl.program_id(0) == part)
         def _(part=part):
@@ -383,27 +425,35 @@
             rows_new_ref[0] = jnp.broadcast_to(rows_new, (TILE, LANES)).T[0:1, :]
 
 
-def update(slots, scalars, pieces, table, rows, cols, so_far):
+def update(places, slots, scalars, pieces, table, rows, cols, so_far):
+    count = len(places)
     parts = len(pieces[0])
     block = pieces[0][0].shape[0]
     width = table.shape[1]
     steps = block // TILE
-    place = lambda p, i, slots: (slots[p] * steps + i, 0)
-    place3 = lambda p, i, slots: (slots[p] * steps + i, 0, 0)
+
+    def slot(p, slots):
+        at = slots[places[0]]
+        for j in range(1, count):
+            at = jnp.where(p == j, slots[places[j]], at)
+        return at
+
+    place = lambda p, i, slots: (slot(p, slots) * steps + i, 0)
+    place3 = lambda p, i, slots: (slot(p, slots) * steps + i, 0, 0)
 
     def own(part):
         return lambda p, i, slots: (jnp.where(p < part, 0, jnp.where(p > part, steps - 1, i)), 0)
 
     fixed = lambda p, i, slots: (0, 0)
     any_space = pl.BlockSpec(memory_space=pl.ANY)
-    given = 5 + 4 * parts
+    given = 5 + count * parts
     return pl.pallas_call(
-        functools.partial(update_kernel, parts),
+        functools.partial(update_kernel, places, parts),
         grid_spec=pltpu.PrefetchScalarGridSpec(
             num_scalar_prefetch=1,
-            grid=(4, steps),
+            grid=(count, steps),
             in_specs=[pl.BlockSpec(memory_space=pltpu.SMEM)]
-            + [pl.BlockSpec((TILE, piece.shape[1]), own(part)) for part in range(4) for piece in pieces[part]]
+            + [pl.BlockSpec((TILE, piece.shape[1]), own(part)) for part in range(count) for piece in pieces[part]]
             + [
                 pl.BlockSpec((TILE, width), place),
                 pl.BlockSpec((1, 1, TILE), place3),
@@ -422,9 +472,9 @@
         input_output_aliases={given: 0, given + 1: 1, given + 2: 2},
         compiler_params=pltpu.CompilerParams(vmem_limit_bytes=vmem),
         cost_estimate=pl.CostEstimate(
-            flops=40 * block * width, bytes_accessed=56 * block * width, transcendentals=4 * block * width
+            flops=10 * count * block * width, bytes_accessed=14 * count * block * width, transcendentals=0
         ),
-    )(slots, scalars, *[piece for four in pieces for piece in four], table, rows, cols, *so_far)
+    )(slots, scalars, *[piece for some in pieces for piece in some], table, rows, cols, *so_far)
 
 
 def stack_kernel(slots_ref, *refs):
@@ -860,11 +910,15 @@
     sides = []
     for stage in range(3):
         if stage:
-            sent = gate.plane(False) + up.plane(False) + down.members() if stage == 1 else gate.members() + up.members()
-            mixed_grad, sides[-1], _ = tie((mixed_grad, sides[-1], sent))
+            if stage == 1:
+                sent = gate.plane(False) + up.plane(False) + down.members()
+            else:
+                sent = gate.members() + up.members()
+            mixed_grad, sides[-1], _, down.came = tie((mixed_grad, sides[-1], sent, down.came))
         sides.append(
             attend_back(lengths, queries, keys, values, mixed_grad, log_sums, cosine, sine, stage * third, third)
         )
+    sides, gate.came, up.came = tie((sides, gate.came, up.came))
     joined_grad = jnp.concatenate([side for parts in zip(*sides) for side in parts], axis=1)
     first_grad = first_sum_grad + contract(joined_grad, near[:, : 3 * width], 1, 1)
     _, pull = jax.vjp(layer_norm, embed.astype(jnp.float32), norms[0], norms[1])
@@ -898,23 +952,22 @@
     group_embed, near_whole, far_whole, share_cols = tie((group_embed, near_whole, far_whole, share_cols))
 
     core = replica % 2
-    half_args = (starts, codes, padded_order, dlogits, group_chosen, group_embed, block)
-    heads = [Fold(0, (2, 4)), Fold(0, (4, 2))]
     middle = width // 2
+    rest = (starts, codes, padded_order, dlogits, group_chosen, group_embed, block)
     if quick:
-        sent = table_grad_half((1 - core)[None], *half_args, low_type)
-        got = flip(sent, 1)
-        value = table_grad_half(core[None], *half_args, jnp.float32) + got.astype(jnp.float32)
+        chunks = ((replica // 2) ^ jnp.arange(3, -1, -1, dtype=jnp.int32)) * 2
+        sent = table_grad_chunks(chunks + 1 - core, *rest, low_type)
+        sent_x, kept_x, sent_y, kept_y = table_grad_chunks(chunks + core, *rest, low_type, flip(sent, 1))
+        one = kept_x + flip(sent_x, 2).astype(jnp.float32)
+        two = kept_y + flip(sent_y, 4).astype(jnp.float32)
+        table_parts = [
+            one[1] + flip(one[0].astype(low_type), 4).astype(jnp.float32),
+            two[1] + flip(two[0].astype(low_type), 2).astype(jnp.float32),
+        ]
     else:
-        both = [table_grad_half(jnp.full((1,), j, jnp.int32), *half_args, jnp.float32) for j in range(2)]
-        value = jnp.stack(both, axis=1).reshape(replicas, block, width)
+        value = table_grad_chunks(jnp.arange(replicas, dtype=jnp.int32), *rest, jnp.float32)
         value = lax.psum_scatter(value, "rep", scatter_dimension=0)
-    for head, part in zip(heads, (value[..., :middle], value[..., middle:])):
-        head.value = part
-        head.plane(True)
-    for head in heads:
-        head.plane(False)
-    table_parts = [head.sum() for head in heads]
+        table_parts = [value[:, :middle], value[:, middle:]]
 
     old_rows = (table_rows, qkv_rows, out_rows, gu_rows, down_rows)
     old_cols = (table_cols, qkv_cols, out_cols, gu_cols, down_cols)
@@ -971,12 +1024,12 @@
                 blank(table.shape, jnp.float32),
                 blank((tiles, 1, TILE), jnp.float32),
             )
-            slots = slots_of()
-            for four in ((0, 2, 4, 6), (1, 3, 5, 7)):
+            for places in ((0,), (2, 4), (6,), (1, 3, 5, 7)):
                 so_far = update(
-                    jnp.stack([slots[part] for part in four]),
+                    places,
+                    slots_of(),
                     scalars,
-                    [[got[part] for got in have] for part in four],
+                    [[got[part] for got in have] for part in places],
                     table,
                     row_tiles,
                     lax.rsqrt(new_cols)[None, :],

time: 1090 us -> 1050 us (0.963)
  other arithmetic: 185 us -> 166 us
  starting transfers between devices: 154 us -> 138 us
  local copies, waits for them, and re-layouts: 102 us -> 89.5 us
    ppermute x33, waiting for transfers between devices: 116 us -> 57.1 us  [turn(): lax.ppermute(value, 'grp', [(i, (i + offset) % size) for i in range(size)])]
    ppermute x72, waiting for transfers between devices: 106 us -> 154 us  [flip(): return lax.ppermute(value, 'rep', [(i, i ^ bit) for i in range(size)])]
    ppermute x33, starting transfers between devices: 69.1 us -> 46.2 us  [turn(): lax.ppermute(value, 'grp', [(i, (i + offset) % size) for i in range(size)])]
    all_gather x1, waiting for transfers between devices: 0.01 us -> 15.5 us  [body(): group_embed = lax.all_gather(embed_low, 'grp', axis=0, tiled=True)]
    convert_element_type x16 -> x12, local copies, waits for them, and re-layouts: 22.7 us -> 18.2 us  [halve(): return (kept, sent.astype(low_type))]
    pallas_call x4 -> x6, Pallas kernels: 65.1 us -> 68.7 us  [the longest x4 38.7 us: update(): pl.pallas_call(functools.partial(update_kernel, places, parts), grid_spec...]
    unnamed x287 -> x285, local copies, waits for them, and re-layouts: 28 us -> 28.6 us
    add x14 -> x12, other arithmetic: 25.1 us -> 24.9 us  [sum(): return self.kept + self.got.astype(jnp.float32)]
  transfers between devices with their start and end apart: 109 -> 109, of which waited for: 30 -> 34; matrix products, arithmetic and copies ran while one was open for 20% -> 21% of each run, Pallas kernels for 12% -> 14%
where the time goes in v7:
time: 1050 us; the launch traced here: 1040 us
  Pallas kernels  246 us (23%)
  waiting for transfers between devices  229 us (22%)
  other arithmetic  166 us (16%)
  starting transfers between devices  138 us (13%)
  matrix products  137 us (13%)
  local copies, waits for them, and re-layouts  89.5 us (9%)
  between operations  32 us (3%)
    ppermute x72, waiting for transfers between devices, flip(): return lax.ppermute(value, 'rep', [(i, i ^ bit) for i in range(size)])  154 us
    dot_general x11, matrix products, contract(): lax.dot_general(left, right, (((left_dim,), (right_dim,)), ((), ())), pre...  111 us
    ppermute x72, starting transfers between devices, flip(): return lax.ppermute(value, 'rep', [(i, i ^ bit) for i in range(size)])  89.6 us
    pallas_call x3, Pallas kernels, attend_back(): pl.pallas_call(functools.partial(attend_back_kernel, first_pair), grid_sp...  65.4 us
    ppermute x33, waiting for transfers between devices, turn(): lax.ppermute(value, 'grp', [(i, (i + offset) % size) for i in range(size)])  57.1 us
    pallas_call x1, Pallas kernels, attend(): pl.pallas_call(attend_kernel, grid_spec=pltpu.PrefetchScalarGridSpec(num_...  47.7 us
    ppermute x33, starting transfers between devices, turn(): lax.ppermute(value, 'grp', [(i, (i + offset) % size) for i in range(size)])  46.2 us
    pallas_call x4, Pallas kernels, update(): pl.pallas_call(functools.partial(update_kernel, places, parts), grid_spec...  38.7 us
  transfers between devices with their start and end apart: 109, of which 34 were waited for; matrix products, arithmetic and copies ran while one was open for 21% of the time, Pallas kernels for 14%

profile of v7, /device:TPU:1, one launch (start us, length us, event | category | flops | bytes accessed | tf_op | source)
XLA Modules:
  0.0 1038.0 jit_solution(4597667104455577182)
XLA Ops:
  37.7 16.9 %shard_map.413 = bf16[4096,768]{1,0:T(8,128)(2,1)} custom-call(s32[9]{0:T(128)} %convert_reduce_fusion.1.starts_ref, s32[4096]{0:T(1024)} %copy-done.78, s32[4096]{0:T(1024)} %get-tuple-element.126.order_ref, f32[7632,768]{1,0:T(8,128)} %rest_8_.1), custom_call_target="tpu_custom_call" | custom-call | bytes 70336512 | tf_op jit(solution)/shard_map/pallas_call | solution.py:294
  73.1 12.9 %collective-permute-done.20 = bf16[96,768]{1,0:T(8,128)(2,1)S(1)} collective-permute-done((bf16[96,768]{1,0:T(8,128)(2,1)S(1)}, bf16[96,768]{1,0:T(8,128)(2,1)S(1)}, u32[]{:S(2)}, u32[]{:S(2)}) %collective-permute-start.20) | collective-permute-done | bytes 147488 | tf_op jit(solution)/shard_map/ppermute | solution.py:580
  98.5 25.6 %collective-permute-done.23.refs_2_ = bf16[3,96,768]{2,1,0:T(8,128)(2,1)S(1)} collective-permute-done((bf16[3,96,768]{2,1,0:T(8,128)(2,1)S(1)}, bf16[3,96,768]{2,1,0:T(8,128)(2,1)S(1)}, u32[]{:S(2)}, u32[]{:S(2)}) %collective-permute-start.23) | collective-permute-done | bytes 442400 | tf_op jit(solution)/shard_map/ppermute | solution.py:575
  146.8 8.6 convert_element_type.332
  160.4 8.2 shard_map.414.w_ref
  183.8 10.8 %shard_map.416 = bf16[768,6144]{1,0:T(8,128)(2,1)} custom-call(s32[4]{0:T(128)} %and_select_fusion.members_ref, s32[8]{0:T(128)} %iota_xor_fusion.slots_ref, f32[192,6144]{1,0:T(8,128)} %own_ref.1, bf16[3,192,768]{2,1,0:T(8,128)(2,1)} %copy-done.27, bf16[3,192,768]{2,1,0:T(8,128)(2,1)} %collective-permute-done.29.refs_1_, bf16[3,192,768]{2,1,0:T(8,128)(2,1)} %copy-done.42, ...), custom_call_target="tpu_custom_call" | custom-call | bytes 18874368 | tf_op jit(solution)/shard_map/pallas_call | solution.py:525
  196.3 9.2 shard_map.417
  205.5 47.7 %shard_map.418 = (bf16[1024,768]{1,0:T(8,128)(2,1)}, f32[6,2,1024]{2,1,0:T(2,128)}) custom-call(s32[1]{0:T(128)S(6)} %copy.145.length_ref, bf16[1024,768]{1,0:T(8,128)(2,1)} %get-tuple-element.144.q_ref, bf16[1024,768]{1,0:T(8,128)(2,1)} %get-tuple-element.145.k_ref, bf16[1024,768]{1,0:T(8,128)(2,1)} %get-tuple-element.146.v_ref), custom_call_target="tpu_custom_call" | custom-call | flops 12884901888 | bytes 6291456 | tf_op jit(solution)/shard_map/pallas_call | solution.py:138
  257.0 18.2 %fusion.113 = f32[1024,6144]{1,0:T(8,128)} fusion(bf16[768,6144]{1,0:T(8,128)(2,1)} %shard_map.416, f32[1024,768]{1,0:T(8,128)S(1)} %get-tuple-element.310, f32[768]{0:T(1024)S(1)} %get-tuple-element.239, f32[768]{0:T(1024)S(1)} %get-tuple-element.240, f32[1024]{0:T(1024)S(1)} %fusion.85, f32[1024]{0:T(1024)S(1)} %broadcast_multiply_fusion.1), kind=kOutput, calls=%fused_computation.313 | convolution fusion | flops 9667608576 | bytes 37763072 | tf_op jit(solution)/shard_map/dot_general | solution.py:855
  275.1 9.9 multiply_convert_fusion.1
  319.0 10.9 %select_reduce_fusion.1 = (f32[512]{0:T(512)S(1)}, f32[7680,512]{1,0:T(8,128)S(1)}) fusion(pred[7680]{0:T(1024)(128)(4,1)S(1)} %iota_compare_fusion.1, bf16[7680,768]{1,0:T(8,128)(2,1)} %pad.21, bf16[512,768]{1,0:T(8,128)(2,1)} %bitcast.21.chosen_ref), kind=kOutput, calls=%fused_computation.9 | convolution fusion | flops 6047661568 | bytes 28321280 | tf_op jit(solution)/shard_map/dot_general | solution.py:722
  352.1 11.8 %fusion.115 = f32[512,768]{1,0:T(8,128)S(1)} fusion(bf16[7680,512]{1,0:T(8,128)(2,1)S(1)} %multiply_convert_fusion.dlogits_ref, bf16[7680,768]{1,0:T(8,128)(2,1)} %pad.21), kind=kOutput, calls=%fused_computation.314 | convolution fusion | flops 6039797760 | bytes 21233664 | tf_op jit(solution)/shard_map/dot_general | solution.py:722
  373.1 23.1 %collective-permute-done.43 = f32[128,768]{1,0:T(8,128)S(1)} collective-permute-done((f32[128,768]{1,0:T(8,128)S(1)}, f32[128,768]{1,0:T(8,128)S(1)}, u32[]{:S(2)}, u32[]{:S(2)}) %collective-permute-start.43) | collective-permute-done | bytes 393248 | tf_op jit(solution)/shard_map/ppermute | solution.py:580
  407.3 8.9 fusion.96
  425.8 23.7 %fusion.32 = (f32[1024,3072]{1,0:T(8,128)}, f32[1024,3072]{1,0:T(8,128)}) fusion(f32[1024,6144]{1,0:T(8,128)} %fusion.113, bf16[3072,768]{1,0:T(8,128)(2,1)} %bitcast.280, f32[1024,768]{1,0:T(8,128)} %copy-done.31, f32[1024]{0:T(1024)S(1)} %negate_multiply_fusion.2), kind=kOutput, calls=%fused_computation.95 | convolution fusion | flops 4871159808 | bytes 58200064 | tf_op jit(solution)/shard_map/dot_general | solution.py:722
  449.5 9.4 add_convert_fusion
  467.4 8.7 fusion.6
  498.6 17.3 %add_add_fusion.4 = f32[1024,768]{1,0:T(8,128)} fusion(f32[1024,768]{1,0:T(8,128)} %copy-done.31, bf16[1024,6144]{1,0:T(8,128)(2,1)} %copy-done.3, bf16[768,6144]{1,0:T(8,128)(2,1)} %shard_map.416, f32[1024]{0:T(1024)S(1)} %negate_multiply_fusion.2), kind=kOutput, calls=%fused_computation.58 | convolution fusion | flops 9665249280 | bytes 28315648 | tf_op jit(solution)/shard_map/dot_general | solution.py:722
  541.2 21.7 %shard_map.419 = (bf16[1024,256]{1,0:T(8,128)(2,1)}, bf16[1024,256]{1,0:T(8,128)(2,1)}, bf16[1024,256]{1,0:T(8,128)(2,1)}) custom-call(s32[1]{0:T(128)S(6)} %copy.145.length_ref, bf16[1024,768]{1,0:T(8,128)(2,1)} %get-tuple-element.144.q_ref, bf16[1024,768]{1,0:T(8,128)(2,1)} %get-tuple-element.145.k_ref, bf16[1024,768]{1,0:T(8,128)(2,1)} %get-tuple-element.146.v_ref, ...), custom_call_target="tpu_custom_call" | custom-call | flops 10737418240 | bytes 4194304 | tf_op jit(solution)/shard_map/pallas_call | solution.py:223
  573.9 21.8 %shard_map.420 = (bf16[1024,256]{1,0:T(8,128)(2,1)}, bf16[1024,256]{1,0:T(8,128)(2,1)}, bf16[1024,256]{1,0:T(8,128)(2,1)}) custom-call(s32[1]{0:T(128)S(6)} %copy.145.length_ref, bf16[1024,768]{1,0:T(8,128)(2,1)} %get-tuple-element.144.q_ref, bf16[1024,768]{1,0:T(8,128)(2,1)} %get-tuple-element.145.k_ref, bf16[1024,768]{1,0:T(8,128)(2,1)} %get-tuple-element.146.v_ref, ...), custom_call_target="tpu_custom_call" | custom-call | flops 10737418240 | bytes 4194304 | tf_op jit(solution)/shard_map/pallas_call | solution.py:223
  606.8 21.9 %shard_map.421 = (bf16[1024,256]{1,0:T(8,128)(2,1)}, bf16[1024,256]{1,0:T(8,128)(2,1)}, bf16[1024,256]{1,0:T(8,128)(2,1)}) custom-call(s32[1]{0:T(128)S(6)} %copy.145.length_ref, bf16[1024,768]{1,0:T(8,128)(2,1)} %get-tuple-element.144.q_ref, bf16[1024,768]{1,0:T(8,128)(2,1)} %get-tuple-element.145.k_ref, bf16[1024,768]{1,0:T(8,128)(2,1)} %get-tuple-element.146.v_ref, ...), custom_call_target="tpu_custom_call" | custom-call | flops 10737418240 | bytes 4194304 | tf_op jit(solution)/shard_map/pallas_call | solution.py:223
  642.9 9.8 fusion.116
  680.8 25.3 %collective-permute-done.64 = bf16[4,2,24,3072]{3,2,0,1:T(8,128)(2,1)S(1)} collective-permute-done((bf16[4,2,24,3072]{3,2,0,1:T(8,128)(2,1)S(1)}, bf16[4,2,24,3072]{3,2,0,1:T(8,128)(2,1)S(1)}, u32[]{:S(2)}, u32[]{:S(2)}) %collective-permute-start.64) | collective-permute-done | bytes 1179680 | tf_op jit(solution)/shard_map/ppermute | solution.py:575
  741.4 12.5 %collective-permute-done.67 = bf16[24,3072]{1,0:T(8,128)(2,1)S(1)} collective-permute-done((bf16[24,3072]{1,0:T(8,128)(2,1)S(1)}, bf16[24,3072]{1,0:T(8,128)(2,1)S(1)}, u32[]{:S(2)}, u32[]{:S(2)}) %collective-permute-start.67) | collective-permute-done | bytes 147488 | tf_op jit(solution)/shard_map/ppermute | solution.py:580
  779.3 15.5 %all-gather.2.cloned.1.call-done.embed_ref = bf16[4096,768]{1,0:T(8,128)(2,1)} async-done(((bf16[1024,768]{1,0:T(8,128)(2,1)}), bf16[4096,768]{1,0:T(8,128)(2,1)}) %all-gather.2.cloned.1.call-update) | async-done | bytes 6291472 | tf_op jit(solution)/shard_map/all_gather | solution.py:928
  794.8 13.3 %shard_map.424 = bf16[4,960,768]{2,1,0:T(8,128)(2,1)} custom-call(s32[4]{0:T(128)} %add_subtract_fusion.chunks_ref, s32[9]{0:T(128)} %convert_reduce_fusion.1.starts_ref, s32[4104]{0:T(1024)} %pad.24.codes_ref, s32[4104]{0:T(1024)} %pad.25.order_ref, bf16[7680,512]{1,0:T(8,128)(2,1)} %copy-done, bf16[512,768]{1,0:T(8,128)(2,1)} %bitcast.21.chosen_ref, ...), custom_call_target="tpu_custom_call" | custom-call | flops 3019898880 | bytes 23592960 | tf_op jit(solution)/shard_map/pallas_call | solution.py:387
  809.6 8.9 collective-permute-done.83.refs_0_
  821.1 16.8 %shard_map.425 = (bf16[2,960,384]{2,1,0:T(8,128)(2,1)}, f32[2,960,384]{2,1,0:T(8,128)}, bf16[2,960,384]{2,1,0:T(8,128)(2,1)}, f32[2,960,384]{2,1,0:T(8,128)}) custom-call(s32[4]{0:T(128)} %broadcast_add_fusion.chunks_ref, s32[9]{0:T(128)} %convert_reduce_fusion.1.starts_ref, s32[4104]{0:T(1024)} %pad.24.codes_ref, s32[4104]{0:T(1024)} %pad.25.order_ref, ...), custom_call_target="tpu_custom_call" | custom-call | flops 3019898880 | bytes 23592960 | tf_op jit(solution)/shard_map/pallas_call | solution.py:387
  840.3 32.0 %collective-permute-done.84 = bf16[2,960,384]{2,1,0:T(8,128)(2,1)S(1)} collective-permute-done((bf16[2,960,384]{2,1,0:T(8,128)(2,1)}, bf16[2,960,384]{2,1,0:T(8,128)(2,1)S(1)}, u32[]{:S(2)}, u32[]{:S(2)}) %collective-permute-start.84) | collective-permute-done | bytes 1474592 | tf_op jit(solution)/shard_map/ppermute | solution.py:575
  977.8 8.6 collective-permute-done.105.rest_1_
  992.2 9.9 shard_map.430
  1009.3 17.8 %shard_map.432 = (f32[7632,768]{1,0:T(8,128)}, f32[7632,768]{1,0:T(8,128)}, f32[16,1,480]{2,1,0:T(1,128)}) custom-call(s32[8]{0:T(128)} %iota_xor_fusion.slots_ref, f32[2]{0:T(128)} %pad_maximum_fusion.9.scalars_ref, bf16[960,384]{1,0:T(8,128)(2,1)} %collective-permute-done.93.rest_0_, ...), custom_call_target="tpu_custom_call", output_to_operand_aliasing={{0}: (13, {}), {1}: (14, {}), {2}: (15, {})} | custom-call | flops 29491200 | bytes 41287680 | tf_op jit(solution)/shard_map/pallas_call | solution.py:450
  (696 shorter events, 488.4 us)
Async XLA Ops:
  7.2 187.4 %reduce-scatter.2.cloned.1.call-start = ((), (), s32[]{:S(2)}) async-start(), calls=%async_computation.1 | async-start | bytes 7864320 | tf_op jit(solution)/shard_map/reduce_scatter | solution.py:819
  19.6 35.0 %collective-permute-start.8 = (bf16[192,768]{1,0:T(8,128)(2,1)}, bf16[192,768]{1,0:T(8,128)(2,1)S(1)}, u32[]{:S(2)}, u32[]{:S(2)}) collective-permute-start(bf16[192,768]{1,0:T(8,128)(2,1)} %dynamic-slice_convert_fusion.6), channel_id=1, source_target_pairs={{0,24},{8,0},{16,8},{24,16},{1,25},{9,1},{17,9},{25,17},{2,26},{10... | collective-permute-start | bytes 884744 | tf_op jit(solution)/shard_map/ppermute | solution.py:580
  23.6 31.0 %collective-permute-start.7 = (bf16[192,768]{1,0:T(8,128)(2,1)}, bf16[192,768]{1,0:T(8,128)(2,1)S(1)}, u32[]{:S(2)}, u32[]{:S(2)}) collective-permute-start(bf16[192,768]{1,0:T(8,128)(2,1)} %dynamic-slice_convert_fusion.6), channel_id=1, source_target_pairs={{0,16},{8,24},{16,0},{24,8},{1,17},{9,25},{17,1},{25,9},{2,18},{10... | collective-permute-start | bytes 884744 | tf_op jit(solution)/shard_map/ppermute | solution.py:580
  55.7 739.1 %all-gather.2.cloned.1.call-start = ((), (), s32[]{:S(2)}) async-start(), calls=%async_computation.2 | async-start | bytes 7864320 | tf_op jit(solution)/shard_map/all_gather | solution.py:928
  93.4 42.5 %collective-permute-start.9 = (bf16[3,192,768]{2,1,0:T(8,128)(2,1)S(1)}, bf16[3,192,768]{2,1,0:T(8,128)(2,1)S(1)}, u32[]{:S(2)}, u32[]{:S(2)}) collective-permute-start(bf16[3,192,768]{2,1,0:T(8,128)(2,1)S(1)} %pad_maximum_fusion.1.refs_0_), channel_id=1, source_target_pairs={{0,2},{1,3},{2,0},{3,1},{4,6},{5,7},{6,4},{7,5},{8,10},{9,11},{10,... | collective-permute-start | bytes 2654216 | tf_op jit(solution)/shard_map/ppermute | solution.py:575
  94.8 30.5 %collective-permute-start.25 = (bf16[3,96,768]{2,1,0:T(8,128)(2,1)S(1)}, bf16[3,96,768]{2,1,0:T(8,128)(2,1)S(1)}, u32[]{:S(2)}, u32[]{:S(2)}) collective-permute-start(bf16[3,96,768]{2,1,0:T(8,128)(2,1)S(1)} %pad_maximum_fusion.6.refs_0_), channel_id=1, source_target_pairs={{0,4},{1,5},{2,6},{3,7},{4,0},{5,1},{6,2},{7,3},{8,12},{9,13},{10,... | collective-permute-start | bytes 1327112 | tf_op jit(solution)/shard_map/ppermute | solution.py:575
  96.0 37.7 %collective-permute-start.17 = (bf16[3,192,384]{2,1,0:T(8,128)(2,1)S(1)}, bf16[3,192,384]{2,1,0:T(8,128)(2,1)S(1)}, u32[]{:S(2)}, u32[]{:S(2)}) collective-permute-start(bf16[3,192,384]{2,1,0:T(8,128)(2,1)S(1)} %collective-permute-done.15.refs_4_), channel_id=1, source_target_pairs={{0,2},{1,3},{2,0},{3,1},{4,6},{5,7},{6,4},{7,5},{8,10},{9,11},{10,... | collective-permute-start | bytes 1327112 | tf_op jit(solution)/shard_map/ppermute | solution.py:575
  97.4 37.5 %collective-permute-start.14 = (bf16[3,192,384]{2,1,0:T(8,128)(2,1)S(1)}, bf16[3,192,384]{2,1,0:T(8,128)(2,1)S(1)}, u32[]{:S(2)}, u32[]{:S(2)}) collective-permute-start(bf16[3,192,384]{2,1,0:T(8,128)(2,1)S(1)} %collective-permute-done.13.refs_2_), channel_id=1, source_target_pairs={{0,1},{1,0},{2,3},{3,2},{4,5},{5,4},{6,7},{7,6},{8,9},{9,8},{10,11... | collective-permute-start | bytes 1327112 | tf_op jit(solution)/shard_map/ppermute | solution.py:575
  134.9 41.9 %collective-permute-start.10 = (bf16[3,192,768]{2,1,0:T(8,128)(2,1)S(1)}, bf16[3,192,768]{2,1,0:T(8,128)(2,1)S(1)}, u32[]{:S(2)}, u32[]{:S(2)}) collective-permute-start(bf16[3,192,768]{2,1,0:T(8,128)(2,1)S(1)} %pad_maximum_fusion.1.refs_0_), channel_id=1, source_target_pairs={{0,4},{1,5},{2,6},{3,7},{4,0},{5,1},{6,2},{7,3},{8,12},{9,13},{10,... | collective-permute-start | bytes 2654216 | tf_op jit(solution)/shard_map/ppermute | solution.py:575
  135.9 40.9 %collective-permute-start.11 = (bf16[3,192,768]{2,1,0:T(8,128)(2,1)S(1)}, bf16[3,192,768]{2,1,0:T(8,128)(2,1)}, u32[]{:S(2)}, u32[]{:S(2)}) collective-permute-start(bf16[3,192,768]{2,1,0:T(8,128)(2,1)S(1)} %collective-permute-done.9.refs_2_), channel_id=1, source_target_pairs={{0,4},{1,5},{2,6},{3,7},{4,0},{5,1},{6,2},{7,3},{8,12},{9,13},{10,... | collective-permute-start | bytes 2654216 | tf_op jit(solution)/shard_map/ppermute | solution.py:575
  136.9 31.7 %collective-permute-start.26 = (bf16[3,96,768]{2,1,0:T(8,128)(2,1)S(1)}, bf16[3,96,768]{2,1,0:T(8,128)(2,1)}, u32[]{:S(2)}, u32[]{:S(2)}) collective-permute-start(bf16[3,96,768]{2,1,0:T(8,128)(2,1)S(1)} %collective-permute-done.25.refs_4_), channel_id=1, source_target_pairs={{0,1},{1,0},{2,3},{3,2},{4,5},{5,4},{6,7},{7,6},{8,9},{9,8},{10,11... | collective-permute-start | bytes 1327112 | tf_op jit(solution)/shard_map/ppermute | solution.py:575
  365.7 30.5 %collective-permute-start.43 = (f32[128,768]{1,0:T(8,128)S(1)}, f32[128,768]{1,0:T(8,128)S(1)}, u32[]{:S(2)}, u32[]{:S(2)}) collective-permute-start(f32[128,768]{1,0:T(8,128)S(1)} %get-tuple-element.276), channel_id=1, source_target_pairs={{0,16},{8,24},{16,0},{24,8},{1,17},{9,25},{17,1},{25,9},{2,18},{10... | collective-permute-start | bytes 1179656 | tf_op jit(solution)/shard_map/ppermute | solution.py:580
  365.7 31.3 %collective-permute-start.42 = (f32[128,768]{1,0:T(8,128)S(1)}, f32[128,768]{1,0:T(8,128)}, u32[]{:S(2)}, u32[]{:S(2)}) collective-permute-start(f32[128,768]{1,0:T(8,128)S(1)} %get-tuple-element.274), channel_id=1, source_target_pairs={{0,8},{8,16},{16,24},{24,0},{1,9},{9,17},{17,25},{25,1},{2,10},{10... | collective-permute-start | bytes 1179656 | tf_op jit(solution)/shard_map/ppermute | solution.py:580
  421.4 37.5 %collective-permute-start.45 = (bf16[4,4,96,768]{3,2,1,0:T(8,128)(2,1)}, bf16[4,4,96,768]{3,2,1,0:T(8,128)(2,1)}, u32[]{:S(2)}, u32[]{:S(2)}) collective-permute-start(bf16[4,4,96,768]{3,2,1,0:T(8,128)(2,1)} %fusion.22), channel_id=1, source_target_pairs={{0,1},{1,0},{2,3},{3,2},{4,5},{5,4},{6,7},{7,6},{8,9},{9,8},{10,11... | collective-permute-start | bytes 7077896 | tf_op jit(solution)/shard_map/ppermute | solution.py:575
  489.2 31.7 %collective-permute-start.46 = (bf16[4,4,24,3072]{3,2,0,1:T(8,128)(2,1)}, bf16[4,4,24,3072]{3,2,0,1:T(8,128)(2,1)}, u32[]{:S(2)}, u32[]{:S(2)}) collective-permute-start(bf16[4,4,24,3072]{3,2,0,1:T(8,128)(2,1)} %fusion.21), channel_id=1, source_target_pairs={{0,1},{1,0},{2,3},{3,2},{4,5},{5,4},{6,7},{7,6},{8,9},{9,8},{10,11... | collective-permute-start | bytes 7077896 | tf_op jit(solution)/shard_map/ppermute | solution.py:575
  491.2 34.9 %collective-permute-start.47 = (bf16[4,4,24,3072]{3,2,1,0:T(8,128)(2,1)}, bf16[4,4,24,3072]{3,2,1,0:T(8,128)(2,1)}, u32[]{:S(2)}, u32[]{:S(2)}) collective-permute-start(bf16[4,4,24,3072]{3,2,1,0:T(8,128)(2,1)} %fusion.23), channel_id=1, source_target_pairs={{0,1},{1,0},{2,3},{3,2},{4,5},{5,4},{6,7},{7,6},{8,9},{9,8},{10,11... | collective-permute-start | bytes 7077896 | tf_op jit(solution)/shard_map/ppermute | solution.py:575
  516.8 57.1 %collective-permute-start.52 = (bf16[96,768]{1,0:T(8,128)(2,1)}, bf16[96,768]{1,0:T(8,128)(2,1)}, u32[]{:S(2)}, u32[]{:S(2)}) collective-permute-start(bf16[96,768]{1,0:T(8,128)(2,1)} %get-tuple-element.288), channel_id=1, source_target_pairs={{0,8},{8,16},{16,24},{24,0},{1,9},{9,17},{17,25},{25,1},{2,10},{10... | collective-permute-start | bytes 442376 | tf_op jit(solution)/shard_map/ppermute | solution.py:580
  516.9 57.1 %collective-permute-start.53 = (bf16[96,768]{1,0:T(8,128)(2,1)}, bf16[96,768]{1,0:T(8,128)(2,1)}, u32[]{:S(2)}, u32[]{:S(2)}) collective-permute-start(bf16[96,768]{1,0:T(8,128)(2,1)} %get-tuple-element.287), channel_id=1, source_target_pairs={{0,16},{8,24},{16,0},{24,8},{1,17},{9,25},{17,1},{25,9},{2,18},{10... | collective-permute-start | bytes 442376 | tf_op jit(solution)/shard_map/ppermute | solution.py:580
  518.6 55.4 %collective-permute-start.54 = (bf16[96,768]{1,0:T(8,128)(2,1)}, bf16[96,768]{1,0:T(8,128)(2,1)}, u32[]{:S(2)}, u32[]{:S(2)}) collective-permute-start(bf16[96,768]{1,0:T(8,128)(2,1)} %get-tuple-element.286), channel_id=1, source_target_pairs={{0,24},{8,0},{16,8},{24,16},{1,25},{9,1},{17,9},{25,17},{2,26},{10... | collective-permute-start | bytes 442376 | tf_op jit(solution)/shard_map/ppermute | solution.py:580
  531.3 36.0 %collective-permute-start.49 = (bf16[4,2,24,3072]{3,2,0,1:T(8,128)(2,1)}, bf16[4,2,24,3072]{3,2,0,1:T(8,128)(2,1)}, u32[]{:S(2)}, u32[]{:S(2)}) collective-permute-start(bf16[4,2,24,3072]{3,2,0,1:T(8,128)(2,1)} %fusion.34), channel_id=1, source_target_pairs={{0,4},{1,5},{2,6},{3,7},{4,0},{5,1},{6,2},{7,3},{8,12},{9,13},{10,... | collective-permute-start | bytes 3538952 | tf_op jit(solution)/shard_map/ppermute | solution.py:575
  531.5 37.4 %collective-permute-start.50 = (bf16[4,2,24,3072]{3,2,0,1:T(8,128)(2,1)}, bf16[4,2,24,3072]{3,2,0,1:T(8,128)(2,1)}, u32[]{:S(2)}, u32[]{:S(2)}) collective-permute-start(bf16[4,2,24,3072]{3,2,0,1:T(8,128)(2,1)} %fusion.35), channel_id=1, source_target_pairs={{0,2},{1,3},{2,0},{3,1},{4,6},{5,7},{6,4},{7,5},{8,10},{9,11},{10,... | collective-permute-start | bytes 3538952 | tf_op jit(solution)/shard_map/ppermute | solution.py:575
  720.7 33.2 %collective-permute-start.67 = (bf16[24,3072]{1,0:T(8,128)(2,1)S(1)}, bf16[24,3072]{1,0:T(8,128)(2,1)S(1)}, u32[]{:S(2)}, u32[]{:S(2)}) collective-permute-start(bf16[24,3072]{1,0:T(8,128)(2,1)S(1)} %get-tuple-element.279), channel_id=1, source_target_pairs={{0,16},{8,24},{16,0},{24,8},{1,17},{9,25},{17,1},{25,9},{2,18},{10... | collective-permute-start | bytes 442376 | tf_op jit(solution)/shard_map/ppermute | solution.py:580
  721.4 33.9 %collective-permute-start.66 = (bf16[24,3072]{1,0:T(8,128)(2,1)S(1)}, bf16[24,3072]{1,0:T(8,128)(2,1)S(1)}, u32[]{:S(2)}, u32[]{:S(2)}) collective-permute-start(bf16[24,3072]{1,0:T(8,128)(2,1)S(1)} %get-tuple-element.277), channel_id=1, source_target_pairs={{0,8},{8,16},{16,24},{24,0},{1,9},{9,17},{17,25},{25,1},{2,10},{10... | collective-permute-start | bytes 442376 | tf_op jit(solution)/shard_map/ppermute | solution.py:580
  837.8 34.5 %collective-permute-start.84 = (bf16[2,960,384]{2,1,0:T(8,128)(2,1)}, bf16[2,960,384]{2,1,0:T(8,128)(2,1)S(1)}, u32[]{:S(2)}, u32[]{:S(2)}) collective-permute-start(bf16[2,960,384]{2,1,0:T(8,128)(2,1)} %get-tuple-element.198), channel_id=1, source_target_pairs={{0,2},{1,3},{2,0},{3,1},{4,6},{5,7},{6,4},{7,5},{8,10},{9,11},{10,... | collective-permute-start | bytes 4423688 | tf_op jit(solution)/shard_map/ppermute | solution.py:575
  838.8 37.5 %collective-permute-start.86 = (bf16[2,960,384]{2,1,0:T(8,128)(2,1)}, bf16[2,960,384]{2,1,0:T(8,128)(2,1)S(1)}, u32[]{:S(2)}, u32[]{:S(2)}) collective-permute-start(bf16[2,960,384]{2,1,0:T(8,128)(2,1)} %get-tuple-element.200), channel_id=1, source_target_pairs={{0,4},{1,5},{2,6},{3,7},{4,0},{5,1},{6,2},{7,3},{8,12},{9,13},{10,... | collective-permute-start | bytes 4423688 | tf_op jit(solution)/shard_map/ppermute | solution.py:575
  917.9 37.0 %collective-permute-start.93 = (bf16[960,384]{1,0:T(8,128)(2,1)}, bf16[960,384]{1,0:T(8,128)(2,1)}, u32[]{:S(2)}, u32[]{:S(2)}) collective-permute-start(bf16[960,384]{1,0:T(8,128)(2,1)} %get-tuple-element.206.rest_0_), channel_id=1, source_target_pairs={{0,1},{1,0},{2,3},{3,2},{4,5},{5,4},{6,7},{7,6},{8,9},{9,8},{10,11... | collective-permute-start | bytes 2211848 | tf_op jit(solution)/shard_map/ppermute | solution.py:575
  919.1 36.7 %collective-permute-start.95 = (bf16[960,384]{1,0:T(8,128)(2,1)}, bf16[960,384]{1,0:T(8,128)(2,1)}, u32[]{:S(2)}, u32[]{:S(2)}) collective-permute-start(bf16[960,384]{1,0:T(8,128)(2,1)} %get-tuple-element.206.rest_0_), channel_id=1, source_target_pairs={{0,2},{1,3},{2,0},{3,1},{4,6},{5,7},{6,4},{7,5},{8,10},{9,11},{10,... | collective-permute-start | bytes 2211848 | tf_op jit(solution)/shard_map/ppermute | solution.py:575
  920.6 54.4 %collective-permute-start.94 = (bf16[960,384]{1,0:T(8,128)(2,1)}, bf16[960,384]{1,0:T(8,128)(2,1)}, u32[]{:S(2)}, u32[]{:S(2)}) collective-permute-start(bf16[960,384]{1,0:T(8,128)(2,1)} %get-tuple-element.207.rest_1_), channel_id=1, source_target_pairs={{0,1},{1,0},{2,3},{3,2},{4,5},{5,4},{6,7},{7,6},{8,9},{9,8},{10,11... | collective-permute-start | bytes 2211848 | tf_op jit(solution)/shard_map/ppermute | solution.py:575
  920.9 39.1 %collective-permute-start.97 = (bf16[960,384]{1,0:T(8,128)(2,1)}, bf16[960,384]{1,0:T(8,128)(2,1)}, u32[]{:S(2)}, u32[]{:S(2)}) collective-permute-start(bf16[960,384]{1,0:T(8,128)(2,1)} %get-tuple-element.207.rest_1_), channel_id=1, source_target_pairs={{0,2},{1,3},{2,0},{3,1},{4,6},{5,7},{6,4},{7,5},{8,10},{9,11},{10,... | collective-permute-start | bytes 2211848 | tf_op jit(solution)/shard_map/ppermute | solution.py:575
  920.9 37.7 %collective-permute-start.99 = (bf16[960,384]{1,0:T(8,128)(2,1)}, bf16[960,384]{1,0:T(8,128)(2,1)}, u32[]{:S(2)}, u32[]{:S(2)}) collective-permute-start(bf16[960,384]{1,0:T(8,128)(2,1)} %get-tuple-element.206.rest_0_), channel_id=1, source_target_pairs={{0,4},{1,5},{2,6},{3,7},{4,0},{5,1},{6,2},{7,3},{8,12},{9,13},{10,... | collective-permute-start | bytes 2211848 | tf_op jit(solution)/shard_map/ppermute | solution.py:575
  975.0 32.6 %collective-permute-start.98 = (bf16[960,384]{1,0:T(8,128)(2,1)}, bf16[960,384]{1,0:T(8,128)(2,1)S(1)}, u32[]{:S(2)}, u32[]{:S(2)}) collective-permute-start(bf16[960,384]{1,0:T(8,128)(2,1)} %collective-permute-done.97.rest_1_), channel_id=1, source_target_pairs={{0,1},{1,0},{2,3},{3,2},{4,5},{5,4},{6,7},{7,6},{8,9},{9,8},{10,11... | collective-permute-start | bytes 2211848 | tf_op jit(solution)/shard_map/ppermute | solution.py:575
  975.6 31.9 %collective-permute-start.100 = (bf16[960,384]{1,0:T(8,128)(2,1)}, bf16[960,384]{1,0:T(8,128)(2,1)S(1)}, u32[]{:S(2)}, u32[]{:S(2)}) collective-permute-start(bf16[960,384]{1,0:T(8,128)(2,1)} %collective-permute-done.99.rest_2_), channel_id=1, source_target_pairs={{0,1},{1,0},{2,3},{3,2},{4,5},{5,4},{6,7},{7,6},{8,9},{9,8},{10,11... | collective-permute-start | bytes 2211848 | tf_op jit(solution)/shard_map/ppermute | solution.py:575
  (215 other events, 3298.5 us)
Sparse Core Ops, SparseCore 0:
  55.9 124.9 reduce-scatter.1
  669.8 124.9 all-gather.1

commit v8 on v7

--- a/solution.py
+++ b/solution.py
@@ -258,6 +258,150 @@
             transcendentals=tokens * tokens * pairs * 2,
         ),
     )(length, q, k, v, d, logs, cosine, sine, cosine, sine, *after)
+
+
+def forward_kernel(mixed_ref, first_ref, norms_ref, out_w_ref, gu_w_ref, down_w_ref, first_sum_ref, second_ref, gate_up_ref, hidden_ref, second_sum_ref, final_ref):
+    width = first_ref.shape[1]
+    middle = gu_w_ref.shape[1] // 2
+    first_sum = first_ref[...] + jnp.dot(mixed_ref[...], out_w_ref[...], preferred_element_type=jnp.float32)
+    first_sum_ref[...] = first_sum
+    second = normalize(first_sum, norms_ref[2:3, :], norms_ref[3:4, :])
+    low = second.astype(low_type)
+    second_ref[...] = low
+    total = second
+    for start in range(0, middle, width):
+        end = start + width
+        gate = jnp.dot(low, gu_w_ref[:, start:end], preferred_element_type=jnp.float32)
+        up = jnp.dot(low, gu_w_ref[:, middle + start : middle + end], preferred_element_type=jnp.float32)
+        gate_up_ref[:, start:end] = gate
+        gate_up_ref[:, middle + start : middle + end] = up
+        hidden = (gate * (1.0 / (1.0 + jnp.exp(-gate))) * up).astype(low_type)
+        hidden_ref[:, start:end] = hidden
+        total = total + jnp.dot(hidden, down_w_ref[start:end, :], preferred_element_type=jnp.float32)
+    second_sum_ref[...] = total
+    final_ref[...] = normalize(total, norms_ref[4:5, :], norms_ref[5:6, :])
+
+
+def feed_forward(mixed, first, norms, near, w_gu, w_down):
+    tokens, width = first.shape
+    middle = w_down.shape[0]
+    row = lambda i: (i, 0)
+    fixed = lambda i: (0, 0)
+    once = pl.Buffered(1)
+    narrow = pl.BlockSpec((ROWS, width), row)
+    high = jax.ShapeDtypeStruct((tokens, width), jnp.float32)
+    return pl.pallas_call(
+        forward_kernel,
+        grid=(tokens // ROWS,),
+        in_specs=[
+            narrow,
+            narrow,
+            pl.BlockSpec(norms.shape, fixed),
+            pl.BlockSpec((width, width), lambda i: (0, 3), pipeline_mode=once),
+            pl.BlockSpec(w_gu.shape, fixed, pipeline_mode=once),
+            pl.BlockSpec(w_down.shape, fixed, pipeline_mode=once),
+        ],
+        out_specs=[
+            narrow,
+            narrow,
+            pl.BlockSpec((ROWS, 2 * middle), row),
+            pl.BlockSpec((ROWS, middle), row),
+            narrow,
+            narrow,
+        ],
+        out_shape=[
+            high,
+            jax.ShapeDtypeStruct((tokens, width), low_type),
+            jax.ShapeDtypeStruct((tokens, 2 * middle), jnp.float32),
+            jax.ShapeDtypeStruct((tokens, middle), low_type),
+            high,
+            high,
+        ],
+        compiler_params=pltpu.CompilerParams(vmem_limit_bytes=vmem),
+        cost_estimate=pl.CostEstimate(
+            flops=2 * tokens * width * (width + 3 * middle), bytes_accessed=14 * tokens * middle, transcendentals=tokens * middle
+        ),
+    )(mixed, first, norms, near, w_gu, w_down)
+
+
+def normalize_back(values, gain, grads):
+    center = values - jnp.mean(values, axis=-1, keepdims=True)
+    inverse = lax.rsqrt(jnp.mean(center * center, axis=-1, keepdims=True) + ln_eps)
+    unit = center * inverse
+    scaled = grads * gain
+    inner = jnp.mean(scaled * unit, axis=-1, keepdims=True)
+    result = inverse * (scaled - jnp.mean(scaled, axis=-1, keepdims=True) - unit * inner)
+    return result, jnp.sum(grads * unit, axis=0, keepdims=True), jnp.sum(grads, axis=0, keepdims=True)
+
+
+def backward_kernel(grad_ref, second_sum_ref, first_sum_ref, gate_up_ref, norms_ref, out_w_ref, gu_w_ref, down_w_ref, branch_ref, gate_low_ref, first_sum_grad_ref, attn_ref, mixed_ref, norms_grad_ref):
+    width = grad_ref.shape[1]
+    middle = down_w_ref.shape[0]
+    sum_grad, gain_three, shift_three = normalize_back(second_sum_ref[...], norms_ref[4:5, :], grad_ref[...])
+    branch = sum_grad.astype(low_type)
+    branch_ref[...] = branch
+    total = sum_grad
+    for start in range(0, middle, width):
+        end = start + width
+        hidden_grad = transposed_dot(branch, down_w_ref[start:end, :])
+        gate = gate_up_ref[:, start:end]
+        up = gate_up_ref[:, middle + start : middle + end]
+        share = 1.0 / (1.0 + jnp.exp(-gate))
+        gate_grad = (hidden_grad * up * (share * (1.0 + gate * (1.0 - share)))).astype(low_type)
+        up_grad = (hidden_grad * (gate * share)).astype(low_type)
+        gate_low_ref[:, start:end] = gate_grad
+        gate_low_ref[:, middle + start : middle + end] = up_grad
+        total = total + transposed_dot(gate_grad, gu_w_ref[:, start:end])
+        total = total + transposed_dot(up_grad, gu_w_ref[:, middle + start : middle + end])
+    first_sum_grad, gain_two, shift_two = normalize_back(first_sum_ref[...], norms_ref[2:3, :], total)
+    first_sum_grad_ref[...] = first_sum_grad
+    attn = first_sum_grad.astype(low_type)
+    attn_ref[...] = attn
+    mixed_ref[...] = transposed_dot(attn, out_w_ref[...]).astype(low_type)
+
+    @pl.when(pl.program_id(0) == 0)
+    def _():
+        norms_grad_ref[...] = jnp.zeros_like(norms_grad_ref)
+
+    norms_grad_ref[...] += jnp.concatenate([gain_two, shift_two, gain_three, shift_three], axis=0)
+
+
+def feed_backward(grad, second_sum, first_sum, gate_up, norms, near, w_gu, w_down):
+    tokens, width = grad.shape
+    middle = w_down.shape[0]
+    row = lambda i: (i, 0)
+    fixed = lambda i: (0, 0)
+    once = pl.Buffered(1)
+    narrow = pl.BlockSpec((ROWS, width), row)
+    wide = pl.BlockSpec((ROWS, 2 * middle), row)
+    low = jax.ShapeDtypeStruct((tokens, width), low_type)
+    return pl.pallas_call(
+        backward_kernel,
+        grid=(tokens // ROWS,),
+        in_specs=[
+            narrow,
+            narrow,
+            narrow,
+            wide,
+            pl.BlockSpec(norms.shape, fixed),
+            pl.BlockSpec((width, width), lambda i: (0, 3), pipeline_mode=once),
+            pl.BlockSpec(w_gu.shape, fixed, pipeline_mode=once),
+            pl.BlockSpec(w_down.shape, fixed, pipeline_mode=once),
+        ],
+        out_specs=[narrow, wide, narrow, narrow, narrow, pl.BlockSpec((4, width), fixed)],
+        out_shape=[
+            low,
+            jax.ShapeDtypeStruct((tokens, 2 * middle), low_type),
+            jax.ShapeDtypeStruct((tokens, width), jnp.float32),
+            low,
+            low,
+            jax.ShapeDtypeStruct((4, width), jnp.float32),
+        ],
+        compiler_params=pltpu.CompilerParams(vmem_limit_bytes=vmem),
+        cost_estimate=pl.CostEstimate(
+            flops=2 * tokens * width * (width + 3 * middle), bytes_accessed=14 * tokens * middle, transcendentals=tokens * middle
+        ),
+    )(grad, second_sum, first_sum, gate_up, norms, near, w_gu, w_down)
 
 
 def blank(shape, dtype):
@@ -740,11 +884,6 @@
     )
 
 
-def swiglu(joined):
-    middle = joined.shape[-1] // 2
-    return jax.nn.silu(joined[:, :middle]) * joined[:, middle:]
-
-
 def merge_stats(first_part, second_part):
     peak = jnp.maximum(first_part[0], second_part[0])
     spread = first_part[1] * jnp.exp(first_part[0] - peak) + second_part[1] * jnp.exp(
@@ -840,7 +979,6 @@
         near = lax.all_gather(near_shard.astype(low_type), "grp", tiled=True)
         w_gu_low = lax.all_gather(w_gu.astype(low_type), "grp", tiled=True)
         w_down_low = lax.all_gather(w_down.astype(low_type), "grp", tiled=True)
-    w_out_low = near[:, 3 * width :]
     cosine, sine = rope_tables(length)
     first, first_low, queries, keys, values = project(embed, norms, cosine, sine, near)
     queries, group_mask = tie((queries, group_mask))
@@ -849,13 +987,9 @@
         loss_count = loss_count + flip(loss_count, 1 << j)
     loss_count = loss_count[0]
     mixed_low, log_sums = attend(lengths, queries, keys, values)
-    first_sum = first + jnp.dot(mixed_low, w_out_low, preferred_element_type=jnp.float32)
-    second = layer_norm(first_sum, norms[2], norms[3])
-    second_low = second.astype(low_type)
-    gate_up = jnp.dot(second_low, w_gu_low, preferred_element_type=jnp.float32)
-    hidden_low = swiglu(gate_up).astype(low_type)
-    second_sum = second + jnp.dot(hidden_low, w_down_low, preferred_element_type=jnp.float32)
-    final = layer_norm(second_sum, norms[4], norms[5])
+    first_sum, second_low, gate_up, hidden_low, second_sum, final = feed_forward(
+        mixed_low, first, norms, near, w_gu_low, w_down_low
+    )
 
     flat_picks = (jnp.arange(seqs, dtype=jnp.int32)[:, None] * length + picks).reshape(-1)
     chosen = final[flat_picks].astype(low_type)
@@ -885,45 +1019,37 @@
     chosen_grad = across_wide(chosen_part.reshape(groups, own_rows, width))
     final_grad = jnp.zeros((tokens, width), jnp.float32).at[flat_picks].add(chosen_grad)
 
-    _, pull = jax.vjp(layer_norm, second_sum, norms[4], norms[5])
-    sum_grad, gain_three, shift_three = pull(final_grad)
-    branch_low = sum_grad.astype(low_type)
-    down = Fold(1, (2, 4))
-    down.cores(gradient_chunks(contract(hidden_low, branch_low, 0, 0)))
-    hidden_grad = contract(branch_low, w_down_low, 1, 1)
-    _, pull = jax.vjp(swiglu, gate_up)
-    gate_low = pull(hidden_grad)[0].astype(low_type)
-    gate_low, _ = tie((gate_low, down.plane(True)))
-    gate, up = Fold(1, (4, 2)), Fold(1, (2, 4))
+    branch_low, gate_low, first_sum_grad, attn_low, mixed_grad, late_norms = feed_backward(
+        final_grad, second_sum, first_sum, gate_up, norms, near, w_gu_low, w_down_low
+    )
+    down, gate, up = Fold(1, (4, 2)), Fold(1, (2, 4)), Fold(1, (4, 2))
     middle = gate_up.shape[1] // 2
+    sent = down.cores(gradient_chunks(contract(hidden_low, branch_low, 0, 0)))
+    gate_low, _ = tie((gate_low, sent))
     sent = gate.cores(gradient_chunks(contract(second_low, gate_low[:, :middle], 0, 0)))
-    sent += up.cores(gradient_chunks(contract(second_low, gate_low[:, middle:], 0, 0)))
     gate_low, _ = tie((gate_low, sent))
-    second_grad = sum_grad + contract(gate_low, w_gu_low, 1, 1)
-    second_grad, _ = tie((second_grad, gate.plane(True) + up.plane(True) + down.plane(False)))
-    _, pull = jax.vjp(layer_norm, first_sum, norms[2], norms[3])
-    first_sum_grad, gain_two, shift_two = pull(second_grad)
-    attn_low = first_sum_grad.astype(low_type)
-    mixed_grad = contract(attn_low, w_out_low, 1, 1).astype(low_type)
+    up.cores(gradient_chunks(contract(second_low, gate_low[:, middle:], 0, 0)))
     pairs = width // LANES
     third = pairs // 3
     sides = []
     for stage in range(3):
-        if stage:
-            if stage == 1:
-                sent = gate.plane(False) + up.plane(False) + down.members()
-            else:
-                sent = gate.members() + up.members()
-            mixed_grad, sides[-1], _, down.came = tie((mixed_grad, sides[-1], sent, down.came))
-        sides.append(
+        if stage == 0:
+            sent = down.plane(True) + gate.plane(True) + up.plane(True)
+        elif stage == 1:
+            sent = down.plane(False) + gate.plane(False)
+        else:
+            sent = down.members() + gate.members() + up.plane(False)
+        mixed_grad, sides, _ = tie((mixed_grad, sides, sent))
+        sides = list(sides) + [
             attend_back(lengths, queries, keys, values, mixed_grad, log_sums, cosine, sine, stage * third, third)
-        )
-    sides, gate.came, up.came = tie((sides, gate.came, up.came))
+        ]
+    sent = up.members()
+    sides, down.came, gate.came, _ = tie((sides, down.came, gate.came, sent))
     joined_grad = jnp.concatenate([side for parts in zip(*sides) for side in parts], axis=1)
     first_grad = first_sum_grad + contract(joined_grad, near[:, : 3 * width], 1, 1)
     _, pull = jax.vjp(layer_norm, embed.astype(jnp.float32), norms[0], norms[1])
     embed_grad, gain_one, shift_one = pull(first_grad)
-    norm_grad = jnp.stack([gain_one, shift_one, gain_two, shift_two, gain_three, shift_three])
+    norm_grad = jnp.concatenate([gain_one[None], shift_one[None], late_norms])
     embed_low, joined_grad = tie((embed_grad.astype(low_type), joined_grad))
     group_embed = lax.all_gather(embed_low, "grp", axis=0, tiled=True)
 

time: 1050 us -> 997 us (0.950)
  matrix products: 137 us -> 65.7 us
  Pallas kernels: 246 us -> 315 us
  other arithmetic: 166 us -> 130 us
  local copies, waits for them, and re-layouts: 89.5 us -> 66.9 us
    pallas_call x0 -> x2, Pallas kernels: none -> 64.2 us  [the longest x1 34 us: feed_backward(): pl.pallas_call(backward_kernel, grid=(tokens // ROWS,), in_specs=[narrow,...]
    dot_general x11 -> x8, matrix products: 111 us -> 65.7 us  [contract(): lax.dot_general(left, right, (((left_dim,), (right_dim,)), ((), ())), pre...]
    dot_general x3 -> x0, matrix products: 26.7 us -> none  [the longest x1 18.2 us: body(): gate_up = jnp.dot(second_low, w_gu_low, preferred_element_type=jnp.float32)]
    convert_element_type x2 -> x0, other arithmetic: 19.3 us -> none  [the longest x1 9.93 us: body(): hidden_low = swiglu(gate_up).astype(low_type)]
    ppermute x33, waiting for transfers between devices: 57.1 us -> 71.8 us  [turn(): lax.ppermute(value, 'grp', [(i, (i + offset) % size) for i in range(size)])]
    unnamed x285 -> x229, local copies, waits for them, and re-layouts: 28.6 us -> 21.3 us
  transfers between devices with their start and end apart: 109 -> 109, of which waited for: 34 -> 39; matrix products, arithmetic and copies ran while one was open for 21% -> 15% of each run, Pallas kernels for 14% -> 14%
where the time goes in v8:
time: 997 us; the launch traced here: 990 us
  Pallas kernels  315 us (32%)
  waiting for transfers between devices  239 us (24%)
  starting transfers between devices  141 us (14%)
  other arithmetic  130 us (13%)
  local copies, waits for them, and re-layouts  66.9 us (7%)
  matrix products  65.7 us (7%)
  between operations  32.4 us (3%)
    ppermute x72, waiting for transfers between devices, flip(): return lax.ppermute(value, 'rep', [(i, i ^ bit) for i in range(size)])  146 us
    ppermute x72, starting transfers between devices, flip(): return lax.ppermute(value, 'rep', [(i, i ^ bit) for i in range(size)])  90.5 us
    ppermute x33, waiting for transfers between devices, turn(): lax.ppermute(value, 'grp', [(i, (i + offset) % size) for i in range(size)])  71.8 us
    dot_general x8, matrix products, contract(): lax.dot_general(left, right, (((left_dim,), (right_dim,)), ((), ())), pre...  65.7 us
    pallas_call x3, Pallas kernels, attend_back(): pl.pallas_call(functools.partial(attend_back_kernel, first_pair), grid_sp...  65.2 us
    ppermute x33, starting transfers between devices, turn(): lax.ppermute(value, 'grp', [(i, (i + offset) % size) for i in range(size)])  50.5 us
    pallas_call x1, Pallas kernels, attend(): pl.pallas_call(attend_kernel, grid_spec=pltpu.PrefetchScalarGridSpec(num_...  47.6 us
    pallas_call x4, Pallas kernels, update(): pl.pallas_call(functools.partial(update_kernel, places, parts), grid_spec...  38.7 us
  transfers between devices with their start and end apart: 109, of which 39 were waited for; matrix products, arithmetic and copies ran while one was open for 15% of the time, Pallas kernels for 14%

profile of v8, /device:TPU:1, one launch (start us, length us, event | category | flops | bytes accessed | tf_op | source)
XLA Modules:
  0.0 990.5 jit_solution(1454675686372128665)
XLA Ops:
  37.7 19.2 %shard_map.413 = bf16[4096,768]{1,0:T(8,128)(2,1)} custom-call(s32[9]{0:T(128)} %convert_reduce_fusion.1.starts_ref, s32[4096]{0:T(1024)} %copy-done.70, s32[4096]{0:T(1024)} %get-tuple-element.135.order_ref, f32[7632,768]{1,0:T(8,128)} %rest_8_.1), custom_call_target="tpu_custom_call" | custom-call | bytes 70336512 | tf_op jit(solution)/shard_map/pallas_call | solution.py:438
  72.8 13.3 %collective-permute-done.20 = bf16[96,768]{1,0:T(8,128)(2,1)S(1)} collective-permute-done((bf16[96,768]{1,0:T(8,128)(2,1)S(1)}, bf16[96,768]{1,0:T(8,128)(2,1)S(1)}, u32[]{:S(2)}, u32[]{:S(2)}) %collective-permute-start.20) | collective-permute-done | bytes 147488 | tf_op jit(solution)/shard_map/ppermute | solution.py:724
  97.9 25.7 %collective-permute-done.23.refs_2_ = bf16[3,96,768]{2,1,0:T(8,128)(2,1)S(1)} collective-permute-done((bf16[3,96,768]{2,1,0:T(8,128)(2,1)S(1)}, bf16[3,96,768]{2,1,0:T(8,128)(2,1)S(1)}, u32[]{:S(2)}, u32[]{:S(2)}) %collective-permute-start.23) | collective-permute-done | bytes 442400 | tf_op jit(solution)/shard_map/ppermute | solution.py:719
  145.4 8.6 convert_element_type.314
  158.9 8.2 shard_map.414.w_ref.out_w_ref
  167.1 8.1 shard_map.415
  182.3 10.7 %shard_map.416.gu_w_ref = bf16[768,6144]{1,0:T(8,128)(2,1)} custom-call(s32[4]{0:T(128)} %and_select_fusion.members_ref, s32[8]{0:T(128)} %iota_xor_fusion.slots_ref, f32[192,6144]{1,0:T(8,128)} %own_ref.1, bf16[3,192,768]{2,1,0:T(8,128)(2,1)} %copy-done.23, bf16[3,192,768]{2,1,0:T(8,128)(2,1)} %collective-permute-done.29.refs_1_, ...), custom_call_target="tpu_custom_call" | custom-call | bytes 18874368 | tf_op jit(solution)/shard_map/pallas_call | solution.py:669
  193.0 9.2 shard_map.417
  202.2 47.6 %shard_map.418 = (bf16[1024,768]{1,0:T(8,128)(2,1)}, f32[6,2,1024]{2,1,0:T(2,128)}) custom-call(s32[1]{0:T(128)S(6)} %copy.137.length_ref, bf16[1024,768]{1,0:T(8,128)(2,1)} %get-tuple-element.152.q_ref, bf16[1024,768]{1,0:T(8,128)(2,1)} %get-tuple-element.153.k_ref, bf16[1024,768]{1,0:T(8,128)(2,1)} %get-tuple-element.154.v_ref), custom_call_target="tpu_custom_call" | custom-call | flops 12884901888 | bytes 6291456 | tf_op jit(solution)/shard_map/pallas_call | solution.py:138
  249.8 30.2 %shard_map.419 = (f32[1024,768]{1,0:T(8,128)}, bf16[1024,768]{1,0:T(8,128)(2,1)}, f32[1024,6144]{1,0:T(8,128)}, bf16[1024,3072]{1,0:T(8,128)(2,1)}, f32[1024,768]{1,0:T(8,128)}, /*index=5*/f32[1024,768]{1,0:T(8,128)}) custom-call(bf16[1024,768]{1,0:T(8,128)(2,1)} %get-tuple-element.155.mixed_ref, f32[1024,768]{1,0:T(8,128)} %get-tuple-element.156.first_ref, ...), custom_call_target="tpu_custom_call" | custom-call | flops 15703474176 | bytes 44040192 | tf_op jit(solution)/shard_map/pallas_call | solution.py:293
  299.5 10.8 %select_reduce_fusion.1 = (f32[512]{0:T(512)S(1)}, f32[7680,512]{1,0:T(8,128)S(1)}) fusion(pred[7680]{0:T(1024)(128)(4,1)S(1)} %iota_compare_fusion.1, bf16[7680,768]{1,0:T(8,128)(2,1)} %pad.15, bf16[512,768]{1,0:T(8,128)(2,1)S(1)} %bitcast.265), kind=kOutput, calls=%fused_computation.7 | convolution fusion | flops 6047661568 | bytes 28321280 | tf_op jit(solution)/shard_map/dot_general | solution.py:866
  335.2 11.8 %fusion.92 = f32[512,768]{1,0:T(8,128)S(1)} fusion(bf16[7680,512]{1,0:T(8,128)(2,1)S(1)} %multiply_convert_fusion.dlogits_ref, bf16[7680,768]{1,0:T(8,128)(2,1)} %pad.15), kind=kOutput, calls=%fused_computation.265 | convolution fusion | flops 6039797760 | bytes 21233664 | tf_op jit(solution)/shard_map/dot_general | solution.py:866
  355.6 25.2 %collective-permute-done.43 = f32[128,768]{1,0:T(8,128)S(1)} collective-permute-done((f32[128,768]{1,0:T(8,128)S(1)}, f32[128,768]{1,0:T(8,128)S(1)}, u32[]{:S(2)}, u32[]{:S(2)}) %collective-permute-start.43) | collective-permute-done | bytes 393248 | tf_op jit(solution)/shard_map/ppermute | solution.py:724
  385.5 34.0 %shard_map.420 = (bf16[1024,768]{1,0:T(8,128)(2,1)}, bf16[1024,6144]{1,0:T(8,128)(2,1)}, f32[1024,768]{1,0:T(8,128)}, bf16[1024,768]{1,0:T(8,128)(2,1)}, bf16[1024,768]{1,0:T(8,128)(2,1)}, /*index=5*/f32[4,768]{1,0:T(4,128)}) custom-call(f32[1024,768]{1,0:T(8,128)} %scatter_custom_fusion.grad_ref, f32[1024,768]{1,0:T(8,128)} %get-tuple-element.161.second_sum_ref, ...), custom_call_target="tpu_custom_call" | custom-call | flops 15703474176 | bytes 44040192 | tf_op jit(solution)/shard_map/pallas_call | solution.py:378
  419.5 7.9 fusion.93
  471.9 21.6 %shard_map.421 = (bf16[1024,256]{1,0:T(8,128)(2,1)}, bf16[1024,256]{1,0:T(8,128)(2,1)}, bf16[1024,256]{1,0:T(8,128)(2,1)}) custom-call(s32[1]{0:T(128)S(6)} %copy.137.length_ref, bf16[1024,768]{1,0:T(8,128)(2,1)} %get-tuple-element.152.q_ref, bf16[1024,768]{1,0:T(8,128)(2,1)} %get-tuple-element.153.k_ref, bf16[1024,768]{1,0:T(8,128)(2,1)} %get-tuple-element.154.v_ref, ...), custom_call_target="tpu_custom_call" | custom-call | flops 10737418240 | bytes 4194304 | tf_op jit(solution)/shard_map/pallas_call | solution.py:223
  503.9 21.8 %shard_map.422 = (bf16[1024,256]{1,0:T(8,128)(2,1)}, bf16[1024,256]{1,0:T(8,128)(2,1)}, bf16[1024,256]{1,0:T(8,128)(2,1)}) custom-call(s32[1]{0:T(128)S(6)} %copy.137.length_ref, bf16[1024,768]{1,0:T(8,128)(2,1)} %get-tuple-element.152.q_ref, bf16[1024,768]{1,0:T(8,128)(2,1)} %get-tuple-element.153.k_ref, bf16[1024,768]{1,0:T(8,128)(2,1)} %get-tuple-element.154.v_ref, ...), custom_call_target="tpu_custom_call" | custom-call | flops 10737418240 | bytes 4194304 | tf_op jit(solution)/shard_map/pallas_call | solution.py:223
  542.7 21.8 %shard_map.423 = (bf16[1024,256]{1,0:T(8,128)(2,1)}, bf16[1024,256]{1,0:T(8,128)(2,1)}, bf16[1024,256]{1,0:T(8,128)(2,1)}) custom-call(s32[1]{0:T(128)S(6)} %copy.137.length_ref, bf16[1024,768]{1,0:T(8,128)(2,1)} %get-tuple-element.152.q_ref, bf16[1024,768]{1,0:T(8,128)(2,1)} %get-tuple-element.153.k_ref, bf16[1024,768]{1,0:T(8,128)(2,1)} %get-tuple-element.154.v_ref, ...), custom_call_target="tpu_custom_call" | custom-call | flops 10737418240 | bytes 4194304 | tf_op jit(solution)/shard_map/pallas_call | solution.py:223
  586.7 9.8 fusion.94
  596.5 8.1 pad_maximum_fusion
  624.1 11.4 %collective-permute-done.74 = bf16[24,3072]{1,0:T(8,128)(2,1)S(1)} collective-permute-done((bf16[24,3072]{1,0:T(8,128)(2,1)S(1)}, bf16[24,3072]{1,0:T(8,128)(2,1)S(1)}, u32[]{:S(2)}, u32[]{:S(2)}) %collective-permute-start.74) | collective-permute-done | bytes 147488 | tf_op jit(solution)/shard_map/ppermute | solution.py:724
  636.5 13.3 %collective-permute-done.61 = bf16[4,2,24,3072]{3,2,0,1:T(8,128)(2,1)S(1)} collective-permute-done((bf16[4,2,24,3072]{3,2,0,1:T(8,128)(2,1)S(1)}, bf16[4,2,24,3072]{3,2,0,1:T(8,128)(2,1)S(1)}, u32[]{:S(2)}, u32[]{:S(2)}) %collective-permute-start.61) | collective-permute-done | bytes 1179680 | tf_op jit(solution)/shard_map/ppermute | solution.py:719
  653.2 9.1 collective-permute-done.77.refs_2_
  685.2 10.0 %collective-permute-done.64 = bf16[24,3072]{1,0:T(8,128)(2,1)S(1)} collective-permute-done((bf16[24,3072]{1,0:T(8,128)(2,1)S(1)}, bf16[24,3072]{1,0:T(8,128)(2,1)S(1)}, u32[]{:S(2)}, u32[]{:S(2)}) %collective-permute-start.64) | collective-permute-done | bytes 147488 | tf_op jit(solution)/shard_map/ppermute | solution.py:724
  727.4 16.9 %all-gather.2.cloned.1.call-done.embed_ref = bf16[4096,768]{1,0:T(8,128)(2,1)} async-done(((bf16[1024,768]{1,0:T(8,128)(2,1)}), bf16[4096,768]{1,0:T(8,128)(2,1)}) %all-gather.2.cloned.1.call-update) | async-done | bytes 6291472 | tf_op jit(solution)/shard_map/all_gather | solution.py:1054
  744.2 14.1 %shard_map.426 = bf16[4,960,768]{2,1,0:T(8,128)(2,1)} custom-call(s32[4]{0:T(128)} %add_subtract_fusion.chunks_ref, s32[9]{0:T(128)} %convert_reduce_fusion.1.starts_ref, s32[4104]{0:T(1024)} %pad.16.codes_ref, s32[4104]{0:T(1024)} %pad.17.order_ref, bf16[7680,512]{1,0:T(8,128)(2,1)} %copy-done, bf16[512,768]{1,0:T(8,128)(2,1)} %bitcast.266, ...), custom_call_target="tpu_custom_call" | custom-call | flops 3019898880 | bytes 23592960 | tf_op jit(solution)/shard_map/pallas_call | solution.py:531
  761.3 8.9 collective-permute-done.83.refs_0_
  772.8 18.7 %shard_map.427 = (bf16[2,960,384]{2,1,0:T(8,128)(2,1)}, f32[2,960,384]{2,1,0:T(8,128)}, bf16[2,960,384]{2,1,0:T(8,128)(2,1)}, f32[2,960,384]{2,1,0:T(8,128)}) custom-call(s32[4]{0:T(128)} %broadcast_add_fusion.chunks_ref, s32[9]{0:T(128)} %convert_reduce_fusion.1.starts_ref, s32[4104]{0:T(1024)} %pad.16.codes_ref, s32[4104]{0:T(1024)} %pad.17.order_ref, ...), custom_call_target="tpu_custom_call" | custom-call | flops 3019898880 | bytes 23592960 | tf_op jit(solution)/shard_map/pallas_call | solution.py:531
  793.5 31.3 %collective-permute-done.84 = bf16[2,960,384]{2,1,0:T(8,128)(2,1)S(1)} collective-permute-done((bf16[2,960,384]{2,1,0:T(8,128)(2,1)}, bf16[2,960,384]{2,1,0:T(8,128)(2,1)S(1)}, u32[]{:S(2)}, u32[]{:S(2)}) %collective-permute-start.84) | collective-permute-done | bytes 1474592 | tf_op jit(solution)/shard_map/ppermute | solution.py:719
  930.9 8.2 collective-permute-done.105.rest_1_
  944.7 9.9 shard_map.432
  961.9 17.8 %shard_map.434 = (f32[7632,768]{1,0:T(8,128)}, f32[7632,768]{1,0:T(8,128)}, f32[16,1,480]{2,1,0:T(1,128)}) custom-call(s32[8]{0:T(128)} %iota_xor_fusion.slots_ref, f32[2]{0:T(128)} %pad_maximum_fusion.10.scalars_ref, bf16[960,384]{1,0:T(8,128)(2,1)} %collective-permute-done.93.rest_0_, ...), custom_call_target="tpu_custom_call", output_to_operand_aliasing={{0}: (13, {}), {1}: (14, {}), {2}: (15, {})} | custom-call | flops 29491200 | bytes 41287680 | tf_op jit(solution)/shard_map/pallas_call | solution.py:594
  (615 shorter events, 435.0 us)
Async XLA Ops:
  7.2 185.8 %reduce-scatter.2.cloned.1.call-start = ((), (), s32[]{:S(2)}) async-start(), calls=%async_computation.1 | async-start | bytes 7864320 | tf_op jit(solution)/shard_map/reduce_scatter | solution.py:958
  19.6 37.3 %collective-permute-start.8 = (bf16[192,768]{1,0:T(8,128)(2,1)}, bf16[192,768]{1,0:T(8,128)(2,1)S(1)}, u32[]{:S(2)}, u32[]{:S(2)}) collective-permute-start(bf16[192,768]{1,0:T(8,128)(2,1)} %dynamic-slice_convert_fusion.7), channel_id=1, source_target_pairs={{0,24},{8,0},{16,8},{24,16},{1,25},{9,1},{17,9},{25,17},{2,26},{10... | collective-permute-start | bytes 884744 | tf_op jit(solution)/shard_map/ppermute | solution.py:724
  23.6 33.4 %collective-permute-start.7 = (bf16[192,768]{1,0:T(8,128)(2,1)}, bf16[192,768]{1,0:T(8,128)(2,1)S(1)}, u32[]{:S(2)}, u32[]{:S(2)}) collective-permute-start(bf16[192,768]{1,0:T(8,128)(2,1)} %dynamic-slice_convert_fusion.7), channel_id=1, source_target_pairs={{0,16},{8,24},{16,0},{24,8},{1,17},{9,25},{17,1},{25,9},{2,18},{10... | collective-permute-start | bytes 884744 | tf_op jit(solution)/shard_map/ppermute | solution.py:724
  26.4 30.6 %collective-permute-start.6 = (bf16[192,768]{1,0:T(8,128)(2,1)}, bf16[192,768]{1,0:T(8,128)(2,1)}, u32[]{:S(2)}, u32[]{:S(2)}) collective-permute-start(bf16[192,768]{1,0:T(8,128)(2,1)} %dynamic-slice_convert_fusion.7), channel_id=1, source_target_pairs={{0,8},{8,16},{16,24},{24,0},{1,9},{9,17},{17,25},{25,1},{2,10},{10... | collective-permute-start | bytes 884744 | tf_op jit(solution)/shard_map/ppermute | solution.py:724
  58.1 686.2 %all-gather.2.cloned.1.call-start = ((), (), s32[]{:S(2)}) async-start(), calls=%async_computation.2 | async-start | bytes 7864320 | tf_op jit(solution)/shard_map/all_gather | solution.py:1054
  92.7 42.7 %collective-permute-start.9 = (bf16[3,192,768]{2,1,0:T(8,128)(2,1)S(1)}, bf16[3,192,768]{2,1,0:T(8,128)(2,1)S(1)}, u32[]{:S(2)}, u32[]{:S(2)}) collective-permute-start(bf16[3,192,768]{2,1,0:T(8,128)(2,1)S(1)} %pad_maximum_fusion.1.refs_0_), channel_id=1, source_target_pairs={{0,2},{1,3},{2,0},{3,1},{4,6},{5,7},{6,4},{7,5},{8,10},{9,11},{10,... | collective-permute-start | bytes 2654216 | tf_op jit(solution)/shard_map/ppermute | solution.py:719
  94.2 30.5 %collective-permute-start.25 = (bf16[3,96,768]{2,1,0:T(8,128)(2,1)S(1)}, bf16[3,96,768]{2,1,0:T(8,128)(2,1)S(1)}, u32[]{:S(2)}, u32[]{:S(2)}) collective-permute-start(bf16[3,96,768]{2,1,0:T(8,128)(2,1)S(1)} %pad_maximum_fusion.6.refs_0_), channel_id=1, source_target_pairs={{0,4},{1,5},{2,6},{3,7},{4,0},{5,1},{6,2},{7,3},{8,12},{9,13},{10,... | collective-permute-start | bytes 1327112 | tf_op jit(solution)/shard_map/ppermute | solution.py:719
  95.4 37.6 %collective-permute-start.17 = (bf16[3,192,384]{2,1,0:T(8,128)(2,1)S(1)}, bf16[3,192,384]{2,1,0:T(8,128)(2,1)S(1)}, u32[]{:S(2)}, u32[]{:S(2)}) collective-permute-start(bf16[3,192,384]{2,1,0:T(8,128)(2,1)S(1)} %collective-permute-done.15.refs_4_), channel_id=1, source_target_pairs={{0,2},{1,3},{2,0},{3,1},{4,6},{5,7},{6,4},{7,5},{8,10},{9,11},{10,... | collective-permute-start | bytes 1327112 | tf_op jit(solution)/shard_map/ppermute | solution.py:719
  96.7 37.5 %collective-permute-start.14 = (bf16[3,192,384]{2,1,0:T(8,128)(2,1)S(1)}, bf16[3,192,384]{2,1,0:T(8,128)(2,1)S(1)}, u32[]{:S(2)}, u32[]{:S(2)}) collective-permute-start(bf16[3,192,384]{2,1,0:T(8,128)(2,1)S(1)} %collective-permute-done.13.refs_2_), channel_id=1, source_target_pairs={{0,1},{1,0},{2,3},{3,2},{4,5},{5,4},{6,7},{7,6},{8,9},{9,8},{10,11... | collective-permute-start | bytes 1327112 | tf_op jit(solution)/shard_map/ppermute | solution.py:719
  134.2 41.1 %collective-permute-start.10 = (bf16[3,192,768]{2,1,0:T(8,128)(2,1)S(1)}, bf16[3,192,768]{2,1,0:T(8,128)(2,1)S(1)}, u32[]{:S(2)}, u32[]{:S(2)}) collective-permute-start(bf16[3,192,768]{2,1,0:T(8,128)(2,1)S(1)} %pad_maximum_fusion.1.refs_0_), channel_id=1, source_target_pairs={{0,4},{1,5},{2,6},{3,7},{4,0},{5,1},{6,2},{7,3},{8,12},{9,13},{10,... | collective-permute-start | bytes 2654216 | tf_op jit(solution)/shard_map/ppermute | solution.py:719
  135.4 39.9 %collective-permute-start.11 = (bf16[3,192,768]{2,1,0:T(8,128)(2,1)S(1)}, bf16[3,192,768]{2,1,0:T(8,128)(2,1)}, u32[]{:S(2)}, u32[]{:S(2)}) collective-permute-start(bf16[3,192,768]{2,1,0:T(8,128)(2,1)S(1)} %collective-permute-done.9.refs_2_), channel_id=1, source_target_pairs={{0,4},{1,5},{2,6},{3,7},{4,0},{5,1},{6,2},{7,3},{8,12},{9,13},{10,... | collective-permute-start | bytes 2654216 | tf_op jit(solution)/shard_map/ppermute | solution.py:719
  136.3 30.9 %collective-permute-start.26 = (bf16[3,96,768]{2,1,0:T(8,128)(2,1)S(1)}, bf16[3,96,768]{2,1,0:T(8,128)(2,1)}, u32[]{:S(2)}, u32[]{:S(2)}) collective-permute-start(bf16[3,96,768]{2,1,0:T(8,128)(2,1)S(1)} %collective-permute-done.25.refs_4_), channel_id=1, source_target_pairs={{0,1},{1,0},{2,3},{3,2},{4,5},{5,4},{6,7},{7,6},{8,9},{9,8},{10,11... | collective-permute-start | bytes 1327112 | tf_op jit(solution)/shard_map/ppermute | solution.py:719
  349.3 31.5 %collective-permute-start.43 = (f32[128,768]{1,0:T(8,128)S(1)}, f32[128,768]{1,0:T(8,128)S(1)}, u32[]{:S(2)}, u32[]{:S(2)}) collective-permute-start(f32[128,768]{1,0:T(8,128)S(1)} %get-tuple-element.278), channel_id=1, source_target_pairs={{0,16},{8,24},{16,0},{24,8},{1,17},{9,25},{17,1},{25,9},{2,18},{10... | collective-permute-start | bytes 1179656 | tf_op jit(solution)/shard_map/ppermute | solution.py:724
  349.3 32.2 %collective-permute-start.42 = (f32[128,768]{1,0:T(8,128)S(1)}, f32[128,768]{1,0:T(8,128)}, u32[]{:S(2)}, u32[]{:S(2)}) collective-permute-start(f32[128,768]{1,0:T(8,128)S(1)} %get-tuple-element.276), channel_id=1, source_target_pairs={{0,8},{8,16},{16,24},{24,0},{1,9},{9,17},{17,25},{25,1},{2,10},{10... | collective-permute-start | bytes 1179656 | tf_op jit(solution)/shard_map/ppermute | solution.py:724
  427.7 34.0 %collective-permute-start.45 = (bf16[4,4,96,768]{3,2,1,0:T(8,128)(2,1)S(1)}, bf16[4,4,96,768]{3,2,1,0:T(8,128)(2,1)}, u32[]{:S(2)}, u32[]{:S(2)}) collective-permute-start(bf16[4,4,96,768]{3,2,1,0:T(8,128)(2,1)S(1)} %fusion.16), channel_id=1, source_target_pairs={{0,1},{1,0},{2,3},{3,2},{4,5},{5,4},{6,7},{7,6},{8,9},{9,8},{10,11... | collective-permute-start | bytes 7077896 | tf_op jit(solution)/shard_map/ppermute | solution.py:719
  460.5 33.0 %collective-permute-start.49 = (bf16[4,2,24,3072]{3,2,0,1:T(8,128)(2,1)}, bf16[4,2,24,3072]{3,2,0,1:T(8,128)(2,1)}, u32[]{:S(2)}, u32[]{:S(2)}) collective-permute-start(bf16[4,2,24,3072]{3,2,0,1:T(8,128)(2,1)} %fusion.27), channel_id=1, source_target_pairs={{0,2},{1,3},{2,0},{3,1},{4,6},{5,7},{6,4},{7,5},{8,10},{9,11},{10,... | collective-permute-start | bytes 3538952 | tf_op jit(solution)/shard_map/ppermute | solution.py:719
  471.5 54.2 %collective-permute-start.52 = (bf16[4,2,24,3072]{3,2,0,1:T(8,128)(2,1)S(1)}, bf16[4,2,24,3072]{3,2,0,1:T(8,128)(2,1)}, u32[]{:S(2)}, u32[]{:S(2)}) collective-permute-start(bf16[4,2,24,3072]{3,2,0,1:T(8,128)(2,1)S(1)} %fusion.26), channel_id=1, source_target_pairs={{0,4},{1,5},{2,6},{3,7},{4,0},{5,1},{6,2},{7,3},{8,12},{9,13},{10,... | collective-permute-start | bytes 3538952 | tf_op jit(solution)/shard_map/ppermute | solution.py:719
  502.5 33.7 %collective-permute-start.51 = (bf16[4,24,3072]{2,1,0:T(8,128)(2,1)S(1)}, bf16[4,24,3072]{2,1,0:T(8,128)(2,1)}, u32[]{:S(2)}, u32[]{:S(2)}) collective-permute-start(bf16[4,24,3072]{2,1,0:T(8,128)(2,1)S(1)} %fusion.35), channel_id=1, source_target_pairs={{0,4},{1,5},{2,6},{3,7},{4,0},{5,1},{6,2},{7,3},{8,12},{9,13},{10,... | collective-permute-start | bytes 1769480 | tf_op jit(solution)/shard_map/ppermute | solution.py:719
  527.5 37.0 %collective-permute-start.59 = (bf16[4,24,3072]{2,1,0:T(8,128)(2,1)S(1)}, bf16[4,24,3072]{2,1,0:T(8,128)(2,1)S(1)}, u32[]{:S(2)}, u32[]{:S(2)}) collective-permute-start(bf16[4,24,3072]{2,1,0:T(8,128)(2,1)S(1)} %fusion.36), channel_id=1, source_target_pairs={{0,2},{1,3},{2,0},{3,1},{4,6},{5,7},{6,4},{7,5},{8,10},{9,11},{10,... | collective-permute-start | bytes 1769480 | tf_op jit(solution)/shard_map/ppermute | solution.py:719
  538.3 30.5 %collective-permute-start.54 = (bf16[96,768]{1,0:T(8,128)(2,1)}, bf16[96,768]{1,0:T(8,128)(2,1)S(1)}, u32[]{:S(2)}, u32[]{:S(2)}) collective-permute-start(bf16[96,768]{1,0:T(8,128)(2,1)} %get-tuple-element.289), channel_id=1, source_target_pairs={{0,16},{8,24},{16,0},{24,8},{1,17},{9,25},{17,1},{25,9},{2,18},{10... | collective-permute-start | bytes 442376 | tf_op jit(solution)/shard_map/ppermute | solution.py:724
  667.5 35.2 %collective-permute-start.63 = (bf16[24,3072]{1,0:T(8,128)(2,1)S(1)}, bf16[24,3072]{1,0:T(8,128)(2,1)S(1)}, u32[]{:S(2)}, u32[]{:S(2)}) collective-permute-start(bf16[24,3072]{1,0:T(8,128)(2,1)S(1)} %get-tuple-element.279), channel_id=1, source_target_pairs={{0,8},{8,16},{16,24},{24,0},{1,9},{9,17},{17,25},{25,1},{2,10},{10... | collective-permute-start | bytes 442376 | tf_op jit(solution)/shard_map/ppermute | solution.py:724
  673.4 30.8 %collective-permute-start.76 = (bf16[24,9216]{1,0:T(8,128)(2,1)S(1)}, bf16[24,9216]{1,0:T(8,128)(2,1)S(1)}, u32[]{:S(2)}, u32[]{:S(2)}) collective-permute-start(bf16[24,9216]{1,0:T(8,128)(2,1)S(1)} %pad_maximum_fusion.7.refs_0_), channel_id=1, source_target_pairs={{0,1},{1,0},{2,3},{3,2},{4,5},{5,4},{6,7},{7,6},{8,9},{9,8},{10,11... | collective-permute-start | bytes 1327112 | tf_op jit(solution)/shard_map/ppermute | solution.py:719
  791.5 33.3 %collective-permute-start.84 = (bf16[2,960,384]{2,1,0:T(8,128)(2,1)}, bf16[2,960,384]{2,1,0:T(8,128)(2,1)S(1)}, u32[]{:S(2)}, u32[]{:S(2)}) collective-permute-start(bf16[2,960,384]{2,1,0:T(8,128)(2,1)} %get-tuple-element.216), channel_id=1, source_target_pairs={{0,2},{1,3},{2,0},{3,1},{4,6},{5,7},{6,4},{7,5},{8,10},{9,11},{10,... | collective-permute-start | bytes 4423688 | tf_op jit(solution)/shard_map/ppermute | solution.py:719
  792.2 37.1 %collective-permute-start.86 = (bf16[2,960,384]{2,1,0:T(8,128)(2,1)}, bf16[2,960,384]{2,1,0:T(8,128)(2,1)S(1)}, u32[]{:S(2)}, u32[]{:S(2)}) collective-permute-start(bf16[2,960,384]{2,1,0:T(8,128)(2,1)} %get-tuple-element.218), channel_id=1, source_target_pairs={{0,4},{1,5},{2,6},{3,7},{4,0},{5,1},{6,2},{7,3},{8,12},{9,13},{10,... | collective-permute-start | bytes 4423688 | tf_op jit(solution)/shard_map/ppermute | solution.py:719
  869.1 38.3 %collective-permute-start.93 = (bf16[960,384]{1,0:T(8,128)(2,1)}, bf16[960,384]{1,0:T(8,128)(2,1)}, u32[]{:S(2)}, u32[]{:S(2)}) collective-permute-start(bf16[960,384]{1,0:T(8,128)(2,1)} %get-tuple-element.224.rest_0_), channel_id=1, source_target_pairs={{0,1},{1,0},{2,3},{3,2},{4,5},{5,4},{6,7},{7,6},{8,9},{9,8},{10,11... | collective-permute-start | bytes 2211848 | tf_op jit(solution)/shard_map/ppermute | solution.py:719
  870.7 38.2 %collective-permute-start.95 = (bf16[960,384]{1,0:T(8,128)(2,1)}, bf16[960,384]{1,0:T(8,128)(2,1)}, u32[]{:S(2)}, u32[]{:S(2)}) collective-permute-start(bf16[960,384]{1,0:T(8,128)(2,1)} %get-tuple-element.224.rest_0_), channel_id=1, source_target_pairs={{0,2},{1,3},{2,0},{3,1},{4,6},{5,7},{6,4},{7,5},{8,10},{9,11},{10,... | collective-permute-start | bytes 2211848 | tf_op jit(solution)/shard_map/ppermute | solution.py:719
  871.8 55.9 %collective-permute-start.94 = (bf16[960,384]{1,0:T(8,128)(2,1)}, bf16[960,384]{1,0:T(8,128)(2,1)}, u32[]{:S(2)}, u32[]{:S(2)}) collective-permute-start(bf16[960,384]{1,0:T(8,128)(2,1)} %get-tuple-element.225.rest_1_), channel_id=1, source_target_pairs={{0,1},{1,0},{2,3},{3,2},{4,5},{5,4},{6,7},{7,6},{8,9},{9,8},{10,11... | collective-permute-start | bytes 2211848 | tf_op jit(solution)/shard_map/ppermute | solution.py:719
  872.1 40.6 %collective-permute-start.97 = (bf16[960,384]{1,0:T(8,128)(2,1)}, bf16[960,384]{1,0:T(8,128)(2,1)}, u32[]{:S(2)}, u32[]{:S(2)}) collective-permute-start(bf16[960,384]{1,0:T(8,128)(2,1)} %get-tuple-element.225.rest_1_), channel_id=1, source_target_pairs={{0,2},{1,3},{2,0},{3,1},{4,6},{5,7},{6,4},{7,5},{8,10},{9,11},{10,... | collective-permute-start | bytes 2211848 | tf_op jit(solution)/shard_map/ppermute | solution.py:719
  873.7 38.0 %collective-permute-start.99 = (bf16[960,384]{1,0:T(8,128)(2,1)}, bf16[960,384]{1,0:T(8,128)(2,1)}, u32[]{:S(2)}, u32[]{:S(2)}) collective-permute-start(bf16[960,384]{1,0:T(8,128)(2,1)} %get-tuple-element.224.rest_0_), channel_id=1, source_target_pairs={{0,4},{1,5},{2,6},{3,7},{4,0},{5,1},{6,2},{7,3},{8,12},{9,13},{10,... | collective-permute-start | bytes 2211848 | tf_op jit(solution)/shard_map/ppermute | solution.py:719
  927.7 32.4 %collective-permute-start.98 = (bf16[960,384]{1,0:T(8,128)(2,1)}, bf16[960,384]{1,0:T(8,128)(2,1)S(1)}, u32[]{:S(2)}, u32[]{:S(2)}) collective-permute-start(bf16[960,384]{1,0:T(8,128)(2,1)} %collective-permute-done.97.rest_1_), channel_id=1, source_target_pairs={{0,1},{1,0},{2,3},{3,2},{4,5},{5,4},{6,7},{7,6},{8,9},{9,8},{10,11... | collective-permute-start | bytes 2211848 | tf_op jit(solution)/shard_map/ppermute | solution.py:719
  928.3 31.7 %collective-permute-start.100 = (bf16[960,384]{1,0:T(8,128)(2,1)}, bf16[960,384]{1,0:T(8,128)(2,1)S(1)}, u32[]{:S(2)}, u32[]{:S(2)}) collective-permute-start(bf16[960,384]{1,0:T(8,128)(2,1)} %collective-permute-done.99.rest_2_), channel_id=1, source_target_pairs={{0,1},{1,0},{2,3},{3,2},{4,5},{5,4},{6,7},{7,6},{8,9},{9,8},{10,11... | collective-permute-start | bytes 2211848 | tf_op jit(solution)/shard_map/ppermute | solution.py:719
  929.5 30.5 %collective-permute-start.102 = (bf16[960,384]{1,0:T(8,128)(2,1)}, bf16[960,384]{1,0:T(8,128)(2,1)S(1)}, u32[]{:S(2)}, u32[]{:S(2)}) collective-permute-start(bf16[960,384]{1,0:T(8,128)(2,1)} %collective-permute-done.101.rest_3_), channel_id=1, source_target_pairs={{0,1},{1,0},{2,3},{3,2},{4,5},{5,4},{6,7},{7,6},{8,9},{9,8},{10,11... | collective-permute-start | bytes 2211848 | tf_op jit(solution)/shard_map/ppermute | solution.py:719
  (187 other events, 2757.7 us)
Sparse Core Ops, SparseCore 0:
  58.2 122.0 reduce-scatter.1
  612.4 131.8 all-gather.1

commit v9 on v8

--- a/solution.py
+++ b/solution.py
@@ -432,8 +432,7 @@
         out_ref[start : start + CHUNK, :] = rows[start : start + CHUNK, :].astype(low_type)
 
 
-def lookup(starts, places, order, table):
-    count = places.shape[0]
+def lookup(starts, places, order, table, count):
     width = table.shape[1]
     return pl.pallas_call(
         lookup_kernel,
@@ -724,10 +723,14 @@
     return lax.ppermute(value, "grp", [(i, (i + offset) % size) for i in range(size)])
 
 
+def wave(have, bit):
+    return have | {place ^ bit: flip(part, bit) for place, part in have.items()}
+
+
 def spread(piece, order):
     have = {0: piece}
     for bit in order:
-        have.update({place ^ bit: flip(part, bit) for place, part in have.items()})
+        have = wave(have, bit)
     return have
 
 
@@ -942,39 +945,74 @@
 
     local_ids = group_ids - member * vocab_rows
     owned = (local_ids >= 0) & (local_ids < vocab_rows)
-    places, order = lax.sort(
-        (jnp.where(owned, local_ids, padded), jnp.arange(local_ids.shape[0], dtype=jnp.int32)), num_keys=1
-    )
+    keys = jnp.where(owned, local_ids, padded)
+    tokens_at = jnp.arange(local_ids.shape[0], dtype=jnp.int32)
+    if quick:
+        slot_rows = tokens // 2
+        owners = group_ids.reshape(groups, tokens) // vocab_rows
+        own_ids = ids.reshape(1, tokens) // vocab_rows
+        asked = jnp.concatenate([owners == member, own_ids == jnp.arange(groups, dtype=jnp.int32)[:, None]])
+        below = jnp.arange(tokens)[:, None] <= jnp.arange(tokens)[None, :]
+        ranks = jnp.dot(asked.astype(low_type), below.astype(low_type), preferred_element_type=jnp.float32)
+        ranks = ranks.astype(jnp.int32) - 1
+        slot_of = (jnp.arange(groups, dtype=jnp.int32) - member + groups) % groups
+        slots_at = slot_of[:, None] * slot_rows + ranks[:groups]
+        slots_at = jnp.where(ranks[:groups] < slot_rows, slots_at, groups * slot_rows).reshape(-1)
+        own_ranks = jnp.sum(jnp.where(asked[groups:], ranks[groups:], 0), axis=0)
+        source = (member - own_ids[0] + groups) % groups * slot_rows + own_ranks
+        asks = jnp.sum((owners[:, None, :] == jnp.arange(groups)[None, :, None]).astype(jnp.int32), axis=-1)
+        uneven = jnp.max((asks > slot_rows).astype(jnp.int32))[None]
+        for j in range(replicas.bit_length() - 1):
+            uneven = jnp.maximum(uneven, flip(uneven, 1 << j))
+        places, order, slots_at = lax.sort((keys, tokens_at, slots_at), num_keys=1)
+    else:
+        places, order = lax.sort((keys, tokens_at), num_keys=1)
     bounds = jnp.arange(replicas + 1, dtype=jnp.int32) * block
     starts = jnp.sum((places[None, :] < bounds[:, None]).astype(jnp.int32), axis=1)
-    if quick:
-        places, near_part = tie((places, near_part))
     again = jnp.concatenate([jnp.zeros((1,), jnp.int32), (places[1:] == places[:-1]).astype(jnp.int32)])
     codes = jnp.pad(places % block * 2 + again, (0, 8))
     padded_order = jnp.pad(order, (0, 8))
-    found = lookup(starts, places, order, table)
+    count = local_ids.shape[0]
     if quick:
+        places, near_part = tie((places, near_part))
+        found = lookup(starts, places, slots_at, table, groups * slot_rows)
         found, gu_part = tie((found, gu_part))
-    embed = lax.psum_scatter(found, "grp", scatter_dimension=0, tiled=True)
+        packs = found.reshape(groups, slot_rows, width)
+        turned = [turn(packs[offset], offset) for offset in range(1, groups)]
+
+        def compact(came):
+            pick = source[:, None] == jnp.arange(groups * slot_rows, dtype=jnp.int32)[None, :]
+            return jnp.dot(pick.astype(low_type), came, preferred_element_type=jnp.float32).astype(low_type)
+
+        def general(came):
+            rows = lookup(starts, places, order, table, count)
+            return lax.psum_scatter(rows, "grp", scatter_dimension=0, tiled=True)
+
+    else:
+        found = lookup(starts, places, order, table, count)
+        embed = lax.psum_scatter(found, "grp", scatter_dimension=0, tiled=True)
     late_table, _ = lax.optimization_barrier((table, found))
     table_low = jnp.pad(late_table.astype(low_type), ((0, padded - vocab_rows), (0, 0)))
 
     if quick:
         members, slots = members_of(), slots_of()
 
-        down_own, _ = tie((cut(w_down, 0), found))
-        down_part = fetch(down_own.astype(low_type))
 
         def listed(have):
             return [have[place] for place in range(replicas)]
 
-        near = lay_columns(members, slots, near_shard, listed(spread(near_part, [4, 2, 1])))
-        w_down_low = lay_rows(members, slots, w_down, listed(spread(down_part, [4, 2, 1])))
-        gu_have = spread(gu_part, [2, 4])
-        gu_have, near, w_down_low, table_low = tie((gu_have, near, w_down_low, table_low))
-        gu_have.update({place ^ 1: flip(part, 1) for place, part in gu_have.items()})
-        w_gu_low = lay_columns(members, slots, w_gu, listed(gu_have))
-        embed, near, w_gu_low, w_down_low, table_low = tie((embed, near, w_gu_low, w_down_low, table_low))
+        near_have, gu_have = wave({0: near_part}, 4), wave({0: gu_part}, 2)
+        near_have, turned[0], turned[-1] = tie((near_have, turned[0], turned[-1]))
+        near_have = wave(near_have, 2)
+        gu_have = wave(gu_have, 4)
+        near = lay_columns(members, slots, near_shard, listed(wave(near_have, 1)))
+        gu_have, near, table_low, turned[1:-1] = tie((gu_have, near, table_low, turned[1:-1]))
+        w_gu_low = lay_columns(members, slots, w_gu, listed(wave(gu_have, 1)))
+        down_own, _ = tie((cut(w_down, 0), turned))
+        down_have = listed(spread(fetch(down_own.astype(low_type)), [4, 2, 1]))
+        came = jnp.concatenate([packs[0]] + turned)
+        came, near, w_gu_low, table_low = tie((came, near, w_gu_low, table_low))
+        embed = lax.cond(uneven[0] > 0, general, compact, came)
     else:
         near = lax.all_gather(near_shard.astype(low_type), "grp", tiled=True)
         w_gu_low = lax.all_gather(w_gu.astype(low_type), "grp", tiled=True)
@@ -987,6 +1025,9 @@
         loss_count = loss_count + flip(loss_count, 1 << j)
     loss_count = loss_count[0]
     mixed_low, log_sums = attend(lengths, queries, keys, values)
+    if quick:
+        mixed_low, down_have = tie((mixed_low, down_have))
+        w_down_low = lay_rows(members, slots, w_down, down_have)
     first_sum, second_low, gate_up, hidden_low, second_sum, final = feed_forward(
         mixed_low, first, norms, near, w_gu_low, w_down_low
     )

time: 997 us -> 1040 us (1.043)
  waiting for transfers between devices: 239 us -> 270 us
    ppermute x33 -> x36, waiting for transfers between devices: 71.8 us -> 115 us  [turn(): lax.ppermute(value, 'grp', [(i, (i + offset) % size) for i in range(size)])]
    ppermute x72 -> x75, starting transfers between devices: 90.5 us -> 78 us  [flip(): return lax.ppermute(value, 'rep', [(i, i ^ bit) for i in range(size)])]
    ppermute x72 -> x75, waiting for transfers between devices: 146 us -> 136 us  [flip(): return lax.ppermute(value, 'rep', [(i, i ^ bit) for i in range(size)])]
    ppermute x33 -> x36, starting transfers between devices: 50.5 us -> 55.6 us  [turn(): lax.ppermute(value, 'grp', [(i, (i + offset) % size) for i in range(size)])]
    unnamed x229 -> x260, local copies, waits for them, and re-layouts: 21.3 us -> 23 us
  transfers between devices with their start and end apart: 109 -> 114, of which waited for: 39 -> 44; matrix products, arithmetic and copies ran while one was open for 15% -> 15% of each run, Pallas kernels for 14% -> 18%
where the time goes in v9:
time: 1040 us; the launch traced here: 1030 us
  Pallas kernels  308 us (30%)
  waiting for transfers between devices  270 us (26%)
  starting transfers between devices  141 us (14%)
  other arithmetic  138 us (13%)
  local copies, waits for them, and re-layouts  72 us (7%)
  matrix products  67.2 us (6%)
  between operations  35.8 us (3%)
    ppermute x75, waiting for transfers between devices, flip(): return lax.ppermute(value, 'rep', [(i, i ^ bit) for i in range(size)])  136 us
    ppermute x36, waiting for transfers between devices, turn(): lax.ppermute(value, 'grp', [(i, (i + offset) % size) for i in range(size)])  115 us
    ppermute x75, starting transfers between devices, flip(): return lax.ppermute(value, 'rep', [(i, i ^ bit) for i in range(size)])  78 us
    pallas_call x3, Pallas kernels, attend_back(): pl.pallas_call(functools.partial(attend_back_kernel, first_pair), grid_sp...  65.1 us
    dot_general x8, matrix products, contract(): lax.dot_general(left, right, (((left_dim,), (right_dim,)), ((), ())), pre...  62 us
    ppermute x36, starting transfers between devices, turn(): lax.ppermute(value, 'grp', [(i, (i + offset) % size) for i in range(size)])  55.6 us
    pallas_call x1, Pallas kernels, attend(): pl.pallas_call(attend_kernel, grid_spec=pltpu.PrefetchScalarGridSpec(num_...  47.5 us
    pallas_call x4, Pallas kernels, update(): pl.pallas_call(functools.partial(update_kernel, places, parts), grid_spec...  38.7 us
  transfers between devices with their start and end apart: 114, of which 44 were waited for; matrix products, arithmetic and copies ran while one was open for 15% of the time, Pallas kernels for 18%

profile of v9, /device:TPU:1, one launch (start us, length us, event | category | flops | bytes accessed | tf_op | source)
XLA Modules:
  0.0 1031.9 jit_solution(15659235777402427351)
XLA Ops:
  34.5 15.1 %shard_map.413 = bf16[2048,768]{1,0:T(8,128)(2,1)} custom-call(s32[9]{0:T(128)S(1)} %convert_reduce_fusion.1.starts_ref, s32[4096]{0:T(1024)S(1)} %get-tuple-element.213.places_ref, s32[4096]{0:T(1024)} %get-tuple-element.214.order_ref, f32[7632,768]{1,0:T(8,128)} %rest_8_.1), custom_call_target="tpu_custom_call" | custom-call | bytes 70336512 | tf_op jit(solution)/shard_map/pallas_call | solution.py:437
  68.8 8.5 collective-permute-done.12.refs_4_
  82.7 16.9 %collective-permute-done.14 = bf16[512,768]{1,0:T(8,128)(2,1)S(1)} collective-permute-done((bf16[512,768]{1,0:T(8,128)(2,1)S(1)}, bf16[512,768]{1,0:T(8,128)(2,1)S(1)}, u32[]{:S(2)}, u32[]{:S(2)}) %collective-permute-start.14) | collective-permute-done | bytes 786464 | tf_op jit(solution)/shard_map/ppermute | solution.py:723
  125.9 8.6 convert_element_type.339
  140.9 8.2 shard_map.414.w_ref.out_w_ref
  158.7 8.4 collective-permute-done.30
  191.2 8.6 collective-permute-done.35.refs_4_
  203.5 10.7 %shard_map.415.gu_w_ref = bf16[768,6144]{1,0:T(8,128)(2,1)} custom-call(s32[4]{0:T(128)} %and_select_fusion.1.members_ref, s32[8]{0:T(128)} %iota_xor_fusion.slots_ref, f32[192,6144]{1,0:T(8,128)} %own_ref.1, bf16[3,192,768]{2,1,0:T(8,128)(2,1)} %copy-done.19, bf16[3,192,768]{2,1,0:T(8,128)(2,1)} %copy-done.28, ...), custom_call_target="tpu_custom_call" | custom-call | bytes 18874368 | tf_op jit(solution)/shard_map/pallas_call | solution.py:668
  219.7 9.2 shard_map.416
  231.7 47.5 %shard_map.417 = (bf16[1024,768]{1,0:T(8,128)(2,1)}, f32[6,2,1024]{2,1,0:T(2,128)}) custom-call(s32[1]{0:T(128)S(6)} %copy.142.length_ref, bf16[1024,768]{1,0:T(8,128)(2,1)} %get-tuple-element.235.q_ref, bf16[1024,768]{1,0:T(8,128)(2,1)} %get-tuple-element.236.k_ref, bf16[1024,768]{1,0:T(8,128)(2,1)} %get-tuple-element.237.v_ref), custom_call_target="tpu_custom_call" | custom-call | flops 12884901888 | bytes 6291456 | tf_op jit(solution)/shard_map/pallas_call | solution.py:138
  295.2 30.0 %shard_map.419 = (f32[1024,768]{1,0:T(8,128)}, bf16[1024,768]{1,0:T(8,128)(2,1)}, f32[1024,6144]{1,0:T(8,128)}, bf16[1024,3072]{1,0:T(8,128)(2,1)}, f32[1024,768]{1,0:T(8,128)}, /*index=5*/f32[1024,768]{1,0:T(8,128)}) custom-call(bf16[1024,768]{1,0:T(8,128)(2,1)} %get-tuple-element.240.mixed_ref, f32[1024,768]{1,0:T(8,128)} %get-tuple-element.241.first_ref, ...), custom_call_target="tpu_custom_call" | custom-call | flops 15703474176 | bytes 44040192 | tf_op jit(solution)/shard_map/pallas_call | solution.py:293
  334.6 10.2 collective-permute-done.40
  344.9 10.8 %select_reduce_fusion.2 = (f32[512]{0:T(512)S(1)}, f32[7680,512]{1,0:T(8,128)S(1)}) fusion(pred[7680]{0:T(1024)(128)(4,1)S(1)} %copy-done.89, bf16[7680,768]{1,0:T(8,128)(2,1)} %pad.15, bf16[512,768]{1,0:T(8,128)(2,1)S(1)} %bitcast.274), kind=kOutput, calls=%fused_computation.19 | convolution fusion | flops 6047661568 | bytes 28321280 | tf_op jit(solution)/shard_map/dot_general | solution.py:869
  380.6 11.8 %fusion.108 = f32[512,768]{1,0:T(8,128)S(1)} fusion(bf16[7680,512]{1,0:T(8,128)(2,1)S(1)} %multiply_convert_fusion.dlogits_ref, bf16[7680,768]{1,0:T(8,128)(2,1)} %pad.15), kind=kOutput, calls=%fused_computation.303 | convolution fusion | flops 6039797760 | bytes 21233664 | tf_op jit(solution)/shard_map/dot_general | solution.py:869
  400.7 23.9 %collective-permute-done.49 = f32[128,768]{1,0:T(8,128)S(1)} collective-permute-done((f32[128,768]{1,0:T(8,128)S(1)}, f32[128,768]{1,0:T(8,128)S(1)}, u32[]{:S(2)}, u32[]{:S(2)}) %collective-permute-start.49) | collective-permute-done | bytes 393248 | tf_op jit(solution)/shard_map/ppermute | solution.py:723
  428.1 33.9 %shard_map.420 = (bf16[1024,768]{1,0:T(8,128)(2,1)}, bf16[1024,6144]{1,0:T(8,128)(2,1)}, f32[1024,768]{1,0:T(8,128)}, bf16[1024,768]{1,0:T(8,128)(2,1)}, bf16[1024,768]{1,0:T(8,128)(2,1)}, /*index=5*/f32[4,768]{1,0:T(4,128)}) custom-call(f32[1024,768]{1,0:T(8,128)} %scatter_custom_fusion.grad_ref, f32[1024,768]{1,0:T(8,128)} %get-tuple-element.253.second_sum_ref, ...), custom_call_target="tpu_custom_call" | custom-call | flops 15703474176 | bytes 44040192 | tf_op jit(solution)/shard_map/pallas_call | solution.py:378
  512.5 21.6 %shard_map.421 = (bf16[1024,256]{1,0:T(8,128)(2,1)}, bf16[1024,256]{1,0:T(8,128)(2,1)}, bf16[1024,256]{1,0:T(8,128)(2,1)}) custom-call(s32[1]{0:T(128)S(6)} %copy.142.length_ref, bf16[1024,768]{1,0:T(8,128)(2,1)} %get-tuple-element.235.q_ref, bf16[1024,768]{1,0:T(8,128)(2,1)} %get-tuple-element.236.k_ref, bf16[1024,768]{1,0:T(8,128)(2,1)} %get-tuple-element.237.v_ref, ...), custom_call_target="tpu_custom_call" | custom-call | flops 10737418240 | bytes 4194304 | tf_op jit(solution)/shard_map/pallas_call | solution.py:223
  543.0 21.8 %shard_map.422 = (bf16[1024,256]{1,0:T(8,128)(2,1)}, bf16[1024,256]{1,0:T(8,128)(2,1)}, bf16[1024,256]{1,0:T(8,128)(2,1)}) custom-call(s32[1]{0:T(128)S(6)} %copy.142.length_ref, bf16[1024,768]{1,0:T(8,128)(2,1)} %get-tuple-element.235.q_ref, bf16[1024,768]{1,0:T(8,128)(2,1)} %get-tuple-element.236.k_ref, bf16[1024,768]{1,0:T(8,128)(2,1)} %get-tuple-element.237.v_ref, ...), custom_call_target="tpu_custom_call" | custom-call | flops 10737418240 | bytes 4194304 | tf_op jit(solution)/shard_map/pallas_call | solution.py:223
  584.8 21.7 %shard_map.423 = (bf16[1024,256]{1,0:T(8,128)(2,1)}, bf16[1024,256]{1,0:T(8,128)(2,1)}, bf16[1024,256]{1,0:T(8,128)(2,1)}) custom-call(s32[1]{0:T(128)S(6)} %copy.142.length_ref, bf16[1024,768]{1,0:T(8,128)(2,1)} %get-tuple-element.235.q_ref, bf16[1024,768]{1,0:T(8,128)(2,1)} %get-tuple-element.236.k_ref, bf16[1024,768]{1,0:T(8,128)(2,1)} %get-tuple-element.237.v_ref, ...), custom_call_target="tpu_custom_call" | custom-call | flops 10737418240 | bytes 4194304 | tf_op jit(solution)/shard_map/pallas_call | solution.py:223
  628.7 9.8 fusion.110
  664.3 16.6 %collective-permute-done.80 = bf16[24,3072]{1,0:T(8,128)(2,1)S(1)} collective-permute-done((bf16[24,3072]{1,0:T(8,128)(2,1)S(1)}, bf16[24,3072]{1,0:T(8,128)(2,1)S(1)}, u32[]{:S(2)}, u32[]{:S(2)}) %collective-permute-start.80) | collective-permute-done | bytes 147488 | tf_op jit(solution)/shard_map/ppermute | solution.py:723
  681.9 9.4 collective-permute-done.67
  693.8 8.8 collective-permute-done.83.refs_2_
  726.7 14.2 %collective-permute-done.70 = bf16[24,3072]{1,0:T(8,128)(2,1)S(1)} collective-permute-done((bf16[24,3072]{1,0:T(8,128)(2,1)S(1)}, bf16[24,3072]{1,0:T(8,128)(2,1)S(1)}, u32[]{:S(2)}, u32[]{:S(2)}) %collective-permute-start.70) | collective-permute-done | bytes 147488 | tf_op jit(solution)/shard_map/ppermute | solution.py:723
  767.1 17.8 %all-gather.2.cloned.1.call-done.embed_ref = bf16[4096,768]{1,0:T(8,128)(2,1)} async-done(((bf16[1024,768]{1,0:T(8,128)(2,1)}), bf16[4096,768]{1,0:T(8,128)(2,1)}) %all-gather.2.cloned.1.call-update) | async-done | bytes 6291472 | tf_op jit(solution)/shard_map/all_gather | solution.py:1095
  784.9 13.6 %shard_map.426 = bf16[4,960,768]{2,1,0:T(8,128)(2,1)} custom-call(s32[4]{0:T(128)} %add_subtract_fusion.chunks_ref, s32[9]{0:T(128)S(1)} %copy-done.110, s32[4104]{0:T(1024)} %pad.16.codes_ref, s32[4104]{0:T(1024)} %pad.17.order_ref, bf16[7680,512]{1,0:T(8,128)(2,1)} %copy-done, bf16[512,768]{1,0:T(8,128)(2,1)} %bitcast.275, ...), custom_call_target="tpu_custom_call" | custom-call | flops 3019898880 | bytes 23592960 | tf_op jit(solution)/shard_map/pallas_call | solution.py:530
  799.1 9.1 collective-permute-done.89.refs_0_
  810.8 16.4 %shard_map.427 = (bf16[2,960,384]{2,1,0:T(8,128)(2,1)}, f32[2,960,384]{2,1,0:T(8,128)}, bf16[2,960,384]{2,1,0:T(8,128)(2,1)}, f32[2,960,384]{2,1,0:T(8,128)}) custom-call(s32[4]{0:T(128)} %broadcast_add_fusion.chunks_ref, s32[9]{0:T(128)S(1)} %copy-done.110, s32[4104]{0:T(1024)} %pad.16.codes_ref, s32[4104]{0:T(1024)} %pad.17.order_ref, ...), custom_call_target="tpu_custom_call" | custom-call | flops 3019898880 | bytes 23592960 | tf_op jit(solution)/shard_map/pallas_call | solution.py:530
  828.3 32.8 %collective-permute-done.90 = bf16[2,960,384]{2,1,0:T(8,128)(2,1)S(1)} collective-permute-done((bf16[2,960,384]{2,1,0:T(8,128)(2,1)}, bf16[2,960,384]{2,1,0:T(8,128)(2,1)S(1)}, u32[]{:S(2)}, u32[]{:S(2)}) %collective-permute-start.90) | collective-permute-done | bytes 1474592 | tf_op jit(solution)/shard_map/ppermute | solution.py:718
  969.3 12.2 %collective-permute-done.111.rest_1_ = bf16[960,384]{1,0:T(8,128)(2,1)} collective-permute-done((bf16[960,384]{1,0:T(8,128)(2,1)}, bf16[960,384]{1,0:T(8,128)(2,1)}, u32[]{:S(2)}, u32[]{:S(2)}) %collective-permute-start.111) | collective-permute-done | bytes 737312 | tf_op jit(solution)/shard_map/ppermute | solution.py:718
  985.6 9.9 shard_map.432
  1002.7 17.8 %shard_map.434 = (f32[7632,768]{1,0:T(8,128)}, f32[7632,768]{1,0:T(8,128)}, f32[16,1,480]{2,1,0:T(1,128)}) custom-call(s32[8]{0:T(128)} %iota_xor_fusion.slots_ref, f32[2]{0:T(128)} %pad_maximum_fusion.11.scalars_ref, bf16[960,384]{1,0:T(8,128)(2,1)} %collective-permute-done.99.rest_0_, ...), custom_call_target="tpu_custom_call", output_to_operand_aliasing={{0}: (13, {}), {1}: (14, {}), {2}: (15, {})} | custom-call | flops 29491200 | bytes 41287680 | tf_op jit(solution)/shard_map/pallas_call | solution.py:593
  (671 shorter events, 485.4 us)
Async XLA Ops:
  24.1 31.7 %collective-permute-start.10 = (bf16[192,768]{1,0:T(8,128)(2,1)}, bf16[192,768]{1,0:T(8,128)(2,1)S(1)}, u32[]{:S(2)}, u32[]{:S(2)}) collective-permute-start(bf16[192,768]{1,0:T(8,128)(2,1)} %dynamic-slice_convert_fusion.7), channel_id=1, source_target_pairs={{0,16},{8,24},{16,0},{24,8},{1,17},{9,25},{17,1},{25,9},{2,18},{10... | collective-permute-start | bytes 884744 | tf_op jit(solution)/shard_map/ppermute | solution.py:723
  66.5 33.1 %collective-permute-start.14 = (bf16[512,768]{1,0:T(8,128)(2,1)S(1)}, bf16[512,768]{1,0:T(8,128)(2,1)S(1)}, u32[]{:S(2)}, u32[]{:S(2)}) collective-permute-start(bf16[512,768]{1,0:T(8,128)(2,1)S(1)} %get-tuple-element.376), channel_id=1, source_target_pairs={{0,24},{8,0},{16,8},{24,16},{1,25},{9,1},{17,9},{25,17},{2,26},{10... | collective-permute-start | bytes 2359304 | tf_op jit(solution)/shard_map/ppermute | solution.py:723
  67.6 36.4 %collective-permute-start.15 = (bf16[3,192,768]{2,1,0:T(8,128)(2,1)S(1)}, bf16[3,192,768]{2,1,0:T(8,128)(2,1)}, u32[]{:S(2)}, u32[]{:S(2)}) collective-permute-start(bf16[3,192,768]{2,1,0:T(8,128)(2,1)S(1)} %pad_maximum_fusion.2.refs_0_), channel_id=1, source_target_pairs={{0,2},{1,3},{2,0},{3,1},{4,6},{5,7},{6,4},{7,5},{8,10},{9,11},{10,... | collective-permute-start | bytes 2654216 | tf_op jit(solution)/shard_map/ppermute | solution.py:718
  102.3 50.0 %collective-permute-start.16 = (bf16[3,192,768]{2,1,0:T(8,128)(2,1)S(1)}, bf16[3,192,768]{2,1,0:T(8,128)(2,1)}, u32[]{:S(2)}, u32[]{:S(2)}) collective-permute-start(bf16[3,192,768]{2,1,0:T(8,128)(2,1)S(1)} %pad_maximum_fusion.2.refs_0_), channel_id=1, source_target_pairs={{0,4},{1,5},{2,6},{3,7},{4,0},{5,1},{6,2},{7,3},{8,12},{9,13},{10,... | collective-permute-start | bytes 2654216 | tf_op jit(solution)/shard_map/ppermute | solution.py:718
  104.3 48.8 %collective-permute-start.17 = (bf16[3,192,768]{2,1,0:T(8,128)(2,1)}, bf16[3,192,768]{2,1,0:T(8,128)(2,1)}, u32[]{:S(2)}, u32[]{:S(2)}) collective-permute-start(bf16[3,192,768]{2,1,0:T(8,128)(2,1)} %collective-permute-done.15.refs_2_), channel_id=1, source_target_pairs={{0,4},{1,5},{2,6},{3,7},{4,0},{5,1},{6,2},{7,3},{8,12},{9,13},{10,... | collective-permute-start | bytes 2654216 | tf_op jit(solution)/shard_map/ppermute | solution.py:718
  113.1 39.1 %collective-permute-start.24 = (bf16[512,768]{1,0:T(8,128)(2,1)}, bf16[512,768]{1,0:T(8,128)(2,1)S(1)}, u32[]{:S(2)}, u32[]{:S(2)}) collective-permute-start(bf16[512,768]{1,0:T(8,128)(2,1)} %get-tuple-element.375), channel_id=1, source_target_pairs={{0,16},{8,24},{16,0},{24,8},{1,17},{9,25},{17,1},{25,9},{2,18},{10... | collective-permute-start | bytes 2359304 | tf_op jit(solution)/shard_map/ppermute | solution.py:723
  199.8 31.7 %collective-permute-start.37 = (bf16[3,96,768]{2,1,0:T(8,128)(2,1)S(1)}, bf16[3,96,768]{2,1,0:T(8,128)(2,1)S(1)}, u32[]{:S(2)}, u32[]{:S(2)}) collective-permute-start(bf16[3,96,768]{2,1,0:T(8,128)(2,1)S(1)} %collective-permute-done.35.refs_4_), channel_id=1, source_target_pairs={{0,2},{1,3},{2,0},{3,1},{4,6},{5,7},{6,4},{7,5},{8,10},{9,11},{10,... | collective-permute-start | bytes 1327112 | tf_op jit(solution)/shard_map/ppermute | solution.py:718
  201.8 84.0 %collective-permute-start.32 = (bf16[3,96,768]{2,1,0:T(8,128)(2,1)}, bf16[3,96,768]{2,1,0:T(8,128)(2,1)S(1)}, u32[]{:S(2)}, u32[]{:S(2)}) collective-permute-start(bf16[3,96,768]{2,1,0:T(8,128)(2,1)} %pad_maximum_fusion.7.refs_0_), channel_id=1, source_target_pairs={{0,1},{1,0},{2,3},{3,2},{4,5},{5,4},{6,7},{7,6},{8,9},{9,8},{10,11... | collective-permute-start | bytes 1327112 | tf_op jit(solution)/shard_map/ppermute | solution.py:718
  202.9 82.9 %collective-permute-start.36 = (bf16[3,96,768]{2,1,0:T(8,128)(2,1)S(1)}, bf16[3,96,768]{2,1,0:T(8,128)(2,1)S(1)}, u32[]{:S(2)}, u32[]{:S(2)}) collective-permute-start(bf16[3,96,768]{2,1,0:T(8,128)(2,1)S(1)} %collective-permute-done.35.refs_4_), channel_id=1, source_target_pairs={{0,1},{1,0},{2,3},{3,2},{4,5},{5,4},{6,7},{7,6},{8,9},{9,8},{10,11... | collective-permute-start | bytes 1327112 | tf_op jit(solution)/shard_map/ppermute | solution.py:718
  203.0 82.8 %collective-permute-start.34 = (bf16[3,96,768]{2,1,0:T(8,128)(2,1)}, bf16[3,96,768]{2,1,0:T(8,128)(2,1)S(1)}, u32[]{:S(2)}, u32[]{:S(2)}) collective-permute-start(bf16[3,96,768]{2,1,0:T(8,128)(2,1)} %collective-permute-done.33.refs_2_), channel_id=1, source_target_pairs={{0,1},{1,0},{2,3},{3,2},{4,5},{5,4},{6,7},{7,6},{8,9},{9,8},{10,11... | collective-permute-start | bytes 1327112 | tf_op jit(solution)/shard_map/ppermute | solution.py:718
  219.2 565.7 %all-gather.2.cloned.1.call-start = ((), (), s32[]{:S(2)}) async-start(), calls=%async_computation.2 | async-start | bytes 7864320 | tf_op jit(solution)/shard_map/all_gather | solution.py:1095
  230.2 49.1 %collective-permute-start.45 = (f32[1]{0:T(128)}, f32[1]{0:T(128)}, u32[]{:S(2)}, u32[]{:S(2)}) collective-permute-start(f32[1]{0:T(128)} %bitcast.41), channel_id=1, source_target_pairs={{0,1},{1,0},{2,3},{3,2},{4,5},{5,4},{6,7},{7,6},{8,9},{9,8},{10,11... | collective-permute-start | bytes 20 | tf_op jit(solution)/shard_map/ppermute | solution.py:718
  231.5 54.4 %collective-permute-start.38 = (bf16[3,96,768]{2,1,0:T(8,128)(2,1)S(1)}, bf16[3,96,768]{2,1,0:T(8,128)(2,1)S(1)}, u32[]{:S(2)}, u32[]{:S(2)}) collective-permute-start(bf16[3,96,768]{2,1,0:T(8,128)(2,1)S(1)} %collective-permute-done.37.refs_6_), channel_id=1, source_target_pairs={{0,1},{1,0},{2,3},{3,2},{4,5},{5,4},{6,7},{7,6},{8,9},{9,8},{10,11... | collective-permute-start | bytes 1327112 | tf_op jit(solution)/shard_map/ppermute | solution.py:718
  471.6 31.7 %collective-permute-start.51 = (bf16[4,4,96,768]{3,2,1,0:T(8,128)(2,1)}, bf16[4,4,96,768]{3,2,1,0:T(8,128)(2,1)}, u32[]{:S(2)}, u32[]{:S(2)}) collective-permute-start(bf16[4,4,96,768]{3,2,1,0:T(8,128)(2,1)} %fusion.23), channel_id=1, source_target_pairs={{0,1},{1,0},{2,3},{3,2},{4,5},{5,4},{6,7},{7,6},{8,9},{9,8},{10,11... | collective-permute-start | bytes 7077896 | tf_op jit(solution)/shard_map/ppermute | solution.py:718
  501.2 32.9 %collective-permute-start.55 = (bf16[4,2,24,3072]{3,2,0,1:T(8,128)(2,1)S(1)}, bf16[4,2,24,3072]{3,2,0,1:T(8,128)(2,1)}, u32[]{:S(2)}, u32[]{:S(2)}) collective-permute-start(bf16[4,2,24,3072]{3,2,0,1:T(8,128)(2,1)S(1)} %fusion.34), channel_id=1, source_target_pairs={{0,2},{1,3},{2,0},{3,1},{4,6},{5,7},{6,4},{7,5},{8,10},{9,11},{10,... | collective-permute-start | bytes 3538952 | tf_op jit(solution)/shard_map/ppermute | solution.py:718
  512.1 52.8 %collective-permute-start.58 = (bf16[4,2,24,3072]{3,2,0,1:T(8,128)(2,1)S(1)}, bf16[4,2,24,3072]{3,2,0,1:T(8,128)(2,1)}, u32[]{:S(2)}, u32[]{:S(2)}) collective-permute-start(bf16[4,2,24,3072]{3,2,0,1:T(8,128)(2,1)S(1)} %fusion.33), channel_id=1, source_target_pairs={{0,4},{1,5},{2,6},{3,7},{4,0},{5,1},{6,2},{7,3},{8,12},{9,13},{10,... | collective-permute-start | bytes 3538952 | tf_op jit(solution)/shard_map/ppermute | solution.py:718
  542.0 34.7 %collective-permute-start.57 = (bf16[4,24,3072]{2,1,0:T(8,128)(2,1)}, bf16[4,24,3072]{2,1,0:T(8,128)(2,1)}, u32[]{:S(2)}, u32[]{:S(2)}) collective-permute-start(bf16[4,24,3072]{2,1,0:T(8,128)(2,1)} %fusion.44), channel_id=1, source_target_pairs={{0,4},{1,5},{2,6},{3,7},{4,0},{5,1},{6,2},{7,3},{8,12},{9,13},{10,... | collective-permute-start | bytes 1769480 | tf_op jit(solution)/shard_map/ppermute | solution.py:718
  567.5 39.1 %collective-permute-start.65 = (bf16[4,24,3072]{2,1,0:T(8,128)(2,1)}, bf16[4,24,3072]{2,1,0:T(8,128)(2,1)}, u32[]{:S(2)}, u32[]{:S(2)}) collective-permute-start(bf16[4,24,3072]{2,1,0:T(8,128)(2,1)} %fusion.45), channel_id=1, source_target_pairs={{0,2},{1,3},{2,0},{3,1},{4,6},{5,7},{6,4},{7,5},{8,10},{9,11},{10,... | collective-permute-start | bytes 1769480 | tf_op jit(solution)/shard_map/ppermute | solution.py:718
  708.7 32.1 %collective-permute-start.70 = (bf16[24,3072]{1,0:T(8,128)(2,1)S(1)}, bf16[24,3072]{1,0:T(8,128)(2,1)S(1)}, u32[]{:S(2)}, u32[]{:S(2)}) collective-permute-start(bf16[24,3072]{1,0:T(8,128)(2,1)S(1)} %get-tuple-element.385), channel_id=1, source_target_pairs={{0,16},{8,24},{16,0},{24,8},{1,17},{9,25},{17,1},{25,9},{2,18},{10... | collective-permute-start | bytes 442376 | tf_op jit(solution)/shard_map/ppermute | solution.py:723
  708.7 34.2 %collective-permute-start.69 = (bf16[24,3072]{1,0:T(8,128)(2,1)S(1)}, bf16[24,3072]{1,0:T(8,128)(2,1)S(1)}, u32[]{:S(2)}, u32[]{:S(2)}) collective-permute-start(bf16[24,3072]{1,0:T(8,128)(2,1)S(1)} %get-tuple-element.383), channel_id=1, source_target_pairs={{0,8},{8,16},{16,24},{24,0},{1,9},{9,17},{17,25},{25,1},{2,10},{10... | collective-permute-start | bytes 442376 | tf_op jit(solution)/shard_map/ppermute | solution.py:723
  827.2 33.9 %collective-permute-start.90 = (bf16[2,960,384]{2,1,0:T(8,128)(2,1)}, bf16[2,960,384]{2,1,0:T(8,128)(2,1)S(1)}, u32[]{:S(2)}, u32[]{:S(2)}) collective-permute-start(bf16[2,960,384]{2,1,0:T(8,128)(2,1)} %get-tuple-element.308), channel_id=1, source_target_pairs={{0,2},{1,3},{2,0},{3,1},{4,6},{5,7},{6,4},{7,5},{8,10},{9,11},{10,... | collective-permute-start | bytes 4423688 | tf_op jit(solution)/shard_map/ppermute | solution.py:718
  827.2 37.4 %collective-permute-start.92 = (bf16[2,960,384]{2,1,0:T(8,128)(2,1)}, bf16[2,960,384]{2,1,0:T(8,128)(2,1)S(1)}, u32[]{:S(2)}, u32[]{:S(2)}) collective-permute-start(bf16[2,960,384]{2,1,0:T(8,128)(2,1)} %get-tuple-element.310), channel_id=1, source_target_pairs={{0,4},{1,5},{2,6},{3,7},{4,0},{5,1},{6,2},{7,3},{8,12},{9,13},{10,... | collective-permute-start | bytes 4423688 | tf_op jit(solution)/shard_map/ppermute | solution.py:718
  910.4 37.8 %collective-permute-start.99 = (bf16[960,384]{1,0:T(8,128)(2,1)}, bf16[960,384]{1,0:T(8,128)(2,1)}, u32[]{:S(2)}, u32[]{:S(2)}) collective-permute-start(bf16[960,384]{1,0:T(8,128)(2,1)} %get-tuple-element.316.rest_0_), channel_id=1, source_target_pairs={{0,1},{1,0},{2,3},{3,2},{4,5},{5,4},{6,7},{7,6},{8,9},{9,8},{10,11... | collective-permute-start | bytes 2211848 | tf_op jit(solution)/shard_map/ppermute | solution.py:718
  911.6 36.9 %collective-permute-start.101 = (bf16[960,384]{1,0:T(8,128)(2,1)}, bf16[960,384]{1,0:T(8,128)(2,1)}, u32[]{:S(2)}, u32[]{:S(2)}) collective-permute-start(bf16[960,384]{1,0:T(8,128)(2,1)} %get-tuple-element.316.rest_0_), channel_id=1, source_target_pairs={{0,2},{1,3},{2,0},{3,1},{4,6},{5,7},{6,4},{7,5},{8,10},{9,11},{10,... | collective-permute-start | bytes 2211848 | tf_op jit(solution)/shard_map/ppermute | solution.py:718
  911.7 54.2 %collective-permute-start.100 = (bf16[960,384]{1,0:T(8,128)(2,1)}, bf16[960,384]{1,0:T(8,128)(2,1)}, u32[]{:S(2)}, u32[]{:S(2)}) collective-permute-start(bf16[960,384]{1,0:T(8,128)(2,1)} %get-tuple-element.317.rest_1_), channel_id=1, source_target_pairs={{0,1},{1,0},{2,3},{3,2},{4,5},{5,4},{6,7},{7,6},{8,9},{9,8},{10,11... | collective-permute-start | bytes 2211848 | tf_op jit(solution)/shard_map/ppermute | solution.py:718
  912.0 37.7 %collective-permute-start.103 = (bf16[960,384]{1,0:T(8,128)(2,1)}, bf16[960,384]{1,0:T(8,128)(2,1)}, u32[]{:S(2)}, u32[]{:S(2)}) collective-permute-start(bf16[960,384]{1,0:T(8,128)(2,1)} %get-tuple-element.317.rest_1_), channel_id=1, source_target_pairs={{0,2},{1,3},{2,0},{3,1},{4,6},{5,7},{6,4},{7,5},{8,10},{9,11},{10,... | collective-permute-start | bytes 2211848 | tf_op jit(solution)/shard_map/ppermute | solution.py:718
  913.5 36.2 %collective-permute-start.105 = (bf16[960,384]{1,0:T(8,128)(2,1)}, bf16[960,384]{1,0:T(8,128)(2,1)}, u32[]{:S(2)}, u32[]{:S(2)}) collective-permute-start(bf16[960,384]{1,0:T(8,128)(2,1)} %get-tuple-element.316.rest_0_), channel_id=1, source_target_pairs={{0,4},{1,5},{2,6},{3,7},{4,0},{5,1},{6,2},{7,3},{8,12},{9,13},{10,... | collective-permute-start | bytes 2211848 | tf_op jit(solution)/shard_map/ppermute | solution.py:718
  949.7 31.9 %collective-permute-start.111 = (bf16[960,384]{1,0:T(8,128)(2,1)}, bf16[960,384]{1,0:T(8,128)(2,1)}, u32[]{:S(2)}, u32[]{:S(2)}) collective-permute-start(bf16[960,384]{1,0:T(8,128)(2,1)} %collective-permute-done.103.rest_1_), channel_id=1, source_target_pairs={{0,4},{1,5},{2,6},{3,7},{4,0},{5,1},{6,2},{7,3},{8,12},{9,13},{10,... | collective-permute-start | bytes 2211848 | tf_op jit(solution)/shard_map/ppermute | solution.py:718
  965.9 35.0 %collective-permute-start.104 = (bf16[960,384]{1,0:T(8,128)(2,1)}, bf16[960,384]{1,0:T(8,128)(2,1)S(1)}, u32[]{:S(2)}, u32[]{:S(2)}) collective-permute-start(bf16[960,384]{1,0:T(8,128)(2,1)} %collective-permute-done.103.rest_1_), channel_id=1, source_target_pairs={{0,1},{1,0},{2,3},{3,2},{4,5},{5,4},{6,7},{7,6},{8,9},{9,8},{10,11... | collective-permute-start | bytes 2211848 | tf_op jit(solution)/shard_map/ppermute | solution.py:718
  966.5 34.4 %collective-permute-start.106 = (bf16[960,384]{1,0:T(8,128)(2,1)}, bf16[960,384]{1,0:T(8,128)(2,1)S(1)}, u32[]{:S(2)}, u32[]{:S(2)}) collective-permute-start(bf16[960,384]{1,0:T(8,128)(2,1)} %collective-permute-done.105.rest_2_), channel_id=1, source_target_pairs={{0,1},{1,0},{2,3},{3,2},{4,5},{5,4},{6,7},{7,6},{8,9},{9,8},{10,11... | collective-permute-start | bytes 2211848 | tf_op jit(solution)/shard_map/ppermute | solution.py:718
  968.8 32.1 %collective-permute-start.108 = (bf16[960,384]{1,0:T(8,128)(2,1)}, bf16[960,384]{1,0:T(8,128)(2,1)S(1)}, u32[]{:S(2)}, u32[]{:S(2)}) collective-permute-start(bf16[960,384]{1,0:T(8,128)(2,1)} %collective-permute-done.107.rest_3_), channel_id=1, source_target_pairs={{0,1},{1,0},{2,3},{3,2},{4,5},{5,4},{6,7},{7,6},{8,9},{9,8},{10,11... | collective-permute-start | bytes 2211848 | tf_op jit(solution)/shard_map/ppermute | solution.py:718
  968.9 32.0 %collective-permute-start.110 = (bf16[960,384]{1,0:T(8,128)(2,1)}, bf16[960,384]{1,0:T(8,128)(2,1)S(1)}, u32[]{:S(2)}, u32[]{:S(2)}) collective-permute-start(bf16[960,384]{1,0:T(8,128)(2,1)} %collective-permute-done.109.rest_0_), channel_id=1, source_target_pairs={{0,1},{1,0},{2,3},{3,2},{4,5},{5,4},{6,7},{7,6},{8,9},{9,8},{10,11... | collective-permute-start | bytes 2211848 | tf_op jit(solution)/shard_map/ppermute | solution.py:718
  (207 other events, 3033.4 us)
Sparse Core Ops, SparseCore 1:
  653.3 131.5 all-gather.1

commit v10 on v8

--- a/solution.py
+++ b/solution.py
@@ -724,10 +724,14 @@
     return lax.ppermute(value, "grp", [(i, (i + offset) % size) for i in range(size)])
 
 
+def wave(have, bit):
+    return have | {place ^ bit: flip(part, bit) for place, part in have.items()}
+
+
 def spread(piece, order):
     have = {0: piece}
     for bit in order:
-        have.update({place ^ bit: flip(part, bit) for place, part in have.items()})
+        have = wave(have, bit)
     return have
 
 
@@ -811,13 +815,13 @@
     return gradient.reshape(groups, replicas, rows // (groups * replicas), columns)
 
 
-def across_wide(chunks):
+def across(chunks):
     member = lax.axis_index("grp")
     size = lax.axis_size("grp")
     total = lax.dynamic_index_in_dim(chunks, member, 0, keepdims=False)
     for offset in range(1, size):
         sent = lax.dynamic_index_in_dim(chunks, (member + offset) % size, 0, keepdims=False)
-        total = total + turn(sent, offset)
+        total = total + turn(sent.astype(low_type), offset).astype(jnp.float32)
     return total
 
 
@@ -1016,7 +1020,7 @@
         (jnp.exp(logits - log_total[None, :]) - hits.astype(jnp.float32)) * row_scale[None, :]
     ).astype(low_type)
     chosen_part = contract(dlogits, table_low, 0, 0)
-    chosen_grad = across_wide(chosen_part.reshape(groups, own_rows, width))
+    chosen_grad = across(chosen_part.reshape(groups, own_rows, width))
     final_grad = jnp.zeros((tokens, width), jnp.float32).at[flat_picks].add(chosen_grad)
 
     branch_low, gate_low, first_sum_grad, attn_low, mixed_grad, late_norms = feed_backward(
@@ -1106,6 +1110,9 @@
     plane_totals = plane_sum(jnp.concatenate(small))
     table_lows = [part.astype(low_type) for part in table_parts]
     plane_totals, table_lows = tie((plane_totals, table_lows))
+    if quick:
+        have = [spread(low, bits) for low, bits in zip(table_lows, ((4, 2), (2, 4)))]
+        plane_totals, have = tie((plane_totals, have))
     totals = rest_sum(plane_totals)
     cuts = []
     start = 0
@@ -1139,9 +1146,7 @@
         row_total = decay * old_totals[place] + (1.0 - decay) * (squares[place] * factor * factor) / columns
         row_mean = row_total / full_rows
         if place == 0 and quick:
-            have = [
-                spread(low, [2, 4, 1] if part % 2 else [4, 2, 1]) for part, low in enumerate(table_lows)
-            ]
+            have = [wave(got, 1) for got in have]
             tiles = padded // TILE
             row_tiles = jnp.pad(table_rows, (0, padded - vocab_rows), constant_values=1.0).reshape(tiles, 1, TILE)
             scalars = jnp.stack([factor, rate_matrix * factor * jnp.sqrt(row_mean)])

time: 997 us -> 1020 us (1.023)
  waiting for transfers between devices: 239 us -> 264 us
    ppermute x72, waiting for transfers between devices: 146 us -> 175 us  [flip(): return lax.ppermute(value, 'rep', [(i, i ^ bit) for i in range(size)])]
    unnamed x229 -> x219, local copies, waits for them, and re-layouts: 21.3 us -> 20 us
  transfers between devices with their start and end apart: 109 -> 109, of which waited for: 39 -> 42; matrix products, arithmetic and copies ran while one was open for 15% -> 15% of each run, Pallas kernels for 14% -> 14%
where the time goes in v10:
time: 1020 us
  Pallas kernels  311 us (30%)
  waiting for transfers between devices  264 us (26%)
  starting transfers between devices  142 us (14%)
  other arithmetic  134 us (13%)
  local copies, waits for them, and re-layouts  66.5 us (7%)
  matrix products  65.7 us (6%)
  between operations  32.3 us (3%)
    ppermute x72, waiting for transfers between devices, flip(): return lax.ppermute(value, 'rep', [(i, i ^ bit) for i in range(size)])  175 us
    ppermute x72, starting transfers between devices, flip(): return lax.ppermute(value, 'rep', [(i, i ^ bit) for i in range(size)])  83 us
    ppermute x33, waiting for transfers between devices, turn(): lax.ppermute(value, 'grp', [(i, (i + offset) % size) for i in range(size)])  68.7 us
    dot_general x8, matrix products, contract(): lax.dot_general(left, right, (((left_dim,), (right_dim,)), ((), ())), pre...  65.7 us
    pallas_call x3, Pallas kernels, attend_back(): pl.pallas_call(functools.partial(attend_back_kernel, first_pair), grid_sp...  65.2 us
    ppermute x33, starting transfers between devices, turn(): lax.ppermute(value, 'grp', [(i, (i + offset) % size) for i in range(size)])  51.7 us
    pallas_call x1, Pallas kernels, attend(): pl.pallas_call(attend_kernel, grid_spec=pltpu.PrefetchScalarGridSpec(num_...  47.6 us
    pallas_call x4, Pallas kernels, update(): pl.pallas_call(functools.partial(update_kernel, places, parts), grid_spec...  38.7 us
  transfers between devices with their start and end apart: 109, of which 42 were waited for; matrix products, arithmetic and copies ran while one was open for 15% of the time, Pallas kernels for 14%

profile of v10, /device:TPU:1, one launch (start us, length us, event | category | flops | bytes accessed | tf_op | source)
XLA Modules:
  0.0 1015.9 jit_solution(11461415272237152242)
XLA Ops:
  37.7 17.3 %shard_map.413 = bf16[4096,768]{1,0:T(8,128)(2,1)} custom-call(s32[9]{0:T(128)} %convert_reduce_fusion.1.starts_ref, s32[4096]{0:T(1024)} %copy-done.67, s32[4096]{0:T(1024)} %get-tuple-element.144.order_ref, f32[7632,768]{1,0:T(8,128)} %rest_8_.1), custom_call_target="tpu_custom_call" | custom-call | bytes 70336512 | tf_op jit(solution)/shard_map/pallas_call | solution.py:438
  72.7 25.7 %collective-permute-done.20 = bf16[96,768]{1,0:T(8,128)(2,1)S(1)} collective-permute-done((bf16[96,768]{1,0:T(8,128)(2,1)S(1)}, bf16[96,768]{1,0:T(8,128)(2,1)S(1)}, u32[]{:S(2)}, u32[]{:S(2)}) %collective-permute-start.20) | collective-permute-done | bytes 147488 | tf_op jit(solution)/shard_map/ppermute | solution.py:724
  106.7 25.6 %collective-permute-done.23.refs_2_ = bf16[3,96,768]{2,1,0:T(8,128)(2,1)S(1)} collective-permute-done((bf16[3,96,768]{2,1,0:T(8,128)(2,1)S(1)}, bf16[3,96,768]{2,1,0:T(8,128)(2,1)S(1)}, u32[]{:S(2)}, u32[]{:S(2)}) %collective-permute-start.23) | collective-permute-done | bytes 442400 | tf_op jit(solution)/shard_map/ppermute | solution.py:719
  154.1 8.6 convert_element_type.341
  167.7 8.2 shard_map.414.w_ref.out_w_ref
  175.9 8.2 shard_map.415
  191.1 10.7 %shard_map.416.gu_w_ref = bf16[768,6144]{1,0:T(8,128)(2,1)} custom-call(s32[4]{0:T(128)} %and_select_fusion.members_ref, s32[8]{0:T(128)} %iota_xor_fusion.slots_ref, f32[192,6144]{1,0:T(8,128)} %own_ref.1, bf16[3,192,768]{2,1,0:T(8,128)(2,1)} %copy-done.23, bf16[3,192,768]{2,1,0:T(8,128)(2,1)} %collective-permute-done.29.refs_1_, ...), custom_call_target="tpu_custom_call" | custom-call | bytes 18874368 | tf_op jit(solution)/shard_map/pallas_call | solution.py:669
  201.8 9.2 shard_map.417
  211.0 47.6 %shard_map.418 = (bf16[1024,768]{1,0:T(8,128)(2,1)}, f32[6,2,1024]{2,1,0:T(2,128)}) custom-call(s32[1]{0:T(128)S(6)} %copy.137.length_ref, bf16[1024,768]{1,0:T(8,128)(2,1)} %get-tuple-element.161.q_ref, bf16[1024,768]{1,0:T(8,128)(2,1)} %get-tuple-element.162.k_ref, bf16[1024,768]{1,0:T(8,128)(2,1)} %get-tuple-element.163.v_ref), custom_call_target="tpu_custom_call" | custom-call | flops 12884901888 | bytes 6291456 | tf_op jit(solution)/shard_map/pallas_call | solution.py:138
  258.6 30.1 %shard_map.419 = (f32[1024,768]{1,0:T(8,128)}, bf16[1024,768]{1,0:T(8,128)(2,1)}, f32[1024,6144]{1,0:T(8,128)}, bf16[1024,3072]{1,0:T(8,128)(2,1)}, f32[1024,768]{1,0:T(8,128)}, /*index=5*/f32[1024,768]{1,0:T(8,128)}) custom-call(bf16[1024,768]{1,0:T(8,128)(2,1)} %get-tuple-element.164.mixed_ref, f32[1024,768]{1,0:T(8,128)} %get-tuple-element.165.first_ref, ...), custom_call_target="tpu_custom_call" | custom-call | flops 15703474176 | bytes 44040192 | tf_op jit(solution)/shard_map/pallas_call | solution.py:293
  307.4 10.8 %select_reduce_fusion.1 = (f32[512]{0:T(512)S(1)}, f32[7680,512]{1,0:T(8,128)S(1)}) fusion(pred[7680]{0:T(1024)(128)(4,1)S(1)} %iota_compare_fusion.1, bf16[7680,768]{1,0:T(8,128)(2,1)} %pad.15, bf16[512,768]{1,0:T(8,128)(2,1)S(1)} %bitcast.265), kind=kOutput, calls=%fused_computation.7 | convolution fusion | flops 6047661568 | bytes 28321280 | tf_op jit(solution)/shard_map/dot_general | solution.py:870
  342.2 11.8 %fusion.98 = f32[512,768]{1,0:T(8,128)S(1)} fusion(bf16[7680,512]{1,0:T(8,128)(2,1)S(1)} %multiply_convert_fusion.dlogits_ref, bf16[7680,768]{1,0:T(8,128)(2,1)} %pad.15), kind=kOutput, calls=%fused_computation.271 | convolution fusion | flops 6039797760 | bytes 21233664 | tf_op jit(solution)/shard_map/dot_general | solution.py:870
  359.9 13.4 %collective-permute-done.43 = bf16[128,768]{1,0:T(8,128)(2,1)S(1)} collective-permute-done((bf16[128,768]{1,0:T(8,128)(2,1)S(1)}, bf16[128,768]{1,0:T(8,128)(2,1)S(1)}, u32[]{:S(2)}, u32[]{:S(2)}) %collective-permute-start.43) | collective-permute-done | bytes 196640 | tf_op jit(solution)/shard_map/ppermute | solution.py:724
  377.0 34.1 %shard_map.420 = (bf16[1024,768]{1,0:T(8,128)(2,1)}, bf16[1024,6144]{1,0:T(8,128)(2,1)}, f32[1024,768]{1,0:T(8,128)}, bf16[1024,768]{1,0:T(8,128)(2,1)}, bf16[1024,768]{1,0:T(8,128)(2,1)}, /*index=5*/f32[4,768]{1,0:T(4,128)}) custom-call(f32[1024,768]{1,0:T(8,128)} %scatter_custom_fusion.grad_ref, f32[1024,768]{1,0:T(8,128)} %get-tuple-element.170.second_sum_ref, ...), custom_call_target="tpu_custom_call" | custom-call | flops 15703474176 | bytes 44040192 | tf_op jit(solution)/shard_map/pallas_call | solution.py:378
  462.2 21.6 %shard_map.421 = (bf16[1024,256]{1,0:T(8,128)(2,1)}, bf16[1024,256]{1,0:T(8,128)(2,1)}, bf16[1024,256]{1,0:T(8,128)(2,1)}) custom-call(s32[1]{0:T(128)S(6)} %copy.137.length_ref, bf16[1024,768]{1,0:T(8,128)(2,1)} %get-tuple-element.161.q_ref, bf16[1024,768]{1,0:T(8,128)(2,1)} %get-tuple-element.162.k_ref, bf16[1024,768]{1,0:T(8,128)(2,1)} %get-tuple-element.163.v_ref, ...), custom_call_target="tpu_custom_call" | custom-call | flops 10737418240 | bytes 4194304 | tf_op jit(solution)/shard_map/pallas_call | solution.py:223
  494.4 21.8 %shard_map.422 = (bf16[1024,256]{1,0:T(8,128)(2,1)}, bf16[1024,256]{1,0:T(8,128)(2,1)}, bf16[1024,256]{1,0:T(8,128)(2,1)}) custom-call(s32[1]{0:T(128)S(6)} %copy.137.length_ref, bf16[1024,768]{1,0:T(8,128)(2,1)} %get-tuple-element.161.q_ref, bf16[1024,768]{1,0:T(8,128)(2,1)} %get-tuple-element.162.k_ref, bf16[1024,768]{1,0:T(8,128)(2,1)} %get-tuple-element.163.v_ref, ...), custom_call_target="tpu_custom_call" | custom-call | flops 10737418240 | bytes 4194304 | tf_op jit(solution)/shard_map/pallas_call | solution.py:223
  532.9 21.8 %shard_map.423 = (bf16[1024,256]{1,0:T(8,128)(2,1)}, bf16[1024,256]{1,0:T(8,128)(2,1)}, bf16[1024,256]{1,0:T(8,128)(2,1)}) custom-call(s32[1]{0:T(128)S(6)} %copy.137.length_ref, bf16[1024,768]{1,0:T(8,128)(2,1)} %get-tuple-element.161.q_ref, bf16[1024,768]{1,0:T(8,128)(2,1)} %get-tuple-element.162.k_ref, bf16[1024,768]{1,0:T(8,128)(2,1)} %get-tuple-element.163.v_ref, ...), custom_call_target="tpu_custom_call" | custom-call | flops 10737418240 | bytes 4194304 | tf_op jit(solution)/shard_map/pallas_call | solution.py:223
  576.8 9.8 fusion.100
  614.7 10.9 %collective-permute-done.74 = bf16[24,3072]{1,0:T(8,128)(2,1)S(1)} collective-permute-done((bf16[24,3072]{1,0:T(8,128)(2,1)S(1)}, bf16[24,3072]{1,0:T(8,128)(2,1)S(1)}, u32[]{:S(2)}, u32[]{:S(2)}) %collective-permute-start.74) | collective-permute-done | bytes 147488 | tf_op jit(solution)/shard_map/ppermute | solution.py:724
  626.8 13.5 %collective-permute-done.61 = bf16[4,2,24,3072]{3,2,0,1:T(8,128)(2,1)S(1)} collective-permute-done((bf16[4,2,24,3072]{3,2,0,1:T(8,128)(2,1)S(1)}, bf16[4,2,24,3072]{3,2,0,1:T(8,128)(2,1)S(1)}, u32[]{:S(2)}, u32[]{:S(2)}) %collective-permute-start.61) | collective-permute-done | bytes 1179680 | tf_op jit(solution)/shard_map/ppermute | solution.py:719
  643.8 8.9 collective-permute-done.77.refs_2_
  675.6 10.4 %collective-permute-done.64 = bf16[24,3072]{1,0:T(8,128)(2,1)S(1)} collective-permute-done((bf16[24,3072]{1,0:T(8,128)(2,1)S(1)}, bf16[24,3072]{1,0:T(8,128)(2,1)S(1)}, u32[]{:S(2)}, u32[]{:S(2)}) %collective-permute-start.64) | collective-permute-done | bytes 147488 | tf_op jit(solution)/shard_map/ppermute | solution.py:724
  717.8 16.8 %all-gather.2.cloned.1.call-done.embed_ref = bf16[4096,768]{1,0:T(8,128)(2,1)} async-done(((bf16[1024,768]{1,0:T(8,128)(2,1)}), bf16[4096,768]{1,0:T(8,128)(2,1)}) %all-gather.2.cloned.1.call-update) | async-done | bytes 6291472 | tf_op jit(solution)/shard_map/all_gather | solution.py:1058
  734.5 14.5 %shard_map.426 = bf16[4,960,768]{2,1,0:T(8,128)(2,1)} custom-call(s32[4]{0:T(128)} %add_subtract_fusion.chunks_ref, s32[9]{0:T(128)} %convert_reduce_fusion.1.starts_ref, s32[4104]{0:T(1024)} %pad.16.codes_ref, s32[4104]{0:T(1024)} %pad.17.order_ref, bf16[7680,512]{1,0:T(8,128)(2,1)} %copy-done, bf16[512,768]{1,0:T(8,128)(2,1)} %bitcast.266, ...), custom_call_target="tpu_custom_call" | custom-call | flops 3019898880 | bytes 23592960 | tf_op jit(solution)/shard_map/pallas_call | solution.py:531
  749.5 9.3 collective-permute-done.83.refs_0_
  761.4 16.1 %shard_map.427 = (bf16[2,960,384]{2,1,0:T(8,128)(2,1)}, f32[2,960,384]{2,1,0:T(8,128)}, bf16[2,960,384]{2,1,0:T(8,128)(2,1)}, f32[2,960,384]{2,1,0:T(8,128)}) custom-call(s32[4]{0:T(128)} %broadcast_add_fusion.chunks_ref, s32[9]{0:T(128)} %convert_reduce_fusion.1.starts_ref, s32[4104]{0:T(1024)} %pad.16.codes_ref, s32[4104]{0:T(1024)} %pad.17.order_ref, ...), custom_call_target="tpu_custom_call" | custom-call | flops 3019898880 | bytes 23592960 | tf_op jit(solution)/shard_map/pallas_call | solution.py:531
  780.4 30.1 %collective-permute-done.84 = bf16[2,960,384]{2,1,0:T(8,128)(2,1)S(1)} collective-permute-done((bf16[2,960,384]{2,1,0:T(8,128)(2,1)}, bf16[2,960,384]{2,1,0:T(8,128)(2,1)S(1)}, u32[]{:S(2)}, u32[]{:S(2)}) %collective-permute-start.84) | collective-permute-done | bytes 1474592 | tf_op jit(solution)/shard_map/ppermute | solution.py:719
  847.2 11.0 %collective-permute-done.91.rest_2_ = bf16[960,384]{1,0:T(8,128)(2,1)} collective-permute-done((bf16[960,384]{1,0:T(8,128)(2,1)}, bf16[960,384]{1,0:T(8,128)(2,1)}, u32[]{:S(2)}, u32[]{:S(2)}) %collective-permute-start.91) | collective-permute-done | bytes 737312 | tf_op jit(solution)/shard_map/ppermute | solution.py:719
  862.0 10.4 %collective-permute-done.90.rest_0_ = bf16[960,384]{1,0:T(8,128)(2,1)} collective-permute-done((bf16[960,384]{1,0:T(8,128)(2,1)}, bf16[960,384]{1,0:T(8,128)(2,1)}, u32[]{:S(2)}, u32[]{:S(2)}) %collective-permute-start.90) | collective-permute-done | bytes 737312 | tf_op jit(solution)/shard_map/ppermute | solution.py:719
  874.0 14.2 %collective-permute-done.92.rest_0_ = bf16[960,384]{1,0:T(8,128)(2,1)} collective-permute-done((bf16[960,384]{1,0:T(8,128)(2,1)}, bf16[960,384]{1,0:T(8,128)(2,1)}, u32[]{:S(2)}, u32[]{:S(2)}) %collective-permute-start.92) | collective-permute-done | bytes 737312 | tf_op jit(solution)/shard_map/ppermute | solution.py:719
  963.7 9.9 shard_map.432
  987.3 17.8 %shard_map.434 = (f32[7632,768]{1,0:T(8,128)}, f32[7632,768]{1,0:T(8,128)}, f32[16,1,480]{2,1,0:T(1,128)}) custom-call(s32[8]{0:T(128)} %iota_xor_fusion.slots_ref, f32[2]{0:T(128)} %pad_maximum_fusion.10.scalars_ref, bf16[960,384]{1,0:T(8,128)(2,1)} %collective-permute-done.99.rest_0_, ...), custom_call_target="tpu_custom_call", output_to_operand_aliasing={{0}: (13, {}), {1}: (14, {}), {2}: (15, {})} | custom-call | flops 29491200 | bytes 41287680 | tf_op jit(solution)/shard_map/pallas_call | solution.py:594
  (605 shorter events, 453.8 us)
Async XLA Ops:
  7.2 194.6 %reduce-scatter.2.cloned.1.call-start = ((), (), s32[]{:S(2)}) async-start(), calls=%async_computation.1 | async-start | bytes 7864320 | tf_op jit(solution)/shard_map/reduce_scatter | solution.py:962
  19.6 35.4 %collective-permute-start.8 = (bf16[192,768]{1,0:T(8,128)(2,1)}, bf16[192,768]{1,0:T(8,128)(2,1)S(1)}, u32[]{:S(2)}, u32[]{:S(2)}) collective-permute-start(bf16[192,768]{1,0:T(8,128)(2,1)} %dynamic-slice_convert_fusion.7), channel_id=1, source_target_pairs={{0,24},{8,0},{16,8},{24,16},{1,25},{9,1},{17,9},{25,17},{2,26},{10... | collective-permute-start | bytes 884744 | tf_op jit(solution)/shard_map/ppermute | solution.py:724
  23.6 31.4 %collective-permute-start.7 = (bf16[192,768]{1,0:T(8,128)(2,1)}, bf16[192,768]{1,0:T(8,128)(2,1)S(1)}, u32[]{:S(2)}, u32[]{:S(2)}) collective-permute-start(bf16[192,768]{1,0:T(8,128)(2,1)} %dynamic-slice_convert_fusion.7), channel_id=1, source_target_pairs={{0,16},{8,24},{16,0},{24,8},{1,17},{9,25},{17,1},{25,9},{2,18},{10... | collective-permute-start | bytes 884744 | tf_op jit(solution)/shard_map/ppermute | solution.py:724
  56.2 678.4 %all-gather.2.cloned.1.call-start = ((), (), s32[]{:S(2)}) async-start(), calls=%async_computation.2 | async-start | bytes 7864320 | tf_op jit(solution)/shard_map/all_gather | solution.py:1058
  61.2 37.1 %collective-permute-start.20 = (bf16[96,768]{1,0:T(8,128)(2,1)S(1)}, bf16[96,768]{1,0:T(8,128)(2,1)S(1)}, u32[]{:S(2)}, u32[]{:S(2)}) collective-permute-start(bf16[96,768]{1,0:T(8,128)(2,1)S(1)} %constant_dynamic-slice_fusion.6), channel_id=1, source_target_pairs={{0,16},{8,24},{16,0},{24,8},{1,17},{9,25},{17,1},{25,9},{2,18},{10... | collective-permute-start | bytes 442376 | tf_op jit(solution)/shard_map/ppermute | solution.py:724
  68.3 30.0 %collective-permute-start.19 = (bf16[96,768]{1,0:T(8,128)(2,1)S(1)}, bf16[96,768]{1,0:T(8,128)(2,1)S(1)}, u32[]{:S(2)}, u32[]{:S(2)}) collective-permute-start(bf16[96,768]{1,0:T(8,128)(2,1)S(1)} %constant_dynamic-slice_fusion.6), channel_id=1, source_target_pairs={{0,8},{8,16},{16,24},{24,0},{1,9},{9,17},{17,25},{25,1},{2,10},{10... | collective-permute-start | bytes 442376 | tf_op jit(solution)/shard_map/ppermute | solution.py:724
  68.8 34.0 %collective-permute-start.12 = (bf16[3,192,384]{2,1,0:T(8,128)(2,1)S(1)}, bf16[3,192,384]{2,1,0:T(8,128)(2,1)S(1)}, u32[]{:S(2)}, u32[]{:S(2)}) collective-permute-start(bf16[3,192,384]{2,1,0:T(8,128)(2,1)S(1)} %pad_maximum_fusion.5.refs_0_), channel_id=1, source_target_pairs={{0,1},{1,0},{2,3},{3,2},{4,5},{5,4},{6,7},{7,6},{8,9},{9,8},{10,11... | collective-permute-start | bytes 1327112 | tf_op jit(solution)/shard_map/ppermute | solution.py:719
  69.9 33.1 %collective-permute-start.13 = (bf16[3,192,384]{2,1,0:T(8,128)(2,1)S(1)}, bf16[3,192,384]{2,1,0:T(8,128)(2,1)S(1)}, u32[]{:S(2)}, u32[]{:S(2)}) collective-permute-start(bf16[3,192,384]{2,1,0:T(8,128)(2,1)S(1)} %pad_maximum_fusion.5.refs_0_), channel_id=1, source_target_pairs={{0,2},{1,3},{2,0},{3,1},{4,6},{5,7},{6,4},{7,5},{8,10},{9,11},{10,... | collective-permute-start | bytes 1327112 | tf_op jit(solution)/shard_map/ppermute | solution.py:719
  71.5 32.8 %collective-permute-start.15 = (bf16[3,192,384]{2,1,0:T(8,128)(2,1)S(1)}, bf16[3,192,384]{2,1,0:T(8,128)(2,1)S(1)}, u32[]{:S(2)}, u32[]{:S(2)}) collective-permute-start(bf16[3,192,384]{2,1,0:T(8,128)(2,1)S(1)} %pad_maximum_fusion.5.refs_0_), channel_id=1, source_target_pairs={{0,4},{1,5},{2,6},{3,7},{4,0},{5,1},{6,2},{7,3},{8,12},{9,13},{10,... | collective-permute-start | bytes 1327112 | tf_op jit(solution)/shard_map/ppermute | solution.py:719
  101.5 42.9 %collective-permute-start.9 = (bf16[3,192,768]{2,1,0:T(8,128)(2,1)S(1)}, bf16[3,192,768]{2,1,0:T(8,128)(2,1)S(1)}, u32[]{:S(2)}, u32[]{:S(2)}) collective-permute-start(bf16[3,192,768]{2,1,0:T(8,128)(2,1)S(1)} %pad_maximum_fusion.1.refs_0_), channel_id=1, source_target_pairs={{0,2},{1,3},{2,0},{3,1},{4,6},{5,7},{6,4},{7,5},{8,10},{9,11},{10,... | collective-permute-start | bytes 2654216 | tf_op jit(solution)/shard_map/ppermute | solution.py:719
  103.0 30.5 %collective-permute-start.25 = (bf16[3,96,768]{2,1,0:T(8,128)(2,1)S(1)}, bf16[3,96,768]{2,1,0:T(8,128)(2,1)S(1)}, u32[]{:S(2)}, u32[]{:S(2)}) collective-permute-start(bf16[3,96,768]{2,1,0:T(8,128)(2,1)S(1)} %pad_maximum_fusion.6.refs_0_), channel_id=1, source_target_pairs={{0,4},{1,5},{2,6},{3,7},{4,0},{5,1},{6,2},{7,3},{8,12},{9,13},{10,... | collective-permute-start | bytes 1327112 | tf_op jit(solution)/shard_map/ppermute | solution.py:719
  104.3 37.5 %collective-permute-start.17 = (bf16[3,192,384]{2,1,0:T(8,128)(2,1)S(1)}, bf16[3,192,384]{2,1,0:T(8,128)(2,1)S(1)}, u32[]{:S(2)}, u32[]{:S(2)}) collective-permute-start(bf16[3,192,384]{2,1,0:T(8,128)(2,1)S(1)} %collective-permute-done.15.refs_4_), channel_id=1, source_target_pairs={{0,2},{1,3},{2,0},{3,1},{4,6},{5,7},{6,4},{7,5},{8,10},{9,11},{10,... | collective-permute-start | bytes 1327112 | tf_op jit(solution)/shard_map/ppermute | solution.py:719
  105.6 37.4 %collective-permute-start.14 = (bf16[3,192,384]{2,1,0:T(8,128)(2,1)S(1)}, bf16[3,192,384]{2,1,0:T(8,128)(2,1)S(1)}, u32[]{:S(2)}, u32[]{:S(2)}) collective-permute-start(bf16[3,192,384]{2,1,0:T(8,128)(2,1)S(1)} %collective-permute-done.13.refs_2_), channel_id=1, source_target_pairs={{0,1},{1,0},{2,3},{3,2},{4,5},{5,4},{6,7},{7,6},{8,9},{9,8},{10,11... | collective-permute-start | bytes 1327112 | tf_op jit(solution)/shard_map/ppermute | solution.py:719
  143.0 41.1 %collective-permute-start.10 = (bf16[3,192,768]{2,1,0:T(8,128)(2,1)S(1)}, bf16[3,192,768]{2,1,0:T(8,128)(2,1)S(1)}, u32[]{:S(2)}, u32[]{:S(2)}) collective-permute-start(bf16[3,192,768]{2,1,0:T(8,128)(2,1)S(1)} %pad_maximum_fusion.1.refs_0_), channel_id=1, source_target_pairs={{0,4},{1,5},{2,6},{3,7},{4,0},{5,1},{6,2},{7,3},{8,12},{9,13},{10,... | collective-permute-start | bytes 2654216 | tf_op jit(solution)/shard_map/ppermute | solution.py:719
  144.3 39.8 %collective-permute-start.11 = (bf16[3,192,768]{2,1,0:T(8,128)(2,1)S(1)}, bf16[3,192,768]{2,1,0:T(8,128)(2,1)}, u32[]{:S(2)}, u32[]{:S(2)}) collective-permute-start(bf16[3,192,768]{2,1,0:T(8,128)(2,1)S(1)} %collective-permute-done.9.refs_2_), channel_id=1, source_target_pairs={{0,4},{1,5},{2,6},{3,7},{4,0},{5,1},{6,2},{7,3},{8,12},{9,13},{10,... | collective-permute-start | bytes 2654216 | tf_op jit(solution)/shard_map/ppermute | solution.py:719
  145.1 30.8 %collective-permute-start.26 = (bf16[3,96,768]{2,1,0:T(8,128)(2,1)S(1)}, bf16[3,96,768]{2,1,0:T(8,128)(2,1)}, u32[]{:S(2)}, u32[]{:S(2)}) collective-permute-start(bf16[3,96,768]{2,1,0:T(8,128)(2,1)S(1)} %collective-permute-done.25.refs_4_), channel_id=1, source_target_pairs={{0,1},{1,0},{2,3},{3,2},{4,5},{5,4},{6,7},{7,6},{8,9},{9,8},{10,11... | collective-permute-start | bytes 1327112 | tf_op jit(solution)/shard_map/ppermute | solution.py:719
  419.3 32.8 %collective-permute-start.45 = (bf16[4,4,96,768]{3,2,1,0:T(8,128)(2,1)S(1)}, bf16[4,4,96,768]{3,2,1,0:T(8,128)(2,1)}, u32[]{:S(2)}, u32[]{:S(2)}) collective-permute-start(bf16[4,4,96,768]{3,2,1,0:T(8,128)(2,1)S(1)} %fusion.16), channel_id=1, source_target_pairs={{0,1},{1,0},{2,3},{3,2},{4,5},{5,4},{6,7},{7,6},{8,9},{9,8},{10,11... | collective-permute-start | bytes 7077896 | tf_op jit(solution)/shard_map/ppermute | solution.py:719
  450.8 33.1 %collective-permute-start.49 = (bf16[4,2,24,3072]{3,2,0,1:T(8,128)(2,1)}, bf16[4,2,24,3072]{3,2,0,1:T(8,128)(2,1)}, u32[]{:S(2)}, u32[]{:S(2)}) collective-permute-start(bf16[4,2,24,3072]{3,2,0,1:T(8,128)(2,1)} %fusion.27), channel_id=1, source_target_pairs={{0,2},{1,3},{2,0},{3,1},{4,6},{5,7},{6,4},{7,5},{8,10},{9,11},{10,... | collective-permute-start | bytes 3538952 | tf_op jit(solution)/shard_map/ppermute | solution.py:719
  462.0 54.2 %collective-permute-start.52 = (bf16[4,2,24,3072]{3,2,0,1:T(8,128)(2,1)S(1)}, bf16[4,2,24,3072]{3,2,0,1:T(8,128)(2,1)}, u32[]{:S(2)}, u32[]{:S(2)}) collective-permute-start(bf16[4,2,24,3072]{3,2,0,1:T(8,128)(2,1)S(1)} %fusion.26), channel_id=1, source_target_pairs={{0,4},{1,5},{2,6},{3,7},{4,0},{5,1},{6,2},{7,3},{8,12},{9,13},{10,... | collective-permute-start | bytes 3538952 | tf_op jit(solution)/shard_map/ppermute | solution.py:719
  493.1 33.2 %collective-permute-start.51 = (bf16[4,24,3072]{2,1,0:T(8,128)(2,1)S(1)}, bf16[4,24,3072]{2,1,0:T(8,128)(2,1)}, u32[]{:S(2)}, u32[]{:S(2)}) collective-permute-start(bf16[4,24,3072]{2,1,0:T(8,128)(2,1)S(1)} %fusion.35), channel_id=1, source_target_pairs={{0,4},{1,5},{2,6},{3,7},{4,0},{5,1},{6,2},{7,3},{8,12},{9,13},{10,... | collective-permute-start | bytes 1769480 | tf_op jit(solution)/shard_map/ppermute | solution.py:719
  518.0 36.8 %collective-permute-start.59 = (bf16[4,24,3072]{2,1,0:T(8,128)(2,1)S(1)}, bf16[4,24,3072]{2,1,0:T(8,128)(2,1)S(1)}, u32[]{:S(2)}, u32[]{:S(2)}) collective-permute-start(bf16[4,24,3072]{2,1,0:T(8,128)(2,1)S(1)} %fusion.36), channel_id=1, source_target_pairs={{0,2},{1,3},{2,0},{3,1},{4,6},{5,7},{6,4},{7,5},{8,10},{9,11},{10,... | collective-permute-start | bytes 1769480 | tf_op jit(solution)/shard_map/ppermute | solution.py:719
  528.5 30.6 %collective-permute-start.54 = (bf16[96,768]{1,0:T(8,128)(2,1)}, bf16[96,768]{1,0:T(8,128)(2,1)S(1)}, u32[]{:S(2)}, u32[]{:S(2)}) collective-permute-start(bf16[96,768]{1,0:T(8,128)(2,1)} %get-tuple-element.307), channel_id=1, source_target_pairs={{0,16},{8,24},{16,0},{24,8},{1,17},{9,25},{17,1},{25,9},{2,18},{10... | collective-permute-start | bytes 442376 | tf_op jit(solution)/shard_map/ppermute | solution.py:724
  658.1 35.1 %collective-permute-start.63 = (bf16[24,3072]{1,0:T(8,128)(2,1)S(1)}, bf16[24,3072]{1,0:T(8,128)(2,1)S(1)}, u32[]{:S(2)}, u32[]{:S(2)}) collective-permute-start(bf16[24,3072]{1,0:T(8,128)(2,1)S(1)} %get-tuple-element.297), channel_id=1, source_target_pairs={{0,8},{8,16},{16,24},{24,0},{1,9},{9,17},{17,25},{25,1},{2,10},{10... | collective-permute-start | bytes 442376 | tf_op jit(solution)/shard_map/ppermute | solution.py:724
  663.8 30.8 %collective-permute-start.76 = (bf16[24,9216]{1,0:T(8,128)(2,1)S(1)}, bf16[24,9216]{1,0:T(8,128)(2,1)S(1)}, u32[]{:S(2)}, u32[]{:S(2)}) collective-permute-start(bf16[24,9216]{1,0:T(8,128)(2,1)S(1)} %pad_maximum_fusion.7.refs_0_), channel_id=1, source_target_pairs={{0,1},{1,0},{2,3},{3,2},{4,5},{5,4},{6,7},{7,6},{8,9},{9,8},{10,11... | collective-permute-start | bytes 1327112 | tf_op jit(solution)/shard_map/ppermute | solution.py:719
  777.5 33.0 %collective-permute-start.84 = (bf16[2,960,384]{2,1,0:T(8,128)(2,1)}, bf16[2,960,384]{2,1,0:T(8,128)(2,1)S(1)}, u32[]{:S(2)}, u32[]{:S(2)}) collective-permute-start(bf16[2,960,384]{2,1,0:T(8,128)(2,1)} %get-tuple-element.225), channel_id=1, source_target_pairs={{0,2},{1,3},{2,0},{3,1},{4,6},{5,7},{6,4},{7,5},{8,10},{9,11},{10,... | collective-permute-start | bytes 4423688 | tf_op jit(solution)/shard_map/ppermute | solution.py:719
  779.1 36.1 %collective-permute-start.86 = (bf16[2,960,384]{2,1,0:T(8,128)(2,1)}, bf16[2,960,384]{2,1,0:T(8,128)(2,1)S(1)}, u32[]{:S(2)}, u32[]{:S(2)}) collective-permute-start(bf16[2,960,384]{2,1,0:T(8,128)(2,1)} %get-tuple-element.227), channel_id=1, source_target_pairs={{0,4},{1,5},{2,6},{3,7},{4,0},{5,1},{6,2},{7,3},{8,12},{9,13},{10,... | collective-permute-start | bytes 4423688 | tf_op jit(solution)/shard_map/ppermute | solution.py:719
  858.8 31.0 %collective-permute-start.95 = (bf16[960,384]{1,0:T(8,128)(2,1)}, bf16[960,384]{1,0:T(8,128)(2,1)}, u32[]{:S(2)}, u32[]{:S(2)}) collective-permute-start(bf16[960,384]{1,0:T(8,128)(2,1)} %collective-permute-done.93.rest_1_), channel_id=1, source_target_pairs={{0,4},{1,5},{2,6},{3,7},{4,0},{5,1},{6,2},{7,3},{8,12},{9,13},{10,... | collective-permute-start | bytes 2211848 | tf_op jit(solution)/shard_map/ppermute | solution.py:719
  907.6 74.3 %collective-permute-start.99 = (bf16[960,384]{1,0:T(8,128)(2,1)}, bf16[960,384]{1,0:T(8,128)(2,1)}, u32[]{:S(2)}, u32[]{:S(2)}) collective-permute-start(bf16[960,384]{1,0:T(8,128)(2,1)} %get-tuple-element.236.rest_0_), channel_id=1, source_target_pairs={{0,1},{1,0},{2,3},{3,2},{4,5},{5,4},{6,7},{7,6},{8,9},{9,8},{10,11... | collective-permute-start | bytes 2211848 | tf_op jit(solution)/shard_map/ppermute | solution.py:719
  908.5 73.5 %collective-permute-start.100 = (bf16[960,384]{1,0:T(8,128)(2,1)}, bf16[960,384]{1,0:T(8,128)(2,1)}, u32[]{:S(2)}, u32[]{:S(2)}) collective-permute-start(bf16[960,384]{1,0:T(8,128)(2,1)} %get-tuple-element.237.rest_1_), channel_id=1, source_target_pairs={{0,1},{1,0},{2,3},{3,2},{4,5},{5,4},{6,7},{7,6},{8,9},{9,8},{10,11... | collective-permute-start | bytes 2211848 | tf_op jit(solution)/shard_map/ppermute | solution.py:719
  908.5 73.8 %collective-permute-start.101 = (bf16[960,384]{1,0:T(8,128)(2,1)}, bf16[960,384]{1,0:T(8,128)(2,1)}, u32[]{:S(2)}, u32[]{:S(2)}) collective-permute-start(bf16[960,384]{1,0:T(8,128)(2,1)} %collective-permute-done.90.rest_0_), channel_id=1, source_target_pairs={{0,1},{1,0},{2,3},{3,2},{4,5},{5,4},{6,7},{7,6},{8,9},{9,8},{10,11... | collective-permute-start | bytes 2211848 | tf_op jit(solution)/shard_map/ppermute | solution.py:719
  909.0 75.8 %collective-permute-start.102 = (bf16[960,384]{1,0:T(8,128)(2,1)}, bf16[960,384]{1,0:T(8,128)(2,1)}, u32[]{:S(2)}, u32[]{:S(2)}) collective-permute-start(bf16[960,384]{1,0:T(8,128)(2,1)} %collective-permute-done.93.rest_1_), channel_id=1, source_target_pairs={{0,1},{1,0},{2,3},{3,2},{4,5},{5,4},{6,7},{7,6},{8,9},{9,8},{10,11... | collective-permute-start | bytes 2211848 | tf_op jit(solution)/shard_map/ppermute | solution.py:719
  911.4 73.4 %collective-permute-start.103 = (bf16[960,384]{1,0:T(8,128)(2,1)}, bf16[960,384]{1,0:T(8,128)(2,1)}, u32[]{:S(2)}, u32[]{:S(2)}) collective-permute-start(bf16[960,384]{1,0:T(8,128)(2,1)} %collective-permute-done.91.rest_2_), channel_id=1, source_target_pairs={{0,1},{1,0},{2,3},{3,2},{4,5},{5,4},{6,7},{7,6},{8,9},{9,8},{10,11... | collective-permute-start | bytes 2211848 | tf_op jit(solution)/shard_map/ppermute | solution.py:719
  (182 other events, 2691.0 us)
Sparse Core Ops, SparseCore 0:
  56.3 124.7 reduce-scatter.1
  602.7 131.8 all-gather.1
